TPU v7x, 256 devices: a whole 4x4x8 slice. The times are simulated.
256 devices in a mesh: seq: 32 (over y, z_hi, x), tensor: 8 (over z_lo, core).
Axes of the slice: x: 4, y: 4, z: 8 (z_hi: 2, z_lo: 4; z = z_hi * 4 + z_lo), core: 2. Of those that a mesh axis runs over, the one named last changes fastest.
Arguments:
- tokens: bfloat16 [16384, 4096], P('seq', 'tensor'), may hold values from -6 to 6
- prior_rows: bfloat16 [129, 4096], P(None, 'tensor'), may hold values from -6 to 6
- norm_gain: bfloat16 [4096], P('tensor'), may hold values from 0.25 to 1.75
- in_weight: bfloat16 [3, 4096, 4096], P(None, 'seq', 'tensor'), may hold values from -0.09375 to 0.09375
- short_filter: float32 [3, 3, 4096], P(None, None, 'tensor'), may hold values from -3 to 3
- mr_filter: bfloat16 [256, 128], P('tensor'), may hold values from -3 to 3
- mr_bias: float32 [4096], P('tensor'), may hold values from -4 to 4
- out_weight: bfloat16 [4096, 4096], P('tensor', 'seq'), may hold values from -0.09375 to 0.09375
Outputs:
- block_out: bfloat16 [16384, 4096], P('seq', 'tensor')
All inputs are finite; a program needn't handle non-finite values.
Results may differ from a plain program's by a relative error of at most 0.02.
Values may be sent and summed in bfloat16 or wider, within the bound.
No kernel may reach another device: no remote copies, remote signals or barrier semaphores. Data moves between devices by JAX's collectives and lax.ppermute only.
A program may use at most 128 MiB of HBM per device.

v0:
```python
import jax
import jax.numpy as jnp
from jax import lax
from jax.sharding import PartitionSpec as P

GSIZE = 16


def passed_along(array, axis, by):
    size = lax.axis_size(axis)
    pairs = [(i, i + by) for i in range(size) if 0 <= i + by < size]
    return lax.ppermute(array, axis, pairs)


def featurize(projected, short_taps):
    lifted = projected.astype(jnp.float32)
    count = lifted.shape[1]
    return (
        short_taps[0][:, None, :] * lifted[:, 2:]
        + short_taps[1][:, None, :] * lifted[:, 1 : count - 1]
        + short_taps[2][:, None, :] * lifted[:, 0 : count - 2]
    )


def toeplitz_pair(filters):
    length = filters.shape[1]
    shape3 = (length, length, length)
    tap_index = lax.broadcasted_iota(jnp.int32, shape3, 0)
    row_index = lax.broadcasted_iota(jnp.int32, shape3, 1)
    col_index = lax.broadcasted_iota(jnp.int32, shape3, 2)
    lagged = row_index - col_index
    current_table = (lagged == tap_index).astype(jnp.bfloat16)
    earlier_table = (lagged + length == tap_index).astype(jnp.bfloat16)
    current_mat = jnp.einsum(
        "gj,jik->gik", filters, current_table, preferred_element_type=jnp.float32
    ).astype(jnp.bfloat16)
    earlier_mat = jnp.einsum(
        "gj,jik->gik", filters, earlier_table, preferred_element_type=jnp.float32
    ).astype(jnp.bfloat16)
    return (current_mat, earlier_mat)


def on_device(
    tokens, prior_rows, norm_gain, in_weight, short_filter, mr_filter, mr_bias, out_weight
):
    leading = lax.axis_index("seq") == 0
    past_rows = prior_rows.shape[0]
    own_rows = tokens.shape[0]
    channels = in_weight.shape[2]
    length = mr_filter.shape[1]
    front_full, token_full, gain_full = (
        lax.all_gather(prior_rows, "tensor", axis=1, tiled=True),
        lax.all_gather(tokens, "tensor", axis=1, tiled=True),
        lax.all_gather(norm_gain, "tensor", axis=0, tiled=True),
    )
    all_rows = jnp.concatenate([front_full, token_full], 0).astype(jnp.float32)
    inv_rms = lax.rsqrt(jnp.mean(all_rows * all_rows, axis=-1, keepdims=True) + 1e-06)
    normed = (all_rows * inv_rms * gain_full.astype(jnp.float32)[None, :]).astype(jnp.bfloat16)
    projected = jnp.einsum(
        "rd,sdc->src",
        normed,
        lax.all_gather(in_weight, "seq", axis=1, tiled=True),
        preferred_element_type=jnp.float32,
    )
    projected = projected.astype(jnp.bfloat16)
    zero_row = jnp.zeros((1, channels), jnp.bfloat16)
    front_proj = projected[:, :past_rows]
    own_proj = projected[:, past_rows:]
    sent_proj = passed_along(own_proj[:, own_rows - 2 :], "seq", 1)
    halo_proj = jnp.where(leading, front_proj[:, past_rows - 2 :], sent_proj)
    own_feats = featurize(jnp.concatenate([halo_proj, own_proj], 1), short_filter)
    mix_own = (own_feats[1] * own_feats[2]).astype(jnp.bfloat16)
    front_feats = featurize(front_proj, short_filter)
    mix_front = (front_feats[1] * front_feats[2]).astype(jnp.bfloat16)
    sent_mix = passed_along(mix_own[own_rows - (length - 1) :], "seq", 1)
    halo_mix = jnp.where(leading, mix_front, sent_mix)
    padded_mix = jnp.concatenate([zero_row, halo_mix, mix_own], 0)
    query_rows = own_feats[0]
    current_mat, earlier_mat = toeplitz_pair(mr_filter)
    blocks = own_rows // length
    groups = channels // GSIZE
    current_blk = padded_mix[length:].reshape(blocks, length, groups, GSIZE)
    previous_blk = padded_mix[:own_rows].reshape(blocks, length, groups, GSIZE)
    filtered = jnp.einsum(
        "gik,bkgc->bigc", current_mat, current_blk, preferred_element_type=jnp.float32
    )
    filtered = filtered + jnp.einsum(
        "gik,bkgc->bigc", earlier_mat, previous_blk, preferred_element_type=jnp.float32
    )
    filtered = filtered.reshape(own_rows, channels)
    gated = (query_rows * (filtered + mr_bias[None, :] * mix_own.astype(jnp.float32))).astype(
        jnp.bfloat16
    )
    partial_terms = jnp.dot(
        gated,
        lax.all_gather(out_weight, "seq", axis=1, tiled=True),
        preferred_element_type=jnp.float32,
    )
    summed = lax.psum_scatter(
        partial_terms.astype(jnp.bfloat16), "tensor", scatter_dimension=1, tiled=True
    ).astype(jnp.float32)
    return (tokens.astype(jnp.float32) + summed).astype(jnp.bfloat16)


def solution(mesh):
    in_specs = (
        P("seq", "tensor"),
        P(None, "tensor"),
        P("tensor"),
        P(None, "seq", "tensor"),
        P(None, None, "tensor"),
        P("tensor", None),
        P("tensor"),
        P("tensor", "seq"),
    )
    out_specs = P("seq", "tensor")
    return jax.shard_map(
        on_device, mesh=mesh, in_specs=in_specs, out_specs=out_specs, check_vma=False
    )
```

profile of v0, /device:TPU:2, one launch (start us, length us, event | category | flops | bytes accessed | tf_op | source)
XLA Modules:
  0.0 508.5 jit_solution(16719892571564181593)
XLA Ops:
  6.5 0.7 all-gather.6.cloned.1.call-update
  7.3 0.0 all-gather.8.cloned.1.call-start
  7.3 0.7 all-gather.8.cloned.1.call-update
  8.0 0.0 all-gather.10.cloned.1.call-start
  8.1 0.7 all-gather.10.cloned.1.call-update
  8.7 0.0 all-gather.12.cloned.1.call-start
  8.8 0.5 all-gather.12.cloned.1.call-update
  9.3 0.0 reduce-scatter.2.cloned.1.call-start
  9.4 0.7 reshape.31
  10.1 13.6 %all-gather = bf16[8,1,512]{2,1,0:T(2,128)(2,1)S(1)} all-gather(bf16[1,1,512]{2,1,0:T(2,128)(2,1)S(1)} %reshape.31), channel_id=1, replica_groups=mesh['seq'=32,'tensor'=8] {'tensor'}, dimensions={0}, use_global_device_ids=true | all-gather | bytes 9216 | tf_op jit(solution)/shard_map/all_gather | solution.py:54
  23.7 0.0 copy-start.5
  23.7 0.0 copy-done
  23.7 2.1 fusion.17
  25.8 2.0 fusion.18
  27.9 21.8 %all-gather.6.cloned.1.call-done = bf16[129,4096]{1,0:T(8,128)(2,1)} async-done(((bf16[129,512]{1,0:T(8,128)(2,1)}), bf16[129,4096]{1,0:T(8,128)(2,1)}) %all-gather.6.cloned.1.call-update) | async-done | bytes 1056784 | tf_op jit(solution)/shard_map/all_gather | solution.py:52
  49.7 55.4 %all-gather.8.cloned.1.call-done = bf16[512,4096]{1,0:T(8,128)(2,1)} async-done(((bf16[512,512]{1,0:T(8,128)(2,1)}), bf16[512,4096]{1,0:T(8,128)(2,1)}) %all-gather.8.cloned.1.call-update) | async-done | bytes 4194320 | tf_op jit(solution)/shard_map/all_gather | solution.py:53
  105.1 4.6 fusion
  109.7 197.4 %all-gather.10.cloned.1.call-done = bf16[3,4096,512]{2,1,0:T(8,128)(2,1)} async-done(((bf16[3,128,512]{2,1,0:T(8,128)(2,1)}), bf16[3,4096,512]{2,1,0:T(8,128)(2,1)}) %all-gather.10.cloned.1.call-update) | async-done | bytes 12582928 | tf_op jit(solution)/shard_map/all_gather | solution.py:62
  307.2 13.9 %convert_bitcast_fusion = bf16[3,641,512]{2,1,0:T(8,128)(2,1)S(1)} fusion(bf16[3,4096,512]{2,1,0:T(8,128)(2,1)} %all-gather.10.cloned.1.call-done, f32[4096]{0:T(1024)S(1)} %bitcast.64, f32[641]{0:T(1024)S(1)} %add_rsqrt_fusion, bf16[512,4096]{1,0:T(8,128)(2,1)} %all-gather.8.cloned.1.call-done, bf16[129,4096]{1,0:T(8,128)(2,1)S(1)} %copy-done.3), kind=kOutput, calls=%fused_computation.22 | convolution fusion | flops 8085009920 | bytes 19822084 | tf_op jit(solution)/shard_map/rd,sdc->src/dot_general | solution.py:59
  321.1 3.4 collective-permute-start
  324.4 0.1 slice_convert_fusion
  324.5 1.2 fusion.26
  325.7 0.4 slice.91
  326.1 0.5 collective-permute-done
  326.6 0.5 maximum_convert_fusion
  327.1 0.9 fusion.11
  328.0 0.9 fusion.20
  329.0 2.1 copy.18
  331.0 0.9 slice_bitcast_fusion.1
  332.0 3.5 collective-permute-start.1
  335.5 2.0 convert_element_type.77
  337.5 3.3 fusion.24
  340.8 0.2 fusion.42
  340.9 0.0 collective-permute-done.1
  340.9 0.0 copy-done.1
  340.9 0.1 fusion.34
  341.0 1.0 pad_maximum_fusion.2
  342.0 2.1 copy.21
  344.1 2.0 reshape.29
  346.0 2.5 fusion.19
  348.6 0.4 copy.24
  349.0 1.1 copy.42
  350.1 2.5 copy.25
  352.6 88.9 %all-gather.12.cloned.1.call-done = bf16[512,4096]{1,0:T(8,128)(2,1)} async-done(((bf16[512,128]{1,0:T(8,128)(2,1)}), bf16[512,4096]{1,0:T(8,128)(2,1)}) %all-gather.12.cloned.1.call-update) | async-done | bytes 4194320 | tf_op jit(solution)/shard_map/all_gather | solution.py:96
  441.5 7.0 %convolution_convert_fusion = bf16[512,4096]{1,0:T(8,128)(2,1)} fusion(bf16[512,4096]{1,0:T(8,128)(2,1)} %all-gather.12.cloned.1.call-done, f32[3,512,512]{2,1,0:T(8,128)S(1)} %fusion.11, f32[512,512]{1,0:T(8,128)} %copy.25, f32[512]{0:T(512)S(1)} %copy-done.6, bf16[1,512,512]{2,1,0:T(8,128)(2,1)} %fusion.20), kind=kOutput, calls=%fused_computation.10 | convolution fusion | flops 2150891520 | bytes 11012096 | tf_op jit(solution)/shard_map/dot_general | solution.py:94
  448.5 0.0 reduce-scatter.2.cloned.1.call-update
  448.5 51.5 %reduce-scatter.2.cloned.1.call-done = bf16[512,512]{1,0:T(8,128)(2,1)} async-done(((bf16[512,4096]{1,0:T(8,128)(2,1)}), bf16[512,512]{1,0:T(8,128)(2,1)}) %reduce-scatter.2.cloned.1.call-update) | async-done | bytes 524304 | tf_op jit(solution)/shard_map/reduce_scatter | solution.py:99
  500.0 2.0 add_convert_fusion
  (20 shorter events, 0.1 us)
Async XLA Ops:
  6.5 17.2 %copy-start = (bf16[32,128]{1,0:T(8,128)(2,1)S(1)}, bf16[32,128]{1,0:T(8,128)(2,1)}, u32[]{:S(2)}) copy-start(bf16[32,128]{1,0:T(8,128)(2,1)} %param.13) | copy-start | bytes 24580
  6.5 19.3 %copy-start.4 = (f32[3,3,512]{2,1,0:T(4,128)S(1)}, f32[3,3,512]{2,1,0:T(4,128)}, u32[]{:S(2)}) copy-start(f32[3,3,512]{2,1,0:T(4,128)} %param.12) | copy-start | bytes 55300
  6.5 43.1 %all-gather.6.cloned.1.call-start = ((), (), s32[]{:S(2)}) async-start(), calls=%async_computation.1 | async-start | bytes 1253376 | tf_op jit(solution)/shard_map/all_gather | solution.py:52
  7.3 97.8 %all-gather.8.cloned.1.call-start = ((), (), s32[]{:S(2)}) async-start(), calls=%async_computation.2 | async-start | bytes 4718592 | tf_op jit(solution)/shard_map/all_gather | solution.py:53
  8.0 299.1 %all-gather.10.cloned.1.call-start = ((), (), s32[]{:S(2)}) async-start(), calls=%async_computation.3 | async-start | bytes 12976128 | tf_op jit(solution)/shard_map/all_gather | solution.py:62
  8.7 432.7 %all-gather.12.cloned.1.call-start = ((), (), s32[]{:S(2)}) async-start(), calls=%async_computation.4 | async-start | bytes 4325376 | tf_op jit(solution)/shard_map/all_gather | solution.py:96
  9.3 490.6 %reduce-scatter.2.cloned.1.call-start = ((), (), s32[]{:S(2)}) async-start(), calls=%async_computation.5 | async-start | bytes 4718592 | tf_op jit(solution)/shard_map/reduce_scatter | solution.py:99
  23.7 4.2 copy-start.5
  49.7 257.5 %copy-start.3 = (bf16[129,4096]{1,0:T(8,128)(2,1)S(1)}, bf16[129,4096]{1,0:T(8,128)(2,1)}, u32[]{:S(2)}) copy-start(bf16[129,4096]{1,0:T(8,128)(2,1)} %all-gather.6.cloned.1.call-done) | copy-start | bytes 3170308
  321.1 5.5 %collective-permute-start = (bf16[3,2,512]{2,1,0:T(2,128)(2,1)S(1)}, bf16[3,2,512]{2,1,0:T(2,128)(2,1)S(1)}, u32[]{:S(2)}, u32[]{:S(2)}) collective-permute-start(bf16[3,2,512]{2,1,0:T(2,128)(2,1)S(1)} %slice.90), channel_id=1, source_target_pairs={{0,8},{8,16},{16,24},{24,32},{32,40},{40,48},{48,56},{56,64},{64,7... | collective-permute-start | bytes 18440 | tf_op jit(solution)/shard_map/ppermute | solution.py:12
  329.0 12.0 %slice-start = ((bf16[640]{0:T(1024)(128)(2,1)}), bf16[512]{0:T(512)(128)(2,1)S(1)}, s32[]{:S(2)}) async-start(bf16[640]{0:T(1024)(128)(2,1)} %copy-done.5), calls=%async_computation.6 | async-start | bytes 2048 | tf_op jit(solution)/shard_map/slice | solution.py:83
  332.0 9.0 %collective-permute-start.1 = (bf16[127,512]{1,0:T(8,128)(2,1)S(1)}, bf16[127,512]{1,0:T(8,128)(2,1)S(1)}, u32[]{:S(2)}, u32[]{:S(2)}) collective-permute-start(bf16[127,512]{1,0:T(8,128)(2,1)S(1)} %slice_bitcast_fusion.1), channel_id=1, source_target_pairs={{0,8},{8,16},{16,24},{24,32},{32,40},{40,48},{48,56},{56,64},{64,7... | collective-permute-start | bytes 390152 | tf_op jit(solution)/shard_map/ppermute | solution.py:12
  337.5 3.4 copy-start.1
  346.0 95.4 %copy-start.6 = (f32[512]{0:T(512)S(1)}, f32[512]{0:T(512)}, u32[]{:S(2)}) copy-start(f32[512]{0:T(512)} %param.14) | copy-start | bytes 6148
  448.5 51.5 %copy-start.2 = (bf16[512,512]{1,0:T(8,128)(2,1)S(1)}, bf16[512,512]{1,0:T(8,128)(2,1)}, u32[]{:S(2)}) copy-start(bf16[512,512]{1,0:T(8,128)(2,1)} %param.8) | copy-start | bytes 1572868
Sparse Core Ops, SparseCore 0:
  9.2 40.4 all-gather.5
  51.5 53.5 all-gather.7
  108.6 198.4 all-gather.9
  310.2 131.1 all-gather.11
  448.6 51.2 reduce-scatter.1
where the time goes:
time: 509 us; the launch traced here: 508 us
  waiting for transfers between devices  418 us (82%)
  matrix products  30.9 us (6%)
  local copies, waits for them, and re-layouts  14.1 us (3%)
  blocking collectives  13.6 us (3%)
  between operations  13.3 us (3%)
  other arithmetic  11.4 us (2%)
  starting transfers between devices  7.07 us (1%)
    all_gather x1, waiting for transfers between devices, on_device(): lax.all_gather(in_weight, 'seq', axis=1, tiled=True)  197 us
    all_gather x1, waiting for transfers between devices, on_device(): lax.all_gather(out_weight, 'seq', axis=1, tiled=True)  88.9 us
    all_gather x1, waiting for transfers between devices, on_device(): lax.all_gather(tokens, 'tensor', axis=1, tiled=True)  55.4 us
    reduce_scatter x1, waiting for transfers between devices, on_device(): lax.psum_scatter(partial_terms.astype(jnp.bfloat16), 'tensor', scatter_di...  51.5 us
    all_gather x1, waiting for transfers between devices, on_device(): lax.all_gather(prior_rows, 'tensor', axis=1, tiled=True)  21.8 us
    dot_general x1, matrix products, on_device(): jnp.einsum('rd,sdc->src', normed, lax.all_gather(in_weight, 'seq', axis=1...  13.9 us
    all_gather x1, blocking collectives, on_device(): lax.all_gather(norm_gain, 'tensor', axis=0, tiled=True)  13.6 us
  transfers between devices with their start and end apart: 7, of which 6 were waited for; matrix products, arithmetic and copies ran while one was open for 9% of the time, Pallas kernels for 0%

commit v1 on v0

v1 whole, which is shorter than its diff:
```python
import functools

import jax
import jax.numpy as jnp
from jax import lax
from jax.experimental import pallas as pl
from jax.experimental.pallas import tpu as pltpu
from jax.sharding import Mesh, PartitionSpec as P

GSIZE = 16
LH = 128
ROWS = 512
FRONT = 80
WIDE = 512
CH = 256
GROUPS = CH // GSIZE
HALO = LH + 16
VMEM = 48 * 1024 * 1024
F32 = jnp.float32
BF16 = jnp.bfloat16


def row_iota(shape):
    return lax.broadcasted_iota(jnp.int32, shape, 0)


def three_taps(rows, taps, s):
    return (
        taps[0, s : s + 1] * rows
        + taps[1, s : s + 1] * pltpu.roll(rows, 1, 0)
        + taps[2, s : s + 1] * pltpu.roll(rows, 2, 0)
    )


def project_kernel(x_ref, w_ref, gain_ref, taps_ref, proj_ref, tail_ref, front_ref, acc, ssq):
    step = pl.program_id(0)

    @pl.when(step == 0)
    def _():
        acc[...] = jnp.zeros_like(acc)
        ssq[...] = jnp.zeros_like(ssq)

    for h in range(2):
        parts = []
        for u in range(2):
            lifted = x_ref[h, u].astype(F32)
            ssq[h] += jnp.sum(lifted * lifted, axis=-1, keepdims=True)
            parts.append((lifted * gain_ref[0, u : u + 1]).astype(BF16))
        scaled = jnp.concatenate(parts, axis=1)
        for s in range(3):
            weights = jnp.concatenate(
                [w_ref[x, u, s] for u in range(2) for x in range(4)], axis=0
            )
            acc[h, s] += jnp.dot(scaled, weights, preferred_element_type=F32)

    @pl.when(step == pl.num_programs(0) - 1)
    def _():
        edges = []
        fronts = []
        for h in range(2):
            inv = lax.rsqrt(ssq[h] * (1.0 / 4096.0) + 1e-6)
            ends = []
            heads = []
            for s in range(3):
                rounded = (acc[h, s] * inv).astype(BF16)
                proj_ref[s, h] = rounded[:ROWS]
                ends.append(rounded[ROWS - HALO : ROWS].astype(F32))
                heads.append(rounded[ROWS:].astype(F32))
            edges.append(ends)
            fronts.append(heads)
        place = row_iota((16, CH)) // 2
        for h in range(2):
            mixing = three_taps(edges[h][1], taps_ref, 1) * three_taps(edges[h][2], taps_ref, 2)
            tail_ref[h, :LH] = mixing[HALO - LH :].astype(BF16)
            last = jnp.zeros((16, CH), F32)
            for s in range(3):
                moved = pltpu.roll(edges[h][s][HALO - 16 :], (2 * s + 2) % 16, 0)
                last = jnp.where(place == s, moved, last)
            tail_ref[h, LH:] = last.astype(BF16)
        ahead = [jnp.concatenate([fronts[0][s], fronts[1][s]], axis=0) for s in range(3)]
        mixing = three_taps(ahead[1], taps_ref, 1) * three_taps(ahead[2], taps_ref, 2)
        front_ref[:LH] = pltpu.roll(mixing, 2 * FRONT - 1, 0)[:LH].astype(BF16)
        last = jnp.zeros((16, CH), F32)
        for s in range(3):
            moved = pltpu.roll(ahead[s][LH - 8 : LH + 8], (2 * s - 7) % 16, 0)
            last = jnp.where(place == s, moved, last)
        front_ref[LH:] = last.astype(BF16)


def project(gathered, weights, gain, taps):
    count = ROWS + FRONT
    return pl.pallas_call(
        project_kernel,
        grid=(4,),
        in_specs=[
            pl.BlockSpec((2, 2, count, WIDE), lambda k: (0, k, 0, 0)),
            pl.BlockSpec((4, 2, 3, 128, CH), lambda k: (k, 0, 0, 0, 0)),
            pl.BlockSpec((1, 2, WIDE), lambda k: (k, 0, 0)),
            pl.BlockSpec((3, 3, CH), lambda k: (0, 0, 0)),
        ],
        out_specs=[
            pl.BlockSpec((3, 2, ROWS, CH), lambda k: (0, 0, 0, 0)),
            pl.BlockSpec((2, HALO, CH), lambda k: (0, 0, 0)),
            pl.BlockSpec((HALO, CH), lambda k: (0, 0)),
        ],
        out_shape=[
            jax.ShapeDtypeStruct((3, 2, ROWS, CH), BF16),
            jax.ShapeDtypeStruct((2, HALO, CH), BF16),
            jax.ShapeDtypeStruct((HALO, CH), BF16),
        ],
        scratch_shapes=[
            pltpu.VMEM((2, 3, count, CH), F32),
            pltpu.VMEM((2, count, 1), F32),
        ],
        compiler_params=pltpu.CompilerParams(vmem_limit_bytes=VMEM),
        cost_estimate=pl.CostEstimate(
            flops=2 * 2 * count * 4096 * 3 * CH, bytes_accessed=18_000_000, transcendentals=0
        ),
        name="project",
    )(gathered, weights, gain, taps)


def toeplitz_kernel(u_ref, out_ref):
    for g in range(GROUPS):
        wide = jnp.broadcast_to(u_ref[g : g + 1], (LH, 3 * LH))
        skewed = pltpu.roll(wide, 0, 1, stride=1, stride_axis=0)
        out_ref[g] = skewed[:, : 2 * LH].astype(BF16)


def toeplitz(filters):
    backwards = jnp.flip(filters.astype(F32), 1)
    row = jnp.pad(backwards, ((0, 0), (1, 2 * LH - 1)))
    return pl.pallas_call(
        toeplitz_kernel,
        out_shape=jax.ShapeDtypeStruct((GROUPS, LH, 2 * LH), BF16),
        compiler_params=pltpu.CompilerParams(vmem_limit_bytes=VMEM),
        name="toeplitz",
    )(row)


def mix_kernel(proj_ref, halo_ref, band_ref, taps_ref, bias_ref, w_ref, out_ref, before, edge):
    step = pl.program_id(0)

    @pl.when(step == 0)
    def _():
        for h in range(2):
            before[h] = halo_ref[h, :LH]
            last = halo_ref[h, LH:].astype(F32)
            for s in range(3):
                edge[h, s] = pltpu.roll(last, (6 - 2 * s) % 16, 0)[:8]

    queries = []
    mixes = []
    windows = []
    for h in range(2):
        feats = []
        for s in range(3):
            lifted = proj_ref[s, h].astype(F32)
            rows = jnp.concatenate([edge[h, s], lifted], axis=0)
            feats.append(three_taps(rows, taps_ref, s)[8:])
            edge[h, s] = lifted[LH - 8 :]
        mixing = (feats[1] * feats[2]).astype(BF16)
        queries.append(feats[0])
        mixes.append(mixing)
        windows.append(jnp.concatenate([before[h], mixing], axis=0))
        before[h] = mixing
    lane_group = lax.broadcasted_iota(jnp.int32, (LH, 2 * LH), 1) % LH // GSIZE
    halves = []
    for half in range(2):
        lanes = slice(half * LH, (half + 1) * LH)
        window = jnp.concatenate([windows[0][:, lanes], windows[1][:, lanes]], axis=1)
        total = jnp.zeros((LH, 2 * LH), F32)
        for g in range(GROUPS // 2):
            one = jnp.dot(band_ref[half * 8 + g], window, preferred_element_type=F32)
            total = jnp.where(lane_group == g, one, total)
        halves.append(total)
    gated = []
    for h in range(2):
        rows = slice(h * LH, (h + 1) * LH)
        filtered = jnp.concatenate([halves[0][:, rows], halves[1][:, rows]], axis=1)
        value = queries[h] * (filtered + bias_ref[...] * mixes[h].astype(F32))
        gated.append(value.astype(BF16))
    stacked = jnp.concatenate(gated, axis=0)
    for t in range(8):
        weights = jnp.concatenate([w_ref[t // 2 * 4 + x, t % 2] for x in range(4)], axis=1)
        partial = jnp.dot(stacked, weights, preferred_element_type=F32).astype(BF16)
        for h in range(2):
            out_ref[h, t] = partial[h * LH : (h + 1) * LH]


def mix_out(proj, halo, band, taps, bias, weights):
    return pl.pallas_call(
        mix_kernel,
        grid=(ROWS // LH,),
        in_specs=[
            pl.BlockSpec((3, 2, LH, CH), lambda b: (0, 0, b, 0)),
            pl.BlockSpec((2, HALO, CH), lambda b: (0, 0, 0)),
            pl.BlockSpec((GROUPS, LH, 2 * LH), lambda b: (0, 0, 0)),
            pl.BlockSpec((3, 3, CH), lambda b: (0, 0, 0)),
            pl.BlockSpec((1, CH), lambda b: (0, 0)),
            pl.BlockSpec((16, 2, CH, 128), lambda b: (0, 0, 0, 0)),
        ],
        out_specs=pl.BlockSpec((2, 8, LH, WIDE), lambda b: (0, 0, b, 0)),
        out_shape=jax.ShapeDtypeStruct((2, 8, ROWS, WIDE), BF16),
        scratch_shapes=[
            pltpu.VMEM((2, LH, CH), BF16),
            pltpu.VMEM((2, 3, 8, CH), F32),
        ],
        compiler_params=pltpu.CompilerParams(vmem_limit_bytes=VMEM),
        cost_estimate=pl.CostEstimate(
            flops=2 * 1024 * CH * 4096 * 2, bytes_accessed=14_000_000, transcendentals=0
        ),
        name="mix_out",
    )(proj, halo, band, taps, bias, weights)


def on_device(
    tokens, prior_rows, norm_gain, in_weight, short_filter, mr_filter, mr_bias, out_weight
):
    zh = lax.axis_index("zh")
    column = lax.axis_index("x")
    leading = (column == 0) & (lax.axis_index("y") == 0)

    padded = jnp.pad(prior_rows, ((0, 2 * FRONT - prior_rows.shape[0]), (0, 0)))
    own_front = lax.dynamic_slice_in_dim(padded, zh * FRONT, FRONT, 0)
    own = jnp.concatenate([tokens, own_front], axis=0)
    gathered = lax.all_gather(own, ("zh", "zl", "c"))
    gathered = gathered.reshape(2, 8, ROWS + FRONT, WIDE)
    gain = lax.all_gather(norm_gain, ("zl", "c")).astype(F32).reshape(4, 2, WIDE)

    halves = in_weight.reshape(3, 128, 2, CH).transpose(2, 0, 1, 3)
    halves = lax.all_to_all(halves, "zh", 0, 0)
    w_in = lax.all_gather(halves, ("y", "x"))
    out_halves = lax.all_to_all(out_weight.reshape(2, CH, 128), "zh", 0, 0)
    w_out = lax.all_gather(out_halves, ("y", "x"))

    taps = lax.dynamic_slice_in_dim(short_filter, zh * CH, CH, 2)
    bias = lax.dynamic_slice_in_dim(mr_bias, zh * CH, CH, 0)[None, :]
    band = toeplitz(lax.dynamic_slice_in_dim(mr_filter, zh * GROUPS, GROUPS, 0))

    proj, tail, front = project(gathered, w_in, gain, taps)

    last = column == 3
    to_first = jnp.where(last, tail[1], tail[0])
    to_second = jnp.where(last, tail[0], tail[1])
    first = lax.ppermute(to_first, ("y", "x"), [(i, i + 1) for i in range(15)])
    second = lax.ppermute(
        to_second, ("y", "x"), [(i, i // 4 * 4 + (i + 1) % 4) for i in range(16)]
    )
    halo = jnp.stack([jnp.where(leading, front, first), second])

    partial = mix_out(proj, halo, band, taps, bias, w_out)
    summed = lax.psum_scatter(
        partial.reshape(16, ROWS, WIDE), ("zh", "zl", "c"), scatter_dimension=0
    )
    return (tokens.astype(F32) + summed.astype(F32)).astype(BF16)


def solution(mesh):
    split = Mesh(mesh.devices.reshape(4, 2, 4, 4, 2), ("y", "zh", "x", "zl", "c"))
    seq, tensor = ("y", "zh", "x"), ("zl", "c")
    in_specs = (
        P(seq, tensor),
        P(None, tensor),
        P(tensor),
        P(None, seq, tensor),
        P(None, None, tensor),
        P(tensor, None),
        P(tensor),
        P(tensor, seq),
    )
    return jax.shard_map(
        on_device, mesh=split, in_specs=in_specs, out_specs=P(seq, tensor), check_vma=False
    )
```

time: 509 us -> 298 us (0.59)
  waiting for transfers between devices: 418 us -> 207 us
  blocking collectives: 13.6 us -> 47 us
  matrix products: 30.9 us -> 0 us
  Pallas kernels: 0 us -> 18.7 us
  local copies, waits for them, and re-layouts: 14.1 us -> 4.15 us
  other arithmetic: 11.4 us -> 2.95 us
    all_gather x4 -> x3, waiting for transfers between devices: 363 us -> 133 us  [the longest x1 63.7 us: on_device(): gathered = lax.all_gather(own, ('zh', 'zl', 'c'))]
    all_to_all x0 -> x2, blocking collectives: none -> 34.1 us  [the longest x1 22.2 us: on_device(): halves = lax.all_to_all(halves, 'zh', 0, 0)]
    dot_general x6 -> x0, matrix products: 30.9 us -> none  [the longest x1 13.9 us: on_device(): jnp.einsum('rd,sdc->src', normed, lax.all_gather(in_weight, 'seq', axis=1...]
    reduce_scatter x1, waiting for transfers between devices: 51.5 us -> 70.5 us  [on_device(): lax.psum_scatter(partial.reshape(16, ROWS, WIDE), ('zh', 'zl', 'c'), scat...]
    pallas_call x0 -> x3, Pallas kernels: none -> 18.7 us  [the longest x1 11.4 us: project(): pl.pallas_call(project_kernel, grid=(4,), in_specs=[pl.BlockSpec((2, 2, c...]
  transfers between devices with their start and end apart: 7 -> 6, of which waited for: 6 -> 6; matrix products, arithmetic and copies ran while one was open for 9% -> 0% of each run, Pallas kernels for 0% -> 4%
where the time goes in v1:
time: 298 us
  waiting for transfers between devices  207 us (69%)
  blocking collectives  47 us (16%)
  Pallas kernels  18.7 us (6%)
  between operations  13.3 us (4%)
  starting transfers between devices  4.76 us (2%)
  local copies, waits for them, and re-layouts  4.15 us (1%)
    reduce_scatter x1, waiting for transfers between devices, on_device(): lax.psum_scatter(partial.reshape(16, ROWS, WIDE), ('zh', 'zl', 'c'), scat...  70.5 us
    all_gather x1, waiting for transfers between devices, on_device(): gathered = lax.all_gather(own, ('zh', 'zl', 'c'))  63.7 us
    all_gather x1, waiting for transfers between devices, on_device(): w_in = lax.all_gather(halves, ('y', 'x'))  38.5 us
    all_gather x1, waiting for transfers between devices, on_device(): w_out = lax.all_gather(out_halves, ('y', 'x'))  30.7 us
    all_to_all x1, blocking collectives, on_device(): halves = lax.all_to_all(halves, 'zh', 0, 0)  22.2 us
    all_gather x1, blocking collectives, on_device(): lax.all_gather(norm_gain, ('zl', 'c')).astype(F32).reshape(4, 2, WIDE)  12.8 us
    all_to_all x1, blocking collectives, on_device(): out_halves = lax.all_to_all(out_weight.reshape(2, CH, 128), 'zh', 0, 0)  12 us
    pallas_call x1, Pallas kernels, project(): pl.pallas_call(project_kernel, grid=(4,), in_specs=[pl.BlockSpec((2, 2, c...  11.4 us
  transfers between devices with their start and end apart: 6, of which 6 were waited for; matrix products, arithmetic and copies ran while one was open for 0% of the time, Pallas kernels for 4%

profile of v1, /device:TPU:2, one launch (start us, length us, event | category | flops | bytes accessed | tf_op | source)
XLA Modules:
  0.0 297.7 jit_solution(17312918445320067072)
XLA Ops:
  6.5 0.0 copy-start
  6.5 0.0 copy-start.3
  6.5 0.0 copy-start.2
  6.5 0.0 all-gather.11.cloned.1.call-start
  6.5 1.3 copy.12
  7.9 0.0 copy-start.4
  7.9 0.0 copy-start.6
  7.9 0.0 copy-start.7
  7.9 22.2 %all_to_all.10 = bf16[2,3,128,256]{2,3,1,0:T(8,128)(2,1)S(1)} all-to-all(bf16[2,3,128,256]{2,3,1,0:T(8,128)(2,1)S(1)} %copy.13), channel_id=1, replica_groups=mesh['y'=4,'zh'=2,'x'=4,'zl'=4,'c'=2] {'zh'}, dimensions={0} | all-to-all | bytes 786432 | tf_op jit(solution)/shard_map/all_to_all | solution.py:232
  30.1 0.9 copy.14
  31.0 0.0 all-gather.11.cloned.1.call-update
  31.1 0.0 all-gather.9.cloned.1.call-start
  31.1 0.0 copy-done.3
  31.2 0.0 copy-done.2
  31.2 0.9 pad_maximum_fusion
  32.1 0.0 all-gather.9.cloned.1.call-update
  32.1 0.0 all-gather.13.cloned.1.call-start
  32.1 0.0 copy-done.4
  32.1 12.0 %all_to_all.11 = bf16[2,256,128]{2,1,0:T(8,128)(2,1)} all-to-all(bf16[2,256,128]{2,1,0:T(8,128)(2,1)S(1)} %bitcast.23), channel_id=1, replica_groups=mesh['y'=4,'zh'=2,'x'=4,'zl'=4,'c'=2] {'zh'}, dimensions={0} | all-to-all | bytes 262144 | tf_op jit(solution)/shard_map/all_to_all | solution.py:234
  44.1 0.0 all-gather.13.cloned.1.call-update
  44.1 0.0 reduce-scatter.2.cloned.1.call-start
  44.2 0.0 copy-done.6
  44.2 12.8 %all-gather.4 = bf16[8,1,512]{2,1,0:T(2,128)(2,1)S(1)} all-gather(bf16[1,1,512]{2,1,0:T(2,128)(2,1)S(1)} %reshape.40), channel_id=4, replica_groups=mesh['y'=4,'zh'=2,'x'=4,'zl'=4,'c'=2] {'zl','c'}, dimensions={0}, use_global_device_ids=true | all-gather | bytes 9216 | tf_op jit(solution)/shard_map/all_gather | solution.py:229
  57.1 0.0 copy-done.7
  57.1 0.1 dynamic_slice.15
  57.2 0.0 copy-done
  57.2 38.5 %all-gather.11.cloned.1.call-done = bf16[32,3,128,256]{3,2,1,0:T(8,128)(2,1)} async-done(((bf16[2,3,128,256]{3,2,1,0:T(8,128)(2,1)}), bf16[32,3,128,256]{3,2,1,0:T(8,128)(2,1)}) %all-gather.11.cloned.1.call-update) | async-done | bytes 6291472 | tf_op jit(solution)/shard_map/all_gather | solution.py:233
  95.6 63.7 %all-gather.9.cloned.1.call-done = bf16[9472,512]{1,0:T(8,128)(2,1)} async-done(((bf16[592,512]{1,0:T(8,128)(2,1)}), bf16[9472,512]{1,0:T(8,128)(2,1)}) %all-gather.9.cloned.1.call-update) | async-done | bytes 9699344 | tf_op jit(solution)/shard_map/all_gather | solution.py:227
  159.3 0.0 copy-start.5
  159.3 11.4 %project.1 = (bf16[3,2,512,256]{3,2,1,0:T(8,128)(2,1)S(1)}, bf16[2,144,256]{2,1,0:T(8,128)(2,1)S(1)}, bf16[144,256]{1,0:T(8,128)(2,1)S(1)}) custom-call(bf16[2,8,592,512]{3,2,1,0:T(8,128)(2,1)} %bitcast.25, bf16[16,2,3,128,256]{4,3,2,1,0:T(8,128)(2,1)} %bitcast.26, f32[4,2,512]{2,1,0:T(2,128)S(1)} %reshape.30.gain_ref, ...), custom_call_target="tpu_custom_call" | custom-call | flops 7449083904 | bytes 18000000 | tf_op jit(solution)/shard_map/project/pallas_call | solution.py:92
  170.8 3.4 %collective-permute-start = (bf16[144,256]{1,0:T(8,128)(2,1)S(1)}, bf16[144,256]{1,0:T(8,128)(2,1)S(1)}, u32[]{:S(2)}, u32[]{:S(2)}) collective-permute-start(bf16[144,256]{1,0:T(8,128)(2,1)S(1)} %get-tuple-element.11), channel_id=1, source_target_pairs={{0,8},{8,16},{16,24},{24,64},{64,72},{72,80},{80,88},{88,128},{128... | collective-permute-start | bytes 221192 | tf_op jit(solution)/shard_map/ppermute | solution.py:246
  174.1 0.0 copy-done.5
  174.2 0.1 rev.4
  174.2 0.1 pad.9.u_ref
  174.3 0.5 toeplitz.1.band_ref
  174.8 1.2 collective-permute-start.1
  176.1 1.1 collective-permute-done
  177.1 2.4 collective-permute-done.1
  179.6 30.7 %all-gather.13.cloned.1.call-done = bf16[32,256,128]{2,1,0:T(8,128)(2,1)} async-done(((bf16[2,256,128]{2,1,0:T(8,128)(2,1)}), bf16[32,256,128]{2,1,0:T(8,128)(2,1)}) %all-gather.13.cloned.1.call-update) | async-done | bytes 2097168 | tf_op jit(solution)/shard_map/all_gather | solution.py:235
  210.2 0.0 copy-start.1
  210.2 1.6 copy-done.1
  211.8 6.9 %mix_out.1 = bf16[2,8,512,512]{3,2,1,0:T(8,128)(2,1)} custom-call(bf16[3,2,512,256]{3,2,1,0:T(8,128)(2,1)S(1)} %get-tuple-element.8.proj_ref, bf16[2,144,256]{2,1,0:T(8,128)(2,1)S(1)} %pad_maximum_fusion.1.halo_ref, bf16[16,128,256]{2,1,0:T(8,128)(2,1)S(1)} %toeplitz.1.band_ref, f32[3,3,256]{2,1,0:T(4,128)S(1)} %constant_dynamic-slice_fusion.taps_ref, ...), custom_call_target="tpu_custom_call" | custom-call | flops 4294967296 | bytes 14000000 | tf_op jit(solution)/shard_map/mix_out/pallas_call | solution.py:192
  218.7 0.0 reduce-scatter.2.cloned.1.call-update
  218.7 70.5 %reduce-scatter.2.cloned.1.call-done = bf16[1,512,512]{2,1,0:T(8,128)(2,1)} async-done(((bf16[16,512,512]{2,1,0:T(8,128)(2,1)}), bf16[1,512,512]{2,1,0:T(8,128)(2,1)}) %reduce-scatter.2.cloned.1.call-update) | async-done | bytes 524304 | tf_op jit(solution)/shard_map/reduce_scatter | solution.py:253
  289.2 2.0 fusion
  (10 shorter events, 0.2 us)
Async XLA Ops:
  6.5 50.6 %copy-start = (f32[3,3,512]{2,1,0:T(4,128)S(1)}, f32[3,3,512]{2,1,0:T(4,128)}, u32[]{:S(2)}) copy-start(f32[3,3,512]{2,1,0:T(4,128)} %param.12) | copy-start | bytes 55300
  6.5 24.6 %copy-start.3 = (bf16[129,512]{1,0:T(8,128)(2,1)S(1)}, bf16[129,512]{1,0:T(8,128)(2,1)}, u32[]{:S(2)}) copy-start(bf16[129,512]{1,0:T(8,128)(2,1)} %param.9) | copy-start | bytes 396292
  6.5 24.6 %copy-start.2 = (bf16[512,512]{1,0:T(8,128)(2,1)S(1)}, bf16[512,512]{1,0:T(8,128)(2,1)}, u32[]{:S(2)}) copy-start(bf16[512,512]{1,0:T(8,128)(2,1)} %param.8) | copy-start | bytes 1572868
  6.5 89.1 %all-gather.11.cloned.1.call-start = ((), (), s32[]{:S(2)}) async-start(), calls=%async_computation.5 | async-start | bytes 6684672 | tf_op jit(solution)/shard_map/all_gather | solution.py:233
  7.9 24.3 %copy-start.4 = (bf16[512,128]{1,0:T(8,128)(2,1)S(1)}, bf16[512,128]{1,0:T(8,128)(2,1)}, u32[]{:S(2)}) copy-start(bf16[512,128]{1,0:T(8,128)(2,1)} %param.15) | copy-start | bytes 393220
  7.9 36.3 %copy-start.6 = (bf16[512]{0:T(512)(128)(2,1)S(1)}, bf16[512]{0:T(512)(128)(2,1)}, u32[]{:S(2)}) copy-start(bf16[512]{0:T(512)(128)(2,1)} %param.10) | copy-start | bytes 3076
  7.9 49.2 %copy-start.7 = (f32[512]{0:T(512)S(1)}, f32[512]{0:T(512)}, u32[]{:S(2)}) copy-start(f32[512]{0:T(512)} %param.14) | copy-start | bytes 6148
  31.1 128.3 %all-gather.9.cloned.1.call-start = ((), (), s32[]{:S(2)}) async-start(), calls=%async_computation.4 | async-start | bytes 10305536 | tf_op jit(solution)/shard_map/all_gather | solution.py:227
  32.1 178.2 %all-gather.13.cloned.1.call-start = ((), (), s32[]{:S(2)}) async-start(), calls=%async_computation.6 | async-start | bytes 2228224 | tf_op jit(solution)/shard_map/all_gather | solution.py:235
  44.1 245.1 %reduce-scatter.2.cloned.1.call-start = ((), (), s32[]{:S(2)}) async-start(), calls=%async_computation.3 | async-start | bytes 8912896 | tf_op jit(solution)/shard_map/reduce_scatter | solution.py:253
  159.3 14.8 %copy-start.5 = (bf16[32,128]{1,0:T(8,128)(2,1)S(1)}, bf16[32,128]{1,0:T(8,128)(2,1)}, u32[]{:S(2)}) copy-start(bf16[32,128]{1,0:T(8,128)(2,1)} %param.13) | copy-start | bytes 24580
  170.8 6.4 %collective-permute-start = (bf16[144,256]{1,0:T(8,128)(2,1)S(1)}, bf16[144,256]{1,0:T(8,128)(2,1)S(1)}, u32[]{:S(2)}, u32[]{:S(2)}) collective-permute-start(bf16[144,256]{1,0:T(8,128)(2,1)S(1)} %get-tuple-element.11), channel_id=1, source_target_pairs={{0,8},{8,16},{16,24},{24,64},{64,72},{72,80},{80,88},{88,128},{128... | collective-permute-start | bytes 221192 | tf_op jit(solution)/shard_map/ppermute | solution.py:246
  174.8 4.7 %collective-permute-start.1 = (bf16[144,256]{1,0:T(8,128)(2,1)S(1)}, bf16[144,256]{1,0:T(8,128)(2,1)S(1)}, u32[]{:S(2)}, u32[]{:S(2)}) collective-permute-start(bf16[144,256]{1,0:T(8,128)(2,1)S(1)} %get-tuple-element.12), channel_id=1, source_target_pairs={{0,8},{8,16},{16,24},{24,0},{64,72},{72,80},{80,88},{88,64},{128,1... | collective-permute-start | bytes 221192 | tf_op jit(solution)/shard_map/ppermute | solution.py:247
  210.2 1.6 copy-start.1
Sparse Core Ops, SparseCore 0:
  31.2 64.4 all-gather.10
  97.5 61.8 all-gather.8
  161.8 48.4 all-gather.12
  218.8 70.2 reduce-scatter.1

commit v2 on v1

--- a/solution.py
+++ b/solution.py
@@ -1,5 +1,3 @@
-import functools
-
 import jax
 import jax.numpy as jnp
 from jax import lax
@@ -32,26 +30,34 @@
     )
 
 
-def project_kernel(x_ref, w_ref, gain_ref, taps_ref, proj_ref, tail_ref, front_ref, acc, ssq):
+def project_kernel(at_ref, x_ref, w_ref, taps_ref, proj_ref, tail_ref, front_ref, scaled, acc, ssq):
     step = pl.program_id(0)
+    z_half = at_ref[1]
+    column = at_ref[2]
 
     @pl.when(step == 0)
     def _():
         acc[...] = jnp.zeros_like(acc)
         ssq[...] = jnp.zeros_like(ssq)
 
+    gains = [x_ref[1, u, ROWS + FRONT - 16 :].astype(F32)[15:] for u in range(2)]
     for h in range(2):
-        parts = []
         for u in range(2):
             lifted = x_ref[h, u].astype(F32)
             ssq[h] += jnp.sum(lifted * lifted, axis=-1, keepdims=True)
-            parts.append((lifted * gain_ref[0, u : u + 1]).astype(BF16))
-        scaled = jnp.concatenate(parts, axis=1)
+            scaled[u] = (lifted * gains[u]).astype(BF16)
+        parts = []
+        for kind in range(2):
+            block = z_half if kind == 0 else 1 - z_half
+            for r in range(4):
+                place = pl.multiple_of(lax.rem(column + r, 4) * 128, 128)
+                parts.append(scaled[block, :, pl.ds(place, 128)])
+        rows = jnp.concatenate(parts, axis=1)
         for s in range(3):
             weights = jnp.concatenate(
-                [w_ref[x, u, s] for u in range(2) for x in range(4)], axis=0
+                [w_ref[0, kind, r, s] for kind in range(2) for r in range(4)], axis=0
             )
-            acc[h, s] += jnp.dot(scaled, weights, preferred_element_type=F32)
+            acc[h, s] += jnp.dot(rows, weights, preferred_element_type=F32)
 
     @pl.when(step == pl.num_programs(0) - 1)
     def _():
@@ -87,37 +93,40 @@
         front_ref[LH:] = last.astype(BF16)
 
 
-def project(gathered, weights, gain, taps):
+def project(at, gathered, weights, taps):
     count = ROWS + FRONT
     return pl.pallas_call(
         project_kernel,
-        grid=(4,),
-        in_specs=[
-            pl.BlockSpec((2, 2, count, WIDE), lambda k: (0, k, 0, 0)),
-            pl.BlockSpec((4, 2, 3, 128, CH), lambda k: (k, 0, 0, 0, 0)),
-            pl.BlockSpec((1, 2, WIDE), lambda k: (k, 0, 0)),
-            pl.BlockSpec((3, 3, CH), lambda k: (0, 0, 0)),
-        ],
-        out_specs=[
-            pl.BlockSpec((3, 2, ROWS, CH), lambda k: (0, 0, 0, 0)),
-            pl.BlockSpec((2, HALO, CH), lambda k: (0, 0, 0)),
-            pl.BlockSpec((HALO, CH), lambda k: (0, 0)),
-        ],
+        grid_spec=pltpu.PrefetchScalarGridSpec(
+            num_scalar_prefetch=1,
+            grid=(4,),
+            in_specs=[
+                pl.BlockSpec((2, 2, count, WIDE), lambda k, at: (0, lax.rem(at[0] + k, 4), 0, 0)),
+                pl.BlockSpec((1, 2, 4, 3, 128, CH), lambda k, at: (k, 0, 0, 0, 0, 0)),
+                pl.BlockSpec((3, 3, CH), lambda k, at: (0, 0, 0)),
+            ],
+            out_specs=[
+                pl.BlockSpec((3, 2, ROWS, CH), lambda k, at: (0, 0, 0, 0)),
+                pl.BlockSpec((2, HALO, CH), lambda k, at: (0, 0, 0)),
+                pl.BlockSpec((HALO, CH), lambda k, at: (0, 0)),
+            ],
+            scratch_shapes=[
+                pltpu.VMEM((2, count, WIDE), BF16),
+                pltpu.VMEM((2, 3, count, CH), F32),
+                pltpu.VMEM((2, count, 1), F32),
+            ],
+        ),
         out_shape=[
             jax.ShapeDtypeStruct((3, 2, ROWS, CH), BF16),
             jax.ShapeDtypeStruct((2, HALO, CH), BF16),
             jax.ShapeDtypeStruct((HALO, CH), BF16),
-        ],
-        scratch_shapes=[
-            pltpu.VMEM((2, 3, count, CH), F32),
-            pltpu.VMEM((2, count, 1), F32),
         ],
         compiler_params=pltpu.CompilerParams(vmem_limit_bytes=VMEM),
         cost_estimate=pl.CostEstimate(
             flops=2 * 2 * count * 4096 * 3 * CH, bytes_accessed=18_000_000, transcendentals=0
         ),
         name="project",
-    )(gathered, weights, gain, taps)
+    )(at, gathered, weights, taps)
 
 
 def toeplitz_kernel(u_ref, out_ref):
@@ -138,7 +147,7 @@
     )(row)
 
 
-def mix_kernel(proj_ref, halo_ref, band_ref, taps_ref, bias_ref, w_ref, out_ref, before, edge):
+def mix_kernel(at_ref, proj_ref, halo_ref, band_ref, taps_ref, bias_ref, w_ref, out_ref, before, edge):
     step = pl.program_id(0)
 
     @pl.when(step == 0)
@@ -181,37 +190,71 @@
         value = queries[h] * (filtered + bias_ref[...] * mixes[h].astype(F32))
         gated.append(value.astype(BF16))
     stacked = jnp.concatenate(gated, axis=0)
-    for t in range(8):
-        weights = jnp.concatenate([w_ref[t // 2 * 4 + x, t % 2] for x in range(4)], axis=1)
-        partial = jnp.dot(stacked, weights, preferred_element_type=F32).astype(BF16)
-        for h in range(2):
-            out_ref[h, t] = partial[h * LH : (h + 1) * LH]
-
-
-def mix_out(proj, halo, band, taps, bias, weights):
+    for k in range(4):
+        for kind in range(2):
+            z_half = at_ref[1] if kind == 0 else 1 - at_ref[1]
+            block = 2 * lax.rem(at_ref[0] + k, 4) + z_half
+            weights = jnp.concatenate([w_ref[k, kind, r] for r in range(4)], axis=1)
+            partial = jnp.dot(stacked, weights, preferred_element_type=F32).astype(BF16)
+            for r in range(4):
+                place = pl.multiple_of(lax.rem(at_ref[2] + r, 4) * 128, 128)
+                for h in range(2):
+                    out_ref[h, block, :, pl.ds(place, 128)] = partial[
+                        h * LH : (h + 1) * LH, r * 128 : (r + 1) * 128
+                    ]
+
+
+def mix_out(at, proj, halo, band, taps, bias, weights):
     return pl.pallas_call(
         mix_kernel,
-        grid=(ROWS // LH,),
-        in_specs=[
-            pl.BlockSpec((3, 2, LH, CH), lambda b: (0, 0, b, 0)),
-            pl.BlockSpec((2, HALO, CH), lambda b: (0, 0, 0)),
-            pl.BlockSpec((GROUPS, LH, 2 * LH), lambda b: (0, 0, 0)),
-            pl.BlockSpec((3, 3, CH), lambda b: (0, 0, 0)),
-            pl.BlockSpec((1, CH), lambda b: (0, 0)),
-            pl.BlockSpec((16, 2, CH, 128), lambda b: (0, 0, 0, 0)),
-        ],
-        out_specs=pl.BlockSpec((2, 8, LH, WIDE), lambda b: (0, 0, b, 0)),
+        grid_spec=pltpu.PrefetchScalarGridSpec(
+            num_scalar_prefetch=1,
+            grid=(ROWS // LH,),
+            in_specs=[
+                pl.BlockSpec((3, 2, LH, CH), lambda b, at: (0, 0, b, 0)),
+                pl.BlockSpec((2, HALO, CH), lambda b, at: (0, 0, 0)),
+                pl.BlockSpec((GROUPS, LH, 2 * LH), lambda b, at: (0, 0, 0)),
+                pl.BlockSpec((3, 3, CH), lambda b, at: (0, 0, 0)),
+                pl.BlockSpec((1, CH), lambda b, at: (0, 0)),
+                pl.BlockSpec((4, 2, 4, CH, 128), lambda b, at: (0, 0, 0, 0, 0)),
+            ],
+            out_specs=pl.BlockSpec((2, 8, LH, WIDE), lambda b, at: (0, 0, b, 0)),
+            scratch_shapes=[
+                pltpu.VMEM((2, LH, CH), BF16),
+                pltpu.VMEM((2, 3, 8, CH), F32),
+            ],
+        ),
         out_shape=jax.ShapeDtypeStruct((2, 8, ROWS, WIDE), BF16),
-        scratch_shapes=[
-            pltpu.VMEM((2, LH, CH), BF16),
-            pltpu.VMEM((2, 3, 8, CH), F32),
-        ],
         compiler_params=pltpu.CompilerParams(vmem_limit_bytes=VMEM),
         cost_estimate=pl.CostEstimate(
             flops=2 * 1024 * CH * 4096 * 2, bytes_accessed=14_000_000, transcendentals=0
         ),
         name="mix_out",
-    )(proj, halo, band, taps, bias, weights)
+    )(at, proj, halo, band, taps, bias, weights)
+
+
+UP = [(i, (i + 1) % 4) for i in range(4)]
+DOWN = [(i, (i + 3) % 4) for i in range(4)]
+
+
+def ring_gather(piece, axis, cut):
+    behind = lax.ppermute(piece, axis, UP)
+    ahead = lax.ppermute(piece, axis, DOWN)
+    half = piece.shape[cut] // 2
+    far = jnp.concatenate(
+        [
+            lax.ppermute(lax.slice_in_dim(behind, 0, half, axis=cut), axis, UP),
+            lax.ppermute(lax.slice_in_dim(ahead, half, 2 * half, axis=cut), axis, DOWN),
+        ],
+        axis=cut,
+    )
+    return jnp.stack([piece, ahead, far, behind])
+
+
+def plane_gather(piece, first):
+    line = ring_gather(piece, first, piece.ndim - 2)
+    both = ring_gather(line, "x" if first == "y" else "y", 0)
+    return both.swapaxes(0, 1) if first == "y" else both
 
 
 def on_device(
@@ -221,24 +264,31 @@
     column = lax.axis_index("x")
     leading = (column == 0) & (lax.axis_index("y") == 0)
 
-    padded = jnp.pad(prior_rows, ((0, 2 * FRONT - prior_rows.shape[0]), (0, 0)))
+    at = jnp.stack([lax.axis_index("y"), zh, column])
+    spare = 2 * FRONT - prior_rows.shape[0]
+    padded = jnp.concatenate(
+        [prior_rows, jnp.zeros((spare - 1, WIDE), BF16), norm_gain[None, :]], axis=0
+    )
     own_front = lax.dynamic_slice_in_dim(padded, zh * FRONT, FRONT, 0)
     own = jnp.concatenate([tokens, own_front], axis=0)
     gathered = lax.all_gather(own, ("zh", "zl", "c"))
     gathered = gathered.reshape(2, 8, ROWS + FRONT, WIDE)
-    gain = lax.all_gather(norm_gain, ("zl", "c")).astype(F32).reshape(4, 2, WIDE)
-
-    halves = in_weight.reshape(3, 128, 2, CH).transpose(2, 0, 1, 3)
-    halves = lax.all_to_all(halves, "zh", 0, 0)
-    w_in = lax.all_gather(halves, ("y", "x"))
-    out_halves = lax.all_to_all(out_weight.reshape(2, CH, 128), "zh", 0, 0)
-    w_out = lax.all_gather(out_halves, ("y", "x"))
+
+    def swapped(left, right):
+        kept = jnp.where(zh == 0, left, right)
+        other = jnp.where(zh == 0, right, left)
+        return kept, lax.ppermute(other, "zh", [(0, 1), (1, 0)])
+
+    kept, got = swapped(in_weight[..., :CH], in_weight[..., CH:])
+    w_in = jnp.stack([plane_gather(kept, "x"), plane_gather(got, "y")], axis=1)
+    kept, got = swapped(out_weight[:CH], out_weight[CH:])
+    w_out = jnp.stack([plane_gather(kept, "x"), plane_gather(got, "y")], axis=1)
 
     taps = lax.dynamic_slice_in_dim(short_filter, zh * CH, CH, 2)
     bias = lax.dynamic_slice_in_dim(mr_bias, zh * CH, CH, 0)[None, :]
     band = toeplitz(lax.dynamic_slice_in_dim(mr_filter, zh * GROUPS, GROUPS, 0))
 
-    proj, tail, front = project(gathered, w_in, gain, taps)
+    proj, tail, front = project(at, gathered, w_in, taps)
 
     last = column == 3
     to_first = jnp.where(last, tail[1], tail[0])
@@ -249,7 +299,7 @@
     )
     halo = jnp.stack([jnp.where(leading, front, first), second])
 
-    partial = mix_out(proj, halo, band, taps, bias, w_out)
+    partial = mix_out(at, proj, halo, band, taps, bias, w_out)
     summed = lax.psum_scatter(
         partial.reshape(16, ROWS, WIDE), ("zh", "zl", "c"), scatter_dimension=0
     )

time: 298 us -> 230 us (0.77)
  waiting for transfers between devices: 207 us -> 105 us
  starting transfers between devices: 4.76 us -> 59.4 us
  blocking collectives: 47 us -> 0 us
  other arithmetic: 2.95 us -> 21.5 us
  Pallas kernels: 18.7 us -> 24.7 us
    all_gather x2 -> x0, waiting for transfers between devices: 69.1 us -> none  [the longest x1 38.5 us: on_device(): w_in = lax.all_gather(halves, ('y', 'x'))]
    all_gather x1, waiting for transfers between devices: 63.7 us -> 0.01 us  [on_device(): gathered = lax.all_gather(own, ('zh', 'zl', 'c'))]
    ppermute x0 -> x34, starting transfers between devices: none -> 52.8 us  [the longest x8 16 us: ring_gather(): ahead = lax.ppermute(piece, axis, DOWN)]
    ppermute x0 -> x34, waiting for transfers between devices: none -> 34.8 us  [the longest x8 26.2 us: ring_gather(): lax.ppermute(lax.slice_in_dim(behind, 0, half, axis=cut), axis, UP)]
    all_to_all x2 -> x0, blocking collectives: 34.1 us -> none  [the longest x1 22.2 us: on_device(): halves = lax.all_to_all(halves, 'zh', 0, 0)]
    another operation x0 -> x19, other arithmetic: none -> 14.7 us  [the longest x12 6.96 us: ring_gather(): return jnp.stack([piece, ahead, far, behind])]
    all_gather x1 -> x0, blocking collectives: 12.8 us -> none  [on_device(): lax.all_gather(norm_gain, ('zl', 'c')).astype(F32).reshape(4, 2, WIDE)]
    pallas_call x2, Pallas kernels: 18.3 us -> 24.2 us  [the longest x1 15.8 us: project(): pl.pallas_call(project_kernel, grid_spec=pltpu.PrefetchScalarGridSpec(num...]
  transfers between devices with their start and end apart: 6 -> 38, of which waited for: 6 -> 10; matrix products, arithmetic and copies ran while one was open for 0% -> 9% of each run, Pallas kernels for 4% -> 0%
where the time goes in v2:
time: 230 us
  waiting for transfers between devices  105 us (46%)
  starting transfers between devices  59.4 us (26%)
  Pallas kernels  24.7 us (11%)
  other arithmetic  21.5 us (9%)
  between operations  13.9 us (6%)
  local copies, waits for them, and re-layouts  5.5 us (2%)
    reduce_scatter x1, waiting for transfers between devices, on_device(): lax.psum_scatter(partial.reshape(16, ROWS, WIDE), ('zh', 'zl', 'c'), scat...  67.8 us
    ppermute x8, waiting for transfers between devices, ring_gather(): lax.ppermute(lax.slice_in_dim(behind, 0, half, axis=cut), axis, UP)  26.2 us
    ppermute x8, starting transfers between devices, ring_gather(): ahead = lax.ppermute(piece, axis, DOWN)  16 us
    pallas_call x1, Pallas kernels, project(): pl.pallas_call(project_kernel, grid_spec=pltpu.PrefetchScalarGridSpec(num...  15.8 us
    ppermute x8, starting transfers between devices, ring_gather(): lax.ppermute(lax.slice_in_dim(ahead, half, 2 * half, axis=cut), axis, DOWN)  15.7 us
    ppermute x2, starting transfers between devices, swapped(): return (kept, lax.ppermute(other, 'zh', [(0, 1), (1, 0)]))  9.04 us
    pallas_call x1, Pallas kernels, mix_out(): pl.pallas_call(mix_kernel, grid_spec=pltpu.PrefetchScalarGridSpec(num_sca...  8.43 us
    ppermute x8, starting transfers between devices, ring_gather(): behind = lax.ppermute(piece, axis, UP)  7.27 us
  transfers between devices with their start and end apart: 38, of which 10 were waited for; matrix products, arithmetic and copies ran while one was open for 9% of the time, Pallas kernels for 0%

profile of v2, /device:TPU:2, one launch (start us, length us, event | category | flops | bytes accessed | tf_op | source)
XLA Modules:
  0.0 229.7 jit_solution(9090716323995041250)
XLA Ops:
  7.3 1.0 fusion.2
  8.3 1.9 pad_maximum_fusion.4
  11.2 1.6 collective-permute-start.20
  13.6 6.8 %collective-permute-start.27 = (bf16[256,128]{1,0:T(8,128)(2,1)S(1)}, bf16[256,128]{1,0:T(8,128)(2,1)S(1)}, u32[]{:S(2)}, u32[]{:S(2)}) collective-permute-start(bf16[256,128]{1,0:T(8,128)(2,1)S(1)} %get-tuple-element.24), channel_id=1, source_target_pairs={{0,32},{32,0},{1,33},{33,1},{2,34},{34,2},{3,35},{35,3},{4,36},{36... | collective-permute-start | bytes 196616 | tf_op jit(solution)/shard_map/ppermute | solution.py:280
  20.4 1.5 collective-permute-start.21
  22.4 1.1 broadcast_select_fusion.1
  23.5 1.6 collective-permute-start.1
  25.1 1.6 collective-permute-start
  26.6 2.3 collective-permute-start.8
  28.9 1.6 collective-permute-start.29
  30.5 1.7 collective-permute-start.28
  32.1 2.2 collective-permute-done.29
  35.1 2.5 %collective-permute-start.31 = (bf16[128,128]{1,0:T(8,128)(2,1)S(1)}, bf16[128,128]{1,0:T(8,128)(2,1)S(1)}, u32[]{:S(2)}, u32[]{:S(2)}) collective-permute-start(bf16[128,128]{1,0:T(8,128)(2,1)S(1)} %slice.103), channel_id=1, source_target_pairs={{0,192},{64,0},{128,64},{192,128},{1,193},{65,1},{129,65},{193,129... | collective-permute-start | bytes 98312 | tf_op jit(solution)/shard_map/ppermute | solution.py:247
  37.8 3.3 %collective-permute-start.23 = (bf16[4,256,128]{2,1,0:T(8,128)(2,1)S(1)}, bf16[4,256,128]{2,1,0:T(8,128)(2,1)S(1)}, u32[]{:S(2)}, u32[]{:S(2)}) collective-permute-start(bf16[4,256,128]{2,1,0:T(8,128)(2,1)S(1)} %get-tuple-element.18), channel_id=1, source_target_pairs={{0,192},{64,0},{128,64},{192,128},{1,193},{65,1},{129,65},{193,129... | collective-permute-start | bytes 786440 | tf_op jit(solution)/shard_map/ppermute | solution.py:242
  41.1 1.6 collective-permute-start.2
  42.7 1.9 collective-permute-start.3
  45.0 1.6 collective-permute-start.10
  46.9 1.4 collective-permute-start.9
  48.3 1.3 fusion.6
  50.2 3.6 %collective-permute-done.10 = bf16[3,128,256]{2,1,0:T(8,128)(2,1)S(1)} collective-permute-done((bf16[3,128,256]{2,1,0:T(8,128)(2,1)S(1)}, bf16[3,128,256]{2,1,0:T(8,128)(2,1)S(1)}, u32[]{:S(2)}, u32[]{:S(2)}) %collective-permute-start.10) | collective-permute-done | bytes 196640 | tf_op jit(solution)/shard_map/ppermute | solution.py:241
  53.8 2.0 collective-permute-start.4
  56.0 3.3 %collective-permute-start.12 = (bf16[3,64,256]{2,1,0:T(8,128)(2,1)S(1)}, bf16[3,64,256]{2,1,0:T(8,128)(2,1)}, u32[]{:S(2)}, u32[]{:S(2)}) collective-permute-start(bf16[3,64,256]{2,1,0:T(8,128)(2,1)S(1)} %slice.95), channel_id=1, source_target_pairs={{0,192},{64,0},{128,64},{192,128},{1,193},{65,1},{129,65},{193,129... | collective-permute-start | bytes 294920 | tf_op jit(solution)/shard_map/ppermute | solution.py:247
  59.7 11.2 %collective-permute-done.11 = bf16[3,64,256]{2,1,0:T(8,128)(2,1)S(1)} collective-permute-done((bf16[3,64,256]{2,1,0:T(8,128)(2,1)S(1)}, bf16[3,64,256]{2,1,0:T(8,128)(2,1)S(1)}, u32[]{:S(2)}, u32[]{:S(2)}) %collective-permute-start.11) | collective-permute-done | bytes 98336 | tf_op jit(solution)/shard_map/ppermute | solution.py:246
  70.9 3.2 %collective-permute-start.32 = (bf16[4,256,128]{2,1,0:T(8,128)(2,1)S(1)}, bf16[4,256,128]{2,1,0:T(8,128)(2,1)}, u32[]{:S(2)}, u32[]{:S(2)}) collective-permute-start(bf16[4,256,128]{2,1,0:T(8,128)(2,1)S(1)} %get-tuple-element.20), channel_id=1, source_target_pairs={{0,24},{8,0},{16,8},{24,16},{1,25},{9,1},{17,9},{25,17},{2,26},{10... | collective-permute-start | bytes 786440 | tf_op jit(solution)/shard_map/ppermute | solution.py:242
  74.2 1.0 maximum_bitcast_fusion.9
  75.2 2.4 %fusion.5 = (bf16[1,4,3,128,256]{4,3,2,0,1:T(8,128)(2,1)}, bf16[4,3,128,256]{3,2,1,0:T(8,128)(2,1)}) fusion(bf16[1,3,128,256]{3,2,1,0:T(8,128)(2,1)} %bitcast.98, bf16[1,3,128,256]{3,2,1,0:T(8,128)(2,1)S(1)} %maximum_bitcast_fusion.9, bf16[1,3,128,256]{3,2,1,0:T(8,128)(2,1)} %bitcast.99, bf16[1,3,128,256]{3,2,1,0:T(8,128)(2,1)} %bitcast.101), kind=kLoop, calls=%fused_computation.39 | loop fusion | flops 1179648 | bytes 2359296 | tf_op jit(solution)/shard_map/stack | solution.py:251
  77.6 3.2 %collective-permute-start.26 = (bf16[2,256,128]{2,1,0:T(8,128)(2,1)S(1)}, bf16[2,256,128]{2,1,0:T(8,128)(2,1)S(1)}, u32[]{:S(2)}, u32[]{:S(2)}) collective-permute-start(bf16[2,256,128]{2,1,0:T(8,128)(2,1)S(1)} %slice.101), channel_id=1, source_target_pairs={{0,192},{64,0},{128,64},{192,128},{1,193},{65,1},{129,65},{193,129... | collective-permute-start | bytes 393224 | tf_op jit(solution)/shard_map/ppermute | solution.py:247
  81.5 2.0 collective-permute-start.13
  86.0 1.0 maximum_bitcast_fusion.6
  87.0 2.1 collective-permute-start.35
  89.5 10.6 %collective-permute-done.34 = bf16[2,256,128]{2,1,0:T(8,128)(2,1)} collective-permute-done((bf16[2,256,128]{2,1,0:T(8,128)(2,1)}, bf16[2,256,128]{2,1,0:T(8,128)(2,1)}, u32[]{:S(2)}, u32[]{:S(2)}) %collective-permute-start.34) | collective-permute-done | bytes 131104 | tf_op jit(solution)/shard_map/ppermute | solution.py:246
  100.5 1.2 maximum_bitcast_fusion.2
  101.7 1.1 maximum_bitcast_fusion.7
  102.8 1.1 maximum_bitcast_fusion.3
  103.9 1.0 slice.96
  105.4 1.0 slice.97
  106.4 1.8 collective-permute-start.16
  108.8 4.1 %collective-permute-done.15 = bf16[2,3,128,256]{3,2,1,0:T(8,128)(2,1)S(1)} collective-permute-done((bf16[2,3,128,256]{3,2,1,0:T(8,128)(2,1)S(1)}, bf16[2,3,128,256]{3,2,1,0:T(8,128)(2,1)S(1)}, u32[]{:S(2)}, u32[]{:S(2)}) %collective-permute-start.15) | collective-permute-done | bytes 393248 | tf_op jit(solution)/shard_map/ppermute | solution.py:246
  112.8 2.3 collective-permute-done.16
  115.2 1.6 maximum_bitcast_fusion.1
  116.8 3.2 %pad_maximum_fusion.w_ref = bf16[4,2,4,3,128,256]{5,4,3,2,1,0:T(8,128)(2,1)} fusion(bf16[4,1,4,3,128,256]{5,4,3,2,1,0:T(8,128)(2,1)S(1)} %maximum_bitcast_fusion.1, bf16[4,1,4,3,128,256]{5,4,3,2,1,0:T(8,128)(2,1)S(1)} %maximum_bitcast_fusion), kind=kLoop, calls=%fused_computation | loop fusion | flops 3145728 | bytes 12582912 | tf_op jit(solution)/shard_map/stack | solution.py:283
  119.9 15.8 %project.1 = (bf16[3,2,512,256]{3,2,1,0:T(8,128)(2,1)S(1)}, bf16[2,144,256]{2,1,0:T(8,128)(2,1)S(1)}, bf16[144,256]{1,0:T(8,128)(2,1)S(1)}) custom-call(s32[3]{0:T(128)S(1)} %pad_add_fusion.at_ref, bf16[2,8,592,512]{3,2,1,0:T(8,128)(2,1)} %bitcast.108, bf16[4,2,4,3,128,256]{5,4,3,2,1,0:T(8,128)(2,1)} %pad_maximum_fusion.w_ref, ...), custom_call_target="tpu_custom_call" | custom-call | flops 7449083904 | bytes 18000000 | tf_op jit(solution)/shard_map/project/pallas_call | solution.py:98
  135.8 3.9 %collective-permute-start.17 = (bf16[144,256]{1,0:T(8,128)(2,1)S(1)}, bf16[144,256]{1,0:T(8,128)(2,1)S(1)}, u32[]{:S(2)}, u32[]{:S(2)}) collective-permute-start(bf16[144,256]{1,0:T(8,128)(2,1)S(1)} %get-tuple-element.21), channel_id=1, source_target_pairs={{0,8},{8,16},{16,24},{24,64},{64,72},{72,80},{80,88},{88,128},{128... | collective-permute-start | bytes 221192 | tf_op jit(solution)/shard_map/ppermute | solution.py:296
  139.9 2.7 %collective-permute-start.18 = (bf16[144,256]{1,0:T(8,128)(2,1)S(1)}, bf16[144,256]{1,0:T(8,128)(2,1)S(1)}, u32[]{:S(2)}, u32[]{:S(2)}) collective-permute-start(bf16[144,256]{1,0:T(8,128)(2,1)S(1)} %get-tuple-element.22), channel_id=1, source_target_pairs={{0,8},{8,16},{16,24},{24,0},{64,72},{72,80},{80,88},{88,64},{128,1... | collective-permute-start | bytes 221192 | tf_op jit(solution)/shard_map/ppermute | solution.py:297
  142.6 2.0 collective-permute-done.18
  144.6 8.4 %mix_out.1 = bf16[2,8,512,512]{3,2,1,0:T(8,128)(2,1)} custom-call(s32[3]{0:T(128)S(1)} %pad_add_fusion.at_ref, bf16[3,2,512,256]{3,2,1,0:T(8,128)(2,1)S(1)} %get-tuple-element.8.proj_ref, bf16[2,144,256]{2,1,0:T(8,128)(2,1)S(1)} %pad_maximum_fusion.7.halo_ref, bf16[16,128,256]{2,1,0:T(8,128)(2,1)S(1)} %toeplitz.1.band_ref, ...), custom_call_target="tpu_custom_call" | custom-call | flops 4294967296 | bytes 14000000 | tf_op jit(solution)/shard_map/mix_out/pallas_call | solution.py:208
  153.1 67.8 %reduce-scatter.2.cloned.1.call-done = bf16[1,512,512]{2,1,0:T(8,128)(2,1)} async-done(((bf16[16,512,512]{2,1,0:T(8,128)(2,1)}), bf16[1,512,512]{2,1,0:T(8,128)(2,1)}) %reduce-scatter.2.cloned.1.call-update) | async-done | bytes 524304 | tf_op jit(solution)/shard_map/reduce_scatter | solution.py:303
  220.9 2.0 fusion
  (124 shorter events, 11.1 us)
Async XLA Ops:
  6.5 77.0 %copy-start = (f32[3,3,512]{2,1,0:T(4,128)S(1)}, f32[3,3,512]{2,1,0:T(4,128)}, u32[]{:S(2)}) copy-start(f32[3,3,512]{2,1,0:T(4,128)} %param.12) | copy-start | bytes 55300
  6.5 113.4 %all-gather.3.cloned.1.call-start = ((), (), s32[]{:S(2)}) async-start(), calls=%async_computation.2 | async-start | bytes 10305536 | tf_op jit(solution)/shard_map/all_gather | solution.py:274
  10.2 210.6 %reduce-scatter.2.cloned.1.call-start = ((), (), s32[]{:S(2)}) async-start(), calls=%async_computation.1 | async-start | bytes 8912896 | tf_op jit(solution)/shard_map/reduce_scatter | solution.py:303
  11.2 9.2 %collective-permute-start.20 = (bf16[256,128]{1,0:T(8,128)(2,1)S(1)}, bf16[256,128]{1,0:T(8,128)(2,1)S(1)}, u32[]{:S(2)}, u32[]{:S(2)}) collective-permute-start(bf16[256,128]{1,0:T(8,128)(2,1)S(1)} %get-tuple-element.23), channel_id=1, source_target_pairs={{0,8},{8,16},{16,24},{24,0},{1,9},{9,17},{17,25},{25,1},{2,10},{10... | collective-permute-start | bytes 196616 | tf_op jit(solution)/shard_map/ppermute | solution.py:241
  12.7 9.2 %collective-permute-start.19 = (bf16[256,128]{1,0:T(8,128)(2,1)S(1)}, bf16[256,128]{1,0:T(8,128)(2,1)S(1)}, u32[]{:S(2)}, u32[]{:S(2)}) collective-permute-start(bf16[256,128]{1,0:T(8,128)(2,1)S(1)} %get-tuple-element.23), channel_id=1, source_target_pairs={{0,24},{8,0},{16,8},{24,16},{1,25},{9,1},{17,9},{25,17},{2,26},{10... | collective-permute-start | bytes 196616 | tf_op jit(solution)/shard_map/ppermute | solution.py:242
  13.6 13.0 %collective-permute-start.27 = (bf16[256,128]{1,0:T(8,128)(2,1)S(1)}, bf16[256,128]{1,0:T(8,128)(2,1)S(1)}, u32[]{:S(2)}, u32[]{:S(2)}) collective-permute-start(bf16[256,128]{1,0:T(8,128)(2,1)S(1)} %get-tuple-element.24), channel_id=1, source_target_pairs={{0,32},{32,0},{1,33},{33,1},{2,34},{34,2},{3,35},{35,3},{4,36},{36... | collective-permute-start | bytes 196616 | tf_op jit(solution)/shard_map/ppermute | solution.py:280
  20.4 8.5 %collective-permute-start.21 = (bf16[128,128]{1,0:T(8,128)(2,1)S(1)}, bf16[128,128]{1,0:T(8,128)(2,1)S(1)}, u32[]{:S(2)}, u32[]{:S(2)}) collective-permute-start(bf16[128,128]{1,0:T(8,128)(2,1)S(1)} %slice.98), channel_id=1, source_target_pairs={{0,8},{8,16},{16,24},{24,0},{1,9},{9,17},{17,25},{25,1},{2,10},{10... | collective-permute-start | bytes 98312 | tf_op jit(solution)/shard_map/ppermute | solution.py:246
  21.9 8.6 %collective-permute-start.22 = (bf16[128,128]{1,0:T(8,128)(2,1)S(1)}, bf16[128,128]{1,0:T(8,128)(2,1)S(1)}, u32[]{:S(2)}, u32[]{:S(2)}) collective-permute-start(bf16[128,128]{1,0:T(8,128)(2,1)S(1)} %slice.99), channel_id=1, source_target_pairs={{0,24},{8,0},{16,8},{24,16},{1,25},{9,1},{17,9},{25,17},{2,26},{10... | collective-permute-start | bytes 98312 | tf_op jit(solution)/shard_map/ppermute | solution.py:247
  23.5 14.2 %collective-permute-start.1 = (bf16[3,128,256]{2,1,0:T(8,128)(2,1)S(1)}, bf16[3,128,256]{2,1,0:T(8,128)(2,1)S(1)}, u32[]{:S(2)}, u32[]{:S(2)}) collective-permute-start(bf16[3,128,256]{2,1,0:T(8,128)(2,1)S(1)} %get-tuple-element.15), channel_id=1, source_target_pairs={{0,8},{8,16},{16,24},{24,0},{1,9},{9,17},{17,25},{25,1},{2,10},{10... | collective-permute-start | bytes 589832 | tf_op jit(solution)/shard_map/ppermute | solution.py:241
  25.1 12.7 %collective-permute-start = (bf16[3,128,256]{2,1,0:T(8,128)(2,1)S(1)}, bf16[3,128,256]{2,1,0:T(8,128)(2,1)S(1)}, u32[]{:S(2)}, u32[]{:S(2)}) collective-permute-start(bf16[3,128,256]{2,1,0:T(8,128)(2,1)S(1)} %get-tuple-element.15), channel_id=1, source_target_pairs={{0,24},{8,0},{16,8},{24,16},{1,25},{9,1},{17,9},{25,17},{2,26},{10... | collective-permute-start | bytes 589832 | tf_op jit(solution)/shard_map/ppermute | solution.py:242
  26.6 18.4 %collective-permute-start.8 = (bf16[3,128,256]{2,1,0:T(8,128)(2,1)S(1)}, bf16[3,128,256]{2,1,0:T(8,128)(2,1)S(1)}, u32[]{:S(2)}, u32[]{:S(2)}) collective-permute-start(bf16[3,128,256]{2,1,0:T(8,128)(2,1)S(1)} %get-tuple-element.16), channel_id=1, source_target_pairs={{0,32},{32,0},{1,33},{33,1},{2,34},{34,2},{3,35},{35,3},{4,36},{36... | collective-permute-start | bytes 589832 | tf_op jit(solution)/shard_map/ppermute | solution.py:280
  28.9 5.5 %collective-permute-start.29 = (bf16[256,128]{1,0:T(8,128)(2,1)S(1)}, bf16[256,128]{1,0:T(8,128)(2,1)S(1)}, u32[]{:S(2)}, u32[]{:S(2)}) collective-permute-start(bf16[256,128]{1,0:T(8,128)(2,1)S(1)} %collective-permute-done.27), channel_id=1, source_target_pairs={{0,64},{64,128},{128,192},{192,0},{1,65},{65,129},{129,193},{193,1... | collective-permute-start | bytes 196616 | tf_op jit(solution)/shard_map/ppermute | solution.py:241
  30.5 4.6 %collective-permute-start.28 = (bf16[256,128]{1,0:T(8,128)(2,1)S(1)}, bf16[256,128]{1,0:T(8,128)(2,1)S(1)}, u32[]{:S(2)}, u32[]{:S(2)}) collective-permute-start(bf16[256,128]{1,0:T(8,128)(2,1)S(1)} %collective-permute-done.27), channel_id=1, source_target_pairs={{0,192},{64,0},{128,64},{192,128},{1,193},{65,1},{129,65},{193,129... | collective-permute-start | bytes 196616 | tf_op jit(solution)/shard_map/ppermute | solution.py:242
  34.4 6.7 %collective-permute-start.30 = (bf16[128,128]{1,0:T(8,128)(2,1)S(1)}, bf16[128,128]{1,0:T(8,128)(2,1)S(1)}, u32[]{:S(2)}, u32[]{:S(2)}) collective-permute-start(bf16[128,128]{1,0:T(8,128)(2,1)S(1)} %slice.102), channel_id=1, source_target_pairs={{0,64},{64,128},{128,192},{192,0},{1,65},{65,129},{129,193},{193,1... | collective-permute-start | bytes 98312 | tf_op jit(solution)/shard_map/ppermute | solution.py:246
  35.1 7.6 %collective-permute-start.31 = (bf16[128,128]{1,0:T(8,128)(2,1)S(1)}, bf16[128,128]{1,0:T(8,128)(2,1)S(1)}, u32[]{:S(2)}, u32[]{:S(2)}) collective-permute-start(bf16[128,128]{1,0:T(8,128)(2,1)S(1)} %slice.103), channel_id=1, source_target_pairs={{0,192},{64,0},{128,64},{192,128},{1,193},{65,1},{129,65},{193,129... | collective-permute-start | bytes 98312 | tf_op jit(solution)/shard_map/ppermute | solution.py:247
  37.7 18.3 %collective-permute-start.24 = (bf16[4,256,128]{2,1,0:T(8,128)(2,1)S(1)}, bf16[4,256,128]{2,1,0:T(8,128)(2,1)S(1)}, u32[]{:S(2)}, u32[]{:S(2)}) collective-permute-start(bf16[4,256,128]{2,1,0:T(8,128)(2,1)S(1)} %get-tuple-element.18), channel_id=1, source_target_pairs={{0,64},{64,128},{128,192},{192,0},{1,65},{65,129},{129,193},{193,1... | collective-permute-start | bytes 786440 | tf_op jit(solution)/shard_map/ppermute | solution.py:241
  37.8 21.6 %collective-permute-start.23 = (bf16[4,256,128]{2,1,0:T(8,128)(2,1)S(1)}, bf16[4,256,128]{2,1,0:T(8,128)(2,1)S(1)}, u32[]{:S(2)}, u32[]{:S(2)}) collective-permute-start(bf16[4,256,128]{2,1,0:T(8,128)(2,1)S(1)} %get-tuple-element.18), channel_id=1, source_target_pairs={{0,192},{64,0},{128,64},{192,128},{1,193},{65,1},{129,65},{193,129... | collective-permute-start | bytes 786440 | tf_op jit(solution)/shard_map/ppermute | solution.py:242
  41.1 5.8 %collective-permute-start.2 = (bf16[3,64,256]{2,1,0:T(8,128)(2,1)S(1)}, bf16[3,64,256]{2,1,0:T(8,128)(2,1)S(1)}, u32[]{:S(2)}, u32[]{:S(2)}) collective-permute-start(bf16[3,64,256]{2,1,0:T(8,128)(2,1)S(1)} %slice.90), channel_id=1, source_target_pairs={{0,8},{8,16},{16,24},{24,0},{1,9},{9,17},{17,25},{25,1},{2,10},{10... | collective-permute-start | bytes 294920 | tf_op jit(solution)/shard_map/ppermute | solution.py:246
  42.7 5.6 %collective-permute-start.3 = (bf16[3,64,256]{2,1,0:T(8,128)(2,1)S(1)}, bf16[3,64,256]{2,1,0:T(8,128)(2,1)S(1)}, u32[]{:S(2)}, u32[]{:S(2)}) collective-permute-start(bf16[3,64,256]{2,1,0:T(8,128)(2,1)S(1)} %slice.91), channel_id=1, source_target_pairs={{0,24},{8,0},{16,8},{24,16},{1,25},{9,1},{17,9},{25,17},{2,26},{10... | collective-permute-start | bytes 294920 | tf_op jit(solution)/shard_map/ppermute | solution.py:247
  45.0 14.6 %copy-start.14 = (bf16[3,128,256]{2,1,0:T(8,128)(2,1)}, bf16[3,128,256]{2,1,0:T(8,128)(2,1)S(1)}, u32[]{:S(2)}) copy-start(bf16[3,128,256]{2,1,0:T(8,128)(2,1)S(1)} %collective-permute-done.8) | copy-start | bytes 589828
  45.0 8.8 %collective-permute-start.10 = (bf16[3,128,256]{2,1,0:T(8,128)(2,1)S(1)}, bf16[3,128,256]{2,1,0:T(8,128)(2,1)S(1)}, u32[]{:S(2)}, u32[]{:S(2)}) collective-permute-start(bf16[3,128,256]{2,1,0:T(8,128)(2,1)S(1)} %collective-permute-done.8), channel_id=1, source_target_pairs={{0,64},{64,128},{128,192},{192,0},{1,65},{65,129},{129,193},{193,1... | collective-permute-start | bytes 589832 | tf_op jit(solution)/shard_map/ppermute | solution.py:241
  46.9 9.0 %collective-permute-start.9 = (bf16[3,128,256]{2,1,0:T(8,128)(2,1)S(1)}, bf16[3,128,256]{2,1,0:T(8,128)(2,1)S(1)}, u32[]{:S(2)}, u32[]{:S(2)}) collective-permute-start(bf16[3,128,256]{2,1,0:T(8,128)(2,1)S(1)} %collective-permute-done.8), channel_id=1, source_target_pairs={{0,192},{64,0},{128,64},{192,128},{1,193},{65,1},{129,65},{193,129... | collective-permute-start | bytes 589832 | tf_op jit(solution)/shard_map/ppermute | solution.py:242
  48.3 35.2 %copy-start.18 = (bf16[32,128]{1,0:T(8,128)(2,1)S(1)}, bf16[32,128]{1,0:T(8,128)(2,1)}, u32[]{:S(2)}) copy-start(bf16[32,128]{1,0:T(8,128)(2,1)} %param.13) | copy-start | bytes 24580
  48.3 36.0 %copy-start.19 = (f32[512]{0:T(512)S(1)}, f32[512]{0:T(512)}, u32[]{:S(2)}) copy-start(f32[512]{0:T(512)} %param.14) | copy-start | bytes 6148
  49.6 37.4 %collective-permute-start.5 = (bf16[4,3,128,256]{3,2,1,0:T(8,128)(2,1)}, bf16[4,3,128,256]{3,2,1,0:T(8,128)(2,1)S(1)}, u32[]{:S(2)}, u32[]{:S(2)}) collective-permute-start(bf16[4,3,128,256]{3,2,1,0:T(8,128)(2,1)} %get-tuple-element.12), channel_id=1, source_target_pairs={{0,64},{64,128},{128,192},{192,0},{1,65},{65,129},{129,193},{193,1... | collective-permute-start | bytes 2359304 | tf_op jit(solution)/shard_map/ppermute | solution.py:241
  53.8 35.3 %collective-permute-start.4 = (bf16[4,3,128,256]{3,2,1,0:T(8,128)(2,1)}, bf16[4,3,128,256]{3,2,1,0:T(8,128)(2,1)S(1)}, u32[]{:S(2)}, u32[]{:S(2)}) collective-permute-start(bf16[4,3,128,256]{3,2,1,0:T(8,128)(2,1)} %get-tuple-element.12), channel_id=1, source_target_pairs={{0,192},{64,0},{128,64},{192,128},{1,193},{65,1},{129,65},{193,129... | collective-permute-start | bytes 2359304 | tf_op jit(solution)/shard_map/ppermute | solution.py:242
  55.9 15.0 %collective-permute-start.11 = (bf16[3,64,256]{2,1,0:T(8,128)(2,1)S(1)}, bf16[3,64,256]{2,1,0:T(8,128)(2,1)S(1)}, u32[]{:S(2)}, u32[]{:S(2)}) collective-permute-start(bf16[3,64,256]{2,1,0:T(8,128)(2,1)S(1)} %slice.94), channel_id=1, source_target_pairs={{0,64},{64,128},{128,192},{192,0},{1,65},{65,129},{129,193},{193,1... | collective-permute-start | bytes 294920 | tf_op jit(solution)/shard_map/ppermute | solution.py:246
  56.0 18.1 %copy-start.8 = (bf16[4,256,128]{2,1,0:T(8,128)(2,1)}, bf16[4,256,128]{2,1,0:T(8,128)(2,1)S(1)}, u32[]{:S(2)}) copy-start(bf16[4,256,128]{2,1,0:T(8,128)(2,1)S(1)} %collective-permute-done.24) | copy-start | bytes 786436
  56.0 18.1 %collective-permute-start.12 = (bf16[3,64,256]{2,1,0:T(8,128)(2,1)S(1)}, bf16[3,64,256]{2,1,0:T(8,128)(2,1)}, u32[]{:S(2)}, u32[]{:S(2)}) collective-permute-start(bf16[3,64,256]{2,1,0:T(8,128)(2,1)S(1)} %slice.95), channel_id=1, source_target_pairs={{0,192},{64,0},{128,64},{192,128},{1,193},{65,1},{129,65},{193,129... | collective-permute-start | bytes 294920 | tf_op jit(solution)/shard_map/ppermute | solution.py:247
  59.4 25.0 %copy-start.9 = (bf16[4,256,128]{2,1,0:T(8,128)(2,1)}, bf16[4,256,128]{2,1,0:T(8,128)(2,1)S(1)}, u32[]{:S(2)}) copy-start(bf16[4,256,128]{2,1,0:T(8,128)(2,1)S(1)} %collective-permute-done.23) | copy-start | bytes 786436
  59.4 18.2 %collective-permute-start.33 = (bf16[4,256,128]{2,1,0:T(8,128)(2,1)S(1)}, bf16[4,256,128]{2,1,0:T(8,128)(2,1)S(1)}, u32[]{:S(2)}, u32[]{:S(2)}) collective-permute-start(bf16[4,256,128]{2,1,0:T(8,128)(2,1)S(1)} %get-tuple-element.20), channel_id=1, source_target_pairs={{0,8},{8,16},{16,24},{24,0},{1,9},{9,17},{17,25},{25,1},{2,10},{10... | collective-permute-start | bytes 786440 | tf_op jit(solution)/shard_map/ppermute | solution.py:241
  70.9 9.9 %collective-permute-start.32 = (bf16[4,256,128]{2,1,0:T(8,128)(2,1)S(1)}, bf16[4,256,128]{2,1,0:T(8,128)(2,1)}, u32[]{:S(2)}, u32[]{:S(2)}) collective-permute-start(bf16[4,256,128]{2,1,0:T(8,128)(2,1)S(1)} %get-tuple-element.20), channel_id=1, source_target_pairs={{0,24},{8,0},{16,8},{24,16},{1,25},{9,1},{17,9},{25,17},{2,26},{10... | collective-permute-start | bytes 786440 | tf_op jit(solution)/shard_map/ppermute | solution.py:242
  74.1 6.7 %collective-permute-start.25 = (bf16[2,256,128]{2,1,0:T(8,128)(2,1)S(1)}, bf16[2,256,128]{2,1,0:T(8,128)(2,1)S(1)}, u32[]{:S(2)}, u32[]{:S(2)}) collective-permute-start(bf16[2,256,128]{2,1,0:T(8,128)(2,1)S(1)} %slice.100), channel_id=1, source_target_pairs={{0,64},{64,128},{128,192},{192,0},{1,65},{65,129},{129,193},{193,1... | collective-permute-start | bytes 393224 | tf_op jit(solution)/shard_map/ppermute | solution.py:246
  77.6 6.6 %collective-permute-start.26 = (bf16[2,256,128]{2,1,0:T(8,128)(2,1)S(1)}, bf16[2,256,128]{2,1,0:T(8,128)(2,1)S(1)}, u32[]{:S(2)}, u32[]{:S(2)}) collective-permute-start(bf16[2,256,128]{2,1,0:T(8,128)(2,1)S(1)} %slice.101), channel_id=1, source_target_pairs={{0,192},{64,0},{128,64},{192,128},{1,193},{65,1},{129,65},{193,129... | collective-permute-start | bytes 393224 | tf_op jit(solution)/shard_map/ppermute | solution.py:247
  80.8 23.1 %collective-permute-start.14 = (bf16[4,3,128,256]{3,2,1,0:T(8,128)(2,1)}, bf16[4,3,128,256]{3,2,1,0:T(8,128)(2,1)}, u32[]{:S(2)}, u32[]{:S(2)}) collective-permute-start(bf16[4,3,128,256]{3,2,1,0:T(8,128)(2,1)} %get-tuple-element.14), channel_id=1, source_target_pairs={{0,8},{8,16},{16,24},{24,0},{1,9},{9,17},{17,25},{25,1},{2,10},{10... | collective-permute-start | bytes 2359304 | tf_op jit(solution)/shard_map/ppermute | solution.py:241
  81.5 23.9 %collective-permute-start.13 = (bf16[4,3,128,256]{3,2,1,0:T(8,128)(2,1)}, bf16[4,3,128,256]{3,2,1,0:T(8,128)(2,1)}, u32[]{:S(2)}, u32[]{:S(2)}) collective-permute-start(bf16[4,3,128,256]{3,2,1,0:T(8,128)(2,1)} %get-tuple-element.14), channel_id=1, source_target_pairs={{0,24},{8,0},{16,8},{24,16},{1,25},{9,1},{17,9},{25,17},{2,26},{10... | collective-permute-start | bytes 2359304 | tf_op jit(solution)/shard_map/ppermute | solution.py:242
  84.2 15.9 %collective-permute-start.34 = (bf16[2,256,128]{2,1,0:T(8,128)(2,1)}, bf16[2,256,128]{2,1,0:T(8,128)(2,1)}, u32[]{:S(2)}, u32[]{:S(2)}) collective-permute-start(bf16[2,256,128]{2,1,0:T(8,128)(2,1)} %slice.104), channel_id=1, source_target_pairs={{0,8},{8,16},{16,24},{24,0},{1,9},{9,17},{17,25},{25,1},{2,10},{10... | collective-permute-start | bytes 393224 | tf_op jit(solution)/shard_map/ppermute | solution.py:246
  85.0 17.8 %copy-start.11 = (bf16[4,256,128]{2,1,0:T(8,128)(2,1)S(1)}, bf16[4,256,128]{2,1,0:T(8,128)(2,1)}, u32[]{:S(2)}) copy-start(bf16[4,256,128]{2,1,0:T(8,128)(2,1)} %copy-done.10) | copy-start | bytes 786436
  87.0 13.5 %copy-start.4 = (bf16[4,3,128,256]{3,2,1,0:T(8,128)(2,1)}, bf16[4,3,128,256]{3,2,1,0:T(8,128)(2,1)S(1)}, u32[]{:S(2)}) copy-start(bf16[4,3,128,256]{3,2,1,0:T(8,128)(2,1)S(1)} %collective-permute-done.5) | copy-start | bytes 2359300
  87.0 14.7 %collective-permute-start.35 = (bf16[2,256,128]{2,1,0:T(8,128)(2,1)S(1)}, bf16[2,256,128]{2,1,0:T(8,128)(2,1)S(1)}, u32[]{:S(2)}, u32[]{:S(2)}) collective-permute-start(bf16[2,256,128]{2,1,0:T(8,128)(2,1)S(1)} %slice.105), channel_id=1, source_target_pairs={{0,24},{8,0},{16,8},{24,16},{1,25},{9,1},{17,9},{25,17},{2,26},{10... | collective-permute-start | bytes 393224 | tf_op jit(solution)/shard_map/ppermute | solution.py:247
  89.1 11.4 %copy-start.6 = (bf16[4,3,128,256]{3,2,1,0:T(8,128)(2,1)}, bf16[4,3,128,256]{3,2,1,0:T(8,128)(2,1)S(1)}, u32[]{:S(2)}) copy-start(bf16[4,3,128,256]{3,2,1,0:T(8,128)(2,1)S(1)} %collective-permute-done.4) | copy-start | bytes 2359300
  89.1 19.1 %collective-permute-start.6 = (bf16[2,3,128,256]{3,2,1,0:T(8,128)(2,1)S(1)}, bf16[2,3,128,256]{3,2,1,0:T(8,128)(2,1)S(1)}, u32[]{:S(2)}, u32[]{:S(2)}) collective-permute-start(bf16[2,3,128,256]{3,2,1,0:T(8,128)(2,1)S(1)} %slice.92), channel_id=1, source_target_pairs={{0,64},{64,128},{128,192},{192,0},{1,65},{65,129},{129,193},{193,1... | collective-permute-start | bytes 1179656 | tf_op jit(solution)/shard_map/ppermute | solution.py:246
  100.1 8.1 %collective-permute-start.7 = (bf16[2,3,128,256]{3,2,1,0:T(8,128)(2,1)S(1)}, bf16[2,3,128,256]{3,2,1,0:T(8,128)(2,1)S(1)}, u32[]{:S(2)}, u32[]{:S(2)}) collective-permute-start(bf16[2,3,128,256]{3,2,1,0:T(8,128)(2,1)S(1)} %slice.93), channel_id=1, source_target_pairs={{0,192},{64,0},{128,64},{192,128},{1,193},{65,1},{129,65},{193,129... | collective-permute-start | bytes 1179656 | tf_op jit(solution)/shard_map/ppermute | solution.py:247
  104.9 7.9 %collective-permute-start.15 = (bf16[2,3,128,256]{3,2,1,0:T(8,128)(2,1)S(1)}, bf16[2,3,128,256]{3,2,1,0:T(8,128)(2,1)S(1)}, u32[]{:S(2)}, u32[]{:S(2)}) collective-permute-start(bf16[2,3,128,256]{3,2,1,0:T(8,128)(2,1)S(1)} %slice.96), channel_id=1, source_target_pairs={{0,8},{8,16},{16,24},{24,0},{1,9},{9,17},{17,25},{25,1},{2,10},{10... | collective-permute-start | bytes 1179656 | tf_op jit(solution)/shard_map/ppermute | solution.py:246
  106.4 8.7 %collective-permute-start.16 = (bf16[2,3,128,256]{3,2,1,0:T(8,128)(2,1)S(1)}, bf16[2,3,128,256]{3,2,1,0:T(8,128)(2,1)S(1)}, u32[]{:S(2)}, u32[]{:S(2)}) collective-permute-start(bf16[2,3,128,256]{3,2,1,0:T(8,128)(2,1)S(1)} %slice.97), channel_id=1, source_target_pairs={{0,24},{8,0},{16,8},{24,16},{1,25},{9,1},{17,9},{25,17},{2,26},{10... | collective-permute-start | bytes 1179656 | tf_op jit(solution)/shard_map/ppermute | solution.py:247
  135.8 6.8 %collective-permute-start.17 = (bf16[144,256]{1,0:T(8,128)(2,1)S(1)}, bf16[144,256]{1,0:T(8,128)(2,1)S(1)}, u32[]{:S(2)}, u32[]{:S(2)}) collective-permute-start(bf16[144,256]{1,0:T(8,128)(2,1)S(1)} %get-tuple-element.21), channel_id=1, source_target_pairs={{0,8},{8,16},{16,24},{24,64},{64,72},{72,80},{80,88},{88,128},{128... | collective-permute-start | bytes 221192 | tf_op jit(solution)/shard_map/ppermute | solution.py:296
  139.9 4.7 %collective-permute-start.18 = (bf16[144,256]{1,0:T(8,128)(2,1)S(1)}, bf16[144,256]{1,0:T(8,128)(2,1)S(1)}, u32[]{:S(2)}, u32[]{:S(2)}) collective-permute-start(bf16[144,256]{1,0:T(8,128)(2,1)S(1)} %get-tuple-element.22), channel_id=1, source_target_pairs={{0,8},{8,16},{16,24},{24,0},{64,72},{72,80},{80,88},{88,64},{128,1... | collective-permute-start | bytes 221192 | tf_op jit(solution)/shard_map/ppermute | solution.py:297
  153.0 67.8 %copy-start.3 = (bf16[512,512]{1,0:T(8,128)(2,1)S(1)}, bf16[512,512]{1,0:T(8,128)(2,1)}, u32[]{:S(2)}) copy-start(bf16[512,512]{1,0:T(8,128)(2,1)} %param.8) | copy-start | bytes 1572868
  (10 other events, 47.3 us)
Sparse Core Ops, SparseCore 0:
  10.3 73.3 all-gather.2
  153.2 67.6 reduce-scatter.1

commit v3 on v1

--- a/solution.py
+++ b/solution.py
@@ -1,5 +1,3 @@
-import functools
-
 import jax
 import jax.numpy as jnp
 from jax import lax
@@ -32,25 +30,54 @@
     )
 
 
-def project_kernel(x_ref, w_ref, gain_ref, taps_ref, proj_ref, tail_ref, front_ref, acc, ssq):
+def project_kernel(at_ref, x_ref, *refs):
+    kept, got = refs[:5], refs[5:10]
+    taps_ref, proj_ref, tail_ref, front_ref, wide, acc, ssq, sems = refs[10:]
     step = pl.program_id(0)
+    row, z_half, column = at_ref[0], at_ref[1], at_ref[2]
+
+    copies = []
+    for kind, parts in enumerate((kept, got)):
+        half = z_half if kind == 0 else 1 - z_half
+        own, ahead, far_a, far_b, behind = parts
+        for i in range(4):
+            for j in range(4):
+                if i == 2:
+                    source = (far_a if j < 2 else far_b).at[j % 2]
+                else:
+                    source = (own, ahead, None, behind)[i].at[j]
+                y, x = (i, j) if kind == 0 else (j, i)
+                place = wide.at[lax.rem(row + y, 4), :, half, lax.rem(column + x, 4)]
+                copies.append((y, pltpu.make_async_copy(source, place, sems.at[kind, i, j])))
 
     @pl.when(step == 0)
     def _():
         acc[...] = jnp.zeros_like(acc)
         ssq[...] = jnp.zeros_like(ssq)
-
+        for k in range(4):
+            for y, copy in copies:
+                if y == k:
+                    copy.start()
+
+    for k in range(4):
+
+        @pl.when(step == k)
+        def _(k=k):
+            for y, copy in copies:
+                if y == k:
+                    copy.wait()
+
+    place = lax.rem(row + step, 4)
+    gains = [x_ref[1, u, ROWS + FRONT - 16 :].astype(F32)[15:] for u in range(2)]
     for h in range(2):
         parts = []
         for u in range(2):
             lifted = x_ref[h, u].astype(F32)
             ssq[h] += jnp.sum(lifted * lifted, axis=-1, keepdims=True)
-            parts.append((lifted * gain_ref[0, u : u + 1]).astype(BF16))
+            parts.append((lifted * gains[u]).astype(BF16))
         scaled = jnp.concatenate(parts, axis=1)
         for s in range(3):
-            weights = jnp.concatenate(
-                [w_ref[x, u, s] for u in range(2) for x in range(4)], axis=0
-            )
+            weights = wide[place, s].reshape(2 * WIDE, CH)
             acc[h, s] += jnp.dot(scaled, weights, preferred_element_type=F32)
 
     @pl.when(step == pl.num_programs(0) - 1)
@@ -87,37 +114,41 @@
         front_ref[LH:] = last.astype(BF16)
 
 
-def project(gathered, weights, gain, taps):
+def project(at, gathered, kept, got, taps):
     count = ROWS + FRONT
     return pl.pallas_call(
         project_kernel,
-        grid=(4,),
-        in_specs=[
-            pl.BlockSpec((2, 2, count, WIDE), lambda k: (0, k, 0, 0)),
-            pl.BlockSpec((4, 2, 3, 128, CH), lambda k: (k, 0, 0, 0, 0)),
-            pl.BlockSpec((1, 2, WIDE), lambda k: (k, 0, 0)),
-            pl.BlockSpec((3, 3, CH), lambda k: (0, 0, 0)),
-        ],
-        out_specs=[
-            pl.BlockSpec((3, 2, ROWS, CH), lambda k: (0, 0, 0, 0)),
-            pl.BlockSpec((2, HALO, CH), lambda k: (0, 0, 0)),
-            pl.BlockSpec((HALO, CH), lambda k: (0, 0)),
-        ],
+        grid_spec=pltpu.PrefetchScalarGridSpec(
+            num_scalar_prefetch=1,
+            grid=(4,),
+            in_specs=[
+                pl.BlockSpec((2, 2, count, WIDE), lambda k, at: (0, lax.rem(at[0] + k, 4), 0, 0)),
+                *[pl.BlockSpec(memory_space=pl.ANY)] * 10,
+                pl.BlockSpec((3, 3, CH), lambda k, at: (0, 0, 0)),
+            ],
+            out_specs=[
+                pl.BlockSpec((3, 2, ROWS, CH), lambda k, at: (0, 0, 0, 0)),
+                pl.BlockSpec((2, HALO, CH), lambda k, at: (0, 0, 0)),
+                pl.BlockSpec((HALO, CH), lambda k, at: (0, 0)),
+            ],
+            scratch_shapes=[
+                pltpu.VMEM((4, 3, 2, 4, 128, CH), BF16),
+                pltpu.VMEM((2, 3, count, CH), F32),
+                pltpu.VMEM((2, count, 1), F32),
+                pltpu.SemaphoreType.DMA((2, 4, 4)),
+            ],
+        ),
         out_shape=[
             jax.ShapeDtypeStruct((3, 2, ROWS, CH), BF16),
             jax.ShapeDtypeStruct((2, HALO, CH), BF16),
             jax.ShapeDtypeStruct((HALO, CH), BF16),
         ],
-        scratch_shapes=[
-            pltpu.VMEM((2, 3, count, CH), F32),
-            pltpu.VMEM((2, count, 1), F32),
-        ],
         compiler_params=pltpu.CompilerParams(vmem_limit_bytes=VMEM),
         cost_estimate=pl.CostEstimate(
             flops=2 * 2 * count * 4096 * 3 * CH, bytes_accessed=18_000_000, transcendentals=0
         ),
         name="project",
-    )(gathered, weights, gain, taps)
+    )(at, gathered, *kept, *got, taps)
 
 
 def toeplitz_kernel(u_ref, out_ref):
@@ -138,7 +169,7 @@
     )(row)
 
 
-def mix_kernel(proj_ref, halo_ref, band_ref, taps_ref, bias_ref, w_ref, out_ref, before, edge):
+def mix_kernel(proj_ref, halo_ref, band_ref, taps_ref, bias_ref, out_ref, before, edge):
     step = pl.program_id(0)
 
     @pl.when(step == 0)
@@ -174,21 +205,14 @@
             one = jnp.dot(band_ref[half * 8 + g], window, preferred_element_type=F32)
             total = jnp.where(lane_group == g, one, total)
         halves.append(total)
-    gated = []
     for h in range(2):
         rows = slice(h * LH, (h + 1) * LH)
         filtered = jnp.concatenate([halves[0][:, rows], halves[1][:, rows]], axis=1)
         value = queries[h] * (filtered + bias_ref[...] * mixes[h].astype(F32))
-        gated.append(value.astype(BF16))
-    stacked = jnp.concatenate(gated, axis=0)
-    for t in range(8):
-        weights = jnp.concatenate([w_ref[t // 2 * 4 + x, t % 2] for x in range(4)], axis=1)
-        partial = jnp.dot(stacked, weights, preferred_element_type=F32).astype(BF16)
-        for h in range(2):
-            out_ref[h, t] = partial[h * LH : (h + 1) * LH]
-
-
-def mix_out(proj, halo, band, taps, bias, weights):
+        out_ref[h] = value.astype(BF16)
+
+
+def mix(proj, halo, band, taps, bias):
     return pl.pallas_call(
         mix_kernel,
         grid=(ROWS // LH,),
@@ -198,20 +222,93 @@
             pl.BlockSpec((GROUPS, LH, 2 * LH), lambda b: (0, 0, 0)),
             pl.BlockSpec((3, 3, CH), lambda b: (0, 0, 0)),
             pl.BlockSpec((1, CH), lambda b: (0, 0)),
-            pl.BlockSpec((16, 2, CH, 128), lambda b: (0, 0, 0, 0)),
         ],
-        out_specs=pl.BlockSpec((2, 8, LH, WIDE), lambda b: (0, 0, b, 0)),
-        out_shape=jax.ShapeDtypeStruct((2, 8, ROWS, WIDE), BF16),
+        out_specs=pl.BlockSpec((2, LH, CH), lambda b: (0, b, 0)),
+        out_shape=jax.ShapeDtypeStruct((2, ROWS, CH), BF16),
         scratch_shapes=[
             pltpu.VMEM((2, LH, CH), BF16),
             pltpu.VMEM((2, 3, 8, CH), F32),
         ],
         compiler_params=pltpu.CompilerParams(vmem_limit_bytes=VMEM),
         cost_estimate=pl.CostEstimate(
-            flops=2 * 1024 * CH * 4096 * 2, bytes_accessed=14_000_000, transcendentals=0
-        ),
-        name="mix_out",
-    )(proj, halo, band, taps, bias, weights)
+            flops=2 * 1024 * CH * 2048, bytes_accessed=4_000_000, transcendentals=0
+        ),
+        name="mix",
+    )(proj, halo, band, taps, bias)
+
+
+def out_kernel(at_ref, mine_ref, other_ref, *refs):
+    parts, (out_ref, wide, sems) = refs[:5], refs[5:]
+    own, ahead, far_a, far_b, behind = parts
+    row, column, crossed = at_ref[0], at_ref[2], at_ref[3]
+    copies = []
+    for i in range(4):
+        for j in range(4):
+            if i == 2:
+                source = (far_a if j < 2 else far_b).at[j % 2]
+            else:
+                source = (own, ahead, None, behind)[i].at[j]
+            lanes = pl.ds(pl.multiple_of(lax.rem(column + j, 4) * 128, 128), 128)
+            place = wide.at[lax.rem(row + i, 4), :, lanes]
+            copies.append(pltpu.make_async_copy(source, place, sems.at[i, j]))
+
+    @pl.when(pl.program_id(0) == 0)
+    def _():
+        for copy in copies:
+            copy.start()
+        for copy in copies:
+            copy.wait()
+
+    swap = crossed == 1
+    first = jnp.where(swap, other_ref[0], mine_ref[0])
+    second = jnp.where(swap, mine_ref[0], other_ref[0])
+    rows = jnp.concatenate([first, second], axis=1)
+    for y in range(4):
+        out_ref[0, y] = jnp.dot(rows, wide[y], preferred_element_type=F32).astype(BF16)
+
+
+def project_out(at, mine, other, parts):
+    return pl.pallas_call(
+        out_kernel,
+        grid_spec=pltpu.PrefetchScalarGridSpec(
+            num_scalar_prefetch=1,
+            grid=(2,),
+            in_specs=[
+                pl.BlockSpec((1, ROWS, CH), lambda h, at: (h, 0, 0)),
+                pl.BlockSpec((1, ROWS, CH), lambda h, at: (h, 0, 0)),
+                *[pl.BlockSpec(memory_space=pl.ANY)] * 5,
+            ],
+            out_specs=pl.BlockSpec((1, 4, ROWS, WIDE), lambda h, at: (h, 0, 0, 0)),
+            scratch_shapes=[
+                pltpu.VMEM((4, 2 * CH, WIDE), BF16),
+                pltpu.SemaphoreType.DMA((4, 4)),
+            ],
+        ),
+        out_shape=jax.ShapeDtypeStruct((2, 4, ROWS, WIDE), BF16),
+        compiler_params=pltpu.CompilerParams(vmem_limit_bytes=VMEM),
+        cost_estimate=pl.CostEstimate(
+            flops=2 * 1024 * 2 * CH * 2048, bytes_accessed=8_000_000, transcendentals=0
+        ),
+        name="project_out",
+    )(at, mine, other, *parts)
+
+
+UP = [(i, (i + 1) % 4) for i in range(4)]
+DOWN = [(i, (i + 3) % 4) for i in range(4)]
+
+
+def ring_parts(piece, axis, cut):
+    behind = lax.ppermute(piece, axis, UP)
+    ahead = lax.ppermute(piece, axis, DOWN)
+    half = piece.shape[cut] // 2
+    far_a = lax.ppermute(lax.slice_in_dim(behind, 0, half, axis=cut), axis, UP)
+    far_b = lax.ppermute(lax.slice_in_dim(ahead, half, 2 * half, axis=cut), axis, DOWN)
+    return piece, ahead, far_a, far_b, behind
+
+
+def ring_line(piece, axis, cut):
+    own, ahead, far_a, far_b, behind = ring_parts(piece, axis, cut)
+    return jnp.stack([own, ahead, jnp.concatenate([far_a, far_b], axis=cut), behind])
 
 
 def on_device(
@@ -221,24 +318,40 @@
     column = lax.axis_index("x")
     leading = (column == 0) & (lax.axis_index("y") == 0)
 
-    padded = jnp.pad(prior_rows, ((0, 2 * FRONT - prior_rows.shape[0]), (0, 0)))
+    core = lax.axis_index("c")
+    at = jnp.stack([lax.axis_index("y"), zh, column, zh ^ core])
+    spare = 2 * FRONT - prior_rows.shape[0]
+    padded = jnp.concatenate(
+        [prior_rows, jnp.zeros((spare - 1, WIDE), BF16), norm_gain[None, :]], axis=0
+    )
     own_front = lax.dynamic_slice_in_dim(padded, zh * FRONT, FRONT, 0)
     own = jnp.concatenate([tokens, own_front], axis=0)
     gathered = lax.all_gather(own, ("zh", "zl", "c"))
     gathered = gathered.reshape(2, 8, ROWS + FRONT, WIDE)
-    gain = lax.all_gather(norm_gain, ("zl", "c")).astype(F32).reshape(4, 2, WIDE)
-
-    halves = in_weight.reshape(3, 128, 2, CH).transpose(2, 0, 1, 3)
-    halves = lax.all_to_all(halves, "zh", 0, 0)
-    w_in = lax.all_gather(halves, ("y", "x"))
-    out_halves = lax.all_to_all(out_weight.reshape(2, CH, 128), "zh", 0, 0)
-    w_out = lax.all_gather(out_halves, ("y", "x"))
+
+    left, right = in_weight[..., :CH], in_weight[..., CH:]
+    kept = jnp.where(zh == 0, left, right)
+    got = lax.ppermute(jnp.where(zh == 0, right, left), "zh", [(0, 1), (1, 0)])
+    kept_line = ring_line(kept, "x", 1)
+    got_line = ring_line(got, "y", 1)
+    kept_parts = ring_parts(kept_line, "y", 0)
+    got_parts = ring_parts(got_line, "x", 0)
+
+    out_weight, kept_parts = lax.optimization_barrier((out_weight, kept_parts))
+    pieces = []
+    for k in range(2):
+        chosen = lax.dynamic_slice_in_dim(out_weight, (core ^ k) * CH, CH, 0)
+        pairs = [(a * 2 + b, (b ^ k) * 2 + a) for a in range(2) for b in range(2)]
+        pieces.append(lax.ppermute(chosen, ("zh", "c"), pairs))
+    out_line = ring_line(jnp.concatenate(pieces, axis=0), "x", 0)
+    out_line, kept_parts, got_parts = lax.optimization_barrier((out_line, kept_parts, got_parts))
+    out_parts = ring_parts(out_line, "y", 0)
 
     taps = lax.dynamic_slice_in_dim(short_filter, zh * CH, CH, 2)
     bias = lax.dynamic_slice_in_dim(mr_bias, zh * CH, CH, 0)[None, :]
     band = toeplitz(lax.dynamic_slice_in_dim(mr_filter, zh * GROUPS, GROUPS, 0))
 
-    proj, tail, front = project(gathered, w_in, gain, taps)
+    proj, tail, front = project(at, gathered, kept_parts, got_parts, taps)
 
     last = column == 3
     to_first = jnp.where(last, tail[1], tail[0])
@@ -249,9 +362,11 @@
     )
     halo = jnp.stack([jnp.where(leading, front, first), second])
 
-    partial = mix_out(proj, halo, band, taps, bias, w_out)
+    mine = mix(proj, halo, band, taps, bias)
+    other = lax.ppermute(mine, "c", [(0, 1), (1, 0)])
+    partial = project_out(at, mine, other, out_parts)
     summed = lax.psum_scatter(
-        partial.reshape(16, ROWS, WIDE), ("zh", "zl", "c"), scatter_dimension=0
+        partial.reshape(8, ROWS, WIDE), ("zh", "zl"), scatter_dimension=0
     )
     return (tokens.astype(F32) + summed.astype(F32)).astype(BF16)
 

time: 298 us -> 220 us (0.74)
  waiting for transfers between devices: 207 us -> 106 us
  starting transfers between devices: 4.76 us -> 57.7 us
  blocking collectives: 47 us -> 0 us
  local copies, waits for them, and re-layouts: 4.15 us -> 11.1 us
  Pallas kernels: 18.7 us -> 23.5 us
  other arithmetic: 2.95 us -> 6.29 us
    all_gather x2 -> x0, waiting for transfers between devices: 69.1 us -> none  [the longest x1 38.5 us: on_device(): w_in = lax.all_gather(halves, ('y', 'x'))]
    all_gather x1, waiting for transfers between devices: 63.7 us -> 0.02 us  [on_device(): gathered = lax.all_gather(own, ('zh', 'zl', 'c'))]
    ppermute x0 -> x28, starting transfers between devices: none -> 52.6 us  [the longest x6 13.4 us: ring_parts(): lax.ppermute(lax.slice_in_dim(ahead, half, 2 * half, axis=cut), axis, DOWN)]
    ppermute x0 -> x28, waiting for transfers between devices: none -> 45.6 us  [the longest x6 19.5 us: ring_parts(): far_a = lax.ppermute(lax.slice_in_dim(behind, 0, half, axis=cut), axis, UP)]
    all_to_all x2 -> x0, blocking collectives: 34.1 us -> none  [the longest x1 22.2 us: on_device(): halves = lax.all_to_all(halves, 'zh', 0, 0)]
    all_gather x1 -> x0, blocking collectives: 12.8 us -> none  [on_device(): lax.all_gather(norm_gain, ('zl', 'c')).astype(F32).reshape(4, 2, WIDE)]
    reduce_scatter x1, waiting for transfers between devices: 70.5 us -> 58.3 us  [on_device(): lax.psum_scatter(partial.reshape(8, ROWS, WIDE), ('zh', 'zl'), scatter_di...]
    slice x0 -> x12, local copies, waits for them, and re-layouts: none -> 5.24 us  [the longest x6 2.68 us: ring_parts(): lax.slice_in_dim(ahead, half, 2 * half, axis=cut)]
  transfers between devices with their start and end apart: 6 -> 32, of which waited for: 6 -> 14; matrix products, arithmetic and copies ran while one was open for 0% -> 4% of each run, Pallas kernels for 4% -> 2%
where the time goes in v3:
time: 220 us; the launch traced here: 219 us
  waiting for transfers between devices  106 us (48%)
  starting transfers between devices  57.7 us (26%)
  Pallas kernels  23.5 us (11%)
  between operations  13.7 us (6%)
  local copies, waits for them, and re-layouts  11.1 us (5%)
  other arithmetic  6.29 us (3%)
    reduce_scatter x1, waiting for transfers between devices, on_device(): lax.psum_scatter(partial.reshape(8, ROWS, WIDE), ('zh', 'zl'), scatter_di...  58.3 us
    ppermute x6, waiting for transfers between devices, ring_parts(): far_a = lax.ppermute(lax.slice_in_dim(behind, 0, half, axis=cut), axis, UP)  19.5 us
    pallas_call x1, Pallas kernels, project(): pl.pallas_call(project_kernel, grid_spec=pltpu.PrefetchScalarGridSpec(num...  15.1 us
    ppermute x6, starting transfers between devices, ring_parts(): lax.ppermute(lax.slice_in_dim(ahead, half, 2 * half, axis=cut), axis, DOWN)  13.4 us
    ppermute x1, waiting for transfers between devices, on_device(): got = lax.ppermute(jnp.where(zh == 0, right, left), 'zh', [(0, 1), (1, 0)])  11.7 us
    ppermute x6, waiting for transfers between devices, ring_parts(): behind = lax.ppermute(piece, axis, UP)  8.93 us
    ppermute x6, starting transfers between devices, ring_parts(): ahead = lax.ppermute(piece, axis, DOWN)  8.93 us
    ppermute x6, starting transfers between devices, ring_parts(): behind = lax.ppermute(piece, axis, UP)  7.94 us
  transfers between devices with their start and end apart: 32, of which 14 were waited for; matrix products, arithmetic and copies ran while one was open for 4% of the time, Pallas kernels for 2%

profile of v3, /device:TPU:2, one launch (start us, length us, event | category | flops | bytes accessed | tf_op | source)
XLA Modules:
  0.0 218.5 jit_solution(12627981293461513351)
XLA Ops:
  7.4 1.0 fusion.2
  8.3 1.9 pad_maximum_fusion.2
  10.4 1.6 collective-permute-start.1
  11.9 0.9 collective-permute-start
  12.8 4.3 %collective-permute-done.1 = bf16[3,128,256]{2,1,0:T(8,128)(2,1)S(1)} collective-permute-done((bf16[3,128,256]{2,1,0:T(8,128)(2,1)S(1)}, bf16[3,128,256]{2,1,0:T(8,128)(2,1)S(1)}, u32[]{:S(2)}, u32[]{:S(2)}) %collective-permute-start.1) | collective-permute-done | bytes 196640 | tf_op jit(solution)/shard_map/ppermute | solution.py:301
  17.1 1.6 collective-permute-start.2
  18.7 1.1 collective-permute-start.3
  19.8 2.5 %collective-permute-done.2 = bf16[3,64,256]{2,1,0:T(8,128)(2,1)S(1)} collective-permute-done((bf16[3,64,256]{2,1,0:T(8,128)(2,1)S(1)}, bf16[3,64,256]{2,1,0:T(8,128)(2,1)S(1)}, u32[]{:S(2)}, u32[]{:S(2)}) %collective-permute-start.2) | collective-permute-done | bytes 98336 | tf_op jit(solution)/shard_map/ppermute | solution.py:304
  22.3 1.1 collective-permute-done.3
  23.5 1.7 collective-permute-start.5
  25.2 1.7 collective-permute-start.4
  26.8 7.1 %collective-permute-start.14 = (bf16[3,128,256]{2,1,0:T(8,128)(2,1)S(1)}, bf16[3,128,256]{2,1,0:T(8,128)(2,1)S(1)}, u32[]{:S(2)}, u32[]{:S(2)}) collective-permute-start(bf16[3,128,256]{2,1,0:T(8,128)(2,1)S(1)} %get-tuple-element.45), channel_id=1, source_target_pairs={{0,32},{32,0},{1,33},{33,1},{2,34},{34,2},{3,35},{35,3},{4,36},{36... | collective-permute-start | bytes 589832 | tf_op jit(solution)/shard_map/ppermute | solution.py:334
  33.9 11.7 %collective-permute-done.14 = bf16[3,128,256]{2,1,0:T(8,128)(2,1)S(1)} collective-permute-done((bf16[3,128,256]{2,1,0:T(8,128)(2,1)S(1)}, bf16[3,128,256]{2,1,0:T(8,128)(2,1)S(1)}, u32[]{:S(2)}, u32[]{:S(2)}) %collective-permute-start.14) | collective-permute-done | bytes 196640 | tf_op jit(solution)/shard_map/ppermute | solution.py:334
  46.0 2.9 %collective-permute-start.15 = (bf16[3,128,256]{2,1,0:T(8,128)(2,1)S(1)}, bf16[3,128,256]{2,1,0:T(8,128)(2,1)S(1)}, u32[]{:S(2)}, u32[]{:S(2)}) collective-permute-start(bf16[3,128,256]{2,1,0:T(8,128)(2,1)S(1)} %collective-permute-done.14), channel_id=1, source_target_pairs={{0,192},{64,0},{128,64},{192,128},{1,193},{65,1},{129,65},{193,129... | collective-permute-start | bytes 589832 | tf_op jit(solution)/shard_map/ppermute | solution.py:302
  48.9 4.6 %collective-permute-done.16 = bf16[3,128,256]{2,1,0:T(8,128)(2,1)S(1)} collective-permute-done((bf16[3,128,256]{2,1,0:T(8,128)(2,1)S(1)}, bf16[3,128,256]{2,1,0:T(8,128)(2,1)S(1)}, u32[]{:S(2)}, u32[]{:S(2)}) %collective-permute-start.16) | collective-permute-done | bytes 196640 | tf_op jit(solution)/shard_map/ppermute | solution.py:301
  53.6 3.3 %collective-permute-start.18 = (bf16[3,64,256]{2,1,0:T(8,128)(2,1)S(1)}, bf16[3,64,256]{2,1,0:T(8,128)(2,1)S(1)}, u32[]{:S(2)}, u32[]{:S(2)}) collective-permute-start(bf16[3,64,256]{2,1,0:T(8,128)(2,1)S(1)} %slice.73), channel_id=1, source_target_pairs={{0,192},{64,0},{128,64},{192,128},{1,193},{65,1},{129,65},{193,129... | collective-permute-start | bytes 294920 | tf_op jit(solution)/shard_map/ppermute | solution.py:305
  56.9 3.3 %collective-permute-done.17 = bf16[3,64,256]{2,1,0:T(8,128)(2,1)S(1)} collective-permute-done((bf16[3,64,256]{2,1,0:T(8,128)(2,1)S(1)}, bf16[3,64,256]{2,1,0:T(8,128)(2,1)S(1)}, u32[]{:S(2)}, u32[]{:S(2)}) %collective-permute-start.17) | collective-permute-done | bytes 98336 | tf_op jit(solution)/shard_map/ppermute | solution.py:304
  61.9 3.2 %collective-permute-start.7 = (bf16[2,3,128,256]{3,2,1,0:T(8,128)(2,1)}, bf16[2,3,128,256]{3,2,1,0:T(8,128)(2,1)S(1)}, u32[]{:S(2)}, u32[]{:S(2)}) collective-permute-start(bf16[2,3,128,256]{3,2,1,0:T(8,128)(2,1)} %slice.69), channel_id=1, source_target_pairs={{0,192},{64,0},{128,64},{192,128},{1,193},{65,1},{129,65},{193,129... | collective-permute-start | bytes 1179656 | tf_op jit(solution)/shard_map/ppermute | solution.py:305
  65.2 1.1 collective-permute-start.20
  66.3 1.0 collective-permute-start.19
  67.3 2.9 %collective-permute-done.6.refs_2_ = bf16[2,3,128,256]{3,2,1,0:T(8,128)(2,1)S(1)} collective-permute-done((bf16[2,3,128,256]{3,2,1,0:T(8,128)(2,1)}, bf16[2,3,128,256]{3,2,1,0:T(8,128)(2,1)S(1)}, u32[]{:S(2)}, u32[]{:S(2)}) %collective-permute-start.6) | collective-permute-done | bytes 393248 | tf_op jit(solution)/shard_map/ppermute | solution.py:304
  71.4 6.5 %collective-permute-start.9 = (bf16[256,128]{1,0:T(8,128)(2,1)S(1)}, bf16[256,128]{1,0:T(8,128)(2,1)S(1)}, u32[]{:S(2)}, u32[]{:S(2)}) collective-permute-start(bf16[256,128]{1,0:T(8,128)(2,1)S(1)} %get-tuple-element.49), channel_id=1, source_target_pairs={{0,32},{1,0},{32,33},{33,1},{2,34},{3,2},{34,35},{35,3},{4,36},{5,... | collective-permute-start | bytes 196616 | tf_op jit(solution)/shard_map/ppermute | solution.py:345
  78.5 1.4 collective-permute-done.9
  80.5 1.5 collective-permute-start.11
  82.6 1.7 slice.74
  84.3 2.3 %collective-permute-start.21 = (bf16[2,3,128,256]{3,2,1,0:T(8,128)(2,1)}, bf16[2,3,128,256]{3,2,1,0:T(8,128)(2,1)}, u32[]{:S(2)}, u32[]{:S(2)}) collective-permute-start(bf16[2,3,128,256]{3,2,1,0:T(8,128)(2,1)} %slice.74), channel_id=1, source_target_pairs={{0,8},{8,16},{16,24},{24,0},{1,9},{9,17},{17,25},{25,1},{2,10},{10... | collective-permute-start | bytes 1179656 | tf_op jit(solution)/shard_map/ppermute | solution.py:304
  86.6 1.8 slice.75
  89.1 1.5 collective-permute-start.12
  90.6 1.9 collective-permute-start.13
  92.7 4.1 %collective-permute-done.12 = bf16[256,128]{1,0:T(8,128)(2,1)S(1)} collective-permute-done((bf16[256,128]{1,0:T(8,128)(2,1)S(1)}, bf16[256,128]{1,0:T(8,128)(2,1)S(1)}, u32[]{:S(2)}, u32[]{:S(2)}) %collective-permute-start.12) | collective-permute-done | bytes 65568 | tf_op jit(solution)/shard_map/ppermute | solution.py:304
  96.8 2.5 %collective-permute-done.13 = bf16[256,128]{1,0:T(8,128)(2,1)S(1)} collective-permute-done((bf16[256,128]{1,0:T(8,128)(2,1)S(1)}, bf16[256,128]{1,0:T(8,128)(2,1)S(1)}, u32[]{:S(2)}, u32[]{:S(2)}) %collective-permute-start.13) | collective-permute-done | bytes 65568 | tf_op jit(solution)/shard_map/ppermute | solution.py:305
  99.3 1.0 pad_maximum_fusion.3.refs_0_
  100.4 1.1 copy-done.2
  101.5 1.0 copy-done.4
  102.5 15.1 %project.1 = (bf16[3,2,512,256]{3,2,1,0:T(8,128)(2,1)}, bf16[2,144,256]{2,1,0:T(8,128)(2,1)S(1)}, bf16[144,256]{1,0:T(8,128)(2,1)S(1)}) custom-call(s32[4]{0:T(128)S(1)} %pad_add_fusion.at_ref, bf16[2,8,592,512]{3,2,1,0:T(8,128)(2,1)} %bitcast.43, bf16[4,3,128,256]{3,2,1,0:T(8,128)(2,1)S(1)} %pad_maximum_fusion.refs_0_, ...), custom_call_target="tpu_custom_call" | custom-call | flops 7449083904 | bytes 18000000 | tf_op jit(solution)/shard_map/project/pallas_call | solution.py:119
  117.7 3.0 %collective-permute-start.23 = (bf16[144,256]{1,0:T(8,128)(2,1)S(1)}, bf16[144,256]{1,0:T(8,128)(2,1)S(1)}, u32[]{:S(2)}, u32[]{:S(2)}) collective-permute-start(bf16[144,256]{1,0:T(8,128)(2,1)S(1)} %get-tuple-element.47), channel_id=1, source_target_pairs={{0,8},{8,16},{16,24},{24,64},{64,72},{72,80},{80,88},{88,128},{128... | collective-permute-start | bytes 221192 | tf_op jit(solution)/shard_map/ppermute | solution.py:359
  121.4 1.8 collective-permute-start.27
  123.2 2.0 collective-permute-start.26
  125.1 2.1 collective-permute-start.24
  127.2 2.2 %collective-permute-done.24 = bf16[144,256]{1,0:T(8,128)(2,1)S(1)} collective-permute-done((bf16[144,256]{1,0:T(8,128)(2,1)S(1)}, bf16[144,256]{1,0:T(8,128)(2,1)S(1)}, u32[]{:S(2)}, u32[]{:S(2)}) %collective-permute-start.24) | collective-permute-done | bytes 73760 | tf_op jit(solution)/shard_map/ppermute | solution.py:360
  129.5 1.4 copy-done.5
  130.9 2.9 %mix.1.mine_ref = bf16[2,512,256]{2,1,0:T(8,128)(2,1)S(1)} custom-call(bf16[3,2,512,256]{3,2,1,0:T(8,128)(2,1)S(1)} %copy-done.5, bf16[2,144,256]{2,1,0:T(8,128)(2,1)S(1)} %pad_maximum_fusion.4.halo_ref, bf16[16,128,256]{2,1,0:T(8,128)(2,1)S(1)} %toeplitz.1.band_ref, f32[3,3,256]{2,1,0:T(4,128)S(1)} %constant_dynamic-slice_fusion.refs_10_.taps_ref, ...), custom_call_target="tpu_custom_call" | custom-call | flops 1073741824 | bytes 4000000 | tf_op jit(solution)/shard_map/mix/pallas_call | solution.py:216
  133.8 2.4 %collective-permute-start.25 = (bf16[2,512,256]{2,1,0:T(8,128)(2,1)S(1)}, bf16[2,512,256]{2,1,0:T(8,128)(2,1)S(1)}, u32[]{:S(2)}, u32[]{:S(2)}) collective-permute-start(bf16[2,512,256]{2,1,0:T(8,128)(2,1)S(1)} %mix.1.mine_ref), channel_id=1, source_target_pairs={{0,1},{1,0},{2,3},{3,2},{4,5},{5,4},{6,7},{7,6},{8,9},{9,8},{10,11... | collective-permute-start | bytes 1572872 | tf_op jit(solution)/shard_map/ppermute | solution.py:366
  136.4 3.2 %collective-permute-start.29 = (bf16[2,512,128]{2,1,0:T(8,128)(2,1)S(1)}, bf16[2,512,128]{2,1,0:T(8,128)(2,1)S(1)}, u32[]{:S(2)}, u32[]{:S(2)}) collective-permute-start(bf16[2,512,128]{2,1,0:T(8,128)(2,1)S(1)} %slice.77), channel_id=1, source_target_pairs={{0,192},{64,0},{128,64},{192,128},{1,193},{65,1},{129,65},{193,129... | collective-permute-start | bytes 786440 | tf_op jit(solution)/shard_map/ppermute | solution.py:305
  139.6 6.7 %collective-permute-done.28.refs_2_ = bf16[2,512,128]{2,1,0:T(8,128)(2,1)S(1)} collective-permute-done((bf16[2,512,128]{2,1,0:T(8,128)(2,1)S(1)}, bf16[2,512,128]{2,1,0:T(8,128)(2,1)S(1)}, u32[]{:S(2)}, u32[]{:S(2)}) %collective-permute-start.28) | collective-permute-done | bytes 262176 | tf_op jit(solution)/shard_map/ppermute | solution.py:304
  146.3 5.0 %project_out.1 = bf16[2,4,512,512]{3,2,1,0:T(8,128)(2,1)} custom-call(s32[4]{0:T(128)S(1)} %pad_add_fusion.at_ref, bf16[2,512,256]{2,1,0:T(8,128)(2,1)S(1)} %mix.1.mine_ref, bf16[2,512,256]{2,1,0:T(8,128)(2,1)S(1)} %collective-permute-done.25.other_ref, bf16[4,512,128]{2,1,0:T(8,128)(2,1)S(1)} %pad_maximum_fusion.3.refs_0_, ...), custom_call_target="tpu_custom_call" | custom-call | flops 2147483648 | bytes 8000000 | tf_op jit(solution)/shard_map/project_out/pallas_call | solution.py:271
  151.4 58.3 %reduce-scatter.2.cloned.1.call-done = bf16[1,512,512]{2,1,0:T(8,128)(2,1)} async-done(((bf16[8,512,512]{2,1,0:T(8,128)(2,1)}), bf16[1,512,512]{2,1,0:T(8,128)(2,1)}) %reduce-scatter.2.cloned.1.call-update) | async-done | bytes 524304 | tf_op jit(solution)/shard_map/reduce_scatter | solution.py:368
  209.7 2.0 fusion
  (83 shorter events, 7.9 us)
Async XLA Ops:
  6.5 82.5 %copy-start = (f32[3,3,512]{2,1,0:T(4,128)S(1)}, f32[3,3,512]{2,1,0:T(4,128)}, u32[]{:S(2)}) copy-start(f32[3,3,512]{2,1,0:T(4,128)} %param.12) | copy-start | bytes 55300
  6.5 3.8 %copy-start.7 = (bf16[3,128,512]{2,1,0:T(8,128)(2,1)S(1)}, bf16[3,128,512]{2,1,0:T(8,128)(2,1)}, u32[]{:S(2)}) copy-start(bf16[3,128,512]{2,1,0:T(8,128)(2,1)} %param.11) | copy-start | bytes 1179652
  6.5 93.9 %all-gather.3.cloned.1.call-start = ((), (), s32[]{:S(2)}) async-start(), calls=%async_computation.2 | async-start | bytes 10305536 | tf_op jit(solution)/shard_map/all_gather | solution.py:329
  10.3 199.4 %reduce-scatter.2.cloned.1.call-start = ((), (), s32[]{:S(2)}) async-start(), calls=%async_computation.1 | async-start | bytes 4718592 | tf_op jit(solution)/shard_map/reduce_scatter | solution.py:368
  10.4 6.7 %collective-permute-start.1 = (bf16[3,128,256]{2,1,0:T(8,128)(2,1)S(1)}, bf16[3,128,256]{2,1,0:T(8,128)(2,1)S(1)}, u32[]{:S(2)}, u32[]{:S(2)}) collective-permute-start(bf16[3,128,256]{2,1,0:T(8,128)(2,1)S(1)} %get-tuple-element.46), channel_id=1, source_target_pairs={{0,8},{8,16},{16,24},{24,0},{1,9},{9,17},{17,25},{25,1},{2,10},{10... | collective-permute-start | bytes 589832 | tf_op jit(solution)/shard_map/ppermute | solution.py:301
  11.9 6.7 %collective-permute-start = (bf16[3,128,256]{2,1,0:T(8,128)(2,1)S(1)}, bf16[3,128,256]{2,1,0:T(8,128)(2,1)S(1)}, u32[]{:S(2)}, u32[]{:S(2)}) collective-permute-start(bf16[3,128,256]{2,1,0:T(8,128)(2,1)S(1)} %get-tuple-element.46), channel_id=1, source_target_pairs={{0,24},{8,0},{16,8},{24,16},{1,25},{9,1},{17,9},{25,17},{2,26},{10... | collective-permute-start | bytes 589832 | tf_op jit(solution)/shard_map/ppermute | solution.py:302
  17.1 5.2 %collective-permute-start.2 = (bf16[3,64,256]{2,1,0:T(8,128)(2,1)S(1)}, bf16[3,64,256]{2,1,0:T(8,128)(2,1)S(1)}, u32[]{:S(2)}, u32[]{:S(2)}) collective-permute-start(bf16[3,64,256]{2,1,0:T(8,128)(2,1)S(1)} %slice.66), channel_id=1, source_target_pairs={{0,8},{8,16},{16,24},{24,0},{1,9},{9,17},{17,25},{25,1},{2,10},{10... | collective-permute-start | bytes 294920 | tf_op jit(solution)/shard_map/ppermute | solution.py:304
  18.7 4.7 %collective-permute-start.3 = (bf16[3,64,256]{2,1,0:T(8,128)(2,1)S(1)}, bf16[3,64,256]{2,1,0:T(8,128)(2,1)S(1)}, u32[]{:S(2)}, u32[]{:S(2)}) collective-permute-start(bf16[3,64,256]{2,1,0:T(8,128)(2,1)S(1)} %slice.67), channel_id=1, source_target_pairs={{0,24},{8,0},{16,8},{24,16},{1,25},{9,1},{17,9},{25,17},{2,26},{10... | collective-permute-start | bytes 294920 | tf_op jit(solution)/shard_map/ppermute | solution.py:305
  23.5 36.7 %collective-permute-start.5 = (bf16[4,3,128,256]{3,2,1,0:T(8,128)(2,1)S(1)}, bf16[4,3,128,256]{3,2,1,0:T(8,128)(2,1)S(1)}, u32[]{:S(2)}, u32[]{:S(2)}) collective-permute-start(bf16[4,3,128,256]{3,2,1,0:T(8,128)(2,1)S(1)} %pad_maximum_fusion.refs_0_), channel_id=1, source_target_pairs={{0,64},{64,128},{128,192},{192,0},{1,65},{65,129},{129,193},{193,1... | collective-permute-start | bytes 2359304 | tf_op jit(solution)/shard_map/ppermute | solution.py:301
  25.2 35.9 %collective-permute-start.4 = (bf16[4,3,128,256]{3,2,1,0:T(8,128)(2,1)S(1)}, bf16[4,3,128,256]{3,2,1,0:T(8,128)(2,1)S(1)}, u32[]{:S(2)}, u32[]{:S(2)}) collective-permute-start(bf16[4,3,128,256]{3,2,1,0:T(8,128)(2,1)S(1)} %pad_maximum_fusion.refs_0_), channel_id=1, source_target_pairs={{0,192},{64,0},{128,64},{192,128},{1,193},{65,1},{129,65},{193,129... | collective-permute-start | bytes 2359304 | tf_op jit(solution)/shard_map/ppermute | solution.py:302
  26.8 18.8 %collective-permute-start.14 = (bf16[3,128,256]{2,1,0:T(8,128)(2,1)S(1)}, bf16[3,128,256]{2,1,0:T(8,128)(2,1)S(1)}, u32[]{:S(2)}, u32[]{:S(2)}) collective-permute-start(bf16[3,128,256]{2,1,0:T(8,128)(2,1)S(1)} %get-tuple-element.45), channel_id=1, source_target_pairs={{0,32},{32,0},{1,33},{33,1},{2,34},{34,2},{3,35},{35,3},{4,36},{36... | collective-permute-start | bytes 589832 | tf_op jit(solution)/shard_map/ppermute | solution.py:334
  45.6 7.9 %collective-permute-start.16 = (bf16[3,128,256]{2,1,0:T(8,128)(2,1)S(1)}, bf16[3,128,256]{2,1,0:T(8,128)(2,1)S(1)}, u32[]{:S(2)}, u32[]{:S(2)}) collective-permute-start(bf16[3,128,256]{2,1,0:T(8,128)(2,1)S(1)} %collective-permute-done.14), channel_id=1, source_target_pairs={{0,64},{64,128},{128,192},{192,0},{1,65},{65,129},{129,193},{193,1... | collective-permute-start | bytes 589832 | tf_op jit(solution)/shard_map/ppermute | solution.py:301
  46.0 7.7 %collective-permute-start.15 = (bf16[3,128,256]{2,1,0:T(8,128)(2,1)S(1)}, bf16[3,128,256]{2,1,0:T(8,128)(2,1)S(1)}, u32[]{:S(2)}, u32[]{:S(2)}) collective-permute-start(bf16[3,128,256]{2,1,0:T(8,128)(2,1)S(1)} %collective-permute-done.14), channel_id=1, source_target_pairs={{0,192},{64,0},{128,64},{192,128},{1,193},{65,1},{129,65},{193,129... | collective-permute-start | bytes 589832 | tf_op jit(solution)/shard_map/ppermute | solution.py:302
  53.5 6.7 %collective-permute-start.17 = (bf16[3,64,256]{2,1,0:T(8,128)(2,1)S(1)}, bf16[3,64,256]{2,1,0:T(8,128)(2,1)S(1)}, u32[]{:S(2)}, u32[]{:S(2)}) collective-permute-start(bf16[3,64,256]{2,1,0:T(8,128)(2,1)S(1)} %slice.72), channel_id=1, source_target_pairs={{0,64},{64,128},{128,192},{192,0},{1,65},{65,129},{129,193},{193,1... | collective-permute-start | bytes 294920 | tf_op jit(solution)/shard_map/ppermute | solution.py:304
  53.6 6.6 %collective-permute-start.18 = (bf16[3,64,256]{2,1,0:T(8,128)(2,1)S(1)}, bf16[3,64,256]{2,1,0:T(8,128)(2,1)S(1)}, u32[]{:S(2)}, u32[]{:S(2)}) collective-permute-start(bf16[3,64,256]{2,1,0:T(8,128)(2,1)S(1)} %slice.73), channel_id=1, source_target_pairs={{0,192},{64,0},{128,64},{192,128},{1,193},{65,1},{129,65},{193,129... | collective-permute-start | bytes 294920 | tf_op jit(solution)/shard_map/ppermute | solution.py:305
  60.2 10.5 %copy-start.9 = (bf16[512,128]{1,0:T(8,128)(2,1)S(1)}, bf16[512,128]{1,0:T(8,128)(2,1)}, u32[]{:S(2)}) copy-start(bf16[512,128]{1,0:T(8,128)(2,1)} %param.15) | copy-start | bytes 393220
  61.0 9.2 %collective-permute-start.6 = (bf16[2,3,128,256]{3,2,1,0:T(8,128)(2,1)}, bf16[2,3,128,256]{3,2,1,0:T(8,128)(2,1)S(1)}, u32[]{:S(2)}, u32[]{:S(2)}) collective-permute-start(bf16[2,3,128,256]{3,2,1,0:T(8,128)(2,1)} %slice.68), channel_id=1, source_target_pairs={{0,64},{64,128},{128,192},{192,0},{1,65},{65,129},{129,193},{193,1... | collective-permute-start | bytes 1179656 | tf_op jit(solution)/shard_map/ppermute | solution.py:304
  61.0 4.1 %copy-start.1 = (bf16[4,3,128,256]{3,2,1,0:T(8,128)(2,1)}, bf16[4,3,128,256]{3,2,1,0:T(8,128)(2,1)S(1)}, u32[]{:S(2)}) copy-start(bf16[4,3,128,256]{3,2,1,0:T(8,128)(2,1)S(1)} %collective-permute-done.4.refs_1_) | copy-start | bytes 2359300
  61.9 8.8 %collective-permute-start.7 = (bf16[2,3,128,256]{3,2,1,0:T(8,128)(2,1)}, bf16[2,3,128,256]{3,2,1,0:T(8,128)(2,1)S(1)}, u32[]{:S(2)}, u32[]{:S(2)}) collective-permute-start(bf16[2,3,128,256]{3,2,1,0:T(8,128)(2,1)} %slice.69), channel_id=1, source_target_pairs={{0,192},{64,0},{128,64},{192,128},{1,193},{65,1},{129,65},{193,129... | collective-permute-start | bytes 1179656 | tf_op jit(solution)/shard_map/ppermute | solution.py:305
  65.1 23.9 %copy-start.11 = (f32[512]{0:T(512)S(1)}, f32[512]{0:T(512)}, u32[]{:S(2)}) copy-start(f32[512]{0:T(512)} %param.14) | copy-start | bytes 6148
  65.2 17.4 %collective-permute-start.20 = (bf16[4,3,128,256]{3,2,1,0:T(8,128)(2,1)S(1)}, bf16[4,3,128,256]{3,2,1,0:T(8,128)(2,1)}, u32[]{:S(2)}, u32[]{:S(2)}) collective-permute-start(bf16[4,3,128,256]{3,2,1,0:T(8,128)(2,1)S(1)} %pad_maximum_fusion.1.refs_5_), channel_id=1, source_target_pairs={{0,8},{8,16},{16,24},{24,0},{1,9},{9,17},{17,25},{25,1},{2,10},{10... | collective-permute-start | bytes 2359304 | tf_op jit(solution)/shard_map/ppermute | solution.py:301
  66.3 20.3 %collective-permute-start.19 = (bf16[4,3,128,256]{3,2,1,0:T(8,128)(2,1)S(1)}, bf16[4,3,128,256]{3,2,1,0:T(8,128)(2,1)}, u32[]{:S(2)}, u32[]{:S(2)}) collective-permute-start(bf16[4,3,128,256]{3,2,1,0:T(8,128)(2,1)S(1)} %pad_maximum_fusion.1.refs_5_), channel_id=1, source_target_pairs={{0,24},{8,0},{16,8},{24,16},{1,25},{9,1},{17,9},{25,17},{2,26},{10... | collective-permute-start | bytes 2359304 | tf_op jit(solution)/shard_map/ppermute | solution.py:302
  70.7 28.6 %copy-start.3 = (bf16[2,3,128,256]{3,2,1,0:T(8,128)(2,1)}, bf16[2,3,128,256]{3,2,1,0:T(8,128)(2,1)S(1)}, u32[]{:S(2)}) copy-start(bf16[2,3,128,256]{3,2,1,0:T(8,128)(2,1)S(1)} %collective-permute-done.7.refs_3_) | copy-start | bytes 1179652
  70.7 7.1 %collective-permute-start.8 = (bf16[256,128]{1,0:T(8,128)(2,1)S(1)}, bf16[256,128]{1,0:T(8,128)(2,1)S(1)}, u32[]{:S(2)}, u32[]{:S(2)}) collective-permute-start(bf16[256,128]{1,0:T(8,128)(2,1)S(1)} %get-tuple-element.50), channel_id=1, source_target_pairs={{0,0},{1,32},{32,1},{33,33},{2,2},{3,34},{34,3},{35,35},{4,4},{5,3... | collective-permute-start | bytes 196616 | tf_op jit(solution)/shard_map/ppermute | solution.py:345
  71.4 8.5 %collective-permute-start.9 = (bf16[256,128]{1,0:T(8,128)(2,1)S(1)}, bf16[256,128]{1,0:T(8,128)(2,1)S(1)}, u32[]{:S(2)}, u32[]{:S(2)}) collective-permute-start(bf16[256,128]{1,0:T(8,128)(2,1)S(1)} %get-tuple-element.49), channel_id=1, source_target_pairs={{0,32},{1,0},{32,33},{33,1},{2,34},{3,2},{34,35},{35,3},{4,36},{5,... | collective-permute-start | bytes 196616 | tf_op jit(solution)/shard_map/ppermute | solution.py:345
  80.5 8.6 %collective-permute-start.11 = (bf16[512,128]{1,0:T(8,128)(2,1)}, bf16[512,128]{1,0:T(8,128)(2,1)S(1)}, u32[]{:S(2)}, u32[]{:S(2)}) collective-permute-start(bf16[512,128]{1,0:T(8,128)(2,1)} %constant_dynamic-update-slice_fusion), channel_id=1, source_target_pairs={{0,8},{8,16},{16,24},{24,0},{1,9},{9,17},{17,25},{25,1},{2,10},{10... | collective-permute-start | bytes 393224 | tf_op jit(solution)/shard_map/ppermute | solution.py:301
  82.1 8.6 %collective-permute-start.10 = (bf16[512,128]{1,0:T(8,128)(2,1)}, bf16[512,128]{1,0:T(8,128)(2,1)S(1)}, u32[]{:S(2)}, u32[]{:S(2)}) collective-permute-start(bf16[512,128]{1,0:T(8,128)(2,1)} %constant_dynamic-update-slice_fusion), channel_id=1, source_target_pairs={{0,24},{8,0},{16,8},{24,16},{1,25},{9,1},{17,9},{25,17},{2,26},{10... | collective-permute-start | bytes 393224 | tf_op jit(solution)/shard_map/ppermute | solution.py:302
  84.3 16.1 %collective-permute-start.21 = (bf16[2,3,128,256]{3,2,1,0:T(8,128)(2,1)}, bf16[2,3,128,256]{3,2,1,0:T(8,128)(2,1)}, u32[]{:S(2)}, u32[]{:S(2)}) collective-permute-start(bf16[2,3,128,256]{3,2,1,0:T(8,128)(2,1)} %slice.74), channel_id=1, source_target_pairs={{0,8},{8,16},{16,24},{24,0},{1,9},{9,17},{17,25},{25,1},{2,10},{10... | collective-permute-start | bytes 1179656 | tf_op jit(solution)/shard_map/ppermute | solution.py:304
  88.4 12.0 %collective-permute-start.22 = (bf16[2,3,128,256]{3,2,1,0:T(8,128)(2,1)}, bf16[2,3,128,256]{3,2,1,0:T(8,128)(2,1)}, u32[]{:S(2)}, u32[]{:S(2)}) collective-permute-start(bf16[2,3,128,256]{3,2,1,0:T(8,128)(2,1)} %slice.75), channel_id=1, source_target_pairs={{0,24},{8,0},{16,8},{24,16},{1,25},{9,1},{17,9},{25,17},{2,26},{10... | collective-permute-start | bytes 1179656 | tf_op jit(solution)/shard_map/ppermute | solution.py:305
  89.1 7.6 %collective-permute-start.12 = (bf16[256,128]{1,0:T(8,128)(2,1)S(1)}, bf16[256,128]{1,0:T(8,128)(2,1)S(1)}, u32[]{:S(2)}, u32[]{:S(2)}) collective-permute-start(bf16[256,128]{1,0:T(8,128)(2,1)S(1)} %slice.70), channel_id=1, source_target_pairs={{0,8},{8,16},{16,24},{24,0},{1,9},{9,17},{17,25},{25,1},{2,10},{10... | collective-permute-start | bytes 196616 | tf_op jit(solution)/shard_map/ppermute | solution.py:304
  90.6 8.7 %copy-start.8 = (bf16[512,128]{1,0:T(8,128)(2,1)}, bf16[512,128]{1,0:T(8,128)(2,1)S(1)}, u32[]{:S(2)}) copy-start(bf16[512,128]{1,0:T(8,128)(2,1)S(1)} %collective-permute-done.10) | copy-start | bytes 393220
  90.6 8.6 %collective-permute-start.13 = (bf16[256,128]{1,0:T(8,128)(2,1)S(1)}, bf16[256,128]{1,0:T(8,128)(2,1)S(1)}, u32[]{:S(2)}, u32[]{:S(2)}) collective-permute-start(bf16[256,128]{1,0:T(8,128)(2,1)S(1)} %slice.71), channel_id=1, source_target_pairs={{0,24},{8,0},{16,8},{24,16},{1,25},{9,1},{17,9},{25,17},{2,26},{10... | collective-permute-start | bytes 196616 | tf_op jit(solution)/shard_map/ppermute | solution.py:305
  100.4 1.1 copy-start.2
  101.5 1.0 copy-start.4
  102.5 18.2 %copy-start.10 = (bf16[32,128]{1,0:T(8,128)(2,1)S(1)}, bf16[32,128]{1,0:T(8,128)(2,1)}, u32[]{:S(2)}) copy-start(bf16[32,128]{1,0:T(8,128)(2,1)} %param.13) | copy-start | bytes 24580
  117.7 9.5 %collective-permute-start.23 = (bf16[144,256]{1,0:T(8,128)(2,1)S(1)}, bf16[144,256]{1,0:T(8,128)(2,1)S(1)}, u32[]{:S(2)}, u32[]{:S(2)}) collective-permute-start(bf16[144,256]{1,0:T(8,128)(2,1)S(1)} %get-tuple-element.47), channel_id=1, source_target_pairs={{0,8},{8,16},{16,24},{24,64},{64,72},{72,80},{80,88},{88,128},{128... | collective-permute-start | bytes 221192 | tf_op jit(solution)/shard_map/ppermute | solution.py:359
  121.4 14.8 %collective-permute-start.27 = (bf16[4,512,128]{2,1,0:T(8,128)(2,1)S(1)}, bf16[4,512,128]{2,1,0:T(8,128)(2,1)S(1)}, u32[]{:S(2)}, u32[]{:S(2)}) collective-permute-start(bf16[4,512,128]{2,1,0:T(8,128)(2,1)S(1)} %pad_maximum_fusion.3.refs_0_), channel_id=1, source_target_pairs={{0,64},{64,128},{128,192},{192,0},{1,65},{65,129},{129,193},{193,1... | collective-permute-start | bytes 1572872 | tf_op jit(solution)/shard_map/ppermute | solution.py:301
  123.2 13.2 %collective-permute-start.26 = (bf16[4,512,128]{2,1,0:T(8,128)(2,1)S(1)}, bf16[4,512,128]{2,1,0:T(8,128)(2,1)S(1)}, u32[]{:S(2)}, u32[]{:S(2)}) collective-permute-start(bf16[4,512,128]{2,1,0:T(8,128)(2,1)S(1)} %pad_maximum_fusion.3.refs_0_), channel_id=1, source_target_pairs={{0,192},{64,0},{128,64},{192,128},{1,193},{65,1},{129,65},{193,129... | collective-permute-start | bytes 1572872 | tf_op jit(solution)/shard_map/ppermute | solution.py:302
  125.1 4.4 %collective-permute-start.24 = (bf16[144,256]{1,0:T(8,128)(2,1)S(1)}, bf16[144,256]{1,0:T(8,128)(2,1)S(1)}, u32[]{:S(2)}, u32[]{:S(2)}) collective-permute-start(bf16[144,256]{1,0:T(8,128)(2,1)S(1)} %get-tuple-element.48), channel_id=1, source_target_pairs={{0,8},{8,16},{16,24},{24,0},{64,72},{72,80},{80,88},{88,64},{128,1... | collective-permute-start | bytes 221192 | tf_op jit(solution)/shard_map/ppermute | solution.py:360
  129.5 1.4 copy-start.5
  133.8 12.5 %collective-permute-start.25 = (bf16[2,512,256]{2,1,0:T(8,128)(2,1)S(1)}, bf16[2,512,256]{2,1,0:T(8,128)(2,1)S(1)}, u32[]{:S(2)}, u32[]{:S(2)}) collective-permute-start(bf16[2,512,256]{2,1,0:T(8,128)(2,1)S(1)} %mix.1.mine_ref), channel_id=1, source_target_pairs={{0,1},{1,0},{2,3},{3,2},{4,5},{5,4},{6,7},{7,6},{8,9},{9,8},{10,11... | collective-permute-start | bytes 1572872 | tf_op jit(solution)/shard_map/ppermute | solution.py:366
  136.2 10.1 %collective-permute-start.28 = (bf16[2,512,128]{2,1,0:T(8,128)(2,1)S(1)}, bf16[2,512,128]{2,1,0:T(8,128)(2,1)S(1)}, u32[]{:S(2)}, u32[]{:S(2)}) collective-permute-start(bf16[2,512,128]{2,1,0:T(8,128)(2,1)S(1)} %slice.76), channel_id=1, source_target_pairs={{0,64},{64,128},{128,192},{192,0},{1,65},{65,129},{129,193},{193,1... | collective-permute-start | bytes 786440 | tf_op jit(solution)/shard_map/ppermute | solution.py:304
  136.4 9.9 %collective-permute-start.29 = (bf16[2,512,128]{2,1,0:T(8,128)(2,1)S(1)}, bf16[2,512,128]{2,1,0:T(8,128)(2,1)S(1)}, u32[]{:S(2)}, u32[]{:S(2)}) collective-permute-start(bf16[2,512,128]{2,1,0:T(8,128)(2,1)S(1)} %slice.77), channel_id=1, source_target_pairs={{0,192},{64,0},{128,64},{192,128},{1,193},{65,1},{129,65},{193,129... | collective-permute-start | bytes 786440 | tf_op jit(solution)/shard_map/ppermute | solution.py:305
  151.3 58.4 %copy-start.6 = (bf16[512,512]{1,0:T(8,128)(2,1)S(1)}, bf16[512,512]{1,0:T(8,128)(2,1)}, u32[]{:S(2)}) copy-start(bf16[512,512]{1,0:T(8,128)(2,1)} %param.8) | copy-start | bytes 1572868
Sparse Core Ops, SparseCore 0:
  10.4 74.7 all-gather.2
  151.5 58.1 reduce-scatter.1

commit v4 on v3

v4 whole, which is shorter than its diff:
```python
import jax
import jax.numpy as jnp
from jax import lax
from jax.experimental import pallas as pl
from jax.experimental.pallas import tpu as pltpu
from jax.sharding import Mesh, PartitionSpec as P

GSIZE = 16
LH = 128
ROWS = 512
TILE = 80
SHARE = 72
HALF = ROWS // 2
WIDE = 512
CH = 256
GROUPS = CH // GSIZE
HALO = LH + 16
MIB = 1024 * 1024
F32 = jnp.float32
BF16 = jnp.bfloat16


def row_iota(shape):
    return lax.broadcasted_iota(jnp.int32, shape, 0)


def three_taps(rows, taps, s):
    return (
        taps[0, s : s + 1] * rows
        + taps[1, s : s + 1] * pltpu.roll(rows, 1, 0)
        + taps[2, s : s + 1] * pltpu.roll(rows, 2, 0)
    )


def weight_copies(at_ref, refs, wide, sems):
    copies = []
    for kind in range(2):
        half = at_ref[8] if kind == 0 else 1 - at_ref[8]
        for i in range(4):
            for j in range(4):
                source = refs[2 * kind + i // 2].at[i % 2, j]
                y, x = (i, j) if kind == 0 else (j, i)
                place = wide.at[:, at_ref[y], half, at_ref[4 + x]]
                copies.append(pltpu.make_async_copy(source, place, sems.at[kind, i, j]))
    return copies


def last_rows(parts, first, shift):
    place = row_iota((16, CH)) // 2
    out = jnp.zeros((16, CH), F32)
    for s in range(3):
        moved = pltpu.roll(parts[s][first : first + 16], (2 * s + shift) % 16, 0)
        out = jnp.where(place == s, moved, out)
    return out.astype(BF16)


def project_kernel(at_ref, x_ref, *refs):
    taps_ref, proj_ref, tail_ref, mid_ref, front_ref, wide, scaled, ahead, sems = refs[4:]
    copies = weight_copies(at_ref, refs, wide, sems)
    first_step = pl.program_id(0) == 0

    @pl.when(first_step)
    def _():
        for copy in copies:
            copy.start()

    ssq = jnp.zeros((ROWS + TILE, 1), F32)
    for t in range(8):
        lifted = x_ref[0, t].astype(F32)
        ssq += jnp.sum(lifted * lifted, axis=-1, keepdims=True)
        gain = lifted[ROWS + TILE - 1 :]
        scaled[:, t * WIDE : (t + 1) * WIDE] = (lifted * gain).astype(BF16)
    inv = lax.rsqrt(ssq * (1.0 / 4096.0) + 1e-6)

    @pl.when(first_step)
    def _():
        for copy in copies:
            copy.wait()

    for s in range(3):
        total = jnp.dot(
            scaled[...], wide[s].reshape(8 * WIDE, CH), preferred_element_type=F32
        )
        rounded = (total * inv).astype(BF16)
        proj_ref[s, 0] = rounded[:ROWS]

        @pl.when(first_step)
        def _(s=s, rounded=rounded):
            ahead[s, :SHARE] = rounded[ROWS:].astype(F32)[:SHARE]

        @pl.when(pl.program_id(0) == 1)
        def _(s=s, rounded=rounded):
            ahead[s, SHARE:] = rounded[ROWS:].astype(F32)

    for end, ref in ((ROWS, tail_ref), (HALF, mid_ref)):
        rows = [proj_ref[s, 0, end - HALO : end].astype(F32) for s in range(3)]
        mixing = three_taps(rows[1], taps_ref, 1) * three_taps(rows[2], taps_ref, 2)
        ref[0, :LH] = mixing[HALO - LH :].astype(BF16)
        ref[0, LH:] = last_rows(rows, HALO - 16, 2)

    @pl.when(pl.program_id(0) == 1)
    def _():
        mixing = three_taps(ahead[1], taps_ref, 1) * three_taps(ahead[2], taps_ref, 2)
        front_ref[:LH] = pltpu.roll(mixing, SHARE + TILE - 1, 0)[:LH].astype(BF16)
        front_ref[LH:] = last_rows(ahead, LH - 8, -7)


def project(at, gathered, weights, taps):
    return pl.pallas_call(
        project_kernel,
        grid_spec=pltpu.PrefetchScalarGridSpec(
            num_scalar_prefetch=1,
            grid=(2,),
            in_specs=[
                pl.BlockSpec((1, 8, ROWS + TILE, WIDE), lambda h, at: (h, 0, 0, 0)),
                *[pl.BlockSpec(memory_space=pl.ANY)] * 4,
                pl.BlockSpec((3, 3, CH), lambda h, at: (0, 0, 0)),
            ],
            out_specs=[
                pl.BlockSpec((3, 1, ROWS, CH), lambda h, at: (0, h, 0, 0)),
                pl.BlockSpec((1, HALO, CH), lambda h, at: (h, 0, 0)),
                pl.BlockSpec((1, HALO, CH), lambda h, at: (h, 0, 0)),
                pl.BlockSpec((HALO, CH), lambda h, at: (0, 0)),
            ],
            scratch_shapes=[
                pltpu.VMEM((3, 4, 2, 4, 128, CH), BF16),
                pltpu.VMEM((ROWS + TILE, 8 * WIDE), BF16),
                pltpu.VMEM((3, SHARE + TILE, CH), F32),
                pltpu.SemaphoreType.DMA((2, 4, 4)),
            ],
        ),
        out_shape=[
            jax.ShapeDtypeStruct((3, 2, ROWS, CH), BF16),
            jax.ShapeDtypeStruct((2, HALO, CH), BF16),
            jax.ShapeDtypeStruct((2, HALO, CH), BF16),
            jax.ShapeDtypeStruct((HALO, CH), BF16),
        ],
        compiler_params=pltpu.CompilerParams(vmem_limit_bytes=46 * MIB),
        cost_estimate=pl.CostEstimate(
            flops=2 * 2 * ROWS * 4096 * 3 * CH, bytes_accessed=18_000_000, transcendentals=0
        ),
        name="project",
    )(at, gathered, *weights, taps)


def toeplitz_kernel(u_ref, out_ref):
    for g in range(GROUPS):
        wide = jnp.broadcast_to(u_ref[g : g + 1], (LH, 3 * LH))
        skewed = pltpu.roll(wide, 0, 1, stride=1, stride_axis=0)
        out_ref[g] = skewed[:, : 2 * LH].astype(BF16)


def toeplitz(filters):
    backwards = jnp.flip(filters.astype(F32), 1)
    row = jnp.pad(backwards, ((0, 0), (1, 2 * LH - 1)))
    return pl.pallas_call(
        toeplitz_kernel,
        out_shape=jax.ShapeDtypeStruct((GROUPS, LH, 2 * LH), BF16),
        compiler_params=pltpu.CompilerParams(vmem_limit_bytes=8 * MIB),
        name="toeplitz",
    )(row)


def mix_kernel(proj_ref, halo_ref, band_ref, taps_ref, bias_ref, out_ref, before, edge):
    step = pl.program_id(0)

    @pl.when(step == 0)
    def _():
        for h in range(2):
            before[h] = halo_ref[h, :LH]
            last = halo_ref[h, LH:].astype(F32)
            for s in range(3):
                edge[h, s] = pltpu.roll(last, (6 - 2 * s) % 16, 0)[:8]

    queries = []
    mixes = []
    windows = []
    for h in range(2):
        feats = []
        for s in range(3):
            lifted = proj_ref[s, h].astype(F32)
            rows = jnp.concatenate([edge[h, s], lifted], axis=0)
            feats.append(three_taps(rows, taps_ref, s)[8:])
            edge[h, s] = lifted[LH - 8 :]
        mixing = (feats[1] * feats[2]).astype(BF16)
        queries.append(feats[0])
        mixes.append(mixing)
        windows.append(jnp.concatenate([before[h], mixing], axis=0))
        before[h] = mixing
    lane_group = lax.broadcasted_iota(jnp.int32, (LH, 2 * LH), 1) % LH // GSIZE
    halves = []
    for half in range(2):
        lanes = slice(half * LH, (half + 1) * LH)
        window = jnp.concatenate([windows[0][:, lanes], windows[1][:, lanes]], axis=1)
        total = jnp.zeros((LH, 2 * LH), F32)
        for g in range(GROUPS // 2):
            one = jnp.dot(band_ref[half * 8 + g], window, preferred_element_type=F32)
            total = jnp.where(lane_group == g, one, total)
        halves.append(total)
    for h in range(2):
        rows = slice(h * LH, (h + 1) * LH)
        filtered = jnp.concatenate([halves[0][:, rows], halves[1][:, rows]], axis=1)
        value = queries[h] * (filtered + bias_ref[...] * mixes[h].astype(F32))
        out_ref[h] = value.astype(BF16)


def mix(proj, halo, band, taps, bias, first, count):
    return pl.pallas_call(
        mix_kernel,
        grid=(count,),
        in_specs=[
            pl.BlockSpec((3, 2, LH, CH), lambda b: (0, 0, b + first, 0)),
            pl.BlockSpec((2, HALO, CH), lambda b: (0, 0, 0)),
            pl.BlockSpec((GROUPS, LH, 2 * LH), lambda b: (0, 0, 0)),
            pl.BlockSpec((3, 3, CH), lambda b: (0, 0, 0)),
            pl.BlockSpec((1, CH), lambda b: (0, 0)),
        ],
        out_specs=pl.BlockSpec((2, LH, CH), lambda b: (0, b, 0)),
        out_shape=jax.ShapeDtypeStruct((2, count * LH, CH), BF16),
        scratch_shapes=[
            pltpu.VMEM((2, LH, CH), BF16),
            pltpu.VMEM((2, 3, 8, CH), F32),
        ],
        compiler_params=pltpu.CompilerParams(vmem_limit_bytes=16 * MIB),
        cost_estimate=pl.CostEstimate(
            flops=2 * 512 * CH * 2048, bytes_accessed=2_000_000, transcendentals=0
        ),
        name="mix",
    )(proj, halo, band, taps, bias)


def out_kernel(at_ref, mine_ref, other_ref, here_ref, there_ref, *refs):
    out_ref, wide, sems = refs[-3:]
    copies = []
    for i in range(4):
        for j in range(4):
            source = (here_ref, there_ref)[i // 2].at[i % 2, j]
            lanes = pl.ds(pl.multiple_of(at_ref[4 + j] * 128, 128), 128)
            place = wide.at[at_ref[i], :, lanes]
            copies.append(pltpu.make_async_copy(source, place, sems.at[i, j]))

    @pl.when(pl.program_id(0) == 0)
    def _():
        for copy in copies:
            copy.start()
        for copy in copies:
            copy.wait()

    swap = at_ref[9] == 1
    first = jnp.where(swap, other_ref[0], mine_ref[0])
    second = jnp.where(swap, mine_ref[0], other_ref[0])
    rows = jnp.concatenate([first, second], axis=1)
    for y in range(4):
        out_ref[0, y] = jnp.dot(rows, wide[y], preferred_element_type=F32).astype(BF16)


def project_out(at, mine, other, parts, half, base=None):
    more = () if base is None else (base,)
    return pl.pallas_call(
        out_kernel,
        grid_spec=pltpu.PrefetchScalarGridSpec(
            num_scalar_prefetch=1,
            grid=(2,),
            in_specs=[
                pl.BlockSpec((1, HALF, CH), lambda h, at: (h, 0, 0)),
                pl.BlockSpec((1, HALF, CH), lambda h, at: (h, 0, 0)),
                *[pl.BlockSpec(memory_space=pl.ANY)] * (2 + len(more)),
            ],
            out_specs=pl.BlockSpec((1, 4, HALF, WIDE), lambda h, at: (h, 0, half, 0)),
            scratch_shapes=[
                pltpu.VMEM((4, 2 * CH, WIDE), BF16),
                pltpu.SemaphoreType.DMA((4, 4)),
            ],
        ),
        out_shape=jax.ShapeDtypeStruct((2, 4, ROWS, WIDE), BF16),
        input_output_aliases={} if base is None else {5: 0},
        compiler_params=pltpu.CompilerParams(vmem_limit_bytes=52 * MIB),
        cost_estimate=pl.CostEstimate(
            flops=2 * 512 * 2 * CH * 2048, bytes_accessed=5_000_000, transcendentals=0
        ),
        name="project_out",
    )(at, mine, other, *parts, *more)


FIRST, SECOND = (1, 3), (3, 1)


def pair_step(value, axis, masks):
    pairs = [(i * 2 + c, (i ^ masks[c]) * 2 + c) for i in range(4) for c in range(2)]
    return lax.ppermute(value, (axis, "c"), pairs)


def ring_pairs(piece, axis):
    here = jnp.stack([piece, pair_step(piece, axis, FIRST)])
    return here, pair_step(here, axis, SECOND)


def ring_line(piece, axis):
    return jnp.concatenate(ring_pairs(piece, axis), axis=0)


def on_device(
    tokens, prior_rows, norm_gain, in_weight, short_filter, mr_filter, mr_bias, out_weight
):
    zh = lax.axis_index("zh")
    column = lax.axis_index("x")
    leading = (column == 0) & (lax.axis_index("y") == 0)

    core = lax.axis_index("c")
    turns = jnp.where(core == 0, jnp.array([0, 1, 3, 2]), jnp.array([0, 3, 1, 2]))
    at = jnp.concatenate(
        [lax.axis_index("y") ^ turns, column ^ turns, jnp.stack([zh, zh ^ core])]
    ).astype(jnp.int32)
    ring = ("zh", "zl", "c")
    padded = jnp.pad(prior_rows, ((0, SHARE + TILE - 1 - prior_rows.shape[0]), (0, 0)))
    some = lax.dynamic_slice_in_dim(padded, zh * SHARE, TILE - 1, 0)
    own = jnp.concatenate([tokens, some, norm_gain[None, :]], axis=0)
    gathered = lax.all_gather(own, ring).reshape(2, 8, ROWS + TILE, WIDE)

    left, right = in_weight[..., :CH], in_weight[..., CH:]
    kept = jnp.where(zh == 0, left, right)
    got = lax.ppermute(jnp.where(zh == 0, right, left), "zh", [(0, 1), (1, 0)])
    kept_line, got_line = ring_line(kept, "x"), ring_line(got, "y")

    out_weight, _, _ = lax.optimization_barrier((out_weight, kept_line, got_line))
    pieces = []
    for k in range(2):
        chosen = lax.dynamic_slice_in_dim(out_weight, (core ^ k) * CH, CH, 0)
        pairs = [(a * 2 + b, (b ^ k) * 2 + a) for a in range(2) for b in range(2)]
        pieces.append(lax.ppermute(chosen, ("zh", "c"), pairs))
    kept_here = jnp.stack([kept_line, pair_step(kept_line, "y", FIRST)])
    got_here = jnp.stack([got_line, pair_step(got_line, "x", FIRST)])
    out_piece = jnp.concatenate(pieces, axis=0)
    out_piece, _, _ = lax.optimization_barrier((out_piece, kept_here, got_here))
    out_line = ring_line(out_piece, "x")
    weights = (
        kept_here,
        pair_step(kept_here, "y", SECOND),
        got_here,
        pair_step(got_here, "x", SECOND),
    )
    out_line, weights, gathered = lax.optimization_barrier((out_line, weights, gathered))
    out_here = jnp.stack([out_line, pair_step(out_line, "y", FIRST)])

    taps = lax.dynamic_slice_in_dim(short_filter, zh * CH, CH, 2)
    bias = lax.dynamic_slice_in_dim(mr_bias, zh * CH, CH, 0)[None, :]
    band = toeplitz(lax.dynamic_slice_in_dim(mr_filter, zh * GROUPS, GROUPS, 0))

    proj, tail, mid, front = project(at, gathered, weights, taps)
    out_here, tail = lax.optimization_barrier((out_here, tail))
    out_parts = (out_here, pair_step(out_here, "y", SECOND))

    last = column == 3
    to_first = jnp.where(last, tail[1], tail[0])
    to_second = jnp.where(last, tail[0], tail[1])
    first = lax.ppermute(to_first, ("y", "x"), [(i, i + 1) for i in range(15)])
    second = lax.ppermute(
        to_second, ("y", "x"), [(i, i // 4 * 4 + (i + 1) % 4) for i in range(16)]
    )
    halo = jnp.stack([jnp.where(leading, front, first), second])

    def swapped(mine):
        return mine, lax.ppermute(mine, "c", [(0, 1), (1, 0)])

    partial = project_out(at, *swapped(mix(proj, mid, band, taps, bias, 2, 2)), out_parts, 1)
    partial = project_out(
        at, *swapped(mix(proj, halo, band, taps, bias, 0, 2)), out_parts, 0, partial
    )
    summed = lax.psum_scatter(
        partial.reshape(8, ROWS, WIDE), ("zh", "zl"), scatter_dimension=0
    )
    return (tokens.astype(F32) + summed.astype(F32)).astype(BF16)


def solution(mesh):
    split = Mesh(mesh.devices.reshape(4, 2, 4, 4, 2), ("y", "zh", "x", "zl", "c"))
    seq, tensor = ("y", "zh", "x"), ("zl", "c")
    in_specs = (
        P(seq, tensor),
        P(None, tensor),
        P(tensor),
        P(None, seq, tensor),
        P(None, None, tensor),
        P(tensor, None),
        P(tensor),
        P(tensor, seq),
    )
    return jax.shard_map(
        on_device, mesh=split, in_specs=in_specs, out_specs=P(seq, tensor), check_vma=False
    )
```

time: 220 us -> 211 us (0.959)
  starting transfers between devices: 57.7 us -> 45.1 us
  Pallas kernels: 23.5 us -> 34.8 us
  local copies, waits for them, and re-layouts: 11.1 us -> 5.68 us
  waiting for transfers between devices: 106 us -> 101 us
  other arithmetic: 6.29 us -> 8.79 us
    ppermute x25 -> x14, starting transfers between devices: 38.3 us -> 15.3 us  [the longest x12 12.6 us: pair_step(): return lax.ppermute(value, (axis, 'c'), pairs)]
    ppermute x2, starting transfers between devices: 7.14 us -> 18.6 us  [on_device(): pieces.append(lax.ppermute(chosen, ('zh', 'c'), pairs))]
    ppermute x1, waiting for transfers between devices: 11.7 us -> 4.45 us  [on_device(): got = lax.ppermute(jnp.where(zh == 0, right, left), 'zh', [(0, 1), (1, 0)])]
    pallas_call x1, Pallas kernels: 15.1 us -> 22 us  [project(): pl.pallas_call(project_kernel, grid_spec=pltpu.PrefetchScalarGridSpec(num...]
    slice x12 -> x0, local copies, waits for them, and re-layouts: 5.24 us -> none  [the longest x6 2.68 us: ring_parts(): lax.slice_in_dim(ahead, half, 2 * half, axis=cut)]
    pallas_call x1 -> x2, Pallas kernels: 5.04 us -> 9.31 us  [project_out(): pl.pallas_call(out_kernel, grid_spec=pltpu.PrefetchScalarGridSpec(num_sca...]
    ppermute x25 -> x14, waiting for transfers between devices: 32.5 us -> 34.2 us  [the longest x12 34.2 us: pair_step(): return lax.ppermute(value, (axis, 'c'), pairs)]
  transfers between devices with their start and end apart: 32 -> 21, of which waited for: 14 -> 11; matrix products, arithmetic and copies ran while one was open for 4% -> 2% of each run, Pallas kernels for 2% -> 14%
where the time goes in v4:
time: 211 us; the launch traced here: 210 us
  waiting for transfers between devices  101 us (48%)
  starting transfers between devices  45.1 us (21%)
  Pallas kernels  34.8 us (16%)
  between operations  13.7 us (6%)
  other arithmetic  8.79 us (4%)
  local copies, waits for them, and re-layouts  5.68 us (3%)
    reduce_scatter x1, waiting for transfers between devices, on_device(): lax.psum_scatter(partial.reshape(8, ROWS, WIDE), ('zh', 'zl'), scatter_di...  57.6 us
    ppermute x12, waiting for transfers between devices, pair_step(): return lax.ppermute(value, (axis, 'c'), pairs)  34.2 us
    pallas_call x1, Pallas kernels, project(): pl.pallas_call(project_kernel, grid_spec=pltpu.PrefetchScalarGridSpec(num...  22 us
    ppermute x2, starting transfers between devices, on_device(): pieces.append(lax.ppermute(chosen, ('zh', 'c'), pairs))  18.6 us
    ppermute x12, starting transfers between devices, pair_step(): return lax.ppermute(value, (axis, 'c'), pairs)  12.6 us
    pallas_call x2, Pallas kernels, project_out(): pl.pallas_call(out_kernel, grid_spec=pltpu.PrefetchScalarGridSpec(num_sca...  9.31 us
    ppermute x1, starting transfers between devices, on_device(): got = lax.ppermute(jnp.where(zh == 0, right, left), 'zh', [(0, 1), (1, 0)])  7.23 us
    ppermute x1, waiting for transfers between devices, on_device(): got = lax.ppermute(jnp.where(zh == 0, right, left), 'zh', [(0, 1), (1, 0)])  4.45 us
  transfers between devices with their start and end apart: 21, of which 11 were waited for; matrix products, arithmetic and copies ran while one was open for 2% of the time, Pallas kernels for 14%

profile of v4, /device:TPU:2, one launch (start us, length us, event | category | flops | bytes accessed | tf_op | source)
XLA Modules:
  0.0 209.5 jit_solution(1988729620725170782)
XLA Ops:
  6.5 0.7 broadcast_in_dim.6
  7.3 0.9 pad_dynamic-slice_fusion
  8.2 1.9 pad_maximum_fusion.5
  10.2 7.2 %collective-permute-start.2 = (bf16[3,128,256]{2,1,0:T(8,128)(2,1)S(1)}, bf16[3,128,256]{2,1,0:T(8,128)(2,1)S(1)}, u32[]{:S(2)}, u32[]{:S(2)}) collective-permute-start(bf16[3,128,256]{2,1,0:T(8,128)(2,1)S(1)} %get-tuple-element.37), channel_id=1, source_target_pairs={{0,32},{32,0},{1,33},{33,1},{2,34},{34,2},{3,35},{35,3},{4,36},{36... | collective-permute-start | bytes 589832 | tf_op jit(solution)/shard_map/ppermute | solution.py:322
  17.5 0.6 collective-permute-start
  18.0 4.4 %collective-permute-done.2 = bf16[3,128,256]{2,1,0:T(8,128)(2,1)S(1)} collective-permute-done((bf16[3,128,256]{2,1,0:T(8,128)(2,1)S(1)}, bf16[3,128,256]{2,1,0:T(8,128)(2,1)S(1)}, u32[]{:S(2)}, u32[]{:S(2)}) %collective-permute-start.2) | collective-permute-done | bytes 196640 | tf_op jit(solution)/shard_map/ppermute | solution.py:322
  22.5 1.6 collective-permute-start.3
  24.1 1.6 collective-permute-start.1
  25.7 2.5 %collective-permute-done.3 = bf16[3,128,256]{2,1,0:T(8,128)(2,1)S(1)} collective-permute-done((bf16[3,128,256]{2,1,0:T(8,128)(2,1)S(1)}, bf16[3,128,256]{2,1,0:T(8,128)(2,1)S(1)}, u32[]{:S(2)}, u32[]{:S(2)}) %collective-permute-start.3) | collective-permute-done | bytes 196640 | tf_op jit(solution)/shard_map/ppermute | solution.py:290
  28.2 3.1 %collective-permute-start.4 = (bf16[2,3,128,256]{3,2,1,0:T(8,128)(2,1)S(1)}, bf16[2,3,128,256]{3,2,1,0:T(8,128)(2,1)S(1)}, u32[]{:S(2)}, u32[]{:S(2)}) collective-permute-start(bf16[2,3,128,256]{3,2,1,0:T(8,128)(2,1)S(1)} %pad_maximum_fusion.8), channel_id=1, source_target_pairs={{0,192},{1,65},{64,128},{65,1},{128,64},{129,193},{192,0},{193,129... | collective-permute-start | bytes 1179656 | tf_op jit(solution)/shard_map/ppermute | solution.py:290
  31.3 0.7 collective-permute-done.1
  31.9 0.1 fusion.4
  32.1 0.7 collective-permute-start.7
  32.8 8.0 %collective-permute-done.4 = bf16[2,3,128,256]{3,2,1,0:T(8,128)(2,1)S(1)} collective-permute-done((bf16[2,3,128,256]{3,2,1,0:T(8,128)(2,1)S(1)}, bf16[2,3,128,256]{3,2,1,0:T(8,128)(2,1)S(1)}, u32[]{:S(2)}, u32[]{:S(2)}) %collective-permute-start.4) | collective-permute-done | bytes 393248 | tf_op jit(solution)/shard_map/ppermute | solution.py:290
  41.0 3.1 %collective-permute-done.7 = bf16[4,3,128,256]{3,2,1,0:T(8,128)(2,1)S(1)} collective-permute-done((bf16[4,3,128,256]{3,2,1,0:T(8,128)(2,1)S(1)}, bf16[4,3,128,256]{3,2,1,0:T(8,128)(2,1)S(1)}, u32[]{:S(2)}, u32[]{:S(2)}) %collective-permute-start.7) | collective-permute-done | bytes 786464 | tf_op jit(solution)/shard_map/ppermute | solution.py:290
  44.1 0.1 pad_maximum_fusion.refs_0_
  44.3 2.3 %collective-permute-start.11 = (bf16[2,4,3,128,256]{4,3,2,1,0:T(8,128)(2,1)S(1)}, bf16[2,4,3,128,256]{4,3,2,1,0:T(8,128)(2,1)}, u32[]{:S(2)}, u32[]{:S(2)}) collective-permute-start(bf16[2,4,3,128,256]{4,3,2,1,0:T(8,128)(2,1)S(1)} %pad_maximum_fusion.refs_0_), channel_id=1, source_target_pairs={{0,192},{1,65},{64,128},{65,1},{128,64},{129,193},{192,0},{193,129... | collective-permute-start | bytes 4718600 | tf_op jit(solution)/shard_map/ppermute | solution.py:290
  46.6 10.3 %collective-permute-done.8 = bf16[4,3,128,256]{3,2,1,0:T(8,128)(2,1)S(1)} collective-permute-done((bf16[4,3,128,256]{3,2,1,0:T(8,128)(2,1)S(1)}, bf16[4,3,128,256]{3,2,1,0:T(8,128)(2,1)S(1)}, u32[]{:S(2)}, u32[]{:S(2)}) %collective-permute-start.8) | collective-permute-done | bytes 786464 | tf_op jit(solution)/shard_map/ppermute | solution.py:290
  56.8 0.1 pad_maximum_fusion.1.refs_2_
  57.0 0.5 collective-permute-start.12
  57.4 0.3 copy-done.7
  57.7 0.7 collective-permute-start.5
  58.4 18.0 %collective-permute-start.6 = (bf16[256,128]{1,0:T(8,128)(2,1)S(1)}, bf16[256,128]{1,0:T(8,128)(2,1)S(1)}, u32[]{:S(2)}, u32[]{:S(2)}) collective-permute-start(bf16[256,128]{1,0:T(8,128)(2,1)S(1)} %get-tuple-element.42), channel_id=1, source_target_pairs={{0,32},{1,0},{32,33},{33,1},{2,34},{3,2},{34,35},{35,3},{4,36},{5,... | collective-permute-start | bytes 196616 | tf_op jit(solution)/shard_map/ppermute | solution.py:330
  76.4 2.5 %collective-permute-done.6 = bf16[256,128]{1,0:T(8,128)(2,1)S(1)} collective-permute-done((bf16[256,128]{1,0:T(8,128)(2,1)S(1)}, bf16[256,128]{1,0:T(8,128)(2,1)S(1)}, u32[]{:S(2)}, u32[]{:S(2)}) %collective-permute-start.6) | collective-permute-done | bytes 65568 | tf_op jit(solution)/shard_map/ppermute | solution.py:330
  78.9 1.3 collective-permute-start.9
  80.2 3.7 %collective-permute-done.9 = bf16[512,128]{1,0:T(8,128)(2,1)S(1)} collective-permute-done((bf16[512,128]{1,0:T(8,128)(2,1)S(1)}, bf16[512,128]{1,0:T(8,128)(2,1)S(1)}, u32[]{:S(2)}, u32[]{:S(2)}) %collective-permute-start.9) | collective-permute-done | bytes 131104 | tf_op jit(solution)/shard_map/ppermute | solution.py:290
  84.0 0.7 pad_maximum_fusion.9
  84.7 0.7 collective-permute-start.10
  85.4 5.9 %collective-permute-done.10 = bf16[2,512,128]{2,1,0:T(8,128)(2,1)} collective-permute-done((bf16[2,512,128]{2,1,0:T(8,128)(2,1)}, bf16[2,512,128]{2,1,0:T(8,128)(2,1)}, u32[]{:S(2)}, u32[]{:S(2)}) %collective-permute-start.10) | collective-permute-done | bytes 262176 | tf_op jit(solution)/shard_map/ppermute | solution.py:290
  91.4 1.8 pad_maximum_fusion.6
  93.2 0.3 collective-permute-start.13
  93.5 22.0 %project.1 = (bf16[3,2,512,256]{3,2,1,0:T(8,128)(2,1)S(1)}, bf16[2,144,256]{2,1,0:T(8,128)(2,1)S(1)}, bf16[2,144,256]{2,1,0:T(8,128)(2,1)S(1)}, bf16[144,256]{1,0:T(8,128)(2,1)S(1)}) custom-call(s32[10]{0:T(128)S(1)} %pad_add_fusion.at_ref, bf16[2,8,592,512]{3,2,1,0:T(8,128)(2,1)} %bitcast.49, bf16[2,4,3,128,256]{4,3,2,1,0:T(8,128)(2,1)S(1)} %pad_maximum_fusion.refs_0_, ...), custom_call_target="tpu_custom_call" | custom-call | flops 6442450944 | bytes 18000000 | tf_op jit(solution)/shard_map/project/pallas_call | solution.py:109
  115.7 1.0 copy-done.1
  116.7 0.7 select_bitcast_fusion.2
  117.4 2.6 %collective-permute-start.14 = (bf16[144,256]{1,0:T(8,128)(2,1)}, bf16[144,256]{1,0:T(8,128)(2,1)}, u32[]{:S(2)}, u32[]{:S(2)}) collective-permute-start(bf16[144,256]{1,0:T(8,128)(2,1)} %get-tuple-element.39), channel_id=1, source_target_pairs={{0,8},{8,16},{16,24},{24,64},{64,72},{72,80},{80,88},{88,128},{128... | collective-permute-start | bytes 221192 | tf_op jit(solution)/shard_map/ppermute | solution.py:356
  120.2 0.5 toeplitz.1.band_ref
  120.7 1.4 copy-done.2
  122.1 1.5 mix.3.mine_ref
  123.6 2.6 %collective-permute-start.18 = (bf16[2,256,256]{2,1,0:T(8,128)(2,1)S(1)}, bf16[2,256,256]{2,1,0:T(8,128)(2,1)S(1)}, u32[]{:S(2)}, u32[]{:S(2)}) collective-permute-start(bf16[2,256,256]{2,1,0:T(8,128)(2,1)S(1)} %mix.3.mine_ref), channel_id=1, source_target_pairs={{0,1},{1,0},{2,3},{3,2},{4,5},{5,4},{6,7},{7,6},{8,9},{9,8},{10,11... | collective-permute-start | bytes 786440 | tf_op jit(solution)/shard_map/ppermute | solution.py:363
  126.2 1.4 collective-permute-start.15
  127.5 0.9 select_bitcast_fusion.1
  128.4 2.6 %collective-permute-done.15 = bf16[144,256]{1,0:T(8,128)(2,1)S(1)} collective-permute-done((bf16[144,256]{1,0:T(8,128)(2,1)}, bf16[144,256]{1,0:T(8,128)(2,1)S(1)}, u32[]{:S(2)}, u32[]{:S(2)}) %collective-permute-start.15) | collective-permute-done | bytes 73760 | tf_op jit(solution)/shard_map/ppermute | solution.py:357
  131.1 1.5 mix.2.mine_ref
  132.7 1.0 copy-done.3
  133.7 4.7 %project_out.2.refs_0_ = bf16[2,4,512,512]{3,2,1,0:T(8,128)(2,1)} custom-call(s32[10]{0:T(128)S(1)} %pad_add_fusion.at_ref, bf16[2,256,256]{2,1,0:T(8,128)(2,1)S(1)} %mix.3.mine_ref, bf16[2,256,256]{2,1,0:T(8,128)(2,1)S(1)} %collective-permute-done.18.other_ref, bf16[2,4,512,128]{3,2,1,0:T(8,128)(2,1)S(1)} %pad_maximum_fusion.2.here_ref, ...), custom_call_target="tpu_custom_call" | custom-call | flops 1073741824 | bytes 5000000 | tf_op jit(solution)/shard_map/project_out/pallas_call | solution.py:259
  138.4 4.6 %project_out.3 = bf16[2,4,512,512]{3,2,1,0:T(8,128)(2,1)} custom-call(s32[10]{0:T(128)S(1)} %pad_add_fusion.at_ref, bf16[2,256,256]{2,1,0:T(8,128)(2,1)S(1)} %mix.2.mine_ref, bf16[2,256,256]{2,1,0:T(8,128)(2,1)S(1)} %collective-permute-done.16.other_ref, bf16[2,4,512,128]{3,2,1,0:T(8,128)(2,1)S(1)} %pad_maximum_fusion.2.here_ref, ...), custom_call_target="tpu_custom_call", output_to_operand_aliasing={{}: (5, {})} | custom-call | flops 1073741824 | bytes 5000000 | tf_op jit(solution)/shard_map/project_out/pallas_call | solution.py:259
  143.1 57.6 %reduce-scatter.2.cloned.1.call-done = bf16[1,512,512]{2,1,0:T(8,128)(2,1)} async-done(((bf16[8,512,512]{2,1,0:T(8,128)(2,1)}), bf16[1,512,512]{2,1,0:T(8,128)(2,1)}) %reduce-scatter.2.cloned.1.call-update) | async-done | bytes 524304 | tf_op jit(solution)/shard_map/reduce_scatter | solution.py:369
  200.7 2.0 fusion
  (52 shorter events, 1.1 us)
Async XLA Ops:
  6.5 78.9 %copy-start = (f32[3,3,512]{2,1,0:T(4,128)S(1)}, f32[3,3,512]{2,1,0:T(4,128)}, u32[]{:S(2)}) copy-start(f32[3,3,512]{2,1,0:T(4,128)} %param.14) | copy-start | bytes 55300
  6.5 3.6 %copy-start.6 = (bf16[3,128,512]{2,1,0:T(8,128)(2,1)S(1)}, bf16[3,128,512]{2,1,0:T(8,128)(2,1)}, u32[]{:S(2)}) copy-start(bf16[3,128,512]{2,1,0:T(8,128)(2,1)} %param.13) | copy-start | bytes 1179652
  6.5 86.6 %all-gather.3.cloned.1.call-start = ((), (), s32[]{:S(2)}) async-start(), calls=%async_computation.2 | async-start | bytes 10305536 | tf_op jit(solution)/shard_map/all_gather | solution.py:318
  10.1 190.6 %reduce-scatter.2.cloned.1.call-start = ((), (), s32[]{:S(2)}) async-start(), calls=%async_computation.1 | async-start | bytes 4718592 | tf_op jit(solution)/shard_map/reduce_scatter | solution.py:369
  10.2 12.2 %collective-permute-start.2 = (bf16[3,128,256]{2,1,0:T(8,128)(2,1)S(1)}, bf16[3,128,256]{2,1,0:T(8,128)(2,1)S(1)}, u32[]{:S(2)}, u32[]{:S(2)}) collective-permute-start(bf16[3,128,256]{2,1,0:T(8,128)(2,1)S(1)} %get-tuple-element.37), channel_id=1, source_target_pairs={{0,32},{32,0},{1,33},{33,1},{2,34},{34,2},{3,35},{35,3},{4,36},{36... | collective-permute-start | bytes 589832 | tf_op jit(solution)/shard_map/ppermute | solution.py:322
  17.5 6.6 %collective-permute-start = (bf16[3,128,256]{2,1,0:T(8,128)(2,1)S(1)}, bf16[3,128,256]{2,1,0:T(8,128)(2,1)S(1)}, u32[]{:S(2)}, u32[]{:S(2)}) collective-permute-start(bf16[3,128,256]{2,1,0:T(8,128)(2,1)S(1)} %get-tuple-element.38), channel_id=1, source_target_pairs={{0,8},{1,25},{8,0},{9,17},{16,24},{17,9},{24,16},{25,1},{2,10},{3,... | collective-permute-start | bytes 589832 | tf_op jit(solution)/shard_map/ppermute | solution.py:290
  22.5 5.7 %collective-permute-start.3 = (bf16[3,128,256]{2,1,0:T(8,128)(2,1)S(1)}, bf16[3,128,256]{2,1,0:T(8,128)(2,1)S(1)}, u32[]{:S(2)}, u32[]{:S(2)}) collective-permute-start(bf16[3,128,256]{2,1,0:T(8,128)(2,1)S(1)} %collective-permute-done.2), channel_id=1, source_target_pairs={{0,64},{1,193},{64,0},{65,129},{128,192},{129,65},{192,128},{193,1... | collective-permute-start | bytes 589832 | tf_op jit(solution)/shard_map/ppermute | solution.py:290
  24.1 7.9 %collective-permute-start.1 = (bf16[2,3,128,256]{3,2,1,0:T(8,128)(2,1)S(1)}, bf16[2,3,128,256]{3,2,1,0:T(8,128)(2,1)S(1)}, u32[]{:S(2)}, u32[]{:S(2)}) collective-permute-start(bf16[2,3,128,256]{3,2,1,0:T(8,128)(2,1)S(1)} %pad_maximum_fusion.7), channel_id=1, source_target_pairs={{0,24},{1,9},{8,16},{9,1},{16,8},{17,25},{24,0},{25,17},{2,26},{3,... | collective-permute-start | bytes 1179656 | tf_op jit(solution)/shard_map/ppermute | solution.py:290
  28.2 12.6 %collective-permute-start.4 = (bf16[2,3,128,256]{3,2,1,0:T(8,128)(2,1)S(1)}, bf16[2,3,128,256]{3,2,1,0:T(8,128)(2,1)S(1)}, u32[]{:S(2)}, u32[]{:S(2)}) collective-permute-start(bf16[2,3,128,256]{3,2,1,0:T(8,128)(2,1)S(1)} %pad_maximum_fusion.8), channel_id=1, source_target_pairs={{0,192},{1,65},{64,128},{65,1},{128,64},{129,193},{192,0},{193,129... | collective-permute-start | bytes 1179656 | tf_op jit(solution)/shard_map/ppermute | solution.py:290
  32.1 12.1 %collective-permute-start.7 = (bf16[4,3,128,256]{3,2,1,0:T(8,128)(2,1)S(1)}, bf16[4,3,128,256]{3,2,1,0:T(8,128)(2,1)S(1)}, u32[]{:S(2)}, u32[]{:S(2)}) collective-permute-start(bf16[4,3,128,256]{3,2,1,0:T(8,128)(2,1)S(1)} %get-tuple-element.36), channel_id=1, source_target_pairs={{0,64},{1,193},{64,0},{65,129},{128,192},{129,65},{192,128},{193,1... | collective-permute-start | bytes 2359304 | tf_op jit(solution)/shard_map/ppermute | solution.py:290
  40.9 15.9 %collective-permute-start.8 = (bf16[4,3,128,256]{3,2,1,0:T(8,128)(2,1)S(1)}, bf16[4,3,128,256]{3,2,1,0:T(8,128)(2,1)S(1)}, u32[]{:S(2)}, u32[]{:S(2)}) collective-permute-start(bf16[4,3,128,256]{3,2,1,0:T(8,128)(2,1)S(1)} %get-tuple-element.34), channel_id=1, source_target_pairs={{0,8},{1,25},{8,0},{9,17},{16,24},{17,9},{24,16},{25,1},{2,10},{3,... | collective-permute-start | bytes 2359304 | tf_op jit(solution)/shard_map/ppermute | solution.py:290
  44.3 48.9 %collective-permute-start.11 = (bf16[2,4,3,128,256]{4,3,2,1,0:T(8,128)(2,1)S(1)}, bf16[2,4,3,128,256]{4,3,2,1,0:T(8,128)(2,1)}, u32[]{:S(2)}, u32[]{:S(2)}) collective-permute-start(bf16[2,4,3,128,256]{4,3,2,1,0:T(8,128)(2,1)S(1)} %pad_maximum_fusion.refs_0_), channel_id=1, source_target_pairs={{0,192},{1,65},{64,128},{65,1},{128,64},{129,193},{192,0},{193,129... | collective-permute-start | bytes 4718600 | tf_op jit(solution)/shard_map/ppermute | solution.py:290
  56.8 0.9 copy-start.7
  56.8 28.5 %copy-start.9 = (s32[4]{0:T(128)S(1)}, s32[4]{0:T(128)}, u32[]{:S(2)}) copy-start(s32[4]{0:T(128)} %constant.43.clone) | copy-start | bytes 52
  56.8 28.5 %copy-start.10 = (s32[4]{0:T(128)S(1)}, s32[4]{0:T(128)}, u32[]{:S(2)}) copy-start(s32[4]{0:T(128)} %constant.44.clone) | copy-start | bytes 52
  57.0 36.2 %collective-permute-start.12 = (bf16[2,4,3,128,256]{4,3,2,1,0:T(8,128)(2,1)S(1)}, bf16[2,4,3,128,256]{4,3,2,1,0:T(8,128)(2,1)}, u32[]{:S(2)}, u32[]{:S(2)}) collective-permute-start(bf16[2,4,3,128,256]{4,3,2,1,0:T(8,128)(2,1)S(1)} %pad_maximum_fusion.1.refs_2_), channel_id=1, source_target_pairs={{0,24},{1,9},{8,16},{9,1},{16,8},{17,25},{24,0},{25,17},{2,26},{3,... | collective-permute-start | bytes 4718600 | tf_op jit(solution)/shard_map/ppermute | solution.py:290
  57.7 18.7 %collective-permute-start.5 = (bf16[256,128]{1,0:T(8,128)(2,1)S(1)}, bf16[256,128]{1,0:T(8,128)(2,1)S(1)}, u32[]{:S(2)}, u32[]{:S(2)}) collective-permute-start(bf16[256,128]{1,0:T(8,128)(2,1)S(1)} %get-tuple-element.41), channel_id=1, source_target_pairs={{0,0},{1,32},{32,1},{33,33},{2,2},{3,34},{34,3},{35,35},{4,4},{5,3... | collective-permute-start | bytes 196616 | tf_op jit(solution)/shard_map/ppermute | solution.py:330
  58.4 20.5 %collective-permute-start.6 = (bf16[256,128]{1,0:T(8,128)(2,1)S(1)}, bf16[256,128]{1,0:T(8,128)(2,1)S(1)}, u32[]{:S(2)}, u32[]{:S(2)}) collective-permute-start(bf16[256,128]{1,0:T(8,128)(2,1)S(1)} %get-tuple-element.42), channel_id=1, source_target_pairs={{0,32},{1,0},{32,33},{33,1},{2,34},{3,2},{34,35},{35,3},{4,36},{5,... | collective-permute-start | bytes 196616 | tf_op jit(solution)/shard_map/ppermute | solution.py:330
  78.9 5.1 %collective-permute-start.9 = (bf16[512,128]{1,0:T(8,128)(2,1)S(1)}, bf16[512,128]{1,0:T(8,128)(2,1)S(1)}, u32[]{:S(2)}, u32[]{:S(2)}) collective-permute-start(bf16[512,128]{1,0:T(8,128)(2,1)S(1)} %pad_maximum_fusion.11), channel_id=1, source_target_pairs={{0,8},{1,25},{8,0},{9,17},{16,24},{17,9},{24,16},{25,1},{2,10},{3,... | collective-permute-start | bytes 393224 | tf_op jit(solution)/shard_map/ppermute | solution.py:290
  84.7 6.7 %collective-permute-start.10 = (bf16[2,512,128]{2,1,0:T(8,128)(2,1)}, bf16[2,512,128]{2,1,0:T(8,128)(2,1)}, u32[]{:S(2)}, u32[]{:S(2)}) collective-permute-start(bf16[2,512,128]{2,1,0:T(8,128)(2,1)} %pad_maximum_fusion.9), channel_id=1, source_target_pairs={{0,24},{1,9},{8,16},{9,1},{16,8},{17,25},{24,0},{25,17},{2,26},{3,... | collective-permute-start | bytes 786440 | tf_op jit(solution)/shard_map/ppermute | solution.py:290
  93.2 22.4 %copy-start.5 = (bf16[4,512,128]{2,1,0:T(8,128)(2,1)S(1)}, bf16[4,512,128]{2,1,0:T(8,128)(2,1)}, u32[]{:S(2)}) copy-start(bf16[4,512,128]{2,1,0:T(8,128)(2,1)} %pad_maximum_fusion.6) | copy-start | bytes 1572868
  93.2 22.4 %collective-permute-start.13 = (bf16[4,512,128]{2,1,0:T(8,128)(2,1)}, bf16[4,512,128]{2,1,0:T(8,128)(2,1)S(1)}, u32[]{:S(2)}, u32[]{:S(2)}) collective-permute-start(bf16[4,512,128]{2,1,0:T(8,128)(2,1)} %pad_maximum_fusion.6), channel_id=1, source_target_pairs={{0,64},{1,193},{64,0},{65,129},{128,192},{129,65},{192,128},{193,1... | collective-permute-start | bytes 1572872 | tf_op jit(solution)/shard_map/ppermute | solution.py:290
  115.5 1.2 copy-start.1
  115.5 4.4 %copy-start.8 = (bf16[32,128]{1,0:T(8,128)(2,1)S(1)}, bf16[32,128]{1,0:T(8,128)(2,1)}, u32[]{:S(2)}) copy-start(bf16[32,128]{1,0:T(8,128)(2,1)} %param.15) | copy-start | bytes 24580
  115.6 4.4 %copy-start.11 = (f32[512]{0:T(512)S(1)}, f32[512]{0:T(512)}, u32[]{:S(2)}) copy-start(f32[512]{0:T(512)} %param.16) | copy-start | bytes 6148
  116.7 16.0 %collective-permute-start.17 = (bf16[2,4,512,128]{3,2,1,0:T(8,128)(2,1)S(1)}, bf16[2,4,512,128]{3,2,1,0:T(8,128)(2,1)S(1)}, u32[]{:S(2)}, u32[]{:S(2)}) collective-permute-start(bf16[2,4,512,128]{3,2,1,0:T(8,128)(2,1)S(1)} %pad_maximum_fusion.2.here_ref), channel_id=1, source_target_pairs={{0,192},{1,65},{64,128},{65,1},{128,64},{129,193},{192,0},{193,129... | collective-permute-start | bytes 3145736 | tf_op jit(solution)/shard_map/ppermute | solution.py:290
  117.4 10.2 %collective-permute-start.14 = (bf16[144,256]{1,0:T(8,128)(2,1)}, bf16[144,256]{1,0:T(8,128)(2,1)}, u32[]{:S(2)}, u32[]{:S(2)}) collective-permute-start(bf16[144,256]{1,0:T(8,128)(2,1)} %get-tuple-element.39), channel_id=1, source_target_pairs={{0,8},{8,16},{16,24},{24,64},{64,72},{72,80},{80,88},{88,128},{128... | collective-permute-start | bytes 221192 | tf_op jit(solution)/shard_map/ppermute | solution.py:356
  120.7 1.4 copy-start.2
  123.6 9.1 %collective-permute-start.18 = (bf16[2,256,256]{2,1,0:T(8,128)(2,1)S(1)}, bf16[2,256,256]{2,1,0:T(8,128)(2,1)S(1)}, u32[]{:S(2)}, u32[]{:S(2)}) collective-permute-start(bf16[2,256,256]{2,1,0:T(8,128)(2,1)S(1)} %mix.3.mine_ref), channel_id=1, source_target_pairs={{0,1},{1,0},{2,3},{3,2},{4,5},{5,4},{6,7},{7,6},{8,9},{9,8},{10,11... | collective-permute-start | bytes 786440 | tf_op jit(solution)/shard_map/ppermute | solution.py:363
  126.2 4.9 %collective-permute-start.15 = (bf16[144,256]{1,0:T(8,128)(2,1)}, bf16[144,256]{1,0:T(8,128)(2,1)S(1)}, u32[]{:S(2)}, u32[]{:S(2)}) collective-permute-start(bf16[144,256]{1,0:T(8,128)(2,1)} %get-tuple-element.40), channel_id=1, source_target_pairs={{0,8},{8,16},{16,24},{24,0},{64,72},{72,80},{80,88},{88,64},{128,1... | collective-permute-start | bytes 221192 | tf_op jit(solution)/shard_map/ppermute | solution.py:357
  132.6 5.9 %collective-permute-start.16 = (bf16[2,256,256]{2,1,0:T(8,128)(2,1)S(1)}, bf16[2,256,256]{2,1,0:T(8,128)(2,1)S(1)}, u32[]{:S(2)}, u32[]{:S(2)}) collective-permute-start(bf16[2,256,256]{2,1,0:T(8,128)(2,1)S(1)} %mix.2.mine_ref), channel_id=1, source_target_pairs={{0,1},{1,0},{2,3},{3,2},{4,5},{5,4},{6,7},{7,6},{8,9},{9,8},{10,11... | collective-permute-start | bytes 786440 | tf_op jit(solution)/shard_map/ppermute | solution.py:363
  132.7 1.0 copy-start.3
  143.1 57.6 %copy-start.4 = (bf16[512,512]{1,0:T(8,128)(2,1)S(1)}, bf16[512,512]{1,0:T(8,128)(2,1)}, u32[]{:S(2)}) copy-start(bf16[512,512]{1,0:T(8,128)(2,1)} %param.10) | copy-start | bytes 1572868
Sparse Core Ops, SparseCore 0:
  10.2 66.2 all-gather.2
  143.2 57.4 reduce-scatter.1

commit v5 on v4

v5 whole, which is shorter than its diff:
```python
import jax
import jax.numpy as jnp
from jax import lax
from jax.experimental import pallas as pl
from jax.experimental.pallas import tpu as pltpu
from jax.sharding import Mesh, PartitionSpec as P

GSIZE = 16
LH = 128
ROWS = 512
TILE = 80
SHARE = 72
HALF = ROWS // 2
WIDE = 512
CH = 256
GROUPS = CH // GSIZE
HALO = LH + 16
MIB = 1024 * 1024
F32 = jnp.float32
BF16 = jnp.bfloat16


def row_iota(shape):
    return lax.broadcasted_iota(jnp.int32, shape, 0)


def three_taps(rows, taps, s):
    return (
        taps[0, s : s + 1] * rows
        + taps[1, s : s + 1] * pltpu.roll(rows, 1, 0)
        + taps[2, s : s + 1] * pltpu.roll(rows, 2, 0)
    )


def last_rows(parts, first, shift):
    place = row_iota((16, CH)) // 2
    out = jnp.zeros((16, CH), F32)
    for s in range(3):
        moved = pltpu.roll(parts[s][first : first + 16], (2 * s + shift) % 16, 0)
        out = jnp.where(place == s, moved, out)
    return out.astype(BF16)


def add_products(kind, at_ref, x_ref, here_ref, there_ref, acc, stat, wide, sems):
    step = pl.program_id(0)
    turns = []
    for y in range(4):
        copies = []
        for x in range(4):
            i, j = (y, x) if kind == 0 else (x, y)
            source = (here_ref, there_ref)[i // 2].at[i % 2, j]
            place = wide.at[y, :, at_ref[4 + x]]
            copies.append(pltpu.make_async_copy(source, place, sems.at[y, x]))
        turns.append(copies)

    @pl.when(step == 0)
    def _():
        for copies in turns:
            for copy in copies:
                copy.start()

    for k in range(4):

        @pl.when(step == k)
        def _(k=k):
            for copy in turns[k]:
                copy.wait()

    for h in range(2):
        rows = x_ref[h, 0]
        stat[h] += rows[ROWS + TILE - 16 :].astype(F32)[8:]
        for s in range(3):
            weights = wide[step, s].reshape(WIDE, CH)
            acc[h, s] += jnp.dot(rows, weights, preferred_element_type=F32)


def first_kernel(at_ref, x_ref, here_ref, there_ref, acc, stat, wide, sems):
    @pl.when(pl.program_id(0) == 0)
    def _():
        acc[...] = jnp.zeros_like(acc)
        stat[...] = jnp.zeros_like(stat)

    add_products(0, at_ref, x_ref, here_ref, there_ref, acc, stat, wide, sems)


def as_column(row):
    column = jnp.broadcast_to(row, (128, row.shape[1])).T
    return jnp.concatenate([column] * (CH // 128), axis=1)


def second_kernel(at_ref, x_ref, here_ref, there_ref, part_ref, sums_ref, taps_ref, *refs):
    proj_ref, tail_ref, mid_ref, front_ref, acc, stat, wide, ahead, sems = refs

    @pl.when(pl.program_id(0) == 0)
    def _():
        acc[...] = part_ref[...]
        stat[...] = sums_ref[...]

    add_products(1, at_ref, x_ref, here_ref, there_ref, acc, stat, wide, sems)

    @pl.when(pl.program_id(0) == pl.num_programs(0) - 1)
    def _():
        for h in range(2):
            sums = stat[h]
            own = lax.rsqrt((sums[0:1] + sums[1:2]) * (1.0 / 4096.0) + 1e-6)
            extra = lax.rsqrt((sums[2:3] + sums[3:4]) * (1.0 / 4096.0) + 1e-6)
            own, extra = as_column(own), as_column(extra[:, :128])[:TILE]
            for s in range(3):
                proj_ref[s, h] = (acc[h, s, :ROWS] * own).astype(BF16)
                carried = (acc[h, s, ROWS:] * extra).astype(BF16).astype(F32)
                if h == 0:
                    ahead[s, :SHARE] = carried[:SHARE]
                else:
                    ahead[s, SHARE:] = carried
            for end, ref in ((ROWS, tail_ref), (HALF, mid_ref)):
                rows = [proj_ref[s, h, end - HALO : end].astype(F32) for s in range(3)]
                mixing = three_taps(rows[1], taps_ref, 1) * three_taps(rows[2], taps_ref, 2)
                ref[h, :LH] = mixing[HALO - LH :].astype(BF16)
                ref[h, LH:] = last_rows(rows, HALO - 16, 2)
        mixing = three_taps(ahead[1], taps_ref, 1) * three_taps(ahead[2], taps_ref, 2)
        front_ref[:LH] = pltpu.roll(mixing, SHARE + TILE - 1, 0)[:LH].astype(BF16)
        front_ref[LH:] = last_rows(ahead, LH - 8, -7)


def project(at, gathered, kept, got, taps):
    count = ROWS + TILE
    acc = (2, 3, count, CH)
    stat = (2, 8, WIDE)
    wide = pltpu.VMEM((4, 3, 4, 128, CH), BF16)
    sems = pltpu.SemaphoreType.DMA((4, 4))

    def whole(shape):
        return pl.BlockSpec(shape, lambda k, at: (0,) * len(shape))

    def inputs(kind):
        def features(k, at):
            return 0, 2 * at[k] + (at[8] if kind == 0 else 1 - at[8]), 0, 0

        return [
            pl.BlockSpec((2, 1, count, WIDE), features),
            *[pl.BlockSpec(memory_space=pl.ANY)] * 2,
        ]

    options = dict(
        compiler_params=pltpu.CompilerParams(vmem_limit_bytes=40 * MIB),
        cost_estimate=pl.CostEstimate(
            flops=2 * count * 4096 * 3 * CH, bytes_accessed=12_000_000, transcendentals=0
        ),
    )
    part, sums = pl.pallas_call(
        first_kernel,
        grid_spec=pltpu.PrefetchScalarGridSpec(
            num_scalar_prefetch=1,
            grid=(4,),
            in_specs=inputs(0),
            out_specs=[whole(acc), whole(stat)],
            scratch_shapes=[wide, sems],
        ),
        out_shape=[jax.ShapeDtypeStruct(acc, F32), jax.ShapeDtypeStruct(stat, F32)],
        name="project_first",
        **options,
    )(at, gathered, *kept)
    shapes = [(3, 2, ROWS, CH), (2, HALO, CH), (2, HALO, CH), (HALO, CH)]
    return pl.pallas_call(
        second_kernel,
        grid_spec=pltpu.PrefetchScalarGridSpec(
            num_scalar_prefetch=1,
            grid=(4,),
            in_specs=[*inputs(1), whole(acc), whole(stat), whole((3, 3, CH))],
            out_specs=[whole(shape) for shape in shapes],
            scratch_shapes=[
                pltpu.VMEM(acc, F32),
                pltpu.VMEM(stat, F32),
                wide,
                pltpu.VMEM((3, SHARE + TILE, CH), F32),
                sems,
            ],
        ),
        out_shape=[jax.ShapeDtypeStruct(shape, BF16) for shape in shapes],
        name="project_second",
        **options,
    )(at, gathered, *got, part, sums, taps)


def toeplitz_kernel(u_ref, out_ref):
    for g in range(GROUPS):
        wide = jnp.broadcast_to(u_ref[g : g + 1], (LH, 3 * LH))
        skewed = pltpu.roll(wide, 0, 1, stride=1, stride_axis=0)
        out_ref[g] = skewed[:, : 2 * LH].astype(BF16)


def toeplitz(filters):
    backwards = jnp.flip(filters.astype(F32), 1)
    row = jnp.pad(backwards, ((0, 0), (1, 2 * LH - 1)))
    return pl.pallas_call(
        toeplitz_kernel,
        out_shape=jax.ShapeDtypeStruct((GROUPS, LH, 2 * LH), BF16),
        compiler_params=pltpu.CompilerParams(vmem_limit_bytes=8 * MIB),
        name="toeplitz",
    )(row)


def mix_kernel(proj_ref, halo_ref, band_ref, taps_ref, bias_ref, out_ref, before, edge):
    step = pl.program_id(0)

    @pl.when(step == 0)
    def _():
        for h in range(2):
            before[h] = halo_ref[h, :LH]
            last = halo_ref[h, LH:].astype(F32)
            for s in range(3):
                edge[h, s] = pltpu.roll(last, (6 - 2 * s) % 16, 0)[:8]

    queries = []
    mixes = []
    windows = []
    for h in range(2):
        feats = []
        for s in range(3):
            lifted = proj_ref[s, h].astype(F32)
            rows = jnp.concatenate([edge[h, s], lifted], axis=0)
            feats.append(three_taps(rows, taps_ref, s)[8:])
            edge[h, s] = lifted[LH - 8 :]
        mixing = (feats[1] * feats[2]).astype(BF16)
        queries.append(feats[0])
        mixes.append(mixing)
        windows.append(jnp.concatenate([before[h], mixing], axis=0))
        before[h] = mixing
    lane_group = lax.broadcasted_iota(jnp.int32, (LH, 2 * LH), 1) % LH // GSIZE
    halves = []
    for half in range(2):
        lanes = slice(half * LH, (half + 1) * LH)
        window = jnp.concatenate([windows[0][:, lanes], windows[1][:, lanes]], axis=1)
        total = jnp.zeros((LH, 2 * LH), F32)
        for g in range(GROUPS // 2):
            one = jnp.dot(band_ref[half * 8 + g], window, preferred_element_type=F32)
            total = jnp.where(lane_group == g, one, total)
        halves.append(total)
    for h in range(2):
        rows = slice(h * LH, (h + 1) * LH)
        filtered = jnp.concatenate([halves[0][:, rows], halves[1][:, rows]], axis=1)
        value = queries[h] * (filtered + bias_ref[...] * mixes[h].astype(F32))
        out_ref[h] = value.astype(BF16)


def mix(proj, halo, band, taps, bias, first, count):
    return pl.pallas_call(
        mix_kernel,
        grid=(count,),
        in_specs=[
            pl.BlockSpec((3, 2, LH, CH), lambda b: (0, 0, b + first, 0)),
            pl.BlockSpec((2, HALO, CH), lambda b: (0, 0, 0)),
            pl.BlockSpec((GROUPS, LH, 2 * LH), lambda b: (0, 0, 0)),
            pl.BlockSpec((3, 3, CH), lambda b: (0, 0, 0)),
            pl.BlockSpec((1, CH), lambda b: (0, 0)),
        ],
        out_specs=pl.BlockSpec((2, LH, CH), lambda b: (0, b, 0)),
        out_shape=jax.ShapeDtypeStruct((2, count * LH, CH), BF16),
        scratch_shapes=[
            pltpu.VMEM((2, LH, CH), BF16),
            pltpu.VMEM((2, 3, 8, CH), F32),
        ],
        compiler_params=pltpu.CompilerParams(vmem_limit_bytes=16 * MIB),
        cost_estimate=pl.CostEstimate(
            flops=2 * 512 * CH * 2048, bytes_accessed=2_000_000, transcendentals=0
        ),
        name="mix",
    )(proj, halo, band, taps, bias)


def out_kernel(at_ref, mine_ref, other_ref, here_ref, there_ref, *refs):
    out_ref, wide, rows, sems = refs[-4:]
    step = pl.program_id(0)
    turns = []
    for i in range(4):
        copies = []
        for j in range(4):
            lanes = pl.ds(pl.multiple_of(at_ref[4 + j] * 128, 128), 128)
            for part in range(4):
                source = (here_ref, there_ref)[i // 2].at[
                    i % 2, j, part // 2, :, pl.ds(part % 2 * 128, 128)
                ]
                place = wide.at[i, pl.ds(part * 128, 128), lanes]
                copies.append(pltpu.make_async_copy(source, place, sems.at[i, j, part]))
        turns.append(copies)

    @pl.when(step == 0)
    def _():
        for copies in turns:
            for copy in copies:
                copy.start()
        swap = at_ref[9] == 1
        for h in range(2):
            place = slice(h * HALF, (h + 1) * HALF)
            rows[place, :CH] = jnp.where(swap, other_ref[h], mine_ref[h])
            rows[place, CH:] = jnp.where(swap, mine_ref[h], other_ref[h])

    for k in range(4):

        @pl.when(step == k)
        def _(k=k):
            for copy in turns[k]:
                copy.wait()

    products = jnp.dot(rows[...], wide[step], preferred_element_type=F32).astype(BF16)
    for h in range(2):
        out_ref[h, 0] = products[h * HALF : (h + 1) * HALF]


def project_out(at, mine, other, parts, half, base=None):
    more = () if base is None else (base,)
    return pl.pallas_call(
        out_kernel,
        grid_spec=pltpu.PrefetchScalarGridSpec(
            num_scalar_prefetch=1,
            grid=(4,),
            in_specs=[
                *[pl.BlockSpec((2, HALF, CH), lambda k, at: (0, 0, 0))] * 2,
                *[pl.BlockSpec(memory_space=pl.ANY)] * (2 + len(more)),
            ],
            out_specs=pl.BlockSpec((2, 1, HALF, WIDE), lambda k, at: (0, at[k], half, 0)),
            scratch_shapes=[
                pltpu.VMEM((4, 2 * CH, WIDE), BF16),
                pltpu.VMEM((2 * HALF, 2 * CH), BF16),
                pltpu.SemaphoreType.DMA((4, 4, 4)),
            ],
        ),
        out_shape=jax.ShapeDtypeStruct((2, 4, ROWS, WIDE), BF16),
        input_output_aliases={} if base is None else {5: 0},
        compiler_params=pltpu.CompilerParams(vmem_limit_bytes=46 * MIB),
        cost_estimate=pl.CostEstimate(
            flops=2 * 512 * 2 * CH * 2048, bytes_accessed=5_000_000, transcendentals=0
        ),
        name="project_out",
    )(at, mine, other, *parts, *more)


FIRST, SECOND = (1, 3), (3, 1)


def pair_step(value, axis, masks):
    pairs = [(i * 2 + c, (i ^ masks[c]) * 2 + c) for i in range(4) for c in range(2)]
    return lax.ppermute(value, (axis, "c"), pairs)


def ring_pairs(piece, axis):
    here = jnp.stack([piece, pair_step(piece, axis, FIRST)])
    return here, pair_step(here, axis, SECOND)


def on_device(
    tokens, prior_rows, norm_gain, in_weight, short_filter, mr_filter, mr_bias, out_weight
):
    zh = lax.axis_index("zh")
    column = lax.axis_index("x")
    leading = (column == 0) & (lax.axis_index("y") == 0)

    core = lax.axis_index("c")
    turns = jnp.where(core == 0, jnp.array([0, 1, 3, 2]), jnp.array([0, 3, 1, 2]))
    at = jnp.concatenate(
        [lax.axis_index("y") ^ turns, column ^ turns, jnp.stack([zh, zh ^ core])]
    ).astype(jnp.int32)
    ring = ("zh", "zl", "c")
    padded = jnp.pad(prior_rows, ((0, 2 * SHARE - prior_rows.shape[0]), (0, 0)))
    some = lax.dynamic_slice_in_dim(padded, zh * SHARE, SHARE, 0)
    lifted, carried = tokens.astype(F32), some.astype(F32)
    gain = norm_gain.astype(F32)
    sums = jnp.sum(lifted * lifted, axis=1)
    more = jnp.pad(jnp.sum(carried * carried, axis=1), (0, WIDE - SHARE))
    sums = jnp.stack([sums, more])
    coarse = lax.reduce_precision(sums, 8, 7)
    terms = jnp.stack([coarse, sums - coarse], axis=1).reshape(4, WIDE).astype(BF16)
    own = jnp.concatenate(
        [
            (lifted * gain).astype(BF16),
            (carried * gain).astype(BF16),
            jnp.pad(terms, ((0, TILE - SHARE - 4), (0, 0))),
        ],
        axis=0,
    )
    gathered = lax.all_gather(own, ring).reshape(2, 8, ROWS + TILE, WIDE)

    left, right = in_weight[..., :CH], in_weight[..., CH:]
    kept = jnp.where(zh == 0, left, right)
    got = lax.ppermute(jnp.where(zh == 0, right, left), "zh", [(0, 1), (1, 0)])
    pieces = []
    for k in range(2):
        chosen = lax.dynamic_slice_in_dim(out_weight, (core ^ k) * CH, CH, 0)
        pairs = [(a * 2 + b, (b ^ k) * 2 + a) for a in range(2) for b in range(2)]
        pieces.append(lax.ppermute(chosen, ("zh", "c"), pairs))
    got, pieces = lax.optimization_barrier((got, pieces))
    pieces = [jnp.concatenate([p[:128], p[128:]], axis=1)[None] for p in pieces]
    kept = jnp.concatenate([kept, *pieces], axis=0)
    kept = jnp.stack([kept, pair_step(kept, "x", FIRST)])
    got = jnp.stack([got, pair_step(got, "y", FIRST)])
    kept, got = lax.optimization_barrier((kept, got))
    line = jnp.concatenate([kept, pair_step(kept, "x", SECOND)], axis=0)
    got = jnp.concatenate([got, pair_step(got, "y", SECOND)], axis=0)
    kept = ring_pairs(line[:, :3], "y")
    got = ring_pairs(got, "x")
    out_line, _ = lax.optimization_barrier((line[:, 3:], kept[1]))
    out_here = jnp.stack([out_line, pair_step(out_line, "y", FIRST)])
    out_here, _ = lax.optimization_barrier((out_here, got[1]))
    out_parts = (out_here, pair_step(out_here, "y", SECOND))

    taps = lax.dynamic_slice_in_dim(short_filter, zh * CH, CH, 2)
    bias = lax.dynamic_slice_in_dim(mr_bias, zh * CH, CH, 0)[None, :]
    band = toeplitz(lax.dynamic_slice_in_dim(mr_filter, zh * GROUPS, GROUPS, 0))

    proj, tail, mid, front = project(at, gathered, kept, got, taps)

    last = column == 3
    to_first = jnp.where(last, tail[1], tail[0])
    to_second = jnp.where(last, tail[0], tail[1])
    first = lax.ppermute(to_first, ("y", "x"), [(i, i + 1) for i in range(15)])
    second = lax.ppermute(
        to_second, ("y", "x"), [(i, i // 4 * 4 + (i + 1) % 4) for i in range(16)]
    )
    halo = jnp.stack([jnp.where(leading, front, first), second])

    def swapped(mine):
        return mine, lax.ppermute(mine, "c", [(0, 1), (1, 0)])

    partial = project_out(at, *swapped(mix(proj, mid, band, taps, bias, 2, 2)), out_parts, 1)
    partial = project_out(
        at, *swapped(mix(proj, halo, band, taps, bias, 0, 2)), out_parts, 0, partial
    )
    summed = lax.psum_scatter(
        partial.reshape(8, ROWS, WIDE), ("zh", "zl"), scatter_dimension=0
    )
    return (tokens.astype(F32) + summed.astype(F32)).astype(BF16)


def solution(mesh):
    split = Mesh(mesh.devices.reshape(4, 2, 4, 4, 2), ("y", "zh", "x", "zl", "c"))
    seq, tensor = ("y", "zh", "x"), ("zl", "c")
    in_specs = (
        P(seq, tensor),
        P(None, tensor),
        P(tensor),
        P(None, seq, tensor),
        P(None, None, tensor),
        P(tensor, None),
        P(tensor),
        P(tensor, seq),
    )
    return jax.shard_map(
        on_device, mesh=split, in_specs=in_specs, out_specs=P(seq, tensor), check_vma=False
    )
```

time: 211 us -> 231 us (1.095)
  waiting for transfers between devices: 101 us -> 131 us
  Pallas kernels: 34.8 us -> 28 us
  starting transfers between devices: 45.1 us -> 39.6 us
  local copies, waits for them, and re-layouts: 5.68 us -> 9.11 us
    ppermute x12 -> x10, waiting for transfers between devices: 34.2 us -> 50.6 us  [pair_step(): return lax.ppermute(value, (axis, 'c'), pairs)]
    reduce_scatter x1, waiting for transfers between devices: 57.6 us -> 71.4 us  [on_device(): lax.psum_scatter(partial.reshape(8, ROWS, WIDE), ('zh', 'zl'), scatter_di...]
    ppermute x2, starting transfers between devices: 18.6 us -> 7.09 us  [on_device(): pieces.append(lax.ppermute(chosen, ('zh', 'c'), pairs))]
    ppermute x12 -> x10, starting transfers between devices: 12.6 us -> 19.1 us  [pair_step(): return lax.ppermute(value, (axis, 'c'), pairs)]
    unnamed x24 -> x32, local copies, waits for them, and re-layouts: 3.78 us -> 8.63 us
    pallas_call x1 -> x2, Pallas kernels: 22 us -> 17.3 us  [the longest x1 8.97 us: project(): pl.pallas_call(second_kernel, grid_spec=pltpu.PrefetchScalarGridSpec(num_...]
    ppermute x1, waiting for transfers between devices: 4.45 us -> 0.01 us  [on_device(): got = lax.ppermute(jnp.where(zh == 0, right, left), 'zh', [(0, 1), (1, 0)])]
    ppermute x2, waiting for transfers between devices: 2.49 us -> 5.87 us  [on_device(): pieces.append(lax.ppermute(chosen, ('zh', 'c'), pairs))]
  transfers between devices with their start and end apart: 21 -> 19, of which waited for: 11 -> 11; matrix products, arithmetic and copies ran while one was open for 2% -> 1% of each run, Pallas kernels for 14% -> 11%
where the time goes in v5:
time: 231 us; the launch traced here: 230 us
  waiting for transfers between devices  131 us (57%)
  starting transfers between devices  39.6 us (17%)
  Pallas kernels  28 us (12%)
  between operations  13.8 us (6%)
  local copies, waits for them, and re-layouts  9.11 us (4%)
  other arithmetic  8.51 us (4%)
    reduce_scatter x1, waiting for transfers between devices, on_device(): lax.psum_scatter(partial.reshape(8, ROWS, WIDE), ('zh', 'zl'), scatter_di...  71.4 us
    ppermute x10, waiting for transfers between devices, pair_step(): return lax.ppermute(value, (axis, 'c'), pairs)  50.6 us
    ppermute x10, starting transfers between devices, pair_step(): return lax.ppermute(value, (axis, 'c'), pairs)  19.1 us
    pallas_call x1, Pallas kernels, project(): pl.pallas_call(second_kernel, grid_spec=pltpu.PrefetchScalarGridSpec(num_...  8.97 us
    unnamed x32, local copies, waits for them, and re-layouts  8.63 us
    pallas_call x1, Pallas kernels, project(): pl.pallas_call(first_kernel, grid_spec=pltpu.PrefetchScalarGridSpec(num_s...  8.33 us
    pallas_call x2, Pallas kernels, project_out(): pl.pallas_call(out_kernel, grid_spec=pltpu.PrefetchScalarGridSpec(num_sca...  7.38 us
    ppermute x1, starting transfers between devices, on_device(): got = lax.ppermute(jnp.where(zh == 0, right, left), 'zh', [(0, 1), (1, 0)])  7.23 us
  transfers between devices with their start and end apart: 19, of which 11 were waited for; matrix products, arithmetic and copies ran while one was open for 1% of the time, Pallas kernels for 11%

profile of v5, /device:TPU:2, one launch (start us, length us, event | category | flops | bytes accessed | tf_op | source)
XLA Modules:
  0.0 229.6 jit_solution(741044346817419102)
XLA Ops:
  6.5 0.7 convert_element_type.41
  7.3 1.3 fusion.1
  8.5 1.1 fusion.5
  9.7 0.9 fusion.4
  10.7 7.2 %collective-permute-start = (bf16[3,128,256]{2,1,0:T(8,128)(2,1)S(1)}, bf16[3,128,256]{2,1,0:T(8,128)(2,1)S(1)}, u32[]{:S(2)}, u32[]{:S(2)}) collective-permute-start(bf16[3,128,256]{2,1,0:T(8,128)(2,1)S(1)} %get-tuple-element.36), channel_id=1, source_target_pairs={{0,32},{32,0},{1,33},{33,1},{2,34},{34,2},{3,35},{35,3},{4,36},{36... | collective-permute-start | bytes 589832 | tf_op jit(solution)/shard_map/ppermute | solution.py:385
  18.0 0.7 collective-permute-start.1
  18.7 6.4 %collective-permute-start.2 = (bf16[256,128]{1,0:T(8,128)(2,1)S(1)}, bf16[256,128]{1,0:T(8,128)(2,1)S(1)}, u32[]{:S(2)}, u32[]{:S(2)}) collective-permute-start(bf16[256,128]{1,0:T(8,128)(2,1)S(1)} %get-tuple-element.43), channel_id=1, source_target_pairs={{0,32},{1,0},{32,33},{33,1},{2,34},{3,2},{34,35},{35,3},{4,36},{5,... | collective-permute-start | bytes 196616 | tf_op jit(solution)/shard_map/ppermute | solution.py:390
  25.1 5.9 %collective-permute-done.2 = bf16[256,128]{1,0:T(8,128)(2,1)S(1)} collective-permute-done((bf16[256,128]{1,0:T(8,128)(2,1)S(1)}, bf16[256,128]{1,0:T(8,128)(2,1)S(1)}, u32[]{:S(2)}, u32[]{:S(2)}) %collective-permute-start.2) | collective-permute-done | bytes 65568 | tf_op jit(solution)/shard_map/ppermute | solution.py:390
  31.1 0.7 collective-permute-start.3
  31.7 1.5 collective-permute-start.4
  33.3 4.1 %collective-permute-done.4 = bf16[3,128,256]{2,1,0:T(8,128)(2,1)S(1)} collective-permute-done((bf16[3,128,256]{2,1,0:T(8,128)(2,1)S(1)}, bf16[3,128,256]{2,1,0:T(8,128)(2,1)S(1)}, u32[]{:S(2)}, u32[]{:S(2)}) %collective-permute-start.4) | collective-permute-done | bytes 196640 | tf_op jit(solution)/shard_map/ppermute | solution.py:343
  37.4 0.8 collective-permute-done.3
  38.3 1.9 collective-permute-start.8
  40.3 8.7 %collective-permute-done.8 = bf16[2,5,128,256]{3,2,1,0:T(8,128)(2,1)S(1)} collective-permute-done((bf16[2,5,128,256]{3,2,1,0:T(8,128)(2,1)S(1)}, bf16[2,5,128,256]{3,2,1,0:T(8,128)(2,1)S(1)}, u32[]{:S(2)}, u32[]{:S(2)}) %collective-permute-start.8) | collective-permute-done | bytes 655392 | tf_op jit(solution)/shard_map/ppermute | solution.py:343
  49.0 0.1 slice_bitcast_fusion
  49.1 2.7 %collective-permute-start.9 = (bf16[4,3,128,256]{3,2,1,0:T(8,128)(2,1)S(1)}, bf16[4,3,128,256]{3,2,1,0:T(8,128)(2,1)S(1)}, u32[]{:S(2)}, u32[]{:S(2)}) collective-permute-start(bf16[4,3,128,256]{3,2,1,0:T(8,128)(2,1)S(1)} %get-tuple-element.32), channel_id=1, source_target_pairs={{0,64},{1,193},{64,0},{65,129},{128,192},{129,65},{192,128},{193,1... | collective-permute-start | bytes 2359304 | tf_op jit(solution)/shard_map/ppermute | solution.py:343
  51.8 2.2 collective-permute-start.5
  54.0 8.3 %collective-permute-done.5 = bf16[2,3,128,256]{3,2,1,0:T(8,128)(2,1)S(1)} collective-permute-done((bf16[2,3,128,256]{3,2,1,0:T(8,128)(2,1)S(1)}, bf16[2,3,128,256]{3,2,1,0:T(8,128)(2,1)S(1)}, u32[]{:S(2)}, u32[]{:S(2)}) %collective-permute-start.5) | collective-permute-done | bytes 393248 | tf_op jit(solution)/shard_map/ppermute | solution.py:343
  62.3 1.8 collective-permute-start.6
  64.1 0.7 collective-permute-done.9
  64.8 0.1 pad_maximum_fusion.1.here_ref
  65.0 2.3 %collective-permute-start.10 = (bf16[2,4,3,128,256]{4,3,2,1,0:T(8,128)(2,1)S(1)}, bf16[2,4,3,128,256]{4,3,2,1,0:T(8,128)(2,1)S(1)}, u32[]{:S(2)}, u32[]{:S(2)}) collective-permute-start(bf16[2,4,3,128,256]{4,3,2,1,0:T(8,128)(2,1)S(1)} %pad_maximum_fusion.1.here_ref), channel_id=1, source_target_pairs={{0,192},{1,65},{64,128},{65,1},{128,64},{129,193},{192,0},{193,129... | collective-permute-start | bytes 4718600 | tf_op jit(solution)/shard_map/ppermute | solution.py:343
  67.3 7.0 %collective-permute-done.6 = bf16[4,3,128,256]{3,2,1,0:T(8,128)(2,1)S(1)} collective-permute-done((bf16[4,3,128,256]{3,2,1,0:T(8,128)(2,1)S(1)}, bf16[4,3,128,256]{3,2,1,0:T(8,128)(2,1)S(1)}, u32[]{:S(2)}, u32[]{:S(2)}) %collective-permute-start.6) | collective-permute-done | bytes 786464 | tf_op jit(solution)/shard_map/ppermute | solution.py:343
  74.4 1.3 pad_maximum_fusion.here_ref
  75.7 2.6 %collective-permute-start.7 = (bf16[2,4,3,128,256]{4,3,2,1,0:T(8,128)(2,1)}, bf16[2,4,3,128,256]{4,3,2,1,0:T(8,128)(2,1)}, u32[]{:S(2)}, u32[]{:S(2)}) collective-permute-start(bf16[2,4,3,128,256]{4,3,2,1,0:T(8,128)(2,1)} %pad_maximum_fusion.here_ref), channel_id=1, source_target_pairs={{0,24},{1,9},{8,16},{9,1},{16,8},{17,25},{24,0},{25,17},{2,26},{3,... | collective-permute-start | bytes 4718600 | tf_op jit(solution)/shard_map/ppermute | solution.py:343
  78.4 9.2 %collective-permute-done.10.there_ref = bf16[2,4,3,128,256]{4,3,2,1,0:T(8,128)(2,1)S(1)} collective-permute-done((bf16[2,4,3,128,256]{4,3,2,1,0:T(8,128)(2,1)S(1)}, bf16[2,4,3,128,256]{4,3,2,1,0:T(8,128)(2,1)S(1)}, u32[]{:S(2)}, u32[]{:S(2)}) %collective-permute-start.10) | collective-permute-done | bytes 1572896 | tf_op jit(solution)/shard_map/ppermute | solution.py:343
  87.6 1.2 copy-done.6
  88.9 11.8 %collective-permute-done.14 = bf16[4,2,128,256]{3,2,1,0:T(8,128)(2,1)S(1)} collective-permute-done((bf16[4,2,128,256]{3,2,1,0:T(8,128)(2,1)S(1)}, bf16[4,2,128,256]{3,2,1,0:T(8,128)(2,1)S(1)}, u32[]{:S(2)}, u32[]{:S(2)}) %collective-permute-start.14) | collective-permute-done | bytes 524320 | tf_op jit(solution)/shard_map/ppermute | solution.py:343
  100.7 0.1 pad_maximum_fusion.2.here_ref
  100.8 3.3 %collective-permute-start.15 = (bf16[2,4,2,128,256]{4,3,2,1,0:T(8,128)(2,1)S(1)}, bf16[2,4,2,128,256]{4,3,2,1,0:T(8,128)(2,1)S(1)}, u32[]{:S(2)}, u32[]{:S(2)}) collective-permute-start(bf16[2,4,2,128,256]{4,3,2,1,0:T(8,128)(2,1)S(1)} %pad_maximum_fusion.2.here_ref), channel_id=1, source_target_pairs={{0,192},{1,65},{64,128},{65,1},{128,64},{129,193},{192,0},{193,129... | collective-permute-start | bytes 3145736 | tf_op jit(solution)/shard_map/ppermute | solution.py:343
  104.1 1.4 copy-done.5
  105.5 1.4 copy-done.7
  106.9 8.3 %project_first.1 = (f32[2,3,592,256]{3,2,1,0:T(8,128)S(1)}, f32[2,8,512]{2,1,0:T(8,128)S(1)}) custom-call(s32[10]{0:T(128)S(1)} %pad_add_fusion.at_ref, bf16[2,8,592,512]{3,2,1,0:T(8,128)(2,1)} %bitcast.36, bf16[2,4,3,128,256]{4,3,2,1,0:T(8,128)(2,1)S(1)} %copy-done.5, bf16[2,4,3,128,256]{4,3,2,1,0:T(8,128)(2,1)S(1)} %copy-done.7), custom_call_target="tpu_custom_call" | custom-call | flops 3724541952 | bytes 12000000 | tf_op jit(solution)/shard_map/project_first/pallas_call | solution.py:150
  115.2 9.0 %project_second.1 = (bf16[3,2,512,256]{3,2,1,0:T(8,128)(2,1)S(1)}, bf16[2,144,256]{2,1,0:T(8,128)(2,1)S(1)}, bf16[2,144,256]{2,1,0:T(8,128)(2,1)S(1)}, bf16[144,256]{1,0:T(8,128)(2,1)S(1)}) custom-call(s32[10]{0:T(128)S(1)} %pad_add_fusion.at_ref, bf16[2,8,592,512]{3,2,1,0:T(8,128)(2,1)} %bitcast.37, bf16[2,4,3,128,256]{4,3,2,1,0:T(8,128)(2,1)} %pad_maximum_fusion.here_ref, ...), custom_call_target="tpu_custom_call" | custom-call | flops 3724541952 | bytes 12000000 | tf_op jit(solution)/shard_map/project_second/pallas_call | solution.py:164
  124.2 1.2 copy-done.2
  125.4 0.7 select_bitcast_fusion.2
  126.1 3.8 %collective-permute-start.11 = (bf16[144,256]{1,0:T(8,128)(2,1)}, bf16[144,256]{1,0:T(8,128)(2,1)S(1)}, u32[]{:S(2)}, u32[]{:S(2)}) collective-permute-start(bf16[144,256]{1,0:T(8,128)(2,1)} %get-tuple-element.39), channel_id=1, source_target_pairs={{0,8},{8,16},{16,24},{24,64},{64,72},{72,80},{80,88},{88,128},{128... | collective-permute-start | bytes 221192 | tf_op jit(solution)/shard_map/ppermute | solution.py:415
  130.1 0.5 toeplitz.1.band_ref
  130.6 1.4 copy-done.3
  132.0 1.4 mix.3.mine_ref
  133.6 2.2 collective-permute-start.12
  135.8 2.7 %collective-permute-done.12 = bf16[144,256]{1,0:T(8,128)(2,1)S(1)} collective-permute-done((bf16[144,256]{1,0:T(8,128)(2,1)}, bf16[144,256]{1,0:T(8,128)(2,1)S(1)}, u32[]{:S(2)}, u32[]{:S(2)}) %collective-permute-start.12) | collective-permute-done | bytes 73760 | tf_op jit(solution)/shard_map/ppermute | solution.py:416
  138.5 1.4 mix.2.mine_ref
  140.1 3.7 %project_out.2.refs_0_ = bf16[2,4,512,512]{3,2,1,0:T(8,128)(2,1)S(1)} custom-call(s32[10]{0:T(128)S(1)} %pad_add_fusion.at_ref, bf16[2,256,256]{2,1,0:T(8,128)(2,1)S(1)} %mix.3.mine_ref, bf16[2,256,256]{2,1,0:T(8,128)(2,1)S(1)} %collective-permute-done.16.other_ref, bf16[2,4,2,128,256]{4,3,2,1,0:T(8,128)(2,1)S(1)} %pad_maximum_fusion.2.here_ref, ...), custom_call_target="tpu_custom_call" | custom-call | flops 1073741824 | bytes 5000000 | tf_op jit(solution)/shard_map/project_out/pallas_call | solution.py:312
  143.8 3.7 %project_out.3 = bf16[2,4,512,512]{3,2,1,0:T(8,128)(2,1)S(1)} custom-call(s32[10]{0:T(128)S(1)} %pad_add_fusion.at_ref, bf16[2,256,256]{2,1,0:T(8,128)(2,1)S(1)} %mix.2.mine_ref, bf16[2,256,256]{2,1,0:T(8,128)(2,1)S(1)} %collective-permute-done.13.other_ref, ...), custom_call_target="tpu_custom_call", output_to_operand_aliasing={{}: (5, {})} | custom-call | flops 1073741824 | bytes 5000000 | tf_op jit(solution)/shard_map/project_out/pallas_call | solution.py:312
  147.5 2.0 copy-done.1
  149.5 71.4 %reduce-scatter.2.cloned.1.call-done = bf16[1,512,512]{2,1,0:T(8,128)(2,1)} async-done(((bf16[8,512,512]{2,1,0:T(8,128)(2,1)}), bf16[1,512,512]{2,1,0:T(8,128)(2,1)}) %reduce-scatter.2.cloned.1.call-update) | async-done | bytes 524304 | tf_op jit(solution)/shard_map/reduce_scatter | solution.py:428
  220.8 2.0 fusion.3
  (65 shorter events, 1.1 us)
Async XLA Ops:
  6.5 82.3 %copy-start = (f32[3,3,512]{2,1,0:T(4,128)S(1)}, f32[3,3,512]{2,1,0:T(4,128)}, u32[]{:S(2)}) copy-start(f32[3,3,512]{2,1,0:T(4,128)} %param.14) | copy-start | bytes 55300
  6.5 97.5 %all-gather.3.cloned.1.call-start = ((), (), s32[]{:S(2)}) async-start(), calls=%async_computation.2 | async-start | bytes 10305536 | tf_op jit(solution)/shard_map/all_gather | solution.py:381
  6.5 4.1 %copy-start.9 = (bf16[3,128,512]{2,1,0:T(8,128)(2,1)S(1)}, bf16[3,128,512]{2,1,0:T(8,128)(2,1)}, u32[]{:S(2)}) copy-start(bf16[3,128,512]{2,1,0:T(8,128)(2,1)} %param.13) | copy-start | bytes 1179652
  8.5 9.4 %copy-start.10 = (bf16[512,128]{1,0:T(8,128)(2,1)S(1)}, bf16[512,128]{1,0:T(8,128)(2,1)}, u32[]{:S(2)}) copy-start(bf16[512,128]{1,0:T(8,128)(2,1)} %param.17) | copy-start | bytes 393220
  10.6 210.2 %reduce-scatter.2.cloned.1.call-start = ((), (), s32[]{:S(2)}) async-start(), calls=%async_computation.1 | async-start | bytes 4718592 | tf_op jit(solution)/shard_map/reduce_scatter | solution.py:428
  10.7 20.2 %collective-permute-start = (bf16[3,128,256]{2,1,0:T(8,128)(2,1)S(1)}, bf16[3,128,256]{2,1,0:T(8,128)(2,1)S(1)}, u32[]{:S(2)}, u32[]{:S(2)}) collective-permute-start(bf16[3,128,256]{2,1,0:T(8,128)(2,1)S(1)} %get-tuple-element.36), channel_id=1, source_target_pairs={{0,32},{32,0},{1,33},{33,1},{2,34},{34,2},{3,35},{35,3},{4,36},{36... | collective-permute-start | bytes 589832 | tf_op jit(solution)/shard_map/ppermute | solution.py:385
  18.0 7.1 %collective-permute-start.1 = (bf16[256,128]{1,0:T(8,128)(2,1)S(1)}, bf16[256,128]{1,0:T(8,128)(2,1)S(1)}, u32[]{:S(2)}, u32[]{:S(2)}) collective-permute-start(bf16[256,128]{1,0:T(8,128)(2,1)S(1)} %get-tuple-element.44), channel_id=1, source_target_pairs={{0,0},{1,32},{32,1},{33,33},{2,2},{3,34},{34,3},{35,35},{4,4},{5,3... | collective-permute-start | bytes 196616 | tf_op jit(solution)/shard_map/ppermute | solution.py:390
  18.7 12.3 %collective-permute-start.2 = (bf16[256,128]{1,0:T(8,128)(2,1)S(1)}, bf16[256,128]{1,0:T(8,128)(2,1)S(1)}, u32[]{:S(2)}, u32[]{:S(2)}) collective-permute-start(bf16[256,128]{1,0:T(8,128)(2,1)S(1)} %get-tuple-element.43), channel_id=1, source_target_pairs={{0,32},{1,0},{32,33},{33,1},{2,34},{3,2},{34,35},{35,3},{4,36},{5,... | collective-permute-start | bytes 196616 | tf_op jit(solution)/shard_map/ppermute | solution.py:390
  31.1 7.2 %collective-permute-start.3 = (bf16[5,128,256]{2,1,0:T(8,128)(2,1)S(1)}, bf16[5,128,256]{2,1,0:T(8,128)(2,1)S(1)}, u32[]{:S(2)}, u32[]{:S(2)}) collective-permute-start(bf16[5,128,256]{2,1,0:T(8,128)(2,1)S(1)} %get-tuple-element.38), channel_id=1, source_target_pairs={{0,8},{1,25},{8,0},{9,17},{16,24},{17,9},{24,16},{25,1},{2,10},{3,... | collective-permute-start | bytes 983048 | tf_op jit(solution)/shard_map/ppermute | solution.py:343
  31.7 5.7 %collective-permute-start.4 = (bf16[3,128,256]{2,1,0:T(8,128)(2,1)S(1)}, bf16[3,128,256]{2,1,0:T(8,128)(2,1)S(1)}, u32[]{:S(2)}, u32[]{:S(2)}) collective-permute-start(bf16[3,128,256]{2,1,0:T(8,128)(2,1)S(1)} %collective-permute-done), channel_id=1, source_target_pairs={{0,64},{1,193},{64,0},{65,129},{128,192},{129,65},{192,128},{193,1... | collective-permute-start | bytes 589832 | tf_op jit(solution)/shard_map/ppermute | solution.py:343
  38.3 10.7 %collective-permute-start.8 = (bf16[2,5,128,256]{3,2,1,0:T(8,128)(2,1)S(1)}, bf16[2,5,128,256]{3,2,1,0:T(8,128)(2,1)S(1)}, u32[]{:S(2)}, u32[]{:S(2)}) collective-permute-start(bf16[2,5,128,256]{3,2,1,0:T(8,128)(2,1)S(1)} %pad_maximum_fusion.3), channel_id=1, source_target_pairs={{0,24},{1,9},{8,16},{9,1},{16,8},{17,25},{24,0},{25,17},{2,26},{3,... | collective-permute-start | bytes 1966088 | tf_op jit(solution)/shard_map/ppermute | solution.py:343
  49.1 15.7 %collective-permute-start.9 = (bf16[4,3,128,256]{3,2,1,0:T(8,128)(2,1)S(1)}, bf16[4,3,128,256]{3,2,1,0:T(8,128)(2,1)S(1)}, u32[]{:S(2)}, u32[]{:S(2)}) collective-permute-start(bf16[4,3,128,256]{3,2,1,0:T(8,128)(2,1)S(1)} %get-tuple-element.32), channel_id=1, source_target_pairs={{0,64},{1,193},{64,0},{65,129},{128,192},{129,65},{192,128},{193,1... | collective-permute-start | bytes 2359304 | tf_op jit(solution)/shard_map/ppermute | solution.py:343
  51.8 10.5 %collective-permute-start.5 = (bf16[2,3,128,256]{3,2,1,0:T(8,128)(2,1)S(1)}, bf16[2,3,128,256]{3,2,1,0:T(8,128)(2,1)S(1)}, u32[]{:S(2)}, u32[]{:S(2)}) collective-permute-start(bf16[2,3,128,256]{3,2,1,0:T(8,128)(2,1)S(1)} %pad_maximum_fusion.4), channel_id=1, source_target_pairs={{0,192},{1,65},{64,128},{65,1},{128,64},{129,193},{192,0},{193,129... | collective-permute-start | bytes 1179656 | tf_op jit(solution)/shard_map/ppermute | solution.py:343
  62.3 12.1 %collective-permute-start.6 = (bf16[4,3,128,256]{3,2,1,0:T(8,128)(2,1)S(1)}, bf16[4,3,128,256]{3,2,1,0:T(8,128)(2,1)S(1)}, u32[]{:S(2)}, u32[]{:S(2)}) collective-permute-start(bf16[4,3,128,256]{3,2,1,0:T(8,128)(2,1)S(1)} %constant_dynamic-update-slice_fusion), channel_id=1, source_target_pairs={{0,8},{1,25},{8,0},{9,17},{16,24},{17,9},{24,16},{25,1},{2,10},{3,... | collective-permute-start | bytes 2359304 | tf_op jit(solution)/shard_map/ppermute | solution.py:343
  65.0 10.7 %copy-start.4 = (bf16[2,4,3,128,256]{4,3,2,1,0:T(8,128)(2,1)}, bf16[2,4,3,128,256]{4,3,2,1,0:T(8,128)(2,1)S(1)}, u32[]{:S(2)}) copy-start(bf16[2,4,3,128,256]{4,3,2,1,0:T(8,128)(2,1)S(1)} %pad_maximum_fusion.1.here_ref) | copy-start | bytes 4718596
  65.0 22.6 %collective-permute-start.10 = (bf16[2,4,3,128,256]{4,3,2,1,0:T(8,128)(2,1)S(1)}, bf16[2,4,3,128,256]{4,3,2,1,0:T(8,128)(2,1)S(1)}, u32[]{:S(2)}, u32[]{:S(2)}) collective-permute-start(bf16[2,4,3,128,256]{4,3,2,1,0:T(8,128)(2,1)S(1)} %pad_maximum_fusion.1.here_ref), channel_id=1, source_target_pairs={{0,192},{1,65},{64,128},{65,1},{128,64},{129,193},{192,0},{193,129... | collective-permute-start | bytes 4718600 | tf_op jit(solution)/shard_map/ppermute | solution.py:343
  74.4 14.4 %copy-start.12 = (s32[4]{0:T(128)S(1)}, s32[4]{0:T(128)}, u32[]{:S(2)}) copy-start(s32[4]{0:T(128)} %constant.44.clone) | copy-start | bytes 52
  74.4 14.4 %copy-start.13 = (s32[4]{0:T(128)S(1)}, s32[4]{0:T(128)}, u32[]{:S(2)}) copy-start(s32[4]{0:T(128)} %constant.45.clone) | copy-start | bytes 52
  75.7 25.1 %collective-permute-start.7 = (bf16[2,4,3,128,256]{4,3,2,1,0:T(8,128)(2,1)}, bf16[2,4,3,128,256]{4,3,2,1,0:T(8,128)(2,1)}, u32[]{:S(2)}, u32[]{:S(2)}) collective-permute-start(bf16[2,4,3,128,256]{4,3,2,1,0:T(8,128)(2,1)} %pad_maximum_fusion.here_ref), channel_id=1, source_target_pairs={{0,24},{1,9},{8,16},{9,1},{16,8},{17,25},{24,0},{25,17},{2,26},{3,... | collective-permute-start | bytes 4718600 | tf_op jit(solution)/shard_map/ppermute | solution.py:343
  87.6 1.2 copy-start.6
  88.7 11.9 %collective-permute-start.14 = (bf16[4,2,128,256]{3,2,1,0:T(8,128)(2,1)S(1)}, bf16[4,2,128,256]{3,2,1,0:T(8,128)(2,1)S(1)}, u32[]{:S(2)}, u32[]{:S(2)}) collective-permute-start(bf16[4,2,128,256]{3,2,1,0:T(8,128)(2,1)S(1)} %slice.43), channel_id=1, source_target_pairs={{0,64},{1,193},{64,0},{65,129},{128,192},{129,65},{192,128},{193,1... | collective-permute-start | bytes 1572872 | tf_op jit(solution)/shard_map/ppermute | solution.py:343
  100.8 39.3 %collective-permute-start.15 = (bf16[2,4,2,128,256]{4,3,2,1,0:T(8,128)(2,1)S(1)}, bf16[2,4,2,128,256]{4,3,2,1,0:T(8,128)(2,1)S(1)}, u32[]{:S(2)}, u32[]{:S(2)}) collective-permute-start(bf16[2,4,2,128,256]{4,3,2,1,0:T(8,128)(2,1)S(1)} %pad_maximum_fusion.2.here_ref), channel_id=1, source_target_pairs={{0,192},{1,65},{64,128},{65,1},{128,64},{129,193},{192,0},{193,129... | collective-permute-start | bytes 3145736 | tf_op jit(solution)/shard_map/ppermute | solution.py:343
  104.1 1.4 copy-start.5
  105.5 1.4 copy-start.7
  115.2 14.6 %copy-start.11 = (bf16[32,128]{1,0:T(8,128)(2,1)S(1)}, bf16[32,128]{1,0:T(8,128)(2,1)}, u32[]{:S(2)}) copy-start(bf16[32,128]{1,0:T(8,128)(2,1)} %param.15) | copy-start | bytes 24580
  115.2 14.7 %copy-start.14 = (f32[512]{0:T(512)S(1)}, f32[512]{0:T(512)}, u32[]{:S(2)}) copy-start(f32[512]{0:T(512)} %param.16) | copy-start | bytes 6148
  124.2 1.2 copy-start.2
  126.1 9.7 %collective-permute-start.11 = (bf16[144,256]{1,0:T(8,128)(2,1)}, bf16[144,256]{1,0:T(8,128)(2,1)S(1)}, u32[]{:S(2)}, u32[]{:S(2)}) collective-permute-start(bf16[144,256]{1,0:T(8,128)(2,1)} %get-tuple-element.39), channel_id=1, source_target_pairs={{0,8},{8,16},{16,24},{24,64},{64,72},{72,80},{80,88},{88,128},{128... | collective-permute-start | bytes 221192 | tf_op jit(solution)/shard_map/ppermute | solution.py:415
  130.6 1.4 copy-start.3
  133.5 6.6 %collective-permute-start.16 = (bf16[2,256,256]{2,1,0:T(8,128)(2,1)S(1)}, bf16[2,256,256]{2,1,0:T(8,128)(2,1)S(1)}, u32[]{:S(2)}, u32[]{:S(2)}) collective-permute-start(bf16[2,256,256]{2,1,0:T(8,128)(2,1)S(1)} %mix.3.mine_ref), channel_id=1, source_target_pairs={{0,1},{1,0},{2,3},{3,2},{4,5},{5,4},{6,7},{7,6},{8,9},{9,8},{10,11... | collective-permute-start | bytes 786440 | tf_op jit(solution)/shard_map/ppermute | solution.py:422
  133.6 4.9 %collective-permute-start.12 = (bf16[144,256]{1,0:T(8,128)(2,1)}, bf16[144,256]{1,0:T(8,128)(2,1)S(1)}, u32[]{:S(2)}, u32[]{:S(2)}) collective-permute-start(bf16[144,256]{1,0:T(8,128)(2,1)} %get-tuple-element.40), channel_id=1, source_target_pairs={{0,8},{8,16},{16,24},{24,0},{64,72},{72,80},{80,88},{88,64},{128,1... | collective-permute-start | bytes 221192 | tf_op jit(solution)/shard_map/ppermute | solution.py:416
  139.9 3.8 %collective-permute-start.13 = (bf16[2,256,256]{2,1,0:T(8,128)(2,1)S(1)}, bf16[2,256,256]{2,1,0:T(8,128)(2,1)S(1)}, u32[]{:S(2)}, u32[]{:S(2)}) collective-permute-start(bf16[2,256,256]{2,1,0:T(8,128)(2,1)S(1)} %mix.2.mine_ref), channel_id=1, source_target_pairs={{0,1},{1,0},{2,3},{3,2},{4,5},{5,4},{6,7},{7,6},{8,9},{9,8},{10,11... | collective-permute-start | bytes 786440 | tf_op jit(solution)/shard_map/ppermute | solution.py:422
  147.5 2.0 copy-start.1
  149.4 71.4 %copy-start.8 = (bf16[512,512]{1,0:T(8,128)(2,1)S(1)}, bf16[512,512]{1,0:T(8,128)(2,1)}, u32[]{:S(2)}) copy-start(bf16[512,512]{1,0:T(8,128)(2,1)} %param.10) | copy-start | bytes 1572868
Sparse Core Ops, SparseCore 0:
  10.8 66.9 all-gather.2
  149.6 71.1 reduce-scatter.1

commit v6 on v5

--- a/solution.py
+++ b/solution.py
@@ -48,9 +48,11 @@
         copies = []
         for x in range(4):
             i, j = (y, x) if kind == 0 else (x, y)
-            source = (here_ref, there_ref)[i // 2].at[i % 2, j]
-            place = wide.at[y, :, at_ref[4 + x]]
-            copies.append(pltpu.make_async_copy(source, place, sems.at[y, x]))
+            rows = pl.ds(pl.multiple_of(at_ref[4 + x] * 128, 128), 128)
+            for s in range(3):
+                source = (here_ref, there_ref)[i // 2].at[i % 2, j, s]
+                place = wide.at[y, rows, pl.ds(s * CH, CH)]
+                copies.append(pltpu.make_async_copy(source, place, sems.at[y, x, s]))
         turns.append(copies)
 
     @pl.when(step == 0)
@@ -66,21 +68,24 @@
             for copy in turns[k]:
                 copy.wait()
 
-    for h in range(2):
-        rows = x_ref[h, 0]
-        stat[h] += rows[ROWS + TILE - 16 :].astype(F32)[8:]
-        for s in range(3):
-            weights = wide[step, s].reshape(WIDE, CH)
-            acc[h, s] += jnp.dot(rows, weights, preferred_element_type=F32)
+    products = jnp.dot(
+        x_ref[...].reshape(2 * (ROWS + TILE), WIDE), wide[step], preferred_element_type=F32
+    )
+    sums = x_ref[:, 0, ROWS + TILE - 16 :].astype(F32)[:, 8:]
+
+    @pl.when(step == 0)
+    def _():
+        acc[...] = products
+        stat[...] = sums
+
+    @pl.when(step > 0)
+    def _():
+        acc[...] += products
+        stat[...] += sums
 
 
 def first_kernel(at_ref, x_ref, here_ref, there_ref, acc, stat, wide, sems):
-    @pl.when(pl.program_id(0) == 0)
-    def _():
-        acc[...] = jnp.zeros_like(acc)
-        stat[...] = jnp.zeros_like(stat)
-
-    add_products(0, at_ref, x_ref, here_ref, there_ref, acc, stat, wide, sems)
+    add_products(1, at_ref, x_ref, here_ref, there_ref, acc, stat, wide, sems)
 
 
 def as_column(row):
@@ -91,23 +96,23 @@
 def second_kernel(at_ref, x_ref, here_ref, there_ref, part_ref, sums_ref, taps_ref, *refs):
     proj_ref, tail_ref, mid_ref, front_ref, acc, stat, wide, ahead, sems = refs
 
-    @pl.when(pl.program_id(0) == 0)
-    def _():
-        acc[...] = part_ref[...]
-        stat[...] = sums_ref[...]
-
-    add_products(1, at_ref, x_ref, here_ref, there_ref, acc, stat, wide, sems)
+    add_products(0, at_ref, x_ref, here_ref, there_ref, acc, stat, wide, sems)
 
     @pl.when(pl.program_id(0) == pl.num_programs(0) - 1)
     def _():
         for h in range(2):
-            sums = stat[h]
+            sums = stat[h] + sums_ref[h]
             own = lax.rsqrt((sums[0:1] + sums[1:2]) * (1.0 / 4096.0) + 1e-6)
             extra = lax.rsqrt((sums[2:3] + sums[3:4]) * (1.0 / 4096.0) + 1e-6)
             own, extra = as_column(own), as_column(extra[:, :128])[:TILE]
+            start = h * (ROWS + TILE)
             for s in range(3):
-                proj_ref[s, h] = (acc[h, s, :ROWS] * own).astype(BF16)
-                carried = (acc[h, s, ROWS:] * extra).astype(BF16).astype(F32)
+                lanes = slice(s * CH, (s + 1) * CH)
+                rows = slice(start, start + ROWS)
+                proj_ref[s, h] = ((acc[rows, lanes] + part_ref[rows, lanes]) * own).astype(BF16)
+                rows = slice(start + ROWS, start + ROWS + TILE)
+                carried = (acc[rows, lanes] + part_ref[rows, lanes]) * extra
+                carried = carried.astype(BF16).astype(F32)
                 if h == 0:
                     ahead[s, :SHARE] = carried[:SHARE]
                 else:
@@ -124,10 +129,10 @@
 
 def project(at, gathered, kept, got, taps):
     count = ROWS + TILE
-    acc = (2, 3, count, CH)
+    acc = (2 * count, 3 * CH)
     stat = (2, 8, WIDE)
-    wide = pltpu.VMEM((4, 3, 4, 128, CH), BF16)
-    sems = pltpu.SemaphoreType.DMA((4, 4))
+    wide = pltpu.VMEM((4, WIDE, 3 * CH), BF16)
+    sems = pltpu.SemaphoreType.DMA((4, 4, 3))
 
     def whole(shape):
         return pl.BlockSpec(shape, lambda k, at: (0,) * len(shape))
@@ -152,21 +157,21 @@
         grid_spec=pltpu.PrefetchScalarGridSpec(
             num_scalar_prefetch=1,
             grid=(4,),
-            in_specs=inputs(0),
+            in_specs=inputs(1),
             out_specs=[whole(acc), whole(stat)],
             scratch_shapes=[wide, sems],
         ),
         out_shape=[jax.ShapeDtypeStruct(acc, F32), jax.ShapeDtypeStruct(stat, F32)],
         name="project_first",
         **options,
-    )(at, gathered, *kept)
+    )(at, gathered, *got)
     shapes = [(3, 2, ROWS, CH), (2, HALO, CH), (2, HALO, CH), (HALO, CH)]
     return pl.pallas_call(
         second_kernel,
         grid_spec=pltpu.PrefetchScalarGridSpec(
             num_scalar_prefetch=1,
             grid=(4,),
-            in_specs=[*inputs(1), whole(acc), whole(stat), whole((3, 3, CH))],
+            in_specs=[*inputs(0), whole(acc), whole(stat), whole((3, 3, CH))],
             out_specs=[whole(shape) for shape in shapes],
             scratch_shapes=[
                 pltpu.VMEM(acc, F32),
@@ -179,7 +184,7 @@
         out_shape=[jax.ShapeDtypeStruct(shape, BF16) for shape in shapes],
         name="project_second",
         **options,
-    )(at, gathered, *got, part, sums, taps)
+    )(at, gathered, *kept, part, sums, taps)
 
 
 def toeplitz_kernel(u_ref, out_ref):
@@ -268,20 +273,18 @@
     )(proj, halo, band, taps, bias)
 
 
-def out_kernel(at_ref, mine_ref, other_ref, here_ref, there_ref, *refs):
+def out_kernel(at_ref, mine_ref, other_ref, w_ref, *refs):
     out_ref, wide, rows, sems = refs[-4:]
     step = pl.program_id(0)
     turns = []
-    for i in range(4):
+    for y in range(4):
         copies = []
         for j in range(4):
             lanes = pl.ds(pl.multiple_of(at_ref[4 + j] * 128, 128), 128)
             for part in range(4):
-                source = (here_ref, there_ref)[i // 2].at[
-                    i % 2, j, part // 2, :, pl.ds(part % 2 * 128, 128)
-                ]
-                place = wide.at[i, pl.ds(part * 128, 128), lanes]
-                copies.append(pltpu.make_async_copy(source, place, sems.at[i, j, part]))
+                source = w_ref.at[y, j, part // 2, :, pl.ds(part % 2 * 128, 128)]
+                place = wide.at[y, pl.ds(part * 128, 128), lanes]
+                copies.append(pltpu.make_async_copy(source, place, sems.at[y, j, part]))
         turns.append(copies)
 
     @pl.when(step == 0)
@@ -307,7 +310,7 @@
         out_ref[h, 0] = products[h * HALF : (h + 1) * HALF]
 
 
-def project_out(at, mine, other, parts, half, base=None):
+def project_out(at, mine, other, weights, half, base=None):
     more = () if base is None else (base,)
     return pl.pallas_call(
         out_kernel,
@@ -316,9 +319,9 @@
             grid=(4,),
             in_specs=[
                 *[pl.BlockSpec((2, HALF, CH), lambda k, at: (0, 0, 0))] * 2,
-                *[pl.BlockSpec(memory_space=pl.ANY)] * (2 + len(more)),
+                *[pl.BlockSpec(memory_space=pl.ANY)] * (1 + len(more)),
             ],
-            out_specs=pl.BlockSpec((2, 1, HALF, WIDE), lambda k, at: (0, at[k], half, 0)),
+            out_specs=pl.BlockSpec((2, 1, HALF, WIDE), lambda k, at: (0, k, half, 0)),
             scratch_shapes=[
                 pltpu.VMEM((4, 2 * CH, WIDE), BF16),
                 pltpu.VMEM((2 * HALF, 2 * CH), BF16),
@@ -326,13 +329,13 @@
             ],
         ),
         out_shape=jax.ShapeDtypeStruct((2, 4, ROWS, WIDE), BF16),
-        input_output_aliases={} if base is None else {5: 0},
-        compiler_params=pltpu.CompilerParams(vmem_limit_bytes=46 * MIB),
+        input_output_aliases={} if base is None else {4: 0},
+        compiler_params=pltpu.CompilerParams(vmem_limit_bytes=52 * MIB),
         cost_estimate=pl.CostEstimate(
             flops=2 * 512 * 2 * CH * 2048, bytes_accessed=5_000_000, transcendentals=0
         ),
         name="project_out",
-    )(at, mine, other, *parts, *more)
+    )(at, mine, other, weights, *more)
 
 
 FIRST, SECOND = (1, 3), (3, 1)
@@ -388,20 +391,12 @@
         chosen = lax.dynamic_slice_in_dim(out_weight, (core ^ k) * CH, CH, 0)
         pairs = [(a * 2 + b, (b ^ k) * 2 + a) for a in range(2) for b in range(2)]
         pieces.append(lax.ppermute(chosen, ("zh", "c"), pairs))
-    got, pieces = lax.optimization_barrier((got, pieces))
     pieces = [jnp.concatenate([p[:128], p[128:]], axis=1)[None] for p in pieces]
-    kept = jnp.concatenate([kept, *pieces], axis=0)
-    kept = jnp.stack([kept, pair_step(kept, "x", FIRST)])
-    got = jnp.stack([got, pair_step(got, "y", FIRST)])
-    kept, got = lax.optimization_barrier((kept, got))
-    line = jnp.concatenate([kept, pair_step(kept, "x", SECOND)], axis=0)
-    got = jnp.concatenate([got, pair_step(got, "y", SECOND)], axis=0)
+    line = jnp.concatenate(ring_pairs(jnp.concatenate([kept, *pieces], axis=0), "x"), axis=0)
     kept = ring_pairs(line[:, :3], "y")
-    got = ring_pairs(got, "x")
-    out_line, _ = lax.optimization_barrier((line[:, 3:], kept[1]))
-    out_here = jnp.stack([out_line, pair_step(out_line, "y", FIRST)])
-    out_here, _ = lax.optimization_barrier((out_here, got[1]))
-    out_parts = (out_here, pair_step(out_here, "y", SECOND))
+    got = ring_pairs(jnp.concatenate(ring_pairs(got, "y"), axis=0), "x")
+    out_line, got = lax.optimization_barrier((line[:, 3:], got))
+    w_out = lax.all_gather(out_line, "y")
 
     taps = lax.dynamic_slice_in_dim(short_filter, zh * CH, CH, 2)
     bias = lax.dynamic_slice_in_dim(mr_bias, zh * CH, CH, 0)[None, :]
@@ -416,14 +411,14 @@
     second = lax.ppermute(
         to_second, ("y", "x"), [(i, i // 4 * 4 + (i + 1) % 4) for i in range(16)]
     )
-    halo = jnp.stack([jnp.where(leading, front, first), second])
-
     def swapped(mine):
         return mine, lax.ppermute(mine, "c", [(0, 1), (1, 0)])
 
-    partial = project_out(at, *swapped(mix(proj, mid, band, taps, bias, 2, 2)), out_parts, 1)
+    partial = project_out(at, *swapped(mix(proj, mid, band, taps, bias, 2, 2)), w_out, 1)
+    first, second, partial = lax.optimization_barrier((first, second, partial))
+    halo = jnp.stack([jnp.where(leading, front, first), second])
     partial = project_out(
-        at, *swapped(mix(proj, halo, band, taps, bias, 0, 2)), out_parts, 0, partial
+        at, *swapped(mix(proj, halo, band, taps, bias, 0, 2)), w_out, 0, partial
     )
     summed = lax.psum_scatter(
         partial.reshape(8, ROWS, WIDE), ("zh", "zl"), scatter_dimension=0

time: 231 us -> 238 us (1.030)
  Pallas kernels: 28 us -> 32.2 us
  waiting for transfers between devices: 131 us -> 135 us
    ppermute x10 -> x8, waiting for transfers between devices: 50.6 us -> 69.6 us  [pair_step(): return lax.ppermute(value, (axis, 'c'), pairs)]
    reduce_scatter x1, waiting for transfers between devices: 71.4 us -> 54.5 us  [on_device(): lax.psum_scatter(partial.reshape(8, ROWS, WIDE), ('zh', 'zl'), scatter_di...]
    ppermute x2, starting transfers between devices: 7.09 us -> 13 us  [on_device(): pieces.append(lax.ppermute(chosen, ('zh', 'c'), pairs))]
    ppermute x1, waiting for transfers between devices: 0.01 us -> 5 us  [on_device(): got = lax.ppermute(jnp.where(zh == 0, right, left), 'zh', [(0, 1), (1, 0)])]
    ppermute x10 -> x8, starting transfers between devices: 19.1 us -> 14.9 us  [pair_step(): return lax.ppermute(value, (axis, 'c'), pairs)]
    unnamed x32 -> x28, local copies, waits for them, and re-layouts: 8.63 us -> 5.14 us
    pallas_call x2, Pallas kernels: 7.38 us -> 10.4 us  [project_out(): pl.pallas_call(out_kernel, grid_spec=pltpu.PrefetchScalarGridSpec(num_sca...]
    ppermute x1, waiting for transfers between devices: 2.7 us -> 0.01 us  [on_device(): lax.ppermute(to_second, ('y', 'x'), [(i, i // 4 * 4 + (i + 1) % 4) for i...]
  transfers between devices with their start and end apart: 19 -> 18, of which waited for: 11 -> 10; matrix products, arithmetic and copies ran while one was open for 1% -> 2% of each run, Pallas kernels for 11% -> 11%
where the time goes in v6:
time: 238 us; the launch traced here: 237 us
  waiting for transfers between devices  135 us (57%)
  starting transfers between devices  40.5 us (17%)
  Pallas kernels  32.2 us (14%)
  between operations  13.4 us (6%)
  other arithmetic  9.13 us (4%)
  local copies, waits for them, and re-layouts  6.78 us (3%)
    ppermute x8, waiting for transfers between devices, pair_step(): return lax.ppermute(value, (axis, 'c'), pairs)  69.6 us
    reduce_scatter x1, waiting for transfers between devices, on_device(): lax.psum_scatter(partial.reshape(8, ROWS, WIDE), ('zh', 'zl'), scatter_di...  54.5 us
    ppermute x8, starting transfers between devices, pair_step(): return lax.ppermute(value, (axis, 'c'), pairs)  14.9 us
    ppermute x2, starting transfers between devices, on_device(): pieces.append(lax.ppermute(chosen, ('zh', 'c'), pairs))  13 us
    pallas_call x2, Pallas kernels, project_out(): pl.pallas_call(out_kernel, grid_spec=pltpu.PrefetchScalarGridSpec(num_sca...  10.4 us
    pallas_call x1, Pallas kernels, project(): pl.pallas_call(second_kernel, grid_spec=pltpu.PrefetchScalarGridSpec(num_...  9.51 us
    pallas_call x1, Pallas kernels, project(): pl.pallas_call(first_kernel, grid_spec=pltpu.PrefetchScalarGridSpec(num_s...  8.91 us
    ppermute x1, starting transfers between devices, on_device(): got = lax.ppermute(jnp.where(zh == 0, right, left), 'zh', [(0, 1), (1, 0)])  7.23 us
  transfers between devices with their start and end apart: 18, of which 10 were waited for; matrix products, arithmetic and copies ran while one was open for 2% of the time, Pallas kernels for 11%

profile of v6, /device:TPU:2, one launch (start us, length us, event | category | flops | bytes accessed | tf_op | source)
XLA Modules:
  0.0 236.6 jit_solution(9697766644787424757)
XLA Ops:
  6.5 0.7 convert_element_type.41
  7.3 1.3 fusion.1
  8.5 1.1 fusion.5
  9.7 0.9 fusion.4
  10.7 7.2 %collective-permute-start.6 = (bf16[3,128,256]{2,1,0:T(8,128)(2,1)S(1)}, bf16[3,128,256]{2,1,0:T(8,128)(2,1)S(1)}, u32[]{:S(2)}, u32[]{:S(2)}) collective-permute-start(bf16[3,128,256]{2,1,0:T(8,128)(2,1)S(1)} %get-tuple-element.35), channel_id=1, source_target_pairs={{0,32},{32,0},{1,33},{33,1},{2,34},{34,2},{3,35},{35,3},{4,36},{36... | collective-permute-start | bytes 589832 | tf_op jit(solution)/shard_map/ppermute | solution.py:388
  18.0 5.0 %collective-permute-done.6 = bf16[3,128,256]{2,1,0:T(8,128)(2,1)S(1)} collective-permute-done((bf16[3,128,256]{2,1,0:T(8,128)(2,1)S(1)}, bf16[3,128,256]{2,1,0:T(8,128)(2,1)S(1)}, u32[]{:S(2)}, u32[]{:S(2)}) %collective-permute-start.6) | collective-permute-done | bytes 196640 | tf_op jit(solution)/shard_map/ppermute | solution.py:388
  23.0 1.6 collective-permute-start.7
  24.6 4.1 %collective-permute-done.7 = bf16[3,128,256]{2,1,0:T(8,128)(2,1)S(1)} collective-permute-done((bf16[3,128,256]{2,1,0:T(8,128)(2,1)S(1)}, bf16[3,128,256]{2,1,0:T(8,128)(2,1)S(1)}, u32[]{:S(2)}, u32[]{:S(2)}) %collective-permute-start.7) | collective-permute-done | bytes 196640 | tf_op jit(solution)/shard_map/ppermute | solution.py:346
  28.7 3.1 %collective-permute-start.8 = (bf16[2,3,128,256]{3,2,1,0:T(8,128)(2,1)S(1)}, bf16[2,3,128,256]{3,2,1,0:T(8,128)(2,1)S(1)}, u32[]{:S(2)}, u32[]{:S(2)}) collective-permute-start(bf16[2,3,128,256]{3,2,1,0:T(8,128)(2,1)S(1)} %pad_maximum_fusion.6), channel_id=1, source_target_pairs={{0,192},{1,65},{64,128},{65,1},{128,64},{129,193},{192,0},{193,129... | collective-permute-start | bytes 1179656 | tf_op jit(solution)/shard_map/ppermute | solution.py:346
  31.8 6.0 %collective-permute-done.8 = bf16[2,3,128,256]{3,2,1,0:T(8,128)(2,1)S(1)} collective-permute-done((bf16[2,3,128,256]{3,2,1,0:T(8,128)(2,1)S(1)}, bf16[2,3,128,256]{3,2,1,0:T(8,128)(2,1)S(1)}, u32[]{:S(2)}, u32[]{:S(2)}) %collective-permute-start.8) | collective-permute-done | bytes 393248 | tf_op jit(solution)/shard_map/ppermute | solution.py:346
  37.8 0.1 fusion.11
  37.9 0.6 collective-permute-start.9
  38.5 0.7 collective-permute-start
  39.2 12.3 %collective-permute-start.1 = (bf16[256,128]{1,0:T(8,128)(2,1)S(1)}, bf16[256,128]{1,0:T(8,128)(2,1)S(1)}, u32[]{:S(2)}, u32[]{:S(2)}) collective-permute-start(bf16[256,128]{1,0:T(8,128)(2,1)S(1)} %get-tuple-element.44), channel_id=1, source_target_pairs={{0,32},{1,0},{32,33},{33,1},{2,34},{3,2},{34,35},{35,3},{4,36},{5,... | collective-permute-start | bytes 196616 | tf_op jit(solution)/shard_map/ppermute | solution.py:393
  51.5 3.8 %collective-permute-done.1 = bf16[256,128]{1,0:T(8,128)(2,1)S(1)} collective-permute-done((bf16[256,128]{1,0:T(8,128)(2,1)S(1)}, bf16[256,128]{1,0:T(8,128)(2,1)S(1)}, u32[]{:S(2)}, u32[]{:S(2)}) %collective-permute-start.1) | collective-permute-done | bytes 65568 | tf_op jit(solution)/shard_map/ppermute | solution.py:393
  55.4 1.6 collective-permute-start.2
  57.0 0.1 pad_maximum_fusion.1.here_ref
  57.2 1.6 collective-permute-start.10
  58.8 3.8 %collective-permute-done.2 = bf16[5,128,256]{2,1,0:T(8,128)(2,1)S(1)} collective-permute-done((bf16[5,128,256]{2,1,0:T(8,128)(2,1)S(1)}, bf16[5,128,256]{2,1,0:T(8,128)(2,1)S(1)}, u32[]{:S(2)}, u32[]{:S(2)}) %collective-permute-start.2) | collective-permute-done | bytes 327712 | tf_op jit(solution)/shard_map/ppermute | solution.py:346
  62.6 2.3 collective-permute-start.3
  65.0 23.3 %collective-permute-done.3 = bf16[2,5,128,256]{3,2,1,0:T(8,128)(2,1)S(1)} collective-permute-done((bf16[2,5,128,256]{3,2,1,0:T(8,128)(2,1)S(1)}, bf16[2,5,128,256]{3,2,1,0:T(8,128)(2,1)S(1)}, u32[]{:S(2)}, u32[]{:S(2)}) %collective-permute-start.3) | collective-permute-done | bytes 655392 | tf_op jit(solution)/shard_map/ppermute | solution.py:346
  88.2 0.1 pad_maximum_fusion.2
  88.4 1.4 slice_bitcast_fusion
  89.7 0.6 collective-permute-start.4
  90.4 0.8 pad_maximum_fusion.5
  91.2 1.1 copy-done.5
  92.4 9.6 %collective-permute-done.4 = bf16[4,3,128,256]{3,2,1,0:T(8,128)(2,1)} collective-permute-done((bf16[4,3,128,256]{3,2,1,0:T(8,128)(2,1)}, bf16[4,3,128,256]{3,2,1,0:T(8,128)(2,1)}, u32[]{:S(2)}, u32[]{:S(2)}) %collective-permute-start.4) | collective-permute-done | bytes 786464 | tf_op jit(solution)/shard_map/ppermute | solution.py:346
  102.1 1.6 pad_maximum_fusion.here_ref
  103.6 3.4 %collective-permute-start.5 = (bf16[2,4,3,128,256]{4,3,2,1,0:T(8,128)(2,1)S(1)}, bf16[2,4,3,128,256]{4,3,2,1,0:T(8,128)(2,1)}, u32[]{:S(2)}, u32[]{:S(2)}) collective-permute-start(bf16[2,4,3,128,256]{4,3,2,1,0:T(8,128)(2,1)S(1)} %pad_maximum_fusion.here_ref), channel_id=1, source_target_pairs={{0,192},{1,65},{64,128},{65,1},{128,64},{129,193},{192,0},{193,129... | collective-permute-start | bytes 4718600 | tf_op jit(solution)/shard_map/ppermute | solution.py:346
  107.2 0.5 toeplitz.1.band_ref
  107.7 0.1 dynamic_slice.23
  107.8 0.1 pad_add_fusion.at_ref
  107.9 1.4 copy-done.4
  109.3 1.4 copy-done.6
  110.7 8.9 %project_first.1 = (f32[1184,768]{1,0:T(8,128)S(1)}, f32[2,8,512]{2,1,0:T(8,128)S(1)}) custom-call(s32[10]{0:T(128)S(1)} %pad_add_fusion.at_ref, bf16[2,8,592,512]{3,2,1,0:T(8,128)(2,1)} %bitcast.36, bf16[2,4,3,128,256]{4,3,2,1,0:T(8,128)(2,1)S(1)} %copy-done.4, bf16[2,4,3,128,256]{4,3,2,1,0:T(8,128)(2,1)S(1)} %copy-done.6), custom_call_target="tpu_custom_call" | custom-call | flops 3724541952 | bytes 12000000 | tf_op jit(solution)/shard_map/project_first/pallas_call | solution.py:155
  119.7 22.8 %collective-permute-done.5.there_ref = bf16[2,4,3,128,256]{4,3,2,1,0:T(8,128)(2,1)} collective-permute-done((bf16[2,4,3,128,256]{4,3,2,1,0:T(8,128)(2,1)S(1)}, bf16[2,4,3,128,256]{4,3,2,1,0:T(8,128)(2,1)}, u32[]{:S(2)}, u32[]{:S(2)}) %collective-permute-start.5) | collective-permute-done | bytes 1572896 | tf_op jit(solution)/shard_map/ppermute | solution.py:346
  142.5 9.5 %project_second.1 = (bf16[3,2,512,256]{3,2,1,0:T(8,128)(2,1)S(1)}, bf16[2,144,256]{2,1,0:T(8,128)(2,1)S(1)}, bf16[2,144,256]{2,1,0:T(8,128)(2,1)S(1)}, bf16[144,256]{1,0:T(8,128)(2,1)S(1)}) custom-call(s32[10]{0:T(128)S(1)} %pad_add_fusion.at_ref, bf16[2,8,592,512]{3,2,1,0:T(8,128)(2,1)} %bitcast.37, ...), custom_call_target="tpu_custom_call" | custom-call | flops 3724541952 | bytes 12000000 | tf_op jit(solution)/shard_map/project_second/pallas_call | solution.py:169
  152.0 1.5 mix.2.mine_ref
  153.5 1.2 copy-done.1
  154.7 3.4 %collective-permute-start.11 = (bf16[144,256]{1,0:T(8,128)(2,1)S(1)}, bf16[144,256]{1,0:T(8,128)(2,1)S(1)}, u32[]{:S(2)}, u32[]{:S(2)}) collective-permute-start(bf16[144,256]{1,0:T(8,128)(2,1)S(1)} %get-tuple-element.40), channel_id=1, source_target_pairs={{0,8},{8,16},{16,24},{24,64},{64,72},{72,80},{80,88},{88,128},{128... | collective-permute-start | bytes 221192 | tf_op jit(solution)/shard_map/ppermute | solution.py:410
  158.1 1.9 collective-permute-start.12
  160.0 5.2 %project_out.2.refs_0_ = bf16[2,4,512,512]{3,2,1,0:T(8,128)(2,1)} custom-call(s32[10]{0:T(128)S(1)} %pad_add_fusion.at_ref, bf16[2,256,256]{2,1,0:T(8,128)(2,1)S(1)} %mix.2.mine_ref, bf16[2,256,256]{2,1,0:T(8,128)(2,1)S(1)} %collective-permute-done.13.other_ref, bf16[4,4,2,128,256]{4,3,2,1,0:T(8,128)(2,1)} %bitcast.38), custom_call_target="tpu_custom_call" | custom-call | flops 1073741824 | bytes 5000000 | tf_op jit(solution)/shard_map/project_out/pallas_call | solution.py:315
  165.3 1.5 mix.3.mine_ref
  166.8 0.1 collective-permute-start.14
  166.9 1.5 collective-permute-done.14.other_ref
  168.4 5.2 %project_out.3 = bf16[2,4,512,512]{3,2,1,0:T(8,128)(2,1)} custom-call(s32[10]{0:T(128)S(1)} %pad_add_fusion.at_ref, bf16[2,256,256]{2,1,0:T(8,128)(2,1)S(1)} %mix.3.mine_ref, bf16[2,256,256]{2,1,0:T(8,128)(2,1)S(1)} %collective-permute-done.14.other_ref, bf16[4,4,2,128,256]{4,3,2,1,0:T(8,128)(2,1)} %bitcast.39, ...), custom_call_target="tpu_custom_call", output_to_operand_aliasing={{}: (4, {})} | custom-call | flops 1073741824 | bytes 5000000 | tf_op jit(solution)/shard_map/project_out/pallas_call | solution.py:315
  173.6 54.5 %reduce-scatter.2.cloned.1.call-done = bf16[1,512,512]{2,1,0:T(8,128)(2,1)} async-done(((bf16[8,512,512]{2,1,0:T(8,128)(2,1)}), bf16[1,512,512]{2,1,0:T(8,128)(2,1)}) %reduce-scatter.2.cloned.1.call-update) | async-done | bytes 524304 | tf_op jit(solution)/shard_map/reduce_scatter | solution.py:423
  228.1 2.0 fusion.3
  (59 shorter events, 0.7 us)
Async XLA Ops:
  6.5 101.4 %copy-start = (f32[3,3,512]{2,1,0:T(4,128)S(1)}, f32[3,3,512]{2,1,0:T(4,128)}, u32[]{:S(2)}) copy-start(f32[3,3,512]{2,1,0:T(4,128)} %param.14) | copy-start | bytes 55300
  6.5 101.4 %all-gather.5.cloned.1.call-start = ((), (), s32[]{:S(2)}) async-start(), calls=%async_computation.2 | async-start | bytes 10305536 | tf_op jit(solution)/shard_map/all_gather | solution.py:384
  6.5 4.2 %copy-start.8 = (bf16[3,128,512]{2,1,0:T(8,128)(2,1)S(1)}, bf16[3,128,512]{2,1,0:T(8,128)(2,1)}, u32[]{:S(2)}) copy-start(bf16[3,128,512]{2,1,0:T(8,128)(2,1)} %param.13) | copy-start | bytes 1179652
  10.6 149.3 %all-gather.7.cloned.1.call-start = ((), (), s32[]{:S(2)}) async-start(), calls=%async_computation.3 | async-start | bytes 2621440 | tf_op jit(solution)/shard_map/all_gather | solution.py:399
  10.7 12.2 %collective-permute-start.6 = (bf16[3,128,256]{2,1,0:T(8,128)(2,1)S(1)}, bf16[3,128,256]{2,1,0:T(8,128)(2,1)S(1)}, u32[]{:S(2)}, u32[]{:S(2)}) collective-permute-start(bf16[3,128,256]{2,1,0:T(8,128)(2,1)S(1)} %get-tuple-element.35), channel_id=1, source_target_pairs={{0,32},{32,0},{1,33},{33,1},{2,34},{34,2},{3,35},{35,3},{4,36},{36... | collective-permute-start | bytes 589832 | tf_op jit(solution)/shard_map/ppermute | solution.py:388
  23.0 5.7 %collective-permute-start.7 = (bf16[3,128,256]{2,1,0:T(8,128)(2,1)S(1)}, bf16[3,128,256]{2,1,0:T(8,128)(2,1)S(1)}, u32[]{:S(2)}, u32[]{:S(2)}) collective-permute-start(bf16[3,128,256]{2,1,0:T(8,128)(2,1)S(1)} %collective-permute-done.6), channel_id=1, source_target_pairs={{0,64},{1,193},{64,0},{65,129},{128,192},{129,65},{192,128},{193,1... | collective-permute-start | bytes 589832 | tf_op jit(solution)/shard_map/ppermute | solution.py:346
  28.6 9.9 %copy-start.9 = (bf16[512,128]{1,0:T(8,128)(2,1)S(1)}, bf16[512,128]{1,0:T(8,128)(2,1)}, u32[]{:S(2)}) copy-start(bf16[512,128]{1,0:T(8,128)(2,1)} %param.17) | copy-start | bytes 393220
  28.7 9.1 %collective-permute-start.8 = (bf16[2,3,128,256]{3,2,1,0:T(8,128)(2,1)S(1)}, bf16[2,3,128,256]{3,2,1,0:T(8,128)(2,1)S(1)}, u32[]{:S(2)}, u32[]{:S(2)}) collective-permute-start(bf16[2,3,128,256]{3,2,1,0:T(8,128)(2,1)S(1)} %pad_maximum_fusion.6), channel_id=1, source_target_pairs={{0,192},{1,65},{64,128},{65,1},{128,64},{129,193},{192,0},{193,129... | collective-permute-start | bytes 1179656 | tf_op jit(solution)/shard_map/ppermute | solution.py:346
  37.9 19.1 %collective-permute-start.9 = (bf16[4,3,128,256]{3,2,1,0:T(8,128)(2,1)S(1)}, bf16[4,3,128,256]{3,2,1,0:T(8,128)(2,1)S(1)}, u32[]{:S(2)}, u32[]{:S(2)}) collective-permute-start(bf16[4,3,128,256]{3,2,1,0:T(8,128)(2,1)S(1)} %get-tuple-element.32), channel_id=1, source_target_pairs={{0,8},{1,25},{8,0},{9,17},{16,24},{17,9},{24,16},{25,1},{2,10},{3,... | collective-permute-start | bytes 2359304 | tf_op jit(solution)/shard_map/ppermute | solution.py:346
  38.5 13.0 %collective-permute-start = (bf16[256,128]{1,0:T(8,128)(2,1)S(1)}, bf16[256,128]{1,0:T(8,128)(2,1)S(1)}, u32[]{:S(2)}, u32[]{:S(2)}) collective-permute-start(bf16[256,128]{1,0:T(8,128)(2,1)S(1)} %get-tuple-element.43), channel_id=1, source_target_pairs={{0,0},{1,32},{32,1},{33,33},{2,2},{3,34},{34,3},{35,35},{4,4},{5,3... | collective-permute-start | bytes 196616 | tf_op jit(solution)/shard_map/ppermute | solution.py:393
  39.2 16.1 %collective-permute-start.1 = (bf16[256,128]{1,0:T(8,128)(2,1)S(1)}, bf16[256,128]{1,0:T(8,128)(2,1)S(1)}, u32[]{:S(2)}, u32[]{:S(2)}) collective-permute-start(bf16[256,128]{1,0:T(8,128)(2,1)S(1)} %get-tuple-element.44), channel_id=1, source_target_pairs={{0,32},{1,0},{32,33},{33,1},{2,34},{3,2},{34,35},{35,3},{4,36},{5,... | collective-permute-start | bytes 196616 | tf_op jit(solution)/shard_map/ppermute | solution.py:393
  55.4 7.2 %collective-permute-start.2 = (bf16[5,128,256]{2,1,0:T(8,128)(2,1)S(1)}, bf16[5,128,256]{2,1,0:T(8,128)(2,1)S(1)}, u32[]{:S(2)}, u32[]{:S(2)}) collective-permute-start(bf16[5,128,256]{2,1,0:T(8,128)(2,1)S(1)} %get-tuple-element.38), channel_id=1, source_target_pairs={{0,8},{1,25},{8,0},{9,17},{16,24},{17,9},{24,16},{25,1},{2,10},{3,... | collective-permute-start | bytes 983048 | tf_op jit(solution)/shard_map/ppermute | solution.py:346
  57.2 31.2 %copy-start.3 = (bf16[2,4,3,128,256]{4,3,2,1,0:T(8,128)(2,1)}, bf16[2,4,3,128,256]{4,3,2,1,0:T(8,128)(2,1)S(1)}, u32[]{:S(2)}) copy-start(bf16[2,4,3,128,256]{4,3,2,1,0:T(8,128)(2,1)S(1)} %pad_maximum_fusion.1.here_ref) | copy-start | bytes 4718596
  57.2 34.0 %collective-permute-start.10 = (bf16[2,4,3,128,256]{4,3,2,1,0:T(8,128)(2,1)S(1)}, bf16[2,4,3,128,256]{4,3,2,1,0:T(8,128)(2,1)S(1)}, u32[]{:S(2)}, u32[]{:S(2)}) collective-permute-start(bf16[2,4,3,128,256]{4,3,2,1,0:T(8,128)(2,1)S(1)} %pad_maximum_fusion.1.here_ref), channel_id=1, source_target_pairs={{0,24},{1,9},{8,16},{9,1},{16,8},{17,25},{24,0},{25,17},{2,26},{3,... | collective-permute-start | bytes 4718600 | tf_op jit(solution)/shard_map/ppermute | solution.py:346
  62.6 25.6 %collective-permute-start.3 = (bf16[2,5,128,256]{3,2,1,0:T(8,128)(2,1)S(1)}, bf16[2,5,128,256]{3,2,1,0:T(8,128)(2,1)S(1)}, u32[]{:S(2)}, u32[]{:S(2)}) collective-permute-start(bf16[2,5,128,256]{3,2,1,0:T(8,128)(2,1)S(1)} %pad_maximum_fusion.4), channel_id=1, source_target_pairs={{0,24},{1,9},{8,16},{9,1},{16,8},{17,25},{24,0},{25,17},{2,26},{3,... | collective-permute-start | bytes 1966088 | tf_op jit(solution)/shard_map/ppermute | solution.py:346
  89.7 12.3 %collective-permute-start.4 = (bf16[4,3,128,256]{3,2,1,0:T(8,128)(2,1)}, bf16[4,3,128,256]{3,2,1,0:T(8,128)(2,1)}, u32[]{:S(2)}, u32[]{:S(2)}) collective-permute-start(bf16[4,3,128,256]{3,2,1,0:T(8,128)(2,1)} %get-tuple-element.30), channel_id=1, source_target_pairs={{0,64},{1,193},{64,0},{65,129},{128,192},{129,65},{192,128},{193,1... | collective-permute-start | bytes 2359304 | tf_op jit(solution)/shard_map/ppermute | solution.py:346
  91.2 1.1 copy-start.5
  92.4 135.7 %reduce-scatter.2.cloned.1.call-start = ((), (), s32[]{:S(2)}) async-start(), calls=%async_computation.1 | async-start | bytes 4718592 | tf_op jit(solution)/shard_map/reduce_scatter | solution.py:423
  102.0 5.0 %copy-start.10 = (bf16[32,128]{1,0:T(8,128)(2,1)S(1)}, bf16[32,128]{1,0:T(8,128)(2,1)}, u32[]{:S(2)}) copy-start(bf16[32,128]{1,0:T(8,128)(2,1)} %param.15) | copy-start | bytes 24580
  102.0 5.7 %copy-start.13 = (f32[512]{0:T(512)S(1)}, f32[512]{0:T(512)}, u32[]{:S(2)}) copy-start(f32[512]{0:T(512)} %param.16) | copy-start | bytes 6148
  102.1 5.7 %copy-start.11 = (s32[4]{0:T(128)S(1)}, s32[4]{0:T(128)}, u32[]{:S(2)}) copy-start(s32[4]{0:T(128)} %constant.44.clone) | copy-start | bytes 52
  102.1 5.7 %copy-start.12 = (s32[4]{0:T(128)S(1)}, s32[4]{0:T(128)}, u32[]{:S(2)}) copy-start(s32[4]{0:T(128)} %constant.45.clone) | copy-start | bytes 52
  103.6 38.9 %collective-permute-start.5 = (bf16[2,4,3,128,256]{4,3,2,1,0:T(8,128)(2,1)S(1)}, bf16[2,4,3,128,256]{4,3,2,1,0:T(8,128)(2,1)}, u32[]{:S(2)}, u32[]{:S(2)}) collective-permute-start(bf16[2,4,3,128,256]{4,3,2,1,0:T(8,128)(2,1)S(1)} %pad_maximum_fusion.here_ref), channel_id=1, source_target_pairs={{0,192},{1,65},{64,128},{65,1},{128,64},{129,193},{192,0},{193,129... | collective-permute-start | bytes 4718600 | tf_op jit(solution)/shard_map/ppermute | solution.py:346
  107.9 1.4 copy-start.4
  109.3 1.4 copy-start.6
  153.5 1.2 copy-start.1
  154.6 5.3 %collective-permute-start.13 = (bf16[2,256,256]{2,1,0:T(8,128)(2,1)S(1)}, bf16[2,256,256]{2,1,0:T(8,128)(2,1)S(1)}, u32[]{:S(2)}, u32[]{:S(2)}) collective-permute-start(bf16[2,256,256]{2,1,0:T(8,128)(2,1)S(1)} %mix.2.mine_ref), channel_id=1, source_target_pairs={{0,1},{1,0},{2,3},{3,2},{4,5},{5,4},{6,7},{7,6},{8,9},{9,8},{10,11... | collective-permute-start | bytes 786440 | tf_op jit(solution)/shard_map/ppermute | solution.py:415
  154.7 10.5 %collective-permute-start.11 = (bf16[144,256]{1,0:T(8,128)(2,1)S(1)}, bf16[144,256]{1,0:T(8,128)(2,1)S(1)}, u32[]{:S(2)}, u32[]{:S(2)}) collective-permute-start(bf16[144,256]{1,0:T(8,128)(2,1)S(1)} %get-tuple-element.40), channel_id=1, source_target_pairs={{0,8},{8,16},{16,24},{24,64},{64,72},{72,80},{80,88},{88,128},{128... | collective-permute-start | bytes 221192 | tf_op jit(solution)/shard_map/ppermute | solution.py:410
  158.1 7.1 %collective-permute-start.12 = (bf16[144,256]{1,0:T(8,128)(2,1)S(1)}, bf16[144,256]{1,0:T(8,128)(2,1)S(1)}, u32[]{:S(2)}, u32[]{:S(2)}) collective-permute-start(bf16[144,256]{1,0:T(8,128)(2,1)S(1)} %get-tuple-element.39), channel_id=1, source_target_pairs={{0,8},{8,16},{16,24},{24,0},{64,72},{72,80},{80,88},{88,64},{128,1... | collective-permute-start | bytes 221192 | tf_op jit(solution)/shard_map/ppermute | solution.py:411
  160.0 5.3 %copy-start.2 = (bf16[3,2,512,256]{3,2,1,0:T(8,128)(2,1)S(1)}, bf16[3,2,512,256]{3,2,1,0:T(8,128)(2,1)}, u32[]{:S(2)}) copy-start(bf16[3,2,512,256]{3,2,1,0:T(8,128)(2,1)} %copy-done.1) | copy-start | bytes 4718596
  166.8 1.6 collective-permute-start.14
  173.6 54.5 %copy-start.7 = (bf16[512,512]{1,0:T(8,128)(2,1)S(1)}, bf16[512,512]{1,0:T(8,128)(2,1)}, u32[]{:S(2)}) copy-start(bf16[512,512]{1,0:T(8,128)(2,1)} %param.10) | copy-start | bytes 1572868
Sparse Core Ops, SparseCore 0:
  10.8 67.7 all-gather.4
  92.5 42.5 all-gather.6
  173.7 54.3 reduce-scatter.1

commit v7 on v4

--- a/solution.py
+++ b/solution.py
@@ -32,19 +32,6 @@
     )
 
 
-def weight_copies(at_ref, refs, wide, sems):
-    copies = []
-    for kind in range(2):
-        half = at_ref[8] if kind == 0 else 1 - at_ref[8]
-        for i in range(4):
-            for j in range(4):
-                source = refs[2 * kind + i // 2].at[i % 2, j]
-                y, x = (i, j) if kind == 0 else (j, i)
-                place = wide.at[:, at_ref[y], half, at_ref[4 + x]]
-                copies.append(pltpu.make_async_copy(source, place, sems.at[kind, i, j]))
-    return copies
-
-
 def last_rows(parts, first, shift):
     place = row_iota((16, CH)) // 2
     out = jnp.zeros((16, CH), F32)
@@ -54,43 +41,54 @@
     return out.astype(BF16)
 
 
+def as_column(row):
+    column = jnp.broadcast_to(row, (128, row.shape[1])).T
+    return jnp.concatenate([column] * (CH // 128), axis=1)
+
+
 def project_kernel(at_ref, x_ref, *refs):
-    taps_ref, proj_ref, tail_ref, mid_ref, front_ref, wide, scaled, ahead, sems = refs[4:]
-    copies = weight_copies(at_ref, refs, wide, sems)
-    first_step = pl.program_id(0) == 0
-
-    @pl.when(first_step)
+    taps_ref, proj_ref, tail_ref, mid_ref, front_ref, wide, ahead, sems = refs[4:]
+    z_half = at_ref[8]
+    copies = []
+    for kind in range(2):
+        half = z_half if kind == 0 else 1 - z_half
+        for i in range(4):
+            for j in range(4):
+                y, x = (i, j) if kind == 0 else (j, i)
+                start = (2 * at_ref[y] + half) * WIDE + at_ref[4 + x] * 128
+                rows = pl.ds(pl.multiple_of(start, 128), 128)
+                for s in range(3):
+                    source = refs[2 * kind + i // 2].at[i % 2, j, s]
+                    place = wide.at[rows, pl.ds(s * CH, CH)]
+                    copies.append(pltpu.make_async_copy(source, place, sems.at[kind, i, j, s]))
+
+    @pl.when(pl.program_id(0) == 0)
     def _():
         for copy in copies:
             copy.start()
-
-    ssq = jnp.zeros((ROWS + TILE, 1), F32)
-    for t in range(8):
-        lifted = x_ref[0, t].astype(F32)
-        ssq += jnp.sum(lifted * lifted, axis=-1, keepdims=True)
-        gain = lifted[ROWS + TILE - 1 :]
-        scaled[:, t * WIDE : (t + 1) * WIDE] = (lifted * gain).astype(BF16)
-    inv = lax.rsqrt(ssq * (1.0 / 4096.0) + 1e-6)
-
-    @pl.when(first_step)
-    def _():
         for copy in copies:
             copy.wait()
 
+    features = jnp.concatenate([x_ref[0, t] for t in range(8)], axis=1)
+    products = jnp.dot(features, wide[...], preferred_element_type=F32)
+    sums = jnp.zeros((8, WIDE), F32)
+    for t in range(8):
+        sums += x_ref[0, t, ROWS + TILE - 16 :].astype(F32)[8:]
+    own = lax.rsqrt((sums[0:1] + sums[1:2]) * (1.0 / 4096.0) + 1e-6)
+    extra = lax.rsqrt((sums[2:3] + sums[3:4]) * (1.0 / 4096.0) + 1e-6)
+    own, extra = as_column(own), as_column(extra[:, :128])[:TILE]
     for s in range(3):
-        total = jnp.dot(
-            scaled[...], wide[s].reshape(8 * WIDE, CH), preferred_element_type=F32
-        )
-        rounded = (total * inv).astype(BF16)
-        proj_ref[s, 0] = rounded[:ROWS]
-
-        @pl.when(first_step)
-        def _(s=s, rounded=rounded):
-            ahead[s, :SHARE] = rounded[ROWS:].astype(F32)[:SHARE]
+        lanes = slice(s * CH, (s + 1) * CH)
+        proj_ref[s, 0] = (products[:ROWS, lanes] * own).astype(BF16)
+        carried = (products[ROWS:, lanes] * extra).astype(BF16).astype(F32)
+
+        @pl.when(pl.program_id(0) == 0)
+        def _(s=s, carried=carried):
+            ahead[s, :SHARE] = carried[:SHARE]
 
         @pl.when(pl.program_id(0) == 1)
-        def _(s=s, rounded=rounded):
-            ahead[s, SHARE:] = rounded[ROWS:].astype(F32)
+        def _(s=s, carried=carried):
+            ahead[s, SHARE:] = carried
 
     for end, ref in ((ROWS, tail_ref), (HALF, mid_ref)):
         rows = [proj_ref[s, 0, end - HALO : end].astype(F32) for s in range(3)]
@@ -123,10 +121,9 @@
                 pl.BlockSpec((HALO, CH), lambda h, at: (0, 0)),
             ],
             scratch_shapes=[
-                pltpu.VMEM((3, 4, 2, 4, 128, CH), BF16),
-                pltpu.VMEM((ROWS + TILE, 8 * WIDE), BF16),
+                pltpu.VMEM((8 * WIDE, 3 * CH), BF16),
                 pltpu.VMEM((3, SHARE + TILE, CH), F32),
-                pltpu.SemaphoreType.DMA((2, 4, 4)),
+                pltpu.SemaphoreType.DMA((2, 4, 4, 3)),
             ],
         ),
         out_shape=[
@@ -229,57 +226,66 @@
     )(proj, halo, band, taps, bias)
 
 
-def out_kernel(at_ref, mine_ref, other_ref, here_ref, there_ref, *refs):
-    out_ref, wide, sems = refs[-3:]
-    copies = []
-    for i in range(4):
-        for j in range(4):
-            source = (here_ref, there_ref)[i // 2].at[i % 2, j]
-            lanes = pl.ds(pl.multiple_of(at_ref[4 + j] * 128, 128), 128)
-            place = wide.at[at_ref[i], :, lanes]
-            copies.append(pltpu.make_async_copy(source, place, sems.at[i, j]))
-
-    @pl.when(pl.program_id(0) == 0)
+def out_kernel(at_ref, mine_ref, other_ref, w_ref, *refs):
+    out_ref, wide, rows, sems = refs[-4:]
+    step = pl.program_id(0)
+    turns = []
+    for y in range(4):
+        copies = []
+        for x in range(4):
+            place = wide.at[y, :, pl.ds(x * 128, 128)]
+            copies.append(pltpu.make_async_copy(w_ref.at[y, x], place, sems.at[y, x]))
+        turns.append(copies)
+
+    @pl.when(step == 0)
     def _():
-        for copy in copies:
-            copy.start()
-        for copy in copies:
-            copy.wait()
-
-    swap = at_ref[9] == 1
-    first = jnp.where(swap, other_ref[0], mine_ref[0])
-    second = jnp.where(swap, mine_ref[0], other_ref[0])
-    rows = jnp.concatenate([first, second], axis=1)
-    for y in range(4):
-        out_ref[0, y] = jnp.dot(rows, wide[y], preferred_element_type=F32).astype(BF16)
-
-
-def project_out(at, mine, other, parts, half, base=None):
+        for copies in turns:
+            for copy in copies:
+                copy.start()
+        swap = at_ref[9] == 1
+        for h in range(2):
+            place = slice(h * HALF, (h + 1) * HALF)
+            rows[place, :CH] = jnp.where(swap, other_ref[h], mine_ref[h])
+            rows[place, CH:] = jnp.where(swap, mine_ref[h], other_ref[h])
+
+    for k in range(4):
+
+        @pl.when(step == k)
+        def _(k=k):
+            for copy in turns[k]:
+                copy.wait()
+
+    products = jnp.dot(rows[...], wide[step], preferred_element_type=F32).astype(BF16)
+    for h in range(2):
+        out_ref[h, 0] = products[h * HALF : (h + 1) * HALF]
+
+
+def project_out(at, mine, other, weights, half, base=None):
     more = () if base is None else (base,)
     return pl.pallas_call(
         out_kernel,
         grid_spec=pltpu.PrefetchScalarGridSpec(
             num_scalar_prefetch=1,
-            grid=(2,),
+            grid=(4,),
             in_specs=[
-                pl.BlockSpec((1, HALF, CH), lambda h, at: (h, 0, 0)),
-                pl.BlockSpec((1, HALF, CH), lambda h, at: (h, 0, 0)),
-                *[pl.BlockSpec(memory_space=pl.ANY)] * (2 + len(more)),
+                *[pl.BlockSpec((2, HALF, CH), lambda k, at: (0, 0, 0))] * 2,
+                *[pl.BlockSpec(memory_space=pl.ANY)] * (1 + len(more)),
             ],
-            out_specs=pl.BlockSpec((1, 4, HALF, WIDE), lambda h, at: (h, 0, half, 0)),
+            out_specs=pl.BlockSpec((2, 1, HALF, WIDE), lambda k, at: (0, k, half, 0)),
             scratch_shapes=[
                 pltpu.VMEM((4, 2 * CH, WIDE), BF16),
+                pltpu.VMEM((2 * HALF, 2 * CH), BF16),
                 pltpu.SemaphoreType.DMA((4, 4)),
             ],
         ),
         out_shape=jax.ShapeDtypeStruct((2, 4, ROWS, WIDE), BF16),
-        input_output_aliases={} if base is None else {5: 0},
+        input_output_aliases={} if base is None else {4: 0},
         compiler_params=pltpu.CompilerParams(vmem_limit_bytes=52 * MIB),
         cost_estimate=pl.CostEstimate(
             flops=2 * 512 * 2 * CH * 2048, bytes_accessed=5_000_000, transcendentals=0
         ),
         name="project_out",
-    )(at, mine, other, *parts, *more)
+    )(at, mine, other, weights, *more)
 
 
 FIRST, SECOND = (1, 3), (3, 1)
@@ -293,10 +299,6 @@
 def ring_pairs(piece, axis):
     here = jnp.stack([piece, pair_step(piece, axis, FIRST)])
     return here, pair_step(here, axis, SECOND)
-
-
-def ring_line(piece, axis):
-    return jnp.concatenate(ring_pairs(piece, axis), axis=0)
 
 
 def on_device(
@@ -312,15 +314,30 @@
         [lax.axis_index("y") ^ turns, column ^ turns, jnp.stack([zh, zh ^ core])]
     ).astype(jnp.int32)
     ring = ("zh", "zl", "c")
-    padded = jnp.pad(prior_rows, ((0, SHARE + TILE - 1 - prior_rows.shape[0]), (0, 0)))
-    some = lax.dynamic_slice_in_dim(padded, zh * SHARE, TILE - 1, 0)
-    own = jnp.concatenate([tokens, some, norm_gain[None, :]], axis=0)
+    padded = jnp.pad(prior_rows, ((0, 2 * SHARE - prior_rows.shape[0]), (0, 0)))
+    some = lax.dynamic_slice_in_dim(padded, zh * SHARE, SHARE, 0)
+    lifted, carried = tokens.astype(F32), some.astype(F32)
+    gain = norm_gain.astype(F32)
+    sums = jnp.sum(lifted * lifted, axis=1)
+    more = jnp.pad(jnp.sum(carried * carried, axis=1), (0, WIDE - SHARE))
+    sums = jnp.stack([sums, more])
+    coarse = lax.reduce_precision(sums, 8, 7)
+    terms = jnp.stack([coarse, sums - coarse], axis=1).reshape(4, WIDE).astype(BF16)
+    own = jnp.concatenate(
+        [
+            (lifted * gain).astype(BF16),
+            (carried * gain).astype(BF16),
+            jnp.pad(terms, ((0, TILE - SHARE - 4), (0, 0))),
+        ],
+        axis=0,
+    )
     gathered = lax.all_gather(own, ring).reshape(2, 8, ROWS + TILE, WIDE)
 
     left, right = in_weight[..., :CH], in_weight[..., CH:]
     kept = jnp.where(zh == 0, left, right)
     got = lax.ppermute(jnp.where(zh == 0, right, left), "zh", [(0, 1), (1, 0)])
-    kept_line, got_line = ring_line(kept, "x"), ring_line(got, "y")
+    kept_line = jnp.concatenate(ring_pairs(kept, "x"), axis=0)
+    got_line = jnp.concatenate(ring_pairs(got, "y"), axis=0)
 
     out_weight, _, _ = lax.optimization_barrier((out_weight, kept_line, got_line))
     pieces = []
@@ -328,27 +345,20 @@
         chosen = lax.dynamic_slice_in_dim(out_weight, (core ^ k) * CH, CH, 0)
         pairs = [(a * 2 + b, (b ^ k) * 2 + a) for a in range(2) for b in range(2)]
         pieces.append(lax.ppermute(chosen, ("zh", "c"), pairs))
-    kept_here = jnp.stack([kept_line, pair_step(kept_line, "y", FIRST)])
-    got_here = jnp.stack([got_line, pair_step(got_line, "x", FIRST)])
-    out_piece = jnp.concatenate(pieces, axis=0)
-    out_piece, _, _ = lax.optimization_barrier((out_piece, kept_here, got_here))
-    out_line = ring_line(out_piece, "x")
-    weights = (
-        kept_here,
-        pair_step(kept_here, "y", SECOND),
-        got_here,
-        pair_step(got_here, "x", SECOND),
-    )
-    out_line, weights, gathered = lax.optimization_barrier((out_line, weights, gathered))
-    out_here = jnp.stack([out_line, pair_step(out_line, "y", FIRST)])
+    kept = jnp.stack([kept_line, pair_step(kept_line, "y", FIRST)])
+    got = jnp.stack([got_line, pair_step(got_line, "x", FIRST)])
+    kept, got, pieces = lax.optimization_barrier((kept, got, pieces))
+    weights = (kept, pair_step(kept, "y", SECOND), got, pair_step(got, "x", SECOND))
+    weights, gathered, pieces = lax.optimization_barrier((weights, gathered, pieces))
+    w_out = lax.all_gather(jnp.concatenate(pieces, axis=0), "x")
 
     taps = lax.dynamic_slice_in_dim(short_filter, zh * CH, CH, 2)
     bias = lax.dynamic_slice_in_dim(mr_bias, zh * CH, CH, 0)[None, :]
     band = toeplitz(lax.dynamic_slice_in_dim(mr_filter, zh * GROUPS, GROUPS, 0))
 
     proj, tail, mid, front = project(at, gathered, weights, taps)
-    out_here, tail = lax.optimization_barrier((out_here, tail))
-    out_parts = (out_here, pair_step(out_here, "y", SECOND))
+    w_out, tail = lax.optimization_barrier((w_out, tail))
+    w_out = lax.all_gather(w_out, "y")
 
     last = column == 3
     to_first = jnp.where(last, tail[1], tail[0])
@@ -357,14 +367,14 @@
     second = lax.ppermute(
         to_second, ("y", "x"), [(i, i // 4 * 4 + (i + 1) % 4) for i in range(16)]
     )
-    halo = jnp.stack([jnp.where(leading, front, first), second])
-
     def swapped(mine):
         return mine, lax.ppermute(mine, "c", [(0, 1), (1, 0)])
 
-    partial = project_out(at, *swapped(mix(proj, mid, band, taps, bias, 2, 2)), out_parts, 1)
+    partial = project_out(at, *swapped(mix(proj, mid, band, taps, bias, 2, 2)), w_out, 1)
+    first, second, partial = lax.optimization_barrier((first, second, partial))
+    halo = jnp.stack([jnp.where(leading, front, first), second])
     partial = project_out(
-        at, *swapped(mix(proj, halo, band, taps, bias, 0, 2)), out_parts, 0, partial
+        at, *swapped(mix(proj, halo, band, taps, bias, 0, 2)), w_out, 0, partial
     )
     summed = lax.psum_scatter(
         partial.reshape(8, ROWS, WIDE), ("zh", "zl"), scatter_dimension=0

time: 211 us -> 230 us (1.090)
  waiting for transfers between devices: 101 us -> 121 us
  blocking collectives: 0 us -> 13.3 us
  starting transfers between devices: 45.1 us -> 38 us
  Pallas kernels: 34.8 us -> 27.8 us
    all_gather x0 -> x1, waiting for transfers between devices: none -> 27.3 us  [on_device(): w_out = lax.all_gather(w_out, 'y')]
    all_gather x0 -> x1, blocking collectives: none -> 13.3 us  [on_device(): w_out = lax.all_gather(jnp.concatenate(pieces, axis=0), 'x')]
    pallas_call x1, Pallas kernels: 22 us -> 14.8 us  [project(): pl.pallas_call(project_kernel, grid_spec=pltpu.PrefetchScalarGridSpec(num...]
    ppermute x2, starting transfers between devices: 18.6 us -> 14.3 us  [on_device(): pieces.append(lax.ppermute(chosen, ('zh', 'c'), pairs))]
    convert_element_type x0 -> x3, other arithmetic: none -> 3.11 us  [the longest x1 1.27 us: on_device(): (lifted * gain).astype(BF16)]
    ppermute x12 -> x8, waiting for transfers between devices: 34.2 us -> 31.2 us  [pair_step(): return lax.ppermute(value, (axis, 'c'), pairs)]
    concatenate x3 -> x2, other arithmetic: 3.7 us -> 0.88 us  [the longest x1 0.87 us: on_device(): jnp.concatenate([(lifted * gain).astype(BF16), (carried * gain).astype(BF...]
    ppermute x1, waiting for transfers between devices: 2.63 us -> 0.01 us  [on_device(): lax.ppermute(to_second, ('y', 'x'), [(i, i // 4 * 4 + (i + 1) % 4) for i...]
  transfers between devices with their start and end apart: 21 -> 18, of which waited for: 11 -> 10; matrix products, arithmetic and copies ran while one was open for 2% -> 2% of each run, Pallas kernels for 14% -> 3%
where the time goes in v7:
time: 230 us; the launch traced here: 229 us
  waiting for transfers between devices  121 us (53%)
  starting transfers between devices  38 us (17%)
  Pallas kernels  27.8 us (12%)
  between operations  13.4 us (6%)
  blocking collectives  13.3 us (6%)
  other arithmetic  9.79 us (4%)
  local copies, waits for them, and re-layouts  5.49 us (2%)
    reduce_scatter x1, waiting for transfers between devices, on_device(): lax.psum_scatter(partial.reshape(8, ROWS, WIDE), ('zh', 'zl'), scatter_di...  55.5 us
    ppermute x8, waiting for transfers between devices, pair_step(): return lax.ppermute(value, (axis, 'c'), pairs)  31.2 us
    all_gather x1, waiting for transfers between devices, on_device(): w_out = lax.all_gather(w_out, 'y')  27.3 us
    pallas_call x1, Pallas kernels, project(): pl.pallas_call(project_kernel, grid_spec=pltpu.PrefetchScalarGridSpec(num...  14.8 us
    ppermute x2, starting transfers between devices, on_device(): pieces.append(lax.ppermute(chosen, ('zh', 'c'), pairs))  14.3 us
    all_gather x1, blocking collectives, on_device(): w_out = lax.all_gather(jnp.concatenate(pieces, axis=0), 'x')  13.3 us
    ppermute x8, starting transfers between devices, pair_step(): return lax.ppermute(value, (axis, 'c'), pairs)  11.3 us
    pallas_call x2, Pallas kernels, project_out(): pl.pallas_call(out_kernel, grid_spec=pltpu.PrefetchScalarGridSpec(num_sca...  9.53 us
  transfers between devices with their start and end apart: 18, of which 10 were waited for; matrix products, arithmetic and copies ran while one was open for 2% of the time, Pallas kernels for 3%

profile of v7, /device:TPU:2, one launch (start us, length us, event | category | flops | bytes accessed | tf_op | source)
XLA Modules:
  0.0 228.7 jit_solution(16284487428527848785)
XLA Ops:
  6.5 0.7 convert_element_type.41
  7.3 1.3 fusion.1
  8.5 1.1 fusion.5
  9.7 0.9 fusion.4
  10.7 7.2 %collective-permute-start.3 = (bf16[3,128,256]{2,1,0:T(8,128)(2,1)S(1)}, bf16[3,128,256]{2,1,0:T(8,128)(2,1)S(1)}, u32[]{:S(2)}, u32[]{:S(2)}) collective-permute-start(bf16[3,128,256]{2,1,0:T(8,128)(2,1)S(1)} %get-tuple-element.53), channel_id=1, source_target_pairs={{0,32},{32,0},{1,33},{33,1},{2,34},{34,2},{3,35},{35,3},{4,36},{36... | collective-permute-start | bytes 589832 | tf_op jit(solution)/shard_map/ppermute | solution.py:338
  18.0 0.6 collective-permute-start
  18.5 4.4 %collective-permute-done.3 = bf16[3,128,256]{2,1,0:T(8,128)(2,1)S(1)} collective-permute-done((bf16[3,128,256]{2,1,0:T(8,128)(2,1)S(1)}, bf16[3,128,256]{2,1,0:T(8,128)(2,1)S(1)}, u32[]{:S(2)}, u32[]{:S(2)}) %collective-permute-start.3) | collective-permute-done | bytes 196640 | tf_op jit(solution)/shard_map/ppermute | solution.py:338
  23.0 1.6 collective-permute-start.4
  24.6 1.6 collective-permute-start.1
  26.2 2.5 %collective-permute-done.4 = bf16[3,128,256]{2,1,0:T(8,128)(2,1)S(1)} collective-permute-done((bf16[3,128,256]{2,1,0:T(8,128)(2,1)S(1)}, bf16[3,128,256]{2,1,0:T(8,128)(2,1)S(1)}, u32[]{:S(2)}, u32[]{:S(2)}) %collective-permute-start.4) | collective-permute-done | bytes 196640 | tf_op jit(solution)/shard_map/ppermute | solution.py:296
  28.7 3.1 %collective-permute-start.5 = (bf16[2,3,128,256]{3,2,1,0:T(8,128)(2,1)S(1)}, bf16[2,3,128,256]{3,2,1,0:T(8,128)(2,1)S(1)}, u32[]{:S(2)}, u32[]{:S(2)}) collective-permute-start(bf16[2,3,128,256]{3,2,1,0:T(8,128)(2,1)S(1)} %pad_maximum_fusion.5), channel_id=1, source_target_pairs={{0,192},{1,65},{64,128},{65,1},{128,64},{129,193},{192,0},{193,129... | collective-permute-start | bytes 1179656 | tf_op jit(solution)/shard_map/ppermute | solution.py:296
  31.8 0.7 collective-permute-done.1
  32.5 0.1 fusion.11
  32.6 0.7 collective-permute-start.2
  33.3 8.0 %collective-permute-done.5 = bf16[2,3,128,256]{3,2,1,0:T(8,128)(2,1)S(1)} collective-permute-done((bf16[2,3,128,256]{3,2,1,0:T(8,128)(2,1)S(1)}, bf16[2,3,128,256]{3,2,1,0:T(8,128)(2,1)S(1)}, u32[]{:S(2)}, u32[]{:S(2)}) %collective-permute-start.5) | collective-permute-done | bytes 393248 | tf_op jit(solution)/shard_map/ppermute | solution.py:296
  41.3 1.4 fusion.10
  42.7 0.7 collective-permute-start.7
  43.3 13.6 %collective-permute-start.8 = (bf16[256,128]{1,0:T(8,128)(2,1)S(1)}, bf16[256,128]{1,0:T(8,128)(2,1)S(1)}, u32[]{:S(2)}, u32[]{:S(2)}) collective-permute-start(bf16[256,128]{1,0:T(8,128)(2,1)S(1)} %get-tuple-element.59), channel_id=1, source_target_pairs={{0,32},{1,0},{32,33},{33,1},{2,34},{3,2},{34,35},{35,3},{4,36},{5,... | collective-permute-start | bytes 196616 | tf_op jit(solution)/shard_map/ppermute | solution.py:347
  56.9 0.1 pad_maximum_fusion.refs_0_
  57.1 1.2 copy-done.5
  58.3 1.3 pad_maximum_fusion.1.refs_2_
  59.7 1.0 collective-permute-done.8
  60.6 2.2 collective-permute-start.10
  62.8 1.1 copy-done.3
  64.0 1.6 collective-permute-start.9
  65.6 0.1 pad_add_fusion.at_ref
  65.6 15.7 %collective-permute-done.10.refs_3_ = bf16[2,4,3,128,256]{4,3,2,1,0:T(8,128)(2,1)} collective-permute-done((bf16[2,4,3,128,256]{4,3,2,1,0:T(8,128)(2,1)S(1)}, bf16[2,4,3,128,256]{4,3,2,1,0:T(8,128)(2,1)}, u32[]{:S(2)}, u32[]{:S(2)}) %collective-permute-start.10) | collective-permute-done | bytes 1572896 | tf_op jit(solution)/shard_map/ppermute | solution.py:296
  81.3 4.4 %collective-permute-done.9.refs_1_ = bf16[2,4,3,128,256]{4,3,2,1,0:T(8,128)(2,1)} collective-permute-done((bf16[2,4,3,128,256]{4,3,2,1,0:T(8,128)(2,1)S(1)}, bf16[2,4,3,128,256]{4,3,2,1,0:T(8,128)(2,1)}, u32[]{:S(2)}, u32[]{:S(2)}) %collective-permute-start.9) | collective-permute-done | bytes 1572896 | tf_op jit(solution)/shard_map/ppermute | solution.py:296
  85.7 13.3 %all-gather.1 = bf16[2048,128]{1,0:T(8,128)(2,1)} all-gather(bf16[512,128]{1,0:T(8,128)(2,1)S(1)} %pad_maximum_fusion.7), channel_id=3, replica_groups=mesh['y'=4,'zh'=2,'x'=4,'zl'=4,'c'=2] {'x'}, dimensions={0}, use_global_device_ids=true | all-gather | bytes 655360 | tf_op jit(solution)/shard_map/all_gather | solution.py:353
  99.1 1.4 copy-done.2
  100.5 1.4 copy-done.4
  101.9 14.8 %project.1 = (bf16[3,2,512,256]{3,2,1,0:T(8,128)(2,1)S(1)}, bf16[2,144,256]{2,1,0:T(8,128)(2,1)S(1)}, bf16[2,144,256]{2,1,0:T(8,128)(2,1)S(1)}, bf16[144,256]{1,0:T(8,128)(2,1)S(1)}) custom-call(s32[10]{0:T(128)S(1)} %pad_add_fusion.at_ref, bf16[2,8,592,512]{3,2,1,0:T(8,128)(2,1)} %bitcast.47, bf16[2,4,3,128,256]{4,3,2,1,0:T(8,128)(2,1)S(1)} %copy-done.2, ...), custom_call_target="tpu_custom_call" | custom-call | flops 6442450944 | bytes 18000000 | tf_op jit(solution)/shard_map/project/pallas_call | solution.py:107
  116.8 0.2 reduce-scatter.2.cloned.1.call-start
  117.0 0.1 dynamic_slice.23
  117.3 0.5 toeplitz.1.band_ref
  117.7 1.5 mix.2.mine_ref
  119.2 0.2 collective-permute-start.13
  119.4 0.6 select_bitcast_fusion.1
  120.1 3.3 %collective-permute-start.11 = (bf16[144,256]{1,0:T(8,128)(2,1)}, bf16[144,256]{1,0:T(8,128)(2,1)S(1)}, u32[]{:S(2)}, u32[]{:S(2)}) collective-permute-start(bf16[144,256]{1,0:T(8,128)(2,1)} %get-tuple-element.56), channel_id=1, source_target_pairs={{0,8},{8,16},{16,24},{24,64},{64,72},{72,80},{80,88},{88,128},{128... | collective-permute-start | bytes 221192 | tf_op jit(solution)/shard_map/ppermute | solution.py:366
  123.4 1.3 collective-permute-start.12
  124.7 27.3 %all-gather.8.cloned.1.call-done = bf16[16,512,128]{2,1,0:T(8,128)(2,1)} async-done(((bf16[4,512,128]{2,1,0:T(8,128)(2,1)}), bf16[16,512,128]{2,1,0:T(8,128)(2,1)}) %all-gather.8.cloned.1.call-update) | async-done | bytes 2097168 | tf_op jit(solution)/shard_map/all_gather | solution.py:361
  152.0 4.8 %project_out.2.refs_0_ = bf16[2,4,512,512]{3,2,1,0:T(8,128)(2,1)} custom-call(s32[10]{0:T(128)S(1)} %pad_add_fusion.at_ref, bf16[2,256,256]{2,1,0:T(8,128)(2,1)S(1)} %mix.2.mine_ref, bf16[2,256,256]{2,1,0:T(8,128)(2,1)S(1)} %collective-permute-done.13.other_ref, bf16[4,4,512,128]{3,2,1,0:T(8,128)(2,1)} %bitcast.32), custom_call_target="tpu_custom_call" | custom-call | flops 1073741824 | bytes 5000000 | tf_op jit(solution)/shard_map/project_out/pallas_call | solution.py:265
  156.8 1.5 mix.3.mine_ref
  158.3 0.1 collective-permute-start.14
  158.4 1.5 collective-permute-done.14.other_ref
  159.9 4.8 %project_out.3 = bf16[2,4,512,512]{3,2,1,0:T(8,128)(2,1)} custom-call(s32[10]{0:T(128)S(1)} %pad_add_fusion.at_ref, bf16[2,256,256]{2,1,0:T(8,128)(2,1)S(1)} %mix.3.mine_ref, bf16[2,256,256]{2,1,0:T(8,128)(2,1)S(1)} %collective-permute-done.14.other_ref, bf16[4,4,512,128]{3,2,1,0:T(8,128)(2,1)} %bitcast.33, ...), custom_call_target="tpu_custom_call", output_to_operand_aliasing={{}: (4, {})} | custom-call | flops 1073741824 | bytes 5000000 | tf_op jit(solution)/shard_map/project_out/pallas_call | solution.py:265
  164.7 55.5 %reduce-scatter.2.cloned.1.call-done = bf16[1,512,512]{2,1,0:T(8,128)(2,1)} async-done(((bf16[8,512,512]{2,1,0:T(8,128)(2,1)}), bf16[1,512,512]{2,1,0:T(8,128)(2,1)}) %reduce-scatter.2.cloned.1.call-update) | async-done | bytes 524304 | tf_op jit(solution)/shard_map/reduce_scatter | solution.py:379
  220.2 2.0 fusion.3
  (52 shorter events, 0.5 us)
Async XLA Ops:
  6.5 59.1 %copy-start = (f32[3,3,512]{2,1,0:T(4,128)S(1)}, f32[3,3,512]{2,1,0:T(4,128)}, u32[]{:S(2)}) copy-start(f32[3,3,512]{2,1,0:T(4,128)} %param.14) | copy-start | bytes 55300
  6.5 79.2 %all-gather.6.cloned.1.call-start = ((), (), s32[]{:S(2)}) async-start(), calls=%async_computation.2 | async-start | bytes 10305536 | tf_op jit(solution)/shard_map/all_gather | solution.py:334
  6.5 4.1 %copy-start.7 = (bf16[3,128,512]{2,1,0:T(8,128)(2,1)S(1)}, bf16[3,128,512]{2,1,0:T(8,128)(2,1)}, u32[]{:S(2)}) copy-start(bf16[3,128,512]{2,1,0:T(8,128)(2,1)} %param.13) | copy-start | bytes 1179652
  10.6 141.4 %all-gather.8.cloned.1.call-start = ((), (), s32[]{:S(2)}) async-start(), calls=%async_computation.3 | async-start | bytes 2621440 | tf_op jit(solution)/shard_map/all_gather | solution.py:361
  10.7 12.2 %collective-permute-start.3 = (bf16[3,128,256]{2,1,0:T(8,128)(2,1)S(1)}, bf16[3,128,256]{2,1,0:T(8,128)(2,1)S(1)}, u32[]{:S(2)}, u32[]{:S(2)}) collective-permute-start(bf16[3,128,256]{2,1,0:T(8,128)(2,1)S(1)} %get-tuple-element.53), channel_id=1, source_target_pairs={{0,32},{32,0},{1,33},{33,1},{2,34},{34,2},{3,35},{35,3},{4,36},{36... | collective-permute-start | bytes 589832 | tf_op jit(solution)/shard_map/ppermute | solution.py:338
  18.0 6.6 %collective-permute-start = (bf16[3,128,256]{2,1,0:T(8,128)(2,1)S(1)}, bf16[3,128,256]{2,1,0:T(8,128)(2,1)S(1)}, u32[]{:S(2)}, u32[]{:S(2)}) collective-permute-start(bf16[3,128,256]{2,1,0:T(8,128)(2,1)S(1)} %get-tuple-element.54), channel_id=1, source_target_pairs={{0,8},{1,25},{8,0},{9,17},{16,24},{17,9},{24,16},{25,1},{2,10},{3,... | collective-permute-start | bytes 589832 | tf_op jit(solution)/shard_map/ppermute | solution.py:296
  23.0 5.7 %collective-permute-start.4 = (bf16[3,128,256]{2,1,0:T(8,128)(2,1)S(1)}, bf16[3,128,256]{2,1,0:T(8,128)(2,1)S(1)}, u32[]{:S(2)}, u32[]{:S(2)}) collective-permute-start(bf16[3,128,256]{2,1,0:T(8,128)(2,1)S(1)} %collective-permute-done.3), channel_id=1, source_target_pairs={{0,64},{1,193},{64,0},{65,129},{128,192},{129,65},{192,128},{193,1... | collective-permute-start | bytes 589832 | tf_op jit(solution)/shard_map/ppermute | solution.py:296
  24.6 7.9 %collective-permute-start.1 = (bf16[2,3,128,256]{3,2,1,0:T(8,128)(2,1)S(1)}, bf16[2,3,128,256]{3,2,1,0:T(8,128)(2,1)S(1)}, u32[]{:S(2)}, u32[]{:S(2)}) collective-permute-start(bf16[2,3,128,256]{3,2,1,0:T(8,128)(2,1)S(1)} %pad_maximum_fusion.4), channel_id=1, source_target_pairs={{0,24},{1,9},{8,16},{9,1},{16,8},{17,25},{24,0},{25,17},{2,26},{3,... | collective-permute-start | bytes 1179656 | tf_op jit(solution)/shard_map/ppermute | solution.py:296
  28.7 12.6 %collective-permute-start.5 = (bf16[2,3,128,256]{3,2,1,0:T(8,128)(2,1)S(1)}, bf16[2,3,128,256]{3,2,1,0:T(8,128)(2,1)S(1)}, u32[]{:S(2)}, u32[]{:S(2)}) collective-permute-start(bf16[2,3,128,256]{3,2,1,0:T(8,128)(2,1)S(1)} %pad_maximum_fusion.5), channel_id=1, source_target_pairs={{0,192},{1,65},{64,128},{65,1},{128,64},{129,193},{192,0},{193,129... | collective-permute-start | bytes 1179656 | tf_op jit(solution)/shard_map/ppermute | solution.py:296
  32.6 10.1 %copy-start.8 = (bf16[512,128]{1,0:T(8,128)(2,1)S(1)}, bf16[512,128]{1,0:T(8,128)(2,1)}, u32[]{:S(2)}) copy-start(bf16[512,128]{1,0:T(8,128)(2,1)} %param.17) | copy-start | bytes 393220
  32.6 24.4 %collective-permute-start.2 = (bf16[4,3,128,256]{3,2,1,0:T(8,128)(2,1)S(1)}, bf16[4,3,128,256]{3,2,1,0:T(8,128)(2,1)S(1)}, u32[]{:S(2)}, u32[]{:S(2)}) collective-permute-start(bf16[4,3,128,256]{3,2,1,0:T(8,128)(2,1)S(1)} %get-tuple-element.50), channel_id=1, source_target_pairs={{0,64},{1,193},{64,0},{65,129},{128,192},{129,65},{192,128},{193,1... | collective-permute-start | bytes 2359304 | tf_op jit(solution)/shard_map/ppermute | solution.py:296
  42.6 14.4 %collective-permute-start.6 = (bf16[4,3,128,256]{3,2,1,0:T(8,128)(2,1)}, bf16[4,3,128,256]{3,2,1,0:T(8,128)(2,1)}, u32[]{:S(2)}, u32[]{:S(2)}) collective-permute-start(bf16[4,3,128,256]{3,2,1,0:T(8,128)(2,1)} %get-tuple-element.48), channel_id=1, source_target_pairs={{0,8},{1,25},{8,0},{9,17},{16,24},{17,9},{24,16},{25,1},{2,10},{3,... | collective-permute-start | bytes 2359304 | tf_op jit(solution)/shard_map/ppermute | solution.py:296
  42.7 17.0 %collective-permute-start.7 = (bf16[256,128]{1,0:T(8,128)(2,1)S(1)}, bf16[256,128]{1,0:T(8,128)(2,1)S(1)}, u32[]{:S(2)}, u32[]{:S(2)}) collective-permute-start(bf16[256,128]{1,0:T(8,128)(2,1)S(1)} %get-tuple-element.60), channel_id=1, source_target_pairs={{0,0},{1,32},{32,1},{33,33},{2,2},{3,34},{34,3},{35,35},{4,4},{5,3... | collective-permute-start | bytes 196616 | tf_op jit(solution)/shard_map/ppermute | solution.py:347
  43.3 17.3 %collective-permute-start.8 = (bf16[256,128]{1,0:T(8,128)(2,1)S(1)}, bf16[256,128]{1,0:T(8,128)(2,1)S(1)}, u32[]{:S(2)}, u32[]{:S(2)}) collective-permute-start(bf16[256,128]{1,0:T(8,128)(2,1)S(1)} %get-tuple-element.59), channel_id=1, source_target_pairs={{0,32},{1,0},{32,33},{33,1},{2,34},{3,2},{34,35},{35,3},{4,36},{5,... | collective-permute-start | bytes 196616 | tf_op jit(solution)/shard_map/ppermute | solution.py:347
  56.9 1.4 copy-start.5
  57.1 5.7 %copy-start.1 = (bf16[2,4,3,128,256]{4,3,2,1,0:T(8,128)(2,1)}, bf16[2,4,3,128,256]{4,3,2,1,0:T(8,128)(2,1)S(1)}, u32[]{:S(2)}) copy-start(bf16[2,4,3,128,256]{4,3,2,1,0:T(8,128)(2,1)S(1)} %pad_maximum_fusion.refs_0_) | copy-start | bytes 4718596
  58.3 7.2 %copy-start.10 = (s32[4]{0:T(128)S(1)}, s32[4]{0:T(128)}, u32[]{:S(2)}) copy-start(s32[4]{0:T(128)} %constant.44.clone) | copy-start | bytes 52
  58.3 7.2 %copy-start.11 = (s32[4]{0:T(128)S(1)}, s32[4]{0:T(128)}, u32[]{:S(2)}) copy-start(s32[4]{0:T(128)} %constant.45.clone) | copy-start | bytes 52
  60.6 20.7 %collective-permute-start.10 = (bf16[2,4,3,128,256]{4,3,2,1,0:T(8,128)(2,1)S(1)}, bf16[2,4,3,128,256]{4,3,2,1,0:T(8,128)(2,1)}, u32[]{:S(2)}, u32[]{:S(2)}) collective-permute-start(bf16[2,4,3,128,256]{4,3,2,1,0:T(8,128)(2,1)S(1)} %pad_maximum_fusion.1.refs_2_), channel_id=1, source_target_pairs={{0,24},{1,9},{8,16},{9,1},{16,8},{17,25},{24,0},{25,17},{2,26},{3,... | collective-permute-start | bytes 4718600 | tf_op jit(solution)/shard_map/ppermute | solution.py:296
  62.8 1.1 copy-start.3
  64.0 21.7 %collective-permute-start.9 = (bf16[2,4,3,128,256]{4,3,2,1,0:T(8,128)(2,1)S(1)}, bf16[2,4,3,128,256]{4,3,2,1,0:T(8,128)(2,1)}, u32[]{:S(2)}, u32[]{:S(2)}) collective-permute-start(bf16[2,4,3,128,256]{4,3,2,1,0:T(8,128)(2,1)S(1)} %pad_maximum_fusion.refs_0_), channel_id=1, source_target_pairs={{0,192},{1,65},{64,128},{65,1},{128,64},{129,193},{192,0},{193,129... | collective-permute-start | bytes 4718600 | tf_op jit(solution)/shard_map/ppermute | solution.py:296
  99.1 1.4 copy-start.2
  100.5 1.4 copy-start.4
  101.9 15.1 %copy-start.12 = (f32[512]{0:T(512)S(1)}, f32[512]{0:T(512)}, u32[]{:S(2)}) copy-start(f32[512]{0:T(512)} %param.16) | copy-start | bytes 6148
  101.9 15.2 %copy-start.9 = (bf16[32,128]{1,0:T(8,128)(2,1)S(1)}, bf16[32,128]{1,0:T(8,128)(2,1)}, u32[]{:S(2)}) copy-start(bf16[32,128]{1,0:T(8,128)(2,1)} %param.15) | copy-start | bytes 24580
  116.8 103.5 %reduce-scatter.2.cloned.1.call-start = ((), (), s32[]{:S(2)}) async-start(), calls=%async_computation.1 | async-start | bytes 4718592 | tf_op jit(solution)/shard_map/reduce_scatter | solution.py:379
  119.2 5.5 %collective-permute-start.13 = (bf16[2,256,256]{2,1,0:T(8,128)(2,1)S(1)}, bf16[2,256,256]{2,1,0:T(8,128)(2,1)S(1)}, u32[]{:S(2)}, u32[]{:S(2)}) collective-permute-start(bf16[2,256,256]{2,1,0:T(8,128)(2,1)S(1)} %mix.2.mine_ref), channel_id=1, source_target_pairs={{0,1},{1,0},{2,3},{3,2},{4,5},{5,4},{6,7},{7,6},{8,9},{9,8},{10,11... | collective-permute-start | bytes 786440 | tf_op jit(solution)/shard_map/ppermute | solution.py:371
  120.1 36.7 %collective-permute-start.11 = (bf16[144,256]{1,0:T(8,128)(2,1)}, bf16[144,256]{1,0:T(8,128)(2,1)S(1)}, u32[]{:S(2)}, u32[]{:S(2)}) collective-permute-start(bf16[144,256]{1,0:T(8,128)(2,1)} %get-tuple-element.56), channel_id=1, source_target_pairs={{0,8},{8,16},{16,24},{24,64},{64,72},{72,80},{80,88},{88,128},{128... | collective-permute-start | bytes 221192 | tf_op jit(solution)/shard_map/ppermute | solution.py:366
  123.4 33.4 %collective-permute-start.12 = (bf16[144,256]{1,0:T(8,128)(2,1)S(1)}, bf16[144,256]{1,0:T(8,128)(2,1)S(1)}, u32[]{:S(2)}, u32[]{:S(2)}) collective-permute-start(bf16[144,256]{1,0:T(8,128)(2,1)S(1)} %get-tuple-element.55), channel_id=1, source_target_pairs={{0,8},{8,16},{16,24},{24,0},{64,72},{72,80},{80,88},{88,64},{128,1... | collective-permute-start | bytes 221192 | tf_op jit(solution)/shard_map/ppermute | solution.py:367
  158.3 1.6 collective-permute-start.14
  164.7 55.5 %copy-start.6 = (bf16[512,512]{1,0:T(8,128)(2,1)S(1)}, bf16[512,512]{1,0:T(8,128)(2,1)}, u32[]{:S(2)}) copy-start(bf16[512,512]{1,0:T(8,128)(2,1)} %param.10) | copy-start | bytes 1572868
Sparse Core Ops, SparseCore 0:
  10.7 67.7 all-gather.5
  116.9 35.0 all-gather.7
  164.9 55.3 reduce-scatter.1

commit v8 on v7

--- a/solution.py
+++ b/solution.py
@@ -47,56 +47,73 @@
 
 
 def project_kernel(at_ref, x_ref, *refs):
-    taps_ref, proj_ref, tail_ref, mid_ref, front_ref, wide, ahead, sems = refs[4:]
-    z_half = at_ref[8]
-    copies = []
-    for kind in range(2):
-        half = z_half if kind == 0 else 1 - z_half
+    taps_ref, proj_ref, tail_ref, mid_ref, front_ref, wide, acc, stat, ahead, sems = refs[4:]
+    first_row, kind = pl.program_id(0) == 0, pl.program_id(1)
+    turns = []
+    for k in range(2):
+        copies = []
         for i in range(4):
             for j in range(4):
-                y, x = (i, j) if kind == 0 else (j, i)
-                start = (2 * at_ref[y] + half) * WIDE + at_ref[4 + x] * 128
+                y, x = (i, j) if k == 0 else (j, i)
+                start = at_ref[y] * WIDE + at_ref[4 + x] * 128
                 rows = pl.ds(pl.multiple_of(start, 128), 128)
                 for s in range(3):
-                    source = refs[2 * kind + i // 2].at[i % 2, j, s]
-                    place = wide.at[rows, pl.ds(s * CH, CH)]
-                    copies.append(pltpu.make_async_copy(source, place, sems.at[kind, i, j, s]))
-
-    @pl.when(pl.program_id(0) == 0)
-    def _():
-        for copy in copies:
-            copy.start()
-        for copy in copies:
-            copy.wait()
-
-    features = jnp.concatenate([x_ref[0, t] for t in range(8)], axis=1)
-    products = jnp.dot(features, wide[...], preferred_element_type=F32)
+                    source = refs[2 * k + i // 2].at[i % 2, j, s]
+                    place = wide.at[k, rows, pl.ds(s * CH, CH)]
+                    copies.append(pltpu.make_async_copy(source, place, sems.at[k, i, j, s]))
+        turns.append(copies)
+
+    @pl.when(first_row & (kind == 0))
+    def _():
+        for copies in turns:
+            for copy in copies:
+                copy.start()
+
+    for k in range(2):
+
+        @pl.when(first_row & (kind == k))
+        def _(k=k):
+            for copy in turns[k]:
+                copy.wait()
+
+    features = jnp.concatenate([x_ref[0, y, 0] for y in range(4)], axis=1)
+    products = jnp.dot(features, wide[kind], preferred_element_type=F32)
     sums = jnp.zeros((8, WIDE), F32)
-    for t in range(8):
-        sums += x_ref[0, t, ROWS + TILE - 16 :].astype(F32)[8:]
-    own = lax.rsqrt((sums[0:1] + sums[1:2]) * (1.0 / 4096.0) + 1e-6)
-    extra = lax.rsqrt((sums[2:3] + sums[3:4]) * (1.0 / 4096.0) + 1e-6)
-    own, extra = as_column(own), as_column(extra[:, :128])[:TILE]
-    for s in range(3):
-        lanes = slice(s * CH, (s + 1) * CH)
-        proj_ref[s, 0] = (products[:ROWS, lanes] * own).astype(BF16)
-        carried = (products[ROWS:, lanes] * extra).astype(BF16).astype(F32)
-
-        @pl.when(pl.program_id(0) == 0)
-        def _(s=s, carried=carried):
-            ahead[s, :SHARE] = carried[:SHARE]
-
-        @pl.when(pl.program_id(0) == 1)
-        def _(s=s, carried=carried):
-            ahead[s, SHARE:] = carried
-
-    for end, ref in ((ROWS, tail_ref), (HALF, mid_ref)):
-        rows = [proj_ref[s, 0, end - HALO : end].astype(F32) for s in range(3)]
-        mixing = three_taps(rows[1], taps_ref, 1) * three_taps(rows[2], taps_ref, 2)
-        ref[0, :LH] = mixing[HALO - LH :].astype(BF16)
-        ref[0, LH:] = last_rows(rows, HALO - 16, 2)
-
-    @pl.when(pl.program_id(0) == 1)
+    for y in range(4):
+        sums += x_ref[0, y, 0, ROWS + TILE - 16 :].astype(F32)[8:]
+
+    @pl.when(kind == 0)
+    def _():
+        acc[...] = products
+        stat[...] = sums
+
+    @pl.when(kind == 1)
+    def _():
+        total = stat[...] + sums
+        own = lax.rsqrt((total[0:1] + total[1:2]) * (1.0 / 4096.0) + 1e-6)
+        extra = lax.rsqrt((total[2:3] + total[3:4]) * (1.0 / 4096.0) + 1e-6)
+        own, extra = as_column(own), as_column(extra[:, :128])[:TILE]
+        for s in range(3):
+            lanes = slice(s * CH, (s + 1) * CH)
+            whole = acc[:, lanes] + products[:, lanes]
+            proj_ref[s, 0] = (whole[:ROWS] * own).astype(BF16)
+            carried = (whole[ROWS:] * extra).astype(BF16).astype(F32)
+
+            @pl.when(first_row)
+            def _(s=s, carried=carried):
+                ahead[s, :SHARE] = carried[:SHARE]
+
+            @pl.when(jnp.logical_not(first_row))
+            def _(s=s, carried=carried):
+                ahead[s, SHARE:] = carried
+
+        for end, ref in ((ROWS, tail_ref), (HALF, mid_ref)):
+            rows = [proj_ref[s, 0, end - HALO : end].astype(F32) for s in range(3)]
+            mixing = three_taps(rows[1], taps_ref, 1) * three_taps(rows[2], taps_ref, 2)
+            ref[0, :LH] = mixing[HALO - LH :].astype(BF16)
+            ref[0, LH:] = last_rows(rows, HALO - 16, 2)
+
+    @pl.when((pl.program_id(0) == 1) & (kind == 1))
     def _():
         mixing = three_taps(ahead[1], taps_ref, 1) * three_taps(ahead[2], taps_ref, 2)
         front_ref[:LH] = pltpu.roll(mixing, SHARE + TILE - 1, 0)[:LH].astype(BF16)
@@ -108,20 +125,25 @@
         project_kernel,
         grid_spec=pltpu.PrefetchScalarGridSpec(
             num_scalar_prefetch=1,
-            grid=(2,),
+            grid=(2, 2),
             in_specs=[
-                pl.BlockSpec((1, 8, ROWS + TILE, WIDE), lambda h, at: (h, 0, 0, 0)),
+                pl.BlockSpec(
+                    (1, 4, 1, ROWS + TILE, WIDE),
+                    lambda h, k, at: (h, 0, at[8] + k - 2 * at[8] * k, 0, 0),
+                ),
                 *[pl.BlockSpec(memory_space=pl.ANY)] * 4,
-                pl.BlockSpec((3, 3, CH), lambda h, at: (0, 0, 0)),
+                pl.BlockSpec((3, 3, CH), lambda h, k, at: (0, 0, 0)),
             ],
             out_specs=[
-                pl.BlockSpec((3, 1, ROWS, CH), lambda h, at: (0, h, 0, 0)),
-                pl.BlockSpec((1, HALO, CH), lambda h, at: (h, 0, 0)),
-                pl.BlockSpec((1, HALO, CH), lambda h, at: (h, 0, 0)),
-                pl.BlockSpec((HALO, CH), lambda h, at: (0, 0)),
+                pl.BlockSpec((3, 1, ROWS, CH), lambda h, k, at: (0, h, 0, 0)),
+                pl.BlockSpec((1, HALO, CH), lambda h, k, at: (h, 0, 0)),
+                pl.BlockSpec((1, HALO, CH), lambda h, k, at: (h, 0, 0)),
+                pl.BlockSpec((HALO, CH), lambda h, k, at: (0, 0)),
             ],
             scratch_shapes=[
-                pltpu.VMEM((8 * WIDE, 3 * CH), BF16),
+                pltpu.VMEM((2, 4 * WIDE, 3 * CH), BF16),
+                pltpu.VMEM((ROWS + TILE, 3 * CH), F32),
+                pltpu.VMEM((8, WIDE), F32),
                 pltpu.VMEM((3, SHARE + TILE, CH), F32),
                 pltpu.SemaphoreType.DMA((2, 4, 4, 3)),
             ],
@@ -226,34 +248,33 @@
     )(proj, halo, band, taps, bias)
 
 
-def out_kernel(at_ref, mine_ref, other_ref, w_ref, *refs):
+def out_kernel(at_ref, mine_ref, other_ref, *refs):
     out_ref, wide, rows, sems = refs[-4:]
     step = pl.program_id(0)
-    turns = []
-    for y in range(4):
+
+    @pl.when(step == 0)
+    def _():
         copies = []
-        for x in range(4):
-            place = wide.at[y, :, pl.ds(x * 128, 128)]
-            copies.append(pltpu.make_async_copy(w_ref.at[y, x], place, sems.at[y, x]))
-        turns.append(copies)
-
-    @pl.when(step == 0)
-    def _():
-        for copies in turns:
-            for copy in copies:
-                copy.start()
+        for k in range(2):
+            for i in range(4):
+                for j in range(4):
+                    y, x = (i, j) if k == 0 else (j, i)
+                    lanes = pl.ds(pl.multiple_of(at_ref[4 + x] * 128, 128), 128)
+                    for part in range(2):
+                        source = refs[2 * k + i // 2].at[i % 2, j, 3, :, pl.ds(part * 128, 128)]
+                        place = wide.at[at_ref[y], pl.ds(k * CH + part * 128, 128), lanes]
+                        sem = sems.at[k, i, j, part]
+                        copies.append(pltpu.make_async_copy(source, place, sem))
+        for copy in copies:
+            copy.start()
         swap = at_ref[9] == 1
         for h in range(2):
             place = slice(h * HALF, (h + 1) * HALF)
             rows[place, :CH] = jnp.where(swap, other_ref[h], mine_ref[h])
             rows[place, CH:] = jnp.where(swap, mine_ref[h], other_ref[h])
 
-    for k in range(4):
-
-        @pl.when(step == k)
-        def _(k=k):
-            for copy in turns[k]:
-                copy.wait()
+        for copy in copies:
+            copy.wait()
 
     products = jnp.dot(rows[...], wide[step], preferred_element_type=F32).astype(BF16)
     for h in range(2):
@@ -269,23 +290,23 @@
             grid=(4,),
             in_specs=[
                 *[pl.BlockSpec((2, HALF, CH), lambda k, at: (0, 0, 0))] * 2,
-                *[pl.BlockSpec(memory_space=pl.ANY)] * (1 + len(more)),
+                *[pl.BlockSpec(memory_space=pl.ANY)] * (4 + len(more)),
             ],
             out_specs=pl.BlockSpec((2, 1, HALF, WIDE), lambda k, at: (0, k, half, 0)),
             scratch_shapes=[
                 pltpu.VMEM((4, 2 * CH, WIDE), BF16),
                 pltpu.VMEM((2 * HALF, 2 * CH), BF16),
-                pltpu.SemaphoreType.DMA((4, 4)),
+                pltpu.SemaphoreType.DMA((2, 4, 4, 2)),
             ],
         ),
         out_shape=jax.ShapeDtypeStruct((2, 4, ROWS, WIDE), BF16),
-        input_output_aliases={} if base is None else {4: 0},
-        compiler_params=pltpu.CompilerParams(vmem_limit_bytes=52 * MIB),
+        input_output_aliases={} if base is None else {7: 0},
+        compiler_params=pltpu.CompilerParams(vmem_limit_bytes=45 * MIB),
         cost_estimate=pl.CostEstimate(
             flops=2 * 512 * 2 * CH * 2048, bytes_accessed=5_000_000, transcendentals=0
         ),
         name="project_out",
-    )(at, mine, other, weights, *more)
+    )(at, mine, other, *weights, *more)
 
 
 FIRST, SECOND = (1, 3), (3, 1)
@@ -331,34 +352,30 @@
         ],
         axis=0,
     )
-    gathered = lax.all_gather(own, ring).reshape(2, 8, ROWS + TILE, WIDE)
+    gathered = lax.all_gather(own, ring).reshape(2, 4, 2, ROWS + TILE, WIDE)
 
     left, right = in_weight[..., :CH], in_weight[..., CH:]
     kept = jnp.where(zh == 0, left, right)
     got = lax.ppermute(jnp.where(zh == 0, right, left), "zh", [(0, 1), (1, 0)])
-    kept_line = jnp.concatenate(ring_pairs(kept, "x"), axis=0)
-    got_line = jnp.concatenate(ring_pairs(got, "y"), axis=0)
-
-    out_weight, _, _ = lax.optimization_barrier((out_weight, kept_line, got_line))
     pieces = []
     for k in range(2):
         chosen = lax.dynamic_slice_in_dim(out_weight, (core ^ k) * CH, CH, 0)
         pairs = [(a * 2 + b, (b ^ k) * 2 + a) for a in range(2) for b in range(2)]
-        pieces.append(lax.ppermute(chosen, ("zh", "c"), pairs))
-    kept = jnp.stack([kept_line, pair_step(kept_line, "y", FIRST)])
-    got = jnp.stack([got_line, pair_step(got_line, "x", FIRST)])
-    kept, got, pieces = lax.optimization_barrier((kept, got, pieces))
-    weights = (kept, pair_step(kept, "y", SECOND), got, pair_step(got, "x", SECOND))
-    weights, gathered, pieces = lax.optimization_barrier((weights, gathered, pieces))
-    w_out = lax.all_gather(jnp.concatenate(pieces, axis=0), "x")
+        chosen = lax.ppermute(chosen, ("zh", "c"), pairs)
+        pieces.append(jnp.concatenate([chosen[:128], chosen[128:]], axis=1)[None])
+    kept = jnp.concatenate([kept, pieces[0]], axis=0)
+    got = jnp.concatenate([got, pieces[1]], axis=0)
+    weights = (
+        *ring_pairs(jnp.concatenate(ring_pairs(kept, "x"), axis=0), "y"),
+        *ring_pairs(jnp.concatenate(ring_pairs(got, "y"), axis=0), "x"),
+    )
+    weights, gathered = lax.optimization_barrier((weights, gathered))
 
     taps = lax.dynamic_slice_in_dim(short_filter, zh * CH, CH, 2)
     bias = lax.dynamic_slice_in_dim(mr_bias, zh * CH, CH, 0)[None, :]
     band = toeplitz(lax.dynamic_slice_in_dim(mr_filter, zh * GROUPS, GROUPS, 0))
 
     proj, tail, mid, front = project(at, gathered, weights, taps)
-    w_out, tail = lax.optimization_barrier((w_out, tail))
-    w_out = lax.all_gather(w_out, "y")
 
     last = column == 3
     to_first = jnp.where(last, tail[1], tail[0])
@@ -370,11 +387,11 @@
     def swapped(mine):
         return mine, lax.ppermute(mine, "c", [(0, 1), (1, 0)])
 
-    partial = project_out(at, *swapped(mix(proj, mid, band, taps, bias, 2, 2)), w_out, 1)
+    partial = project_out(at, *swapped(mix(proj, mid, band, taps, bias, 2, 2)), weights, 1)
     first, second, partial = lax.optimization_barrier((first, second, partial))
     halo = jnp.stack([jnp.where(leading, front, first), second])
     partial = project_out(
-        at, *swapped(mix(proj, halo, band, taps, bias, 0, 2)), w_out, 0, partial
+        at, *swapped(mix(proj, halo, band, taps, bias, 0, 2)), weights, 0, partial
     )
     summed = lax.psum_scatter(
         partial.reshape(8, ROWS, WIDE), ("zh", "zl"), scatter_dimension=0

time: 230 us -> 206 us (0.90)
  blocking collectives: 13.3 us -> 0 us
  starting transfers between devices: 38 us -> 28.1 us
  local copies, waits for them, and re-layouts: 5.49 us -> 1.47 us
    all_gather x2 -> x1, waiting for transfers between devices: 27.3 us -> 0.01 us  [on_device(): gathered = lax.all_gather(own, ring).reshape(2, 4, 2, ROWS + TILE, WIDE)]
    ppermute x8, waiting for transfers between devices: 31.2 us -> 47.1 us  [pair_step(): return lax.ppermute(value, (axis, 'c'), pairs)]
    all_gather x1 -> x0, blocking collectives: 13.3 us -> none  [on_device(): w_out = lax.all_gather(jnp.concatenate(pieces, axis=0), 'x')]
    reduce_scatter x1, waiting for transfers between devices: 55.5 us -> 63.2 us  [on_device(): lax.psum_scatter(partial.reshape(8, ROWS, WIDE), ('zh', 'zl'), scatter_di...]
    ppermute x2, starting transfers between devices: 14.3 us -> 7.88 us  [on_device(): chosen = lax.ppermute(chosen, ('zh', 'c'), pairs)]
    ppermute x1, waiting for transfers between devices: 4.45 us -> 10.4 us  [on_device(): got = lax.ppermute(jnp.where(zh == 0, right, left), 'zh', [(0, 1), (1, 0)])]
    ppermute x1, starting transfers between devices: 7.23 us -> 1.37 us  [on_device(): got = lax.ppermute(jnp.where(zh == 0, right, left), 'zh', [(0, 1), (1, 0)])]
    unnamed x26 -> x22, local copies, waits for them, and re-layouts: 5.23 us -> 1.2 us
  transfers between devices with their start and end apart: 18 -> 17, of which waited for: 10 -> 10; matrix products, arithmetic and copies ran while one was open for 2% -> 2% of each run, Pallas kernels for 3% -> 3%
where the time goes in v8:
time: 206 us; the launch traced here: 205 us
  waiting for transfers between devices  122 us (59%)
  Pallas kernels  30 us (15%)
  starting transfers between devices  28.1 us (14%)
  between operations  13.7 us (7%)
  other arithmetic  9.31 us (5%)
    reduce_scatter x1, waiting for transfers between devices, on_device(): lax.psum_scatter(partial.reshape(8, ROWS, WIDE), ('zh', 'zl'), scatter_di...  63.2 us
    ppermute x8, waiting for transfers between devices, pair_step(): return lax.ppermute(value, (axis, 'c'), pairs)  47.1 us
    pallas_call x1, Pallas kernels, project(): pl.pallas_call(project_kernel, grid_spec=pltpu.PrefetchScalarGridSpec(num...  14.6 us
    ppermute x8, starting transfers between devices, pair_step(): return lax.ppermute(value, (axis, 'c'), pairs)  12.9 us
    pallas_call x2, Pallas kernels, project_out(): pl.pallas_call(out_kernel, grid_spec=pltpu.PrefetchScalarGridSpec(num_sca...  12 us
    ppermute x1, waiting for transfers between devices, on_device(): got = lax.ppermute(jnp.where(zh == 0, right, left), 'zh', [(0, 1), (1, 0)])  10.4 us
    ppermute x2, starting transfers between devices, on_device(): chosen = lax.ppermute(chosen, ('zh', 'c'), pairs)  7.88 us
  transfers between devices with their start and end apart: 17, of which 10 were waited for; matrix products, arithmetic and copies ran while one was open for 2% of the time, Pallas kernels for 3%

profile of v8, /device:TPU:2, one launch (start us, length us, event | category | flops | bytes accessed | tf_op | source)
XLA Modules:
  0.0 204.8 jit_solution(17820343480518058241)
XLA Ops:
  6.6 0.7 convert_element_type.41
  7.3 1.3 fusion.1
  8.6 1.1 fusion.5
  9.7 0.9 fusion.4
  10.6 0.0 reduce-scatter.2.cloned.1.call-start
  10.7 7.2 %collective-permute-start.6 = (bf16[256,128]{1,0:T(8,128)(2,1)S(1)}, bf16[256,128]{1,0:T(8,128)(2,1)S(1)}, u32[]{:S(2)}, u32[]{:S(2)}) collective-permute-start(bf16[256,128]{1,0:T(8,128)(2,1)S(1)} %get-tuple-element.45), channel_id=1, source_target_pairs={{0,32},{1,0},{32,33},{33,1},{2,34},{3,2},{34,35},{35,3},{4,36},{5,... | collective-permute-start | bytes 196616 | tf_op jit(solution)/shard_map/ppermute | solution.py:364
  18.0 0.7 collective-permute-start
  18.7 1.4 collective-permute-start.5
  20.1 1.2 collective-permute-start.1
  21.4 10.4 %collective-permute-done.5 = bf16[3,128,256]{2,1,0:T(8,128)(2,1)S(1)} collective-permute-done((bf16[3,128,256]{2,1,0:T(8,128)(2,1)S(1)}, bf16[3,128,256]{2,1,0:T(8,128)(2,1)S(1)}, u32[]{:S(2)}, u32[]{:S(2)}) %collective-permute-start.5) | collective-permute-done | bytes 196640 | tf_op jit(solution)/shard_map/ppermute | solution.py:359
  31.8 1.6 collective-permute-start.7
  33.4 0.1 pad_maximum_fusion.4
  33.5 1.6 collective-permute-start.2
  35.0 3.2 %collective-permute-done.7 = bf16[4,128,256]{2,1,0:T(8,128)(2,1)S(1)} collective-permute-done((bf16[4,128,256]{2,1,0:T(8,128)(2,1)S(1)}, bf16[4,128,256]{2,1,0:T(8,128)(2,1)S(1)}, u32[]{:S(2)}, u32[]{:S(2)}) %collective-permute-start.7) | collective-permute-done | bytes 262176 | tf_op jit(solution)/shard_map/ppermute | solution.py:317
  38.2 0.1 pad_maximum_fusion.5
  38.3 2.8 %collective-permute-start.8 = (bf16[2,4,128,256]{3,2,1,0:T(8,128)(2,1)S(1)}, bf16[2,4,128,256]{3,2,1,0:T(8,128)(2,1)S(1)}, u32[]{:S(2)}, u32[]{:S(2)}) collective-permute-start(bf16[2,4,128,256]{3,2,1,0:T(8,128)(2,1)S(1)} %pad_maximum_fusion.5), channel_id=1, source_target_pairs={{0,192},{1,65},{64,128},{65,1},{128,64},{129,193},{192,0},{193,129... | collective-permute-start | bytes 1572872 | tf_op jit(solution)/shard_map/ppermute | solution.py:317
  41.1 1.6 collective-permute-done.2
  42.7 0.1 fusion.13
  42.9 0.6 collective-permute-start.3
  43.5 7.1 %collective-permute-done.8 = bf16[2,4,128,256]{3,2,1,0:T(8,128)(2,1)S(1)} collective-permute-done((bf16[2,4,128,256]{3,2,1,0:T(8,128)(2,1)S(1)}, bf16[2,4,128,256]{3,2,1,0:T(8,128)(2,1)S(1)}, u32[]{:S(2)}, u32[]{:S(2)}) %collective-permute-start.8) | collective-permute-done | bytes 524320 | tf_op jit(solution)/shard_map/ppermute | solution.py:317
  50.6 0.1 fusion.12
  50.7 0.9 collective-permute-start.9
  51.6 7.9 %collective-permute-done.3 = bf16[4,4,128,256]{3,2,1,0:T(8,128)(2,1)S(1)} collective-permute-done((bf16[4,4,128,256]{3,2,1,0:T(8,128)(2,1)S(1)}, bf16[4,4,128,256]{3,2,1,0:T(8,128)(2,1)S(1)}, u32[]{:S(2)}, u32[]{:S(2)}) %collective-permute-start.3) | collective-permute-done | bytes 1048608 | tf_op jit(solution)/shard_map/ppermute | solution.py:317
  59.5 0.2 pad_maximum_fusion.refs_0_
  59.7 2.7 %collective-permute-start.4 = (bf16[2,4,4,128,256]{4,3,2,1,0:T(8,128)(2,1)S(1)}, bf16[2,4,4,128,256]{4,3,2,1,0:T(8,128)(2,1)}, u32[]{:S(2)}, u32[]{:S(2)}) collective-permute-start(bf16[2,4,4,128,256]{4,3,2,1,0:T(8,128)(2,1)S(1)} %pad_maximum_fusion.refs_0_), channel_id=1, source_target_pairs={{0,192},{1,65},{64,128},{65,1},{128,64},{129,193},{192,0},{193,129... | collective-permute-start | bytes 6291464 | tf_op jit(solution)/shard_map/ppermute | solution.py:317
  62.4 3.2 %collective-permute-done.9 = bf16[4,4,128,256]{3,2,1,0:T(8,128)(2,1)S(1)} collective-permute-done((bf16[4,4,128,256]{3,2,1,0:T(8,128)(2,1)S(1)}, bf16[4,4,128,256]{3,2,1,0:T(8,128)(2,1)S(1)}, u32[]{:S(2)}, u32[]{:S(2)}) %collective-permute-start.9) | collective-permute-done | bytes 1048608 | tf_op jit(solution)/shard_map/ppermute | solution.py:317
  65.6 1.6 pad_maximum_fusion.1.refs_2_
  67.2 1.5 collective-permute-start.10
  68.7 0.1 rev.4
  68.7 0.1 pad.19.u_ref
  68.8 0.5 toeplitz.1.band_ref
  69.3 0.1 dynamic_slice.23
  69.4 0.1 pad_add_fusion.at_ref
  69.5 17.7 %collective-permute-done.4.refs_1_ = bf16[2,4,4,128,256]{4,3,2,1,0:T(8,128)(2,1)} collective-permute-done((bf16[2,4,4,128,256]{4,3,2,1,0:T(8,128)(2,1)S(1)}, bf16[2,4,4,128,256]{4,3,2,1,0:T(8,128)(2,1)}, u32[]{:S(2)}, u32[]{:S(2)}) %collective-permute-start.4) | collective-permute-done | bytes 2097184 | tf_op jit(solution)/shard_map/ppermute | solution.py:317
  87.1 6.4 %collective-permute-done.10.refs_3_ = bf16[2,4,4,128,256]{4,3,2,1,0:T(8,128)(2,1)} collective-permute-done((bf16[2,4,4,128,256]{4,3,2,1,0:T(8,128)(2,1)}, bf16[2,4,4,128,256]{4,3,2,1,0:T(8,128)(2,1)}, u32[]{:S(2)}, u32[]{:S(2)}) %collective-permute-start.10) | collective-permute-done | bytes 2097184 | tf_op jit(solution)/shard_map/ppermute | solution.py:317
  93.5 14.6 %project.1 = (bf16[3,2,512,256]{3,2,1,0:T(8,128)(2,1)S(1)}, bf16[2,144,256]{2,1,0:T(8,128)(2,1)S(1)}, bf16[2,144,256]{2,1,0:T(8,128)(2,1)S(1)}, bf16[144,256]{1,0:T(8,128)(2,1)S(1)}) custom-call(s32[10]{0:T(128)S(1)} %pad_add_fusion.at_ref, bf16[2,4,2,592,512]{4,3,2,1,0:T(8,128)(2,1)} %bitcast.45, bf16[2,4,4,128,256]{4,3,2,1,0:T(8,128)(2,1)S(1)} %pad_maximum_fusion.refs_0_, ...), custom_call_target="tpu_custom_call" | custom-call | flops 6442450944 | bytes 18000000 | tf_op jit(solution)/shard_map/project/pallas_call | solution.py:124
  108.2 1.5 mix.2.mine_ref
  109.7 1.2 copy-done.1
  110.9 0.9 select_bitcast_fusion.1
  111.8 3.4 %collective-permute-start.11 = (bf16[144,256]{1,0:T(8,128)(2,1)S(1)}, bf16[144,256]{1,0:T(8,128)(2,1)S(1)}, u32[]{:S(2)}, u32[]{:S(2)}) collective-permute-start(bf16[144,256]{1,0:T(8,128)(2,1)S(1)} %get-tuple-element.42), channel_id=1, source_target_pairs={{0,8},{8,16},{16,24},{24,64},{64,72},{72,80},{80,88},{88,128},{128... | collective-permute-start | bytes 221192 | tf_op jit(solution)/shard_map/ppermute | solution.py:383
  115.2 2.5 %collective-permute-start.12 = (bf16[144,256]{1,0:T(8,128)(2,1)S(1)}, bf16[144,256]{1,0:T(8,128)(2,1)S(1)}, u32[]{:S(2)}, u32[]{:S(2)}) collective-permute-start(bf16[144,256]{1,0:T(8,128)(2,1)S(1)} %get-tuple-element.41), channel_id=1, source_target_pairs={{0,8},{8,16},{16,24},{24,0},{64,72},{72,80},{80,88},{88,64},{128,1... | collective-permute-start | bytes 221192 | tf_op jit(solution)/shard_map/ppermute | solution.py:384
  117.6 6.5 %project_out.2.refs_4_ = bf16[2,4,512,512]{3,2,1,0:T(8,128)(2,1)} custom-call(s32[10]{0:T(128)S(1)} %pad_add_fusion.at_ref, bf16[2,256,256]{2,1,0:T(8,128)(2,1)S(1)} %mix.2.mine_ref, bf16[2,256,256]{2,1,0:T(8,128)(2,1)} %collective-permute-done.13.other_ref, bf16[2,4,4,128,256]{4,3,2,1,0:T(8,128)(2,1)S(1)} %pad_maximum_fusion.refs_0_, ...), custom_call_target="tpu_custom_call" | custom-call | flops 1073741824 | bytes 5000000 | tf_op jit(solution)/shard_map/project_out/pallas_call | solution.py:286
  124.2 1.5 mix.3.mine_ref
  125.7 0.1 collective-permute-start.14
  125.8 1.5 collective-permute-done.14.other_ref
  127.3 5.5 %project_out.3 = bf16[2,4,512,512]{3,2,1,0:T(8,128)(2,1)} custom-call(s32[10]{0:T(128)S(1)} %pad_add_fusion.at_ref, bf16[2,256,256]{2,1,0:T(8,128)(2,1)S(1)} %mix.3.mine_ref, bf16[2,256,256]{2,1,0:T(8,128)(2,1)S(1)} %collective-permute-done.14.other_ref, bf16[2,4,4,128,256]{4,3,2,1,0:T(8,128)(2,1)S(1)} %pad_maximum_fusion.refs_0_, ...), custom_call_target="tpu_custom_call", output_to_operand_aliasing={{}: (7, {})} | custom-call | flops 1073741824 | bytes 5000000 | tf_op jit(solution)/shard_map/project_out/pallas_call | solution.py:286
  132.9 63.2 %reduce-scatter.2.cloned.1.call-done = bf16[1,512,512]{2,1,0:T(8,128)(2,1)} async-done(((bf16[8,512,512]{2,1,0:T(8,128)(2,1)}), bf16[1,512,512]{2,1,0:T(8,128)(2,1)}) %reduce-scatter.2.cloned.1.call-update) | async-done | bytes 524304 | tf_op jit(solution)/shard_map/reduce_scatter | solution.py:396
  196.0 2.0 fusion.3
  (49 shorter events, 0.3 us)
Async XLA Ops:
  6.5 62.9 %copy-start = (f32[3,3,512]{2,1,0:T(4,128)S(1)}, f32[3,3,512]{2,1,0:T(4,128)}, u32[]{:S(2)}) copy-start(f32[3,3,512]{2,1,0:T(4,128)} %param.14) | copy-start | bytes 55300
  6.5 4.2 %copy-start.6 = (bf16[512,128]{1,0:T(8,128)(2,1)S(1)}, bf16[512,128]{1,0:T(8,128)(2,1)}, u32[]{:S(2)}) copy-start(bf16[512,128]{1,0:T(8,128)(2,1)} %param.17) | copy-start | bytes 393220
  6.5 12.1 %copy-start.5 = (bf16[3,128,512]{2,1,0:T(8,128)(2,1)S(1)}, bf16[3,128,512]{2,1,0:T(8,128)(2,1)}, u32[]{:S(2)}) copy-start(bf16[3,128,512]{2,1,0:T(8,128)(2,1)} %param.13) | copy-start | bytes 1179652
  6.5 87.0 %all-gather.3.cloned.1.call-start = ((), (), s32[]{:S(2)}) async-start(), calls=%async_computation.2 | async-start | bytes 10305536 | tf_op jit(solution)/shard_map/all_gather | solution.py:355
  10.6 185.4 %reduce-scatter.2.cloned.1.call-start = ((), (), s32[]{:S(2)}) async-start(), calls=%async_computation.1 | async-start | bytes 4718592 | tf_op jit(solution)/shard_map/reduce_scatter | solution.py:396
  10.7 10.6 %collective-permute-start.6 = (bf16[256,128]{1,0:T(8,128)(2,1)S(1)}, bf16[256,128]{1,0:T(8,128)(2,1)S(1)}, u32[]{:S(2)}, u32[]{:S(2)}) collective-permute-start(bf16[256,128]{1,0:T(8,128)(2,1)S(1)} %get-tuple-element.45), channel_id=1, source_target_pairs={{0,32},{1,0},{32,33},{33,1},{2,34},{3,2},{34,35},{35,3},{4,36},{5,... | collective-permute-start | bytes 196616 | tf_op jit(solution)/shard_map/ppermute | solution.py:364
  18.0 2.1 %collective-permute-start = (bf16[256,128]{1,0:T(8,128)(2,1)S(1)}, bf16[256,128]{1,0:T(8,128)(2,1)S(1)}, u32[]{:S(2)}, u32[]{:S(2)}) collective-permute-start(bf16[256,128]{1,0:T(8,128)(2,1)S(1)} %get-tuple-element.46), channel_id=1, source_target_pairs={{0,0},{1,32},{32,1},{33,33},{2,2},{3,34},{34,3},{35,35},{4,4},{5,3... | collective-permute-start | bytes 196616 | tf_op jit(solution)/shard_map/ppermute | solution.py:364
  18.7 13.1 %collective-permute-start.5 = (bf16[3,128,256]{2,1,0:T(8,128)(2,1)S(1)}, bf16[3,128,256]{2,1,0:T(8,128)(2,1)S(1)}, u32[]{:S(2)}, u32[]{:S(2)}) collective-permute-start(bf16[3,128,256]{2,1,0:T(8,128)(2,1)S(1)} %get-tuple-element.35), channel_id=1, source_target_pairs={{0,32},{32,0},{1,33},{33,1},{2,34},{34,2},{3,35},{35,3},{4,36},{36... | collective-permute-start | bytes 589832 | tf_op jit(solution)/shard_map/ppermute | solution.py:359
  20.1 13.3 %collective-permute-start.1 = (bf16[4,128,256]{2,1,0:T(8,128)(2,1)S(1)}, bf16[4,128,256]{2,1,0:T(8,128)(2,1)S(1)}, u32[]{:S(2)}, u32[]{:S(2)}) collective-permute-start(bf16[4,128,256]{2,1,0:T(8,128)(2,1)S(1)} %get-tuple-element.40), channel_id=1, source_target_pairs={{0,8},{1,25},{8,0},{9,17},{16,24},{17,9},{24,16},{25,1},{2,10},{3,... | collective-permute-start | bytes 786440 | tf_op jit(solution)/shard_map/ppermute | solution.py:317
  31.8 6.5 %collective-permute-start.7 = (bf16[4,128,256]{2,1,0:T(8,128)(2,1)S(1)}, bf16[4,128,256]{2,1,0:T(8,128)(2,1)S(1)}, u32[]{:S(2)}, u32[]{:S(2)}) collective-permute-start(bf16[4,128,256]{2,1,0:T(8,128)(2,1)S(1)} %get-tuple-element.38), channel_id=1, source_target_pairs={{0,64},{1,193},{64,0},{65,129},{128,192},{129,65},{192,128},{193,1... | collective-permute-start | bytes 786440 | tf_op jit(solution)/shard_map/ppermute | solution.py:317
  33.5 9.3 %collective-permute-start.2 = (bf16[2,4,128,256]{3,2,1,0:T(8,128)(2,1)S(1)}, bf16[2,4,128,256]{3,2,1,0:T(8,128)(2,1)S(1)}, u32[]{:S(2)}, u32[]{:S(2)}) collective-permute-start(bf16[2,4,128,256]{3,2,1,0:T(8,128)(2,1)S(1)} %pad_maximum_fusion.4), channel_id=1, source_target_pairs={{0,24},{1,9},{8,16},{9,1},{16,8},{17,25},{24,0},{25,17},{2,26},{3,... | collective-permute-start | bytes 1572872 | tf_op jit(solution)/shard_map/ppermute | solution.py:317
  38.3 12.3 %collective-permute-start.8 = (bf16[2,4,128,256]{3,2,1,0:T(8,128)(2,1)S(1)}, bf16[2,4,128,256]{3,2,1,0:T(8,128)(2,1)S(1)}, u32[]{:S(2)}, u32[]{:S(2)}) collective-permute-start(bf16[2,4,128,256]{3,2,1,0:T(8,128)(2,1)S(1)} %pad_maximum_fusion.5), channel_id=1, source_target_pairs={{0,192},{1,65},{64,128},{65,1},{128,64},{129,193},{192,0},{193,129... | collective-permute-start | bytes 1572872 | tf_op jit(solution)/shard_map/ppermute | solution.py:317
  42.9 16.6 %collective-permute-start.3 = (bf16[4,4,128,256]{3,2,1,0:T(8,128)(2,1)S(1)}, bf16[4,4,128,256]{3,2,1,0:T(8,128)(2,1)S(1)}, u32[]{:S(2)}, u32[]{:S(2)}) collective-permute-start(bf16[4,4,128,256]{3,2,1,0:T(8,128)(2,1)S(1)} %get-tuple-element.32), channel_id=1, source_target_pairs={{0,64},{1,193},{64,0},{65,129},{128,192},{129,65},{192,128},{193,1... | collective-permute-start | bytes 3145736 | tf_op jit(solution)/shard_map/ppermute | solution.py:317
  50.7 14.9 %collective-permute-start.9 = (bf16[4,4,128,256]{3,2,1,0:T(8,128)(2,1)S(1)}, bf16[4,4,128,256]{3,2,1,0:T(8,128)(2,1)S(1)}, u32[]{:S(2)}, u32[]{:S(2)}) collective-permute-start(bf16[4,4,128,256]{3,2,1,0:T(8,128)(2,1)S(1)} %get-tuple-element.30), channel_id=1, source_target_pairs={{0,8},{1,25},{8,0},{9,17},{16,24},{17,9},{24,16},{25,1},{2,10},{3,... | collective-permute-start | bytes 3145736 | tf_op jit(solution)/shard_map/ppermute | solution.py:317
  59.7 27.4 %collective-permute-start.4 = (bf16[2,4,4,128,256]{4,3,2,1,0:T(8,128)(2,1)S(1)}, bf16[2,4,4,128,256]{4,3,2,1,0:T(8,128)(2,1)}, u32[]{:S(2)}, u32[]{:S(2)}) collective-permute-start(bf16[2,4,4,128,256]{4,3,2,1,0:T(8,128)(2,1)S(1)} %pad_maximum_fusion.refs_0_), channel_id=1, source_target_pairs={{0,192},{1,65},{64,128},{65,1},{128,64},{129,193},{192,0},{193,129... | collective-permute-start | bytes 6291464 | tf_op jit(solution)/shard_map/ppermute | solution.py:317
  65.6 3.0 %copy-start.7 = (bf16[32,128]{1,0:T(8,128)(2,1)S(1)}, bf16[32,128]{1,0:T(8,128)(2,1)}, u32[]{:S(2)}) copy-start(bf16[32,128]{1,0:T(8,128)(2,1)} %param.15) | copy-start | bytes 24580
  65.6 3.7 %copy-start.10 = (f32[512]{0:T(512)S(1)}, f32[512]{0:T(512)}, u32[]{:S(2)}) copy-start(f32[512]{0:T(512)} %param.16) | copy-start | bytes 6148
  65.6 3.7 %copy-start.8 = (s32[4]{0:T(128)S(1)}, s32[4]{0:T(128)}, u32[]{:S(2)}) copy-start(s32[4]{0:T(128)} %constant.44.clone) | copy-start | bytes 52
  65.6 3.7 %copy-start.9 = (s32[4]{0:T(128)S(1)}, s32[4]{0:T(128)}, u32[]{:S(2)}) copy-start(s32[4]{0:T(128)} %constant.45.clone) | copy-start | bytes 52
  67.2 26.4 %collective-permute-start.10 = (bf16[2,4,4,128,256]{4,3,2,1,0:T(8,128)(2,1)}, bf16[2,4,4,128,256]{4,3,2,1,0:T(8,128)(2,1)}, u32[]{:S(2)}, u32[]{:S(2)}) collective-permute-start(bf16[2,4,4,128,256]{4,3,2,1,0:T(8,128)(2,1)} %pad_maximum_fusion.1.refs_2_), channel_id=1, source_target_pairs={{0,24},{1,9},{8,16},{9,1},{16,8},{17,25},{24,0},{25,17},{2,26},{3,... | collective-permute-start | bytes 6291464 | tf_op jit(solution)/shard_map/ppermute | solution.py:317
  108.2 1.5 copy-start.3
  109.7 1.2 copy-start.1
  110.9 6.8 %collective-permute-start.13 = (bf16[2,256,256]{2,1,0:T(8,128)(2,1)S(1)}, bf16[2,256,256]{2,1,0:T(8,128)(2,1)}, u32[]{:S(2)}, u32[]{:S(2)}) collective-permute-start(bf16[2,256,256]{2,1,0:T(8,128)(2,1)S(1)} %mix.2.mine_ref), channel_id=1, source_target_pairs={{0,1},{1,0},{2,3},{3,2},{4,5},{5,4},{6,7},{7,6},{8,9},{9,8},{10,11... | collective-permute-start | bytes 786440 | tf_op jit(solution)/shard_map/ppermute | solution.py:388
  111.8 12.3 %collective-permute-start.11 = (bf16[144,256]{1,0:T(8,128)(2,1)S(1)}, bf16[144,256]{1,0:T(8,128)(2,1)S(1)}, u32[]{:S(2)}, u32[]{:S(2)}) collective-permute-start(bf16[144,256]{1,0:T(8,128)(2,1)S(1)} %get-tuple-element.42), channel_id=1, source_target_pairs={{0,8},{8,16},{16,24},{24,64},{64,72},{72,80},{80,88},{88,128},{128... | collective-permute-start | bytes 221192 | tf_op jit(solution)/shard_map/ppermute | solution.py:383
  115.2 9.1 %copy-start.2 = (bf16[3,2,512,256]{3,2,1,0:T(8,128)(2,1)S(1)}, bf16[3,2,512,256]{3,2,1,0:T(8,128)(2,1)}, u32[]{:S(2)}) copy-start(bf16[3,2,512,256]{3,2,1,0:T(8,128)(2,1)} %copy-done.1) | copy-start | bytes 4718596
  115.2 9.0 %collective-permute-start.12 = (bf16[144,256]{1,0:T(8,128)(2,1)S(1)}, bf16[144,256]{1,0:T(8,128)(2,1)S(1)}, u32[]{:S(2)}, u32[]{:S(2)}) collective-permute-start(bf16[144,256]{1,0:T(8,128)(2,1)S(1)} %get-tuple-element.41), channel_id=1, source_target_pairs={{0,8},{8,16},{16,24},{24,0},{64,72},{72,80},{80,88},{88,64},{128,1... | collective-permute-start | bytes 221192 | tf_op jit(solution)/shard_map/ppermute | solution.py:384
  125.7 1.6 collective-permute-start.14
  132.8 63.2 %copy-start.4 = (bf16[512,512]{1,0:T(8,128)(2,1)S(1)}, bf16[512,512]{1,0:T(8,128)(2,1)}, u32[]{:S(2)}) copy-start(bf16[512,512]{1,0:T(8,128)(2,1)} %param.10) | copy-start | bytes 1572868
Sparse Core Ops, SparseCore 0:
  10.8 70.1 all-gather.2
  133.0 63.0 reduce-scatter.1

commit v9 on v8

--- a/solution.py
+++ b/solution.py
@@ -47,9 +47,11 @@
 
 
 def project_kernel(at_ref, x_ref, *refs):
-    taps_ref, proj_ref, tail_ref, mid_ref, front_ref, wide, acc, stat, ahead, sems = refs[4:]
+    taps_ref, proj_ref, tail_ref, mid_ref, front_ref, out_w_ref = refs[4:10]
+    wide, acc, stat, ahead, sems, out_sems = refs[10:]
     first_row, kind = pl.program_id(0) == 0, pl.program_id(1)
     turns = []
+    out_copies = []
     for k in range(2):
         copies = []
         for i in range(4):
@@ -61,6 +63,12 @@
                     source = refs[2 * k + i // 2].at[i % 2, j, s]
                     place = wide.at[k, rows, pl.ds(s * CH, CH)]
                     copies.append(pltpu.make_async_copy(source, place, sems.at[k, i, j, s]))
+                lanes = pl.ds(pl.multiple_of(at_ref[4 + x] * 128, 128), 128)
+                for part in range(2):
+                    source = refs[2 * k + i // 2].at[i % 2, j, 3, :, pl.ds(part * 128, 128)]
+                    place = out_w_ref.at[at_ref[y], pl.ds(k * CH + part * 128, 128), lanes]
+                    sem = out_sems.at[k, i, j, part]
+                    out_copies.append(pltpu.make_async_copy(source, place, sem))
         turns.append(copies)
 
     @pl.when(first_row & (kind == 0))
@@ -68,6 +76,8 @@
         for copies in turns:
             for copy in copies:
                 copy.start()
+        for copy in out_copies:
+            copy.start()
 
     for k in range(2):
 
@@ -118,6 +128,8 @@
         mixing = three_taps(ahead[1], taps_ref, 1) * three_taps(ahead[2], taps_ref, 2)
         front_ref[:LH] = pltpu.roll(mixing, SHARE + TILE - 1, 0)[:LH].astype(BF16)
         front_ref[LH:] = last_rows(ahead, LH - 8, -7)
+        for copy in out_copies:
+            copy.wait()
 
 
 def project(at, gathered, weights, taps):
@@ -139,6 +151,7 @@
                 pl.BlockSpec((1, HALO, CH), lambda h, k, at: (h, 0, 0)),
                 pl.BlockSpec((1, HALO, CH), lambda h, k, at: (h, 0, 0)),
                 pl.BlockSpec((HALO, CH), lambda h, k, at: (0, 0)),
+                pl.BlockSpec(memory_space=pl.ANY),
             ],
             scratch_shapes=[
                 pltpu.VMEM((2, 4 * WIDE, 3 * CH), BF16),
@@ -146,6 +159,7 @@
                 pltpu.VMEM((8, WIDE), F32),
                 pltpu.VMEM((3, SHARE + TILE, CH), F32),
                 pltpu.SemaphoreType.DMA((2, 4, 4, 3)),
+                pltpu.SemaphoreType.DMA((2, 4, 4, 2)),
             ],
         ),
         out_shape=[
@@ -153,6 +167,7 @@
             jax.ShapeDtypeStruct((2, HALO, CH), BF16),
             jax.ShapeDtypeStruct((2, HALO, CH), BF16),
             jax.ShapeDtypeStruct((HALO, CH), BF16),
+            jax.ShapeDtypeStruct((4, 2 * CH, WIDE), BF16),
         ],
         compiler_params=pltpu.CompilerParams(vmem_limit_bytes=46 * MIB),
         cost_estimate=pl.CostEstimate(
@@ -248,35 +263,18 @@
     )(proj, halo, band, taps, bias)
 
 
-def out_kernel(at_ref, mine_ref, other_ref, *refs):
-    out_ref, wide, rows, sems = refs[-4:]
-    step = pl.program_id(0)
-
-    @pl.when(step == 0)
-    def _():
-        copies = []
-        for k in range(2):
-            for i in range(4):
-                for j in range(4):
-                    y, x = (i, j) if k == 0 else (j, i)
-                    lanes = pl.ds(pl.multiple_of(at_ref[4 + x] * 128, 128), 128)
-                    for part in range(2):
-                        source = refs[2 * k + i // 2].at[i % 2, j, 3, :, pl.ds(part * 128, 128)]
-                        place = wide.at[at_ref[y], pl.ds(k * CH + part * 128, 128), lanes]
-                        sem = sems.at[k, i, j, part]
-                        copies.append(pltpu.make_async_copy(source, place, sem))
-        for copy in copies:
-            copy.start()
+def out_kernel(at_ref, mine_ref, other_ref, w_ref, *refs):
+    out_ref, rows = refs[-2:]
+
+    @pl.when(pl.program_id(0) == 0)
+    def _():
         swap = at_ref[9] == 1
         for h in range(2):
             place = slice(h * HALF, (h + 1) * HALF)
             rows[place, :CH] = jnp.where(swap, other_ref[h], mine_ref[h])
             rows[place, CH:] = jnp.where(swap, mine_ref[h], other_ref[h])
 
-        for copy in copies:
-            copy.wait()
-
-    products = jnp.dot(rows[...], wide[step], preferred_element_type=F32).astype(BF16)
+    products = jnp.dot(rows[...], w_ref[0], preferred_element_type=F32).astype(BF16)
     for h in range(2):
         out_ref[h, 0] = products[h * HALF : (h + 1) * HALF]
 
@@ -290,23 +288,20 @@
             grid=(4,),
             in_specs=[
                 *[pl.BlockSpec((2, HALF, CH), lambda k, at: (0, 0, 0))] * 2,
-                *[pl.BlockSpec(memory_space=pl.ANY)] * (4 + len(more)),
+                pl.BlockSpec((1, 2 * CH, WIDE), lambda k, at: (k, 0, 0)),
+                *[pl.BlockSpec(memory_space=pl.ANY)] * len(more),
             ],
             out_specs=pl.BlockSpec((2, 1, HALF, WIDE), lambda k, at: (0, k, half, 0)),
-            scratch_shapes=[
-                pltpu.VMEM((4, 2 * CH, WIDE), BF16),
-                pltpu.VMEM((2 * HALF, 2 * CH), BF16),
-                pltpu.SemaphoreType.DMA((2, 4, 4, 2)),
-            ],
+            scratch_shapes=[pltpu.VMEM((2 * HALF, 2 * CH), BF16)],
         ),
         out_shape=jax.ShapeDtypeStruct((2, 4, ROWS, WIDE), BF16),
-        input_output_aliases={} if base is None else {7: 0},
-        compiler_params=pltpu.CompilerParams(vmem_limit_bytes=45 * MIB),
+        input_output_aliases={} if base is None else {4: 0},
+        compiler_params=pltpu.CompilerParams(vmem_limit_bytes=52 * MIB),
         cost_estimate=pl.CostEstimate(
             flops=2 * 512 * 2 * CH * 2048, bytes_accessed=5_000_000, transcendentals=0
         ),
         name="project_out",
-    )(at, mine, other, *weights, *more)
+    )(at, mine, other, weights, *more)
 
 
 FIRST, SECOND = (1, 3), (3, 1)
@@ -352,7 +347,6 @@
         ],
         axis=0,
     )
-    gathered = lax.all_gather(own, ring).reshape(2, 4, 2, ROWS + TILE, WIDE)
 
     left, right = in_weight[..., :CH], in_weight[..., CH:]
     kept = jnp.where(zh == 0, left, right)
@@ -363,6 +357,8 @@
         pairs = [(a * 2 + b, (b ^ k) * 2 + a) for a in range(2) for b in range(2)]
         chosen = lax.ppermute(chosen, ("zh", "c"), pairs)
         pieces.append(jnp.concatenate([chosen[:128], chosen[128:]], axis=1)[None])
+    own, got, pieces = lax.optimization_barrier((own, got, pieces))
+    gathered = lax.all_gather(own, ring).reshape(2, 4, 2, ROWS + TILE, WIDE)
     kept = jnp.concatenate([kept, pieces[0]], axis=0)
     got = jnp.concatenate([got, pieces[1]], axis=0)
     weights = (
@@ -375,7 +371,7 @@
     bias = lax.dynamic_slice_in_dim(mr_bias, zh * CH, CH, 0)[None, :]
     band = toeplitz(lax.dynamic_slice_in_dim(mr_filter, zh * GROUPS, GROUPS, 0))
 
-    proj, tail, mid, front = project(at, gathered, weights, taps)
+    proj, tail, mid, front, w_out = project(at, gathered, weights, taps)
 
     last = column == 3
     to_first = jnp.where(last, tail[1], tail[0])
@@ -387,11 +383,11 @@
     def swapped(mine):
         return mine, lax.ppermute(mine, "c", [(0, 1), (1, 0)])
 
-    partial = project_out(at, *swapped(mix(proj, mid, band, taps, bias, 2, 2)), weights, 1)
+    partial = project_out(at, *swapped(mix(proj, mid, band, taps, bias, 2, 2)), w_out, 1)
     first, second, partial = lax.optimization_barrier((first, second, partial))
     halo = jnp.stack([jnp.where(leading, front, first), second])
     partial = project_out(
-        at, *swapped(mix(proj, halo, band, taps, bias, 0, 2)), weights, 0, partial
+        at, *swapped(mix(proj, halo, band, taps, bias, 0, 2)), w_out, 0, partial
     )
     summed = lax.psum_scatter(
         partial.reshape(8, ROWS, WIDE), ("zh", "zl"), scatter_dimension=0

time: 206 us -> 197 us (0.956)
  waiting for transfers between devices: 122 us -> 112 us
  local copies, waits for them, and re-layouts: 1.47 us -> 5.54 us
    reduce_scatter x1, waiting for transfers between devices: 63.2 us -> 55.5 us  [on_device(): lax.psum_scatter(partial.reshape(8, ROWS, WIDE), ('zh', 'zl'), scatter_di...]
    unnamed x22 -> x21, local copies, waits for them, and re-layouts: 1.2 us -> 4.35 us
  transfers between devices with their start and end apart: 17 -> 17, of which waited for: 10 -> 9; matrix products, arithmetic and copies ran while one was open for 2% -> 3% of each run, Pallas kernels for 3% -> 3%
where the time goes in v9:
time: 197 us; the launch traced here: 196 us
  waiting for transfers between devices  112 us (57%)
  Pallas kernels  29.1 us (15%)
  starting transfers between devices  27.3 us (14%)
  between operations  13.7 us (7%)
  other arithmetic  8.33 us (4%)
  local copies, waits for them, and re-layouts  5.54 us (3%)
    reduce_scatter x1, waiting for transfers between devices, on_device(): lax.psum_scatter(partial.reshape(8, ROWS, WIDE), ('zh', 'zl'), scatter_di...  55.5 us
    ppermute x8, waiting for transfers between devices, pair_step(): return lax.ppermute(value, (axis, 'c'), pairs)  46.3 us
    pallas_call x1, Pallas kernels, project(): pl.pallas_call(project_kernel, grid_spec=pltpu.PrefetchScalarGridSpec(num...  15.3 us
    ppermute x8, starting transfers between devices, pair_step(): return lax.ppermute(value, (axis, 'c'), pairs)  12.1 us
    pallas_call x2, Pallas kernels, project_out(): pl.pallas_call(out_kernel, grid_spec=pltpu.PrefetchScalarGridSpec(num_sca...  10.4 us
    ppermute x1, waiting for transfers between devices, on_device(): got = lax.ppermute(jnp.where(zh == 0, right, left), 'zh', [(0, 1), (1, 0)])  8.52 us
    ppermute x2, starting transfers between devices, on_device(): chosen = lax.ppermute(chosen, ('zh', 'c'), pairs)  7.93 us
    unnamed x21, local copies, waits for them, and re-layouts  4.35 us
  transfers between devices with their start and end apart: 17, of which 9 were waited for; matrix products, arithmetic and copies ran while one was open for 3% of the time, Pallas kernels for 3%

profile of v9, /device:TPU:2, one launch (start us, length us, event | category | flops | bytes accessed | tf_op | source)
XLA Modules:
  0.0 195.8 jit_solution(16895211449923290400)
XLA Ops:
  6.5 0.9 constant_dynamic-slice_fusion.1
  7.5 7.3 %collective-permute-start.2 = (bf16[256,128]{1,0:T(8,128)(2,1)S(1)}, bf16[256,128]{1,0:T(8,128)(2,1)S(1)}, u32[]{:S(2)}, u32[]{:S(2)}) collective-permute-start(bf16[256,128]{1,0:T(8,128)(2,1)S(1)} %get-tuple-element.53), channel_id=1, source_target_pairs={{0,32},{1,0},{32,33},{33,1},{2,34},{3,2},{34,35},{35,3},{4,36},{5,... | collective-permute-start | bytes 196616 | tf_op jit(solution)/shard_map/ppermute | solution.py:358
  14.7 0.7 collective-permute-start.1
  15.4 1.1 broadcast_select_fusion.1
  16.5 1.4 collective-permute-start
  17.8 0.7 convert_element_type.41
  18.5 1.3 fusion.1
  19.8 0.1 fusion.5
  20.0 0.9 fusion.4
  20.9 8.5 %collective-permute-done = bf16[3,128,256]{2,1,0:T(8,128)(2,1)S(1)} collective-permute-done((bf16[3,128,256]{2,1,0:T(8,128)(2,1)S(1)}, bf16[3,128,256]{2,1,0:T(8,128)(2,1)S(1)}, u32[]{:S(2)}, u32[]{:S(2)}) %collective-permute-start) | collective-permute-done | bytes 196640 | tf_op jit(solution)/shard_map/ppermute | solution.py:353
  29.5 1.7 collective-permute-start.7
  31.2 0.6 collective-permute-start.3
  31.9 4.1 %collective-permute-done.7 = bf16[4,128,256]{2,1,0:T(8,128)(2,1)S(1)} collective-permute-done((bf16[4,128,256]{2,1,0:T(8,128)(2,1)S(1)}, bf16[4,128,256]{2,1,0:T(8,128)(2,1)S(1)}, u32[]{:S(2)}, u32[]{:S(2)}) %collective-permute-start.7) | collective-permute-done | bytes 262176 | tf_op jit(solution)/shard_map/ppermute | solution.py:312
  36.0 3.1 %collective-permute-start.8 = (bf16[2,4,128,256]{3,2,1,0:T(8,128)(2,1)S(1)}, bf16[2,4,128,256]{3,2,1,0:T(8,128)(2,1)S(1)}, u32[]{:S(2)}, u32[]{:S(2)}) collective-permute-start(bf16[2,4,128,256]{3,2,1,0:T(8,128)(2,1)S(1)} %pad_maximum_fusion.5), channel_id=1, source_target_pairs={{0,192},{1,65},{64,128},{65,1},{128,64},{129,193},{192,0},{193,129... | collective-permute-start | bytes 1572872 | tf_op jit(solution)/shard_map/ppermute | solution.py:312
  39.2 1.6 collective-permute-start.4
  40.8 5.7 %collective-permute-done.8 = bf16[2,4,128,256]{3,2,1,0:T(8,128)(2,1)S(1)} collective-permute-done((bf16[2,4,128,256]{3,2,1,0:T(8,128)(2,1)S(1)}, bf16[2,4,128,256]{3,2,1,0:T(8,128)(2,1)S(1)}, u32[]{:S(2)}, u32[]{:S(2)}) %collective-permute-start.8) | collective-permute-done | bytes 524320 | tf_op jit(solution)/shard_map/ppermute | solution.py:312
  46.5 0.1 fusion.11
  46.7 0.4 collective-permute-start.9
  47.1 2.2 %collective-permute-done.4 = bf16[2,4,128,256]{3,2,1,0:T(8,128)(2,1)S(1)} collective-permute-done((bf16[2,4,128,256]{3,2,1,0:T(8,128)(2,1)S(1)}, bf16[2,4,128,256]{3,2,1,0:T(8,128)(2,1)S(1)}, u32[]{:S(2)}, u32[]{:S(2)}) %collective-permute-start.4) | collective-permute-done | bytes 524320 | tf_op jit(solution)/shard_map/ppermute | solution.py:312
  49.3 0.1 fusion.12
  49.4 0.1 collective-permute-start.5
  49.5 12.1 %collective-permute-done.9 = bf16[4,4,128,256]{3,2,1,0:T(8,128)(2,1)S(1)} collective-permute-done((bf16[4,4,128,256]{3,2,1,0:T(8,128)(2,1)S(1)}, bf16[4,4,128,256]{3,2,1,0:T(8,128)(2,1)S(1)}, u32[]{:S(2)}, u32[]{:S(2)}) %collective-permute-start.9) | collective-permute-done | bytes 1048608 | tf_op jit(solution)/shard_map/ppermute | solution.py:312
  61.6 1.6 pad_maximum_fusion.1.refs_2_
  63.1 1.5 collective-permute-start.10
  64.6 0.2 pad_maximum_fusion.refs_0_
  64.8 3.1 %collective-permute-start.6 = (bf16[2,4,4,128,256]{4,3,2,1,0:T(8,128)(2,1)S(1)}, bf16[2,4,4,128,256]{4,3,2,1,0:T(8,128)(2,1)}, u32[]{:S(2)}, u32[]{:S(2)}) collective-permute-start(bf16[2,4,4,128,256]{4,3,2,1,0:T(8,128)(2,1)S(1)} %pad_maximum_fusion.refs_0_), channel_id=1, source_target_pairs={{0,192},{1,65},{64,128},{65,1},{128,64},{129,193},{192,0},{193,129... | collective-permute-start | bytes 6291464 | tf_op jit(solution)/shard_map/ppermute | solution.py:312
  67.9 1.3 copy-done.2
  69.3 0.1 rev.4
  69.4 0.1 pad.19.u_ref
  69.4 0.5 toeplitz.1.band_ref
  69.9 0.1 dynamic_slice.23
  70.0 0.1 pad_add_fusion.at_ref
  70.1 19.4 %collective-permute-done.10.refs_3_ = bf16[2,4,4,128,256]{4,3,2,1,0:T(8,128)(2,1)} collective-permute-done((bf16[2,4,4,128,256]{4,3,2,1,0:T(8,128)(2,1)}, bf16[2,4,4,128,256]{4,3,2,1,0:T(8,128)(2,1)}, u32[]{:S(2)}, u32[]{:S(2)}) %collective-permute-start.10) | collective-permute-done | bytes 2097184 | tf_op jit(solution)/shard_map/ppermute | solution.py:312
  89.5 2.8 %collective-permute-done.6.refs_1_ = bf16[2,4,4,128,256]{4,3,2,1,0:T(8,128)(2,1)} collective-permute-done((bf16[2,4,4,128,256]{4,3,2,1,0:T(8,128)(2,1)S(1)}, bf16[2,4,4,128,256]{4,3,2,1,0:T(8,128)(2,1)}, u32[]{:S(2)}, u32[]{:S(2)}) %collective-permute-start.6) | collective-permute-done | bytes 2097184 | tf_op jit(solution)/shard_map/ppermute | solution.py:312
  92.3 1.6 copy-done.3
  93.9 15.3 %project.1 = (bf16[3,2,512,256]{3,2,1,0:T(8,128)(2,1)S(1)}, bf16[2,144,256]{2,1,0:T(8,128)(2,1)S(1)}, bf16[2,144,256]{2,1,0:T(8,128)(2,1)S(1)}, bf16[144,256]{1,0:T(8,128)(2,1)S(1)}, bf16[4,512,512]{2,1,0:T(8,128)(2,1)S(1)}) custom-call(s32[10]{0:T(128)S(1)} %pad_add_fusion.at_ref, bf16[2,4,2,592,512]{4,3,2,1,0:T(8,128)(2,1)} %bitcast.46, ...), custom_call_target="tpu_custom_call" | custom-call | flops 6442450944 | bytes 18000000 | tf_op jit(solution)/shard_map/project/pallas_call | solution.py:136
  109.2 1.4 copy-done.1
  110.6 1.5 mix.2.mine_ref
  112.0 0.3 collective-permute-start.13
  112.4 3.0 %collective-permute-start.11 = (bf16[144,256]{1,0:T(8,128)(2,1)S(1)}, bf16[144,256]{1,0:T(8,128)(2,1)S(1)}, u32[]{:S(2)}, u32[]{:S(2)}) collective-permute-start(bf16[144,256]{1,0:T(8,128)(2,1)S(1)} %get-tuple-element.50), channel_id=1, source_target_pairs={{0,8},{8,16},{16,24},{24,64},{64,72},{72,80},{80,88},{88,128},{128... | collective-permute-start | bytes 221192 | tf_op jit(solution)/shard_map/ppermute | solution.py:379
  115.4 2.5 %collective-permute-start.12 = (bf16[144,256]{1,0:T(8,128)(2,1)S(1)}, bf16[144,256]{1,0:T(8,128)(2,1)S(1)}, u32[]{:S(2)}, u32[]{:S(2)}) collective-permute-start(bf16[144,256]{1,0:T(8,128)(2,1)S(1)} %get-tuple-element.49), channel_id=1, source_target_pairs={{0,8},{8,16},{16,24},{24,0},{64,72},{72,80},{80,88},{88,64},{128,1... | collective-permute-start | bytes 221192 | tf_op jit(solution)/shard_map/ppermute | solution.py:380
  117.9 5.2 %project_out.2.refs_0_ = bf16[2,4,512,512]{3,2,1,0:T(8,128)(2,1)} custom-call(s32[10]{0:T(128)S(1)} %pad_add_fusion.at_ref, bf16[2,256,256]{2,1,0:T(8,128)(2,1)S(1)} %mix.2.mine_ref, bf16[2,256,256]{2,1,0:T(8,128)(2,1)S(1)} %collective-permute-done.13.other_ref, bf16[4,512,512]{2,1,0:T(8,128)(2,1)} %copy-done.1), custom_call_target="tpu_custom_call" | custom-call | flops 1073741824 | bytes 5000000 | tf_op jit(solution)/shard_map/project_out/pallas_call | solution.py:284
  123.2 1.4 mix.3.mine_ref
  124.6 0.1 collective-permute-start.14
  124.7 1.5 collective-permute-done.14.other_ref
  126.3 5.2 %project_out.3 = bf16[2,4,512,512]{3,2,1,0:T(8,128)(2,1)} custom-call(s32[10]{0:T(128)S(1)} %pad_add_fusion.at_ref, bf16[2,256,256]{2,1,0:T(8,128)(2,1)S(1)} %mix.3.mine_ref, bf16[2,256,256]{2,1,0:T(8,128)(2,1)S(1)} %collective-permute-done.14.other_ref, bf16[4,512,512]{2,1,0:T(8,128)(2,1)} %copy-done.1, ...), custom_call_target="tpu_custom_call", output_to_operand_aliasing={{}: (4, {})} | custom-call | flops 1073741824 | bytes 5000000 | tf_op jit(solution)/shard_map/project_out/pallas_call | solution.py:284
  131.5 55.5 %reduce-scatter.2.cloned.1.call-done = bf16[1,512,512]{2,1,0:T(8,128)(2,1)} async-done(((bf16[8,512,512]{2,1,0:T(8,128)(2,1)}), bf16[1,512,512]{2,1,0:T(8,128)(2,1)}) %reduce-scatter.2.cloned.1.call-update) | async-done | bytes 524304 | tf_op jit(solution)/shard_map/reduce_scatter | solution.py:392
  186.9 2.0 %fusion.3 = bf16[512,512]{1,0:T(8,128)(2,1)} fusion(bf16[512,512]{1,0:T(8,128)(2,1)S(1)} %copy-done.4, bf16[1,512,512]{2,1,0:T(8,128)(2,1)} %reduce-scatter.2.cloned.1.call-done), kind=kLoop, calls=%fused_computation.9 | loop fusion | flops 1048576 | bytes 1572864 | tf_op jit(solution)/shard_map/convert_element_type | solution.py:395
  (47 shorter events, 0.4 us)
Async XLA Ops:
  6.5 63.6 %copy-start = (f32[3,3,512]{2,1,0:T(4,128)S(1)}, f32[3,3,512]{2,1,0:T(4,128)}, u32[]{:S(2)}) copy-start(f32[3,3,512]{2,1,0:T(4,128)} %param.14) | copy-start | bytes 55300
  6.5 13.2 %copy-start.5 = (bf16[129,512]{1,0:T(8,128)(2,1)S(1)}, bf16[129,512]{1,0:T(8,128)(2,1)}, u32[]{:S(2)}) copy-start(bf16[129,512]{1,0:T(8,128)(2,1)} %param.11) | copy-start | bytes 396292
  6.5 85.7 %all-gather.3.cloned.1.call-start = ((), (), s32[]{:S(2)}) async-start(), calls=%async_computation.2 | async-start | bytes 10305536 | tf_op jit(solution)/shard_map/all_gather | solution.py:361
  7.5 13.4 %collective-permute-start.2 = (bf16[256,128]{1,0:T(8,128)(2,1)S(1)}, bf16[256,128]{1,0:T(8,128)(2,1)S(1)}, u32[]{:S(2)}, u32[]{:S(2)}) collective-permute-start(bf16[256,128]{1,0:T(8,128)(2,1)S(1)} %get-tuple-element.53), channel_id=1, source_target_pairs={{0,32},{1,0},{32,33},{33,1},{2,34},{3,2},{34,35},{35,3},{4,36},{5,... | collective-permute-start | bytes 196616 | tf_op jit(solution)/shard_map/ppermute | solution.py:358
  14.7 6.1 %collective-permute-start.1 = (bf16[256,128]{1,0:T(8,128)(2,1)S(1)}, bf16[256,128]{1,0:T(8,128)(2,1)S(1)}, u32[]{:S(2)}, u32[]{:S(2)}) collective-permute-start(bf16[256,128]{1,0:T(8,128)(2,1)S(1)} %get-tuple-element.54), channel_id=1, source_target_pairs={{0,0},{1,32},{32,1},{33,33},{2,2},{3,34},{34,3},{35,35},{4,4},{5,3... | collective-permute-start | bytes 196616 | tf_op jit(solution)/shard_map/ppermute | solution.py:358
  16.5 13.0 %collective-permute-start = (bf16[3,128,256]{2,1,0:T(8,128)(2,1)S(1)}, bf16[3,128,256]{2,1,0:T(8,128)(2,1)S(1)}, u32[]{:S(2)}, u32[]{:S(2)}) collective-permute-start(bf16[3,128,256]{2,1,0:T(8,128)(2,1)S(1)} %get-tuple-element.46), channel_id=1, source_target_pairs={{0,32},{32,0},{1,33},{33,1},{2,34},{34,2},{3,35},{35,3},{4,36},{36... | collective-permute-start | bytes 589832 | tf_op jit(solution)/shard_map/ppermute | solution.py:353
  29.5 157.5 %reduce-scatter.2.cloned.1.call-start = ((), (), s32[]{:S(2)}) async-start(), calls=%async_computation.1 | async-start | bytes 4718592 | tf_op jit(solution)/shard_map/reduce_scatter | solution.py:392
  29.5 6.5 %collective-permute-start.7 = (bf16[4,128,256]{2,1,0:T(8,128)(2,1)S(1)}, bf16[4,128,256]{2,1,0:T(8,128)(2,1)S(1)}, u32[]{:S(2)}, u32[]{:S(2)}) collective-permute-start(bf16[4,128,256]{2,1,0:T(8,128)(2,1)S(1)} %constant_dynamic-update-slice_fusion), channel_id=1, source_target_pairs={{0,64},{1,193},{64,0},{65,129},{128,192},{129,65},{192,128},{193,1... | collective-permute-start | bytes 786440 | tf_op jit(solution)/shard_map/ppermute | solution.py:312
  31.2 7.9 %collective-permute-start.3 = (bf16[4,128,256]{2,1,0:T(8,128)(2,1)S(1)}, bf16[4,128,256]{2,1,0:T(8,128)(2,1)S(1)}, u32[]{:S(2)}, u32[]{:S(2)}) collective-permute-start(bf16[4,128,256]{2,1,0:T(8,128)(2,1)S(1)} %get-tuple-element.48), channel_id=1, source_target_pairs={{0,8},{1,25},{8,0},{9,17},{16,24},{17,9},{24,16},{25,1},{2,10},{3,... | collective-permute-start | bytes 786440 | tf_op jit(solution)/shard_map/ppermute | solution.py:312
  36.0 10.5 %collective-permute-start.8 = (bf16[2,4,128,256]{3,2,1,0:T(8,128)(2,1)S(1)}, bf16[2,4,128,256]{3,2,1,0:T(8,128)(2,1)S(1)}, u32[]{:S(2)}, u32[]{:S(2)}) collective-permute-start(bf16[2,4,128,256]{3,2,1,0:T(8,128)(2,1)S(1)} %pad_maximum_fusion.5), channel_id=1, source_target_pairs={{0,192},{1,65},{64,128},{65,1},{128,64},{129,193},{192,0},{193,129... | collective-permute-start | bytes 1572872 | tf_op jit(solution)/shard_map/ppermute | solution.py:312
  39.2 10.0 %collective-permute-start.4 = (bf16[2,4,128,256]{3,2,1,0:T(8,128)(2,1)S(1)}, bf16[2,4,128,256]{3,2,1,0:T(8,128)(2,1)S(1)}, u32[]{:S(2)}, u32[]{:S(2)}) collective-permute-start(bf16[2,4,128,256]{3,2,1,0:T(8,128)(2,1)S(1)} %pad_maximum_fusion.4), channel_id=1, source_target_pairs={{0,24},{1,9},{8,16},{9,1},{16,8},{17,25},{24,0},{25,17},{2,26},{3,... | collective-permute-start | bytes 1572872 | tf_op jit(solution)/shard_map/ppermute | solution.py:312
  46.7 14.9 %collective-permute-start.9 = (bf16[4,4,128,256]{3,2,1,0:T(8,128)(2,1)S(1)}, bf16[4,4,128,256]{3,2,1,0:T(8,128)(2,1)S(1)}, u32[]{:S(2)}, u32[]{:S(2)}) collective-permute-start(bf16[4,4,128,256]{3,2,1,0:T(8,128)(2,1)S(1)} %get-tuple-element.40), channel_id=1, source_target_pairs={{0,8},{1,25},{8,0},{9,17},{16,24},{17,9},{24,16},{25,1},{2,10},{3,... | collective-permute-start | bytes 3145736 | tf_op jit(solution)/shard_map/ppermute | solution.py:312
  49.4 15.2 %collective-permute-start.5 = (bf16[4,4,128,256]{3,2,1,0:T(8,128)(2,1)S(1)}, bf16[4,4,128,256]{3,2,1,0:T(8,128)(2,1)S(1)}, u32[]{:S(2)}, u32[]{:S(2)}) collective-permute-start(bf16[4,4,128,256]{3,2,1,0:T(8,128)(2,1)S(1)} %get-tuple-element.42), channel_id=1, source_target_pairs={{0,64},{1,193},{64,0},{65,129},{128,192},{129,65},{192,128},{193,1... | collective-permute-start | bytes 3145736 | tf_op jit(solution)/shard_map/ppermute | solution.py:312
  63.1 26.4 %collective-permute-start.10 = (bf16[2,4,4,128,256]{4,3,2,1,0:T(8,128)(2,1)}, bf16[2,4,4,128,256]{4,3,2,1,0:T(8,128)(2,1)}, u32[]{:S(2)}, u32[]{:S(2)}) collective-permute-start(bf16[2,4,4,128,256]{4,3,2,1,0:T(8,128)(2,1)} %pad_maximum_fusion.1.refs_2_), channel_id=1, source_target_pairs={{0,24},{1,9},{8,16},{9,1},{16,8},{17,25},{24,0},{25,17},{2,26},{3,... | collective-permute-start | bytes 6291464 | tf_op jit(solution)/shard_map/ppermute | solution.py:312
  64.6 4.7 %copy-start.6 = (bf16[32,128]{1,0:T(8,128)(2,1)S(1)}, bf16[32,128]{1,0:T(8,128)(2,1)}, u32[]{:S(2)}) copy-start(bf16[32,128]{1,0:T(8,128)(2,1)} %param.15) | copy-start | bytes 24580
  64.6 5.3 %copy-start.9 = (f32[512]{0:T(512)S(1)}, f32[512]{0:T(512)}, u32[]{:S(2)}) copy-start(f32[512]{0:T(512)} %param.16) | copy-start | bytes 6148
  64.6 5.4 %copy-start.7 = (s32[4]{0:T(128)S(1)}, s32[4]{0:T(128)}, u32[]{:S(2)}) copy-start(s32[4]{0:T(128)} %constant.44.clone) | copy-start | bytes 52
  64.6 5.4 %copy-start.8 = (s32[4]{0:T(128)S(1)}, s32[4]{0:T(128)}, u32[]{:S(2)}) copy-start(s32[4]{0:T(128)} %constant.45.clone) | copy-start | bytes 52
  64.8 27.4 %collective-permute-start.6 = (bf16[2,4,4,128,256]{4,3,2,1,0:T(8,128)(2,1)S(1)}, bf16[2,4,4,128,256]{4,3,2,1,0:T(8,128)(2,1)}, u32[]{:S(2)}, u32[]{:S(2)}) collective-permute-start(bf16[2,4,4,128,256]{4,3,2,1,0:T(8,128)(2,1)S(1)} %pad_maximum_fusion.refs_0_), channel_id=1, source_target_pairs={{0,192},{1,65},{64,128},{65,1},{128,64},{129,193},{192,0},{193,129... | collective-permute-start | bytes 6291464 | tf_op jit(solution)/shard_map/ppermute | solution.py:312
  67.9 1.3 copy-start.2
  92.3 1.6 copy-start.3
  109.2 1.4 copy-start.1
  112.0 5.9 %collective-permute-start.13 = (bf16[2,256,256]{2,1,0:T(8,128)(2,1)S(1)}, bf16[2,256,256]{2,1,0:T(8,128)(2,1)S(1)}, u32[]{:S(2)}, u32[]{:S(2)}) collective-permute-start(bf16[2,256,256]{2,1,0:T(8,128)(2,1)S(1)} %mix.2.mine_ref), channel_id=1, source_target_pairs={{0,1},{1,0},{2,3},{3,2},{4,5},{5,4},{6,7},{7,6},{8,9},{9,8},{10,11... | collective-permute-start | bytes 786440 | tf_op jit(solution)/shard_map/ppermute | solution.py:384
  112.4 10.8 %collective-permute-start.11 = (bf16[144,256]{1,0:T(8,128)(2,1)S(1)}, bf16[144,256]{1,0:T(8,128)(2,1)S(1)}, u32[]{:S(2)}, u32[]{:S(2)}) collective-permute-start(bf16[144,256]{1,0:T(8,128)(2,1)S(1)} %get-tuple-element.50), channel_id=1, source_target_pairs={{0,8},{8,16},{16,24},{24,64},{64,72},{72,80},{80,88},{88,128},{128... | collective-permute-start | bytes 221192 | tf_op jit(solution)/shard_map/ppermute | solution.py:379
  115.4 7.7 %collective-permute-start.12 = (bf16[144,256]{1,0:T(8,128)(2,1)S(1)}, bf16[144,256]{1,0:T(8,128)(2,1)S(1)}, u32[]{:S(2)}, u32[]{:S(2)}) collective-permute-start(bf16[144,256]{1,0:T(8,128)(2,1)S(1)} %get-tuple-element.49), channel_id=1, source_target_pairs={{0,8},{8,16},{16,24},{24,0},{64,72},{72,80},{80,88},{88,64},{128,1... | collective-permute-start | bytes 221192 | tf_op jit(solution)/shard_map/ppermute | solution.py:380
  124.6 1.6 collective-permute-start.14
  131.4 55.5 %copy-start.4 = (bf16[512,512]{1,0:T(8,128)(2,1)S(1)}, bf16[512,512]{1,0:T(8,128)(2,1)}, u32[]{:S(2)}) copy-start(bf16[512,512]{1,0:T(8,128)(2,1)} %param.10) | copy-start | bytes 1572868
Sparse Core Ops, SparseCore 0:
  29.6 61.9 all-gather.2
  131.6 55.3 reduce-scatter.1

commit v10 on v9

--- a/solution.py
+++ b/solution.py
@@ -263,8 +263,7 @@
     )(proj, halo, band, taps, bias)
 
 
-def out_kernel(at_ref, mine_ref, other_ref, w_ref, *refs):
-    out_ref, rows = refs[-2:]
+def out_kernel(at_ref, mine_ref, other_ref, w_ref, out_ref, rows):
 
     @pl.when(pl.program_id(0) == 0)
     def _():
@@ -279,8 +278,7 @@
         out_ref[h, 0] = products[h * HALF : (h + 1) * HALF]
 
 
-def project_out(at, mine, other, weights, half, base=None):
-    more = () if base is None else (base,)
+def project_out(at, mine, other, weights):
     return pl.pallas_call(
         out_kernel,
         grid_spec=pltpu.PrefetchScalarGridSpec(
@@ -289,19 +287,17 @@
             in_specs=[
                 *[pl.BlockSpec((2, HALF, CH), lambda k, at: (0, 0, 0))] * 2,
                 pl.BlockSpec((1, 2 * CH, WIDE), lambda k, at: (k, 0, 0)),
-                *[pl.BlockSpec(memory_space=pl.ANY)] * len(more),
             ],
-            out_specs=pl.BlockSpec((2, 1, HALF, WIDE), lambda k, at: (0, k, half, 0)),
+            out_specs=pl.BlockSpec((2, 1, HALF, WIDE), lambda k, at: (0, k, 0, 0)),
             scratch_shapes=[pltpu.VMEM((2 * HALF, 2 * CH), BF16)],
         ),
-        out_shape=jax.ShapeDtypeStruct((2, 4, ROWS, WIDE), BF16),
-        input_output_aliases={} if base is None else {4: 0},
+        out_shape=jax.ShapeDtypeStruct((2, 4, HALF, WIDE), BF16),
         compiler_params=pltpu.CompilerParams(vmem_limit_bytes=52 * MIB),
         cost_estimate=pl.CostEstimate(
             flops=2 * 512 * 2 * CH * 2048, bytes_accessed=5_000_000, transcendentals=0
         ),
         name="project_out",
-    )(at, mine, other, weights, *more)
+    )(at, mine, other, weights)
 
 
 FIRST, SECOND = (1, 3), (3, 1)
@@ -315,6 +311,30 @@
 def ring_pairs(piece, axis):
     here = jnp.stack([piece, pair_step(piece, axis, FIRST)])
     return here, pair_step(here, axis, SECOND)
+
+
+def ring_scatter(partial, place):
+    ring = ("zh", "zl")
+    up = [(i, (i + 1) % 8) for i in range(8)]
+    down = [(i, (i + 7) % 8) for i in range(8)]
+    half = partial.shape[1] // 2
+
+    def term(offset):
+        return lax.dynamic_index_in_dim(partial, (place + offset) % 8, 0, keepdims=False)
+
+    def plus(left, right):
+        return (left.astype(F32) + right.astype(F32)).astype(BF16)
+
+    far = term(4)
+    rising = lax.ppermute(far[:half], ring, up)
+    falling = lax.ppermute(far[half:], ring, down)
+    above, below = term(3), term(-3)
+    rising = jnp.concatenate([plus(above[:half], rising), above[half:]], axis=0)
+    falling = jnp.concatenate([below[:half], plus(below[half:], falling)], axis=0)
+    for offset in (2, 1):
+        rising = plus(term(offset), lax.ppermute(rising, ring, up))
+        falling = plus(term(-offset), lax.ppermute(falling, ring, down))
+    return term(0), lax.ppermute(rising, ring, up), lax.ppermute(falling, ring, down)
 
 
 def on_device(
@@ -351,6 +371,7 @@
     left, right = in_weight[..., :CH], in_weight[..., CH:]
     kept = jnp.where(zh == 0, left, right)
     got = lax.ppermute(jnp.where(zh == 0, right, left), "zh", [(0, 1), (1, 0)])
+    out_weight, own = lax.optimization_barrier((out_weight, own))
     pieces = []
     for k in range(2):
         chosen = lax.dynamic_slice_in_dim(out_weight, (core ^ k) * CH, CH, 0)
@@ -383,16 +404,17 @@
     def swapped(mine):
         return mine, lax.ppermute(mine, "c", [(0, 1), (1, 0)])
 
-    partial = project_out(at, *swapped(mix(proj, mid, band, taps, bias, 2, 2)), w_out, 1)
-    first, second, partial = lax.optimization_barrier((first, second, partial))
+    late = project_out(at, *swapped(mix(proj, mid, band, taps, bias, 2, 2)), w_out)
+    first, second, late = lax.optimization_barrier((first, second, late))
     halo = jnp.stack([jnp.where(leading, front, first), second])
-    partial = project_out(
-        at, *swapped(mix(proj, halo, band, taps, bias, 0, 2)), w_out, 0, partial
-    )
-    summed = lax.psum_scatter(
-        partial.reshape(8, ROWS, WIDE), ("zh", "zl"), scatter_dimension=0
-    )
-    return (tokens.astype(F32) + summed.astype(F32)).astype(BF16)
+    early = project_out(at, *swapped(mix(proj, halo, band, taps, bias, 0, 2)), w_out)
+    terms = ring_scatter(late.reshape(8, HALF, WIDE), zh * 4 + lax.axis_index("zl"))
+    late_sum = sum(term.astype(F32) for term in terms)
+    early_sum = lax.psum_scatter(
+        early.reshape(8, HALF, WIDE), ("zh", "zl"), scatter_dimension=0
+    )
+    summed = jnp.concatenate([early_sum.astype(F32), late_sum], axis=0)
+    return (tokens.astype(F32) + summed).astype(BF16)
 
 
 def solution(mesh):

time: 197 us -> 203 us (1.030)
  starting transfers between devices: 27.3 us -> 41.9 us
  waiting for transfers between devices: 112 us -> 99.1 us
  other arithmetic: 8.33 us -> 12.1 us
    reduce_scatter x1, waiting for transfers between devices: 55.5 us -> 0.02 us  [on_device(): lax.psum_scatter(early.reshape(8, HALF, WIDE), ('zh', 'zl'), scatter_dime...]
    ppermute x0 -> x8, waiting for transfers between devices: none -> 40.7 us  [the longest x2 26.5 us: ring_scatter(): rising = plus(term(offset), lax.ppermute(rising, ring, up))]
    ppermute x0 -> x8, starting transfers between devices: none -> 13.6 us  [the longest x1 3.68 us: ring_scatter(): rising = lax.ppermute(far[:half], ring, up)]
    ppermute x1, waiting for transfers between devices: 8.52 us -> 11.6 us  [on_device(): got = lax.ppermute(jnp.where(zh == 0, right, left), 'zh', [(0, 1), (1, 0)])]
    convert_element_type x1 -> x6, other arithmetic: 1.97 us -> 4.66 us  [the longest x4 2.7 us: plus(): return (left.astype(F32) + right.astype(F32)).astype(BF16)]
    unnamed x21 -> x25, local copies, waits for them, and re-layouts: 4.35 us -> 5.84 us
  transfers between devices with their start and end apart: 17 -> 25, of which waited for: 9 -> 13; matrix products, arithmetic and copies ran while one was open for 3% -> 3% of each run, Pallas kernels for 3% -> 3%
where the time goes in v10:
time: 203 us; the launch traced here: 202 us
  waiting for transfers between devices  99.1 us (49%)
  starting transfers between devices  41.9 us (21%)
  Pallas kernels  29.1 us (14%)
  between operations  13.8 us (7%)
  other arithmetic  12.1 us (6%)
  local copies, waits for them, and re-layouts  6.15 us (3%)
    ppermute x8, waiting for transfers between devices, pair_step(): return lax.ppermute(value, (axis, 'c'), pairs)  45.2 us
    ppermute x2, waiting for transfers between devices, ring_scatter(): rising = plus(term(offset), lax.ppermute(rising, ring, up))  26.5 us
    pallas_call x1, Pallas kernels, project(): pl.pallas_call(project_kernel, grid_spec=pltpu.PrefetchScalarGridSpec(num...  15.3 us
    ppermute x8, starting transfers between devices, pair_step(): return lax.ppermute(value, (axis, 'c'), pairs)  13.1 us
    ppermute x1, waiting for transfers between devices, on_device(): got = lax.ppermute(jnp.where(zh == 0, right, left), 'zh', [(0, 1), (1, 0)])  11.6 us
    pallas_call x2, Pallas kernels, project_out(): pl.pallas_call(out_kernel, grid_spec=pltpu.PrefetchScalarGridSpec(num_sca...  10.4 us
    ppermute x2, starting transfers between devices, on_device(): chosen = lax.ppermute(chosen, ('zh', 'c'), pairs)  7.88 us
    ppermute x2, waiting for transfers between devices, ring_scatter(): falling = plus(term(-offset), lax.ppermute(falling, ring, down))  6.14 us
  transfers between devices with their start and end apart: 25, of which 13 were waited for; matrix products, arithmetic and copies ran while one was open for 3% of the time, Pallas kernels for 3%

profile of v10, /device:TPU:2, one launch (start us, length us, event | category | flops | bytes accessed | tf_op | source)
XLA Modules:
  0.0 202.1 jit_solution(4750888904719897227)
XLA Ops:
  7.3 1.3 fusion.1
  8.6 1.1 fusion.12
  9.7 0.9 fusion.4
  10.6 7.2 %collective-permute-start.2 = (bf16[256,128]{1,0:T(8,128)(2,1)S(1)}, bf16[256,128]{1,0:T(8,128)(2,1)S(1)}, u32[]{:S(2)}, u32[]{:S(2)}) collective-permute-start(bf16[256,128]{1,0:T(8,128)(2,1)S(1)} %get-tuple-element.65), channel_id=1, source_target_pairs={{0,32},{1,0},{32,33},{33,1},{2,34},{3,2},{34,35},{35,3},{4,36},{5,... | collective-permute-start | bytes 196616 | tf_op jit(solution)/shard_map/ppermute | solution.py:379
  18.6 1.4 collective-permute-start
  20.0 11.6 %collective-permute-done = bf16[3,128,256]{2,1,0:T(8,128)(2,1)S(1)} collective-permute-done((bf16[3,128,256]{2,1,0:T(8,128)(2,1)S(1)}, bf16[3,128,256]{2,1,0:T(8,128)(2,1)S(1)}, u32[]{:S(2)}, u32[]{:S(2)}) %collective-permute-start) | collective-permute-done | bytes 196640 | tf_op jit(solution)/shard_map/ppermute | solution.py:373
  31.7 1.7 collective-permute-start.7
  34.0 4.1 %collective-permute-done.7 = bf16[4,128,256]{2,1,0:T(8,128)(2,1)S(1)} collective-permute-done((bf16[4,128,256]{2,1,0:T(8,128)(2,1)S(1)}, bf16[4,128,256]{2,1,0:T(8,128)(2,1)S(1)}, u32[]{:S(2)}, u32[]{:S(2)}) %collective-permute-start.7) | collective-permute-done | bytes 262176 | tf_op jit(solution)/shard_map/ppermute | solution.py:308
  38.2 3.1 %collective-permute-start.8 = (bf16[2,4,128,256]{3,2,1,0:T(8,128)(2,1)S(1)}, bf16[2,4,128,256]{3,2,1,0:T(8,128)(2,1)S(1)}, u32[]{:S(2)}, u32[]{:S(2)}) collective-permute-start(bf16[2,4,128,256]{3,2,1,0:T(8,128)(2,1)S(1)} %pad_maximum_fusion.5), channel_id=1, source_target_pairs={{0,192},{1,65},{64,128},{65,1},{128,64},{129,193},{192,0},{193,129... | collective-permute-start | bytes 1572872 | tf_op jit(solution)/shard_map/ppermute | solution.py:308
  41.4 1.6 collective-permute-start.4
  43.0 5.7 %collective-permute-done.8 = bf16[2,4,128,256]{3,2,1,0:T(8,128)(2,1)S(1)} collective-permute-done((bf16[2,4,128,256]{3,2,1,0:T(8,128)(2,1)S(1)}, bf16[2,4,128,256]{3,2,1,0:T(8,128)(2,1)S(1)}, u32[]{:S(2)}, u32[]{:S(2)}) %collective-permute-start.8) | collective-permute-done | bytes 524320 | tf_op jit(solution)/shard_map/ppermute | solution.py:308
  48.9 1.5 collective-permute-start.9
  50.4 1.1 collective-permute-done.4
  51.7 12.1 %collective-permute-done.9 = bf16[4,4,128,256]{3,2,1,0:T(8,128)(2,1)S(1)} collective-permute-done((bf16[4,4,128,256]{3,2,1,0:T(8,128)(2,1)S(1)}, bf16[4,4,128,256]{3,2,1,0:T(8,128)(2,1)S(1)}, u32[]{:S(2)}, u32[]{:S(2)}) %collective-permute-start.9) | collective-permute-done | bytes 1048608 | tf_op jit(solution)/shard_map/ppermute | solution.py:308
  63.8 1.5 pad_maximum_fusion.1.refs_2_
  65.3 1.5 collective-permute-start.10
  67.0 3.1 %collective-permute-start.6 = (bf16[2,4,4,128,256]{4,3,2,1,0:T(8,128)(2,1)S(1)}, bf16[2,4,4,128,256]{4,3,2,1,0:T(8,128)(2,1)}, u32[]{:S(2)}, u32[]{:S(2)}) collective-permute-start(bf16[2,4,4,128,256]{4,3,2,1,0:T(8,128)(2,1)S(1)} %pad_maximum_fusion.refs_0_), channel_id=1, source_target_pairs={{0,192},{1,65},{64,128},{65,1},{128,64},{129,193},{192,0},{193,129... | collective-permute-start | bytes 6291464 | tf_op jit(solution)/shard_map/ppermute | solution.py:308
  70.1 1.3 copy-done.2
  72.3 19.4 %collective-permute-done.10.refs_3_ = bf16[2,4,4,128,256]{4,3,2,1,0:T(8,128)(2,1)} collective-permute-done((bf16[2,4,4,128,256]{4,3,2,1,0:T(8,128)(2,1)}, bf16[2,4,4,128,256]{4,3,2,1,0:T(8,128)(2,1)}, u32[]{:S(2)}, u32[]{:S(2)}) %collective-permute-start.10) | collective-permute-done | bytes 2097184 | tf_op jit(solution)/shard_map/ppermute | solution.py:308
  91.6 2.8 %collective-permute-done.6.refs_1_ = bf16[2,4,4,128,256]{4,3,2,1,0:T(8,128)(2,1)} collective-permute-done((bf16[2,4,4,128,256]{4,3,2,1,0:T(8,128)(2,1)S(1)}, bf16[2,4,4,128,256]{4,3,2,1,0:T(8,128)(2,1)}, u32[]{:S(2)}, u32[]{:S(2)}) %collective-permute-start.6) | collective-permute-done | bytes 2097184 | tf_op jit(solution)/shard_map/ppermute | solution.py:308
  94.4 1.6 copy-done.3
  96.0 15.3 %project.1 = (bf16[3,2,512,256]{3,2,1,0:T(8,128)(2,1)S(1)}, bf16[2,144,256]{2,1,0:T(8,128)(2,1)S(1)}, bf16[2,144,256]{2,1,0:T(8,128)(2,1)S(1)}, bf16[144,256]{1,0:T(8,128)(2,1)S(1)}, bf16[4,512,512]{2,1,0:T(8,128)(2,1)S(1)}) custom-call(s32[10]{0:T(128)S(1)} %pad_add_fusion.at_ref, bf16[2,4,2,592,512]{4,3,2,1,0:T(8,128)(2,1)} %bitcast.86, ...), custom_call_target="tpu_custom_call" | custom-call | flops 6442450944 | bytes 18000000 | tf_op jit(solution)/shard_map/project/pallas_call | solution.py:136
  111.4 1.3 copy-done.1
  112.7 1.5 mix.2.mine_ref
  114.5 3.3 %collective-permute-start.11 = (bf16[144,256]{1,0:T(8,128)(2,1)S(1)}, bf16[144,256]{1,0:T(8,128)(2,1)S(1)}, u32[]{:S(2)}, u32[]{:S(2)}) collective-permute-start(bf16[144,256]{1,0:T(8,128)(2,1)S(1)} %get-tuple-element.62), channel_id=1, source_target_pairs={{0,8},{8,16},{16,24},{24,64},{64,72},{72,80},{80,88},{88,128},{128... | collective-permute-start | bytes 221192 | tf_op jit(solution)/shard_map/ppermute | solution.py:400
  117.8 2.2 %collective-permute-start.12 = (bf16[144,256]{1,0:T(8,128)(2,1)S(1)}, bf16[144,256]{1,0:T(8,128)(2,1)S(1)}, u32[]{:S(2)}, u32[]{:S(2)}) collective-permute-start(bf16[144,256]{1,0:T(8,128)(2,1)S(1)} %get-tuple-element.61), channel_id=1, source_target_pairs={{0,8},{8,16},{16,24},{24,0},{64,72},{72,80},{80,88},{88,64},{128,1... | collective-permute-start | bytes 221192 | tf_op jit(solution)/shard_map/ppermute | solution.py:401
  120.0 5.2 %project_out.2 = bf16[2,4,256,512]{3,2,1,0:T(8,128)(2,1)} custom-call(s32[10]{0:T(128)S(1)} %pad_add_fusion.at_ref, bf16[2,256,256]{2,1,0:T(8,128)(2,1)S(1)} %mix.2.mine_ref, bf16[2,256,256]{2,1,0:T(8,128)(2,1)S(1)} %collective-permute-done.13.other_ref, bf16[4,512,512]{2,1,0:T(8,128)(2,1)} %copy-done.1), custom_call_target="tpu_custom_call" | custom-call | flops 1073741824 | bytes 5000000 | tf_op jit(solution)/shard_map/project_out/pallas_call | solution.py:282
  125.3 1.5 mix.3.mine_ref
  126.8 1.5 collective-permute-done.14.other_ref
  128.4 5.2 %project_out.3 = bf16[2,4,256,512]{3,2,1,0:T(8,128)(2,1)} custom-call(s32[10]{0:T(128)S(1)} %pad_add_fusion.at_ref, bf16[2,256,256]{2,1,0:T(8,128)(2,1)S(1)} %mix.3.mine_ref, bf16[2,256,256]{2,1,0:T(8,128)(2,1)S(1)} %collective-permute-done.14.other_ref, bf16[4,512,512]{2,1,0:T(8,128)(2,1)} %copy-done.1), custom_call_target="tpu_custom_call" | custom-call | flops 1073741824 | bytes 5000000 | tf_op jit(solution)/shard_map/project_out/pallas_call | solution.py:282
  133.6 1.5 copy-done.4
  135.2 3.7 %collective-permute-start.15 = (bf16[128,512]{1,0:T(8,128)(2,1)S(1)}, bf16[128,512]{1,0:T(8,128)(2,1)S(1)}, u32[]{:S(2)}, u32[]{:S(2)}) collective-permute-start(bf16[128,512]{1,0:T(8,128)(2,1)S(1)} %get-tuple-element.47), channel_id=1, source_target_pairs={{0,2},{2,4},{4,6},{6,32},{32,34},{34,36},{36,38},{38,0},{1,3},{3,5... | collective-permute-start | bytes 393224 | tf_op jit(solution)/shard_map/ppermute | solution.py:329
  138.9 2.0 %collective-permute-start.19 = (bf16[128,512]{1,0:T(8,128)(2,1)S(1)}, bf16[128,512]{1,0:T(8,128)(2,1)S(1)}, u32[]{:S(2)}, u32[]{:S(2)}) collective-permute-start(bf16[128,512]{1,0:T(8,128)(2,1)S(1)} %get-tuple-element.49), channel_id=1, source_target_pairs={{0,38},{2,0},{4,2},{6,4},{32,6},{34,32},{36,34},{38,36},{1,39},{3,... | collective-permute-start | bytes 393224 | tf_op jit(solution)/shard_map/ppermute | solution.py:330
  140.9 3.7 %collective-permute-done.15 = bf16[128,512]{1,0:T(8,128)(2,1)S(1)} collective-permute-done((bf16[128,512]{1,0:T(8,128)(2,1)S(1)}, bf16[128,512]{1,0:T(8,128)(2,1)S(1)}, u32[]{:S(2)}, u32[]{:S(2)}) %collective-permute-start.15) | collective-permute-done | bytes 131104 | tf_op jit(solution)/shard_map/ppermute | solution.py:329
  145.4 2.8 %collective-permute-start.20 = (bf16[256,512]{1,0:T(8,128)(2,1)S(1)}, bf16[256,512]{1,0:T(8,128)(2,1)S(1)}, u32[]{:S(2)}, u32[]{:S(2)}) collective-permute-start(bf16[256,512]{1,0:T(8,128)(2,1)S(1)} %pad_maximum_fusion.8), channel_id=1, source_target_pairs={{0,38},{2,0},{4,2},{6,4},{32,6},{34,32},{36,34},{38,36},{1,39},{3,... | collective-permute-start | bytes 786440 | tf_op jit(solution)/shard_map/ppermute | solution.py:336
  148.1 11.4 %collective-permute-done.16 = bf16[256,512]{1,0:T(8,128)(2,1)S(1)} collective-permute-done((bf16[256,512]{1,0:T(8,128)(2,1)S(1)}, bf16[256,512]{1,0:T(8,128)(2,1)S(1)}, u32[]{:S(2)}, u32[]{:S(2)}) %collective-permute-start.16) | collective-permute-done | bytes 262176 | tf_op jit(solution)/shard_map/ppermute | solution.py:335
  159.5 0.8 fusion.7
  160.3 15.1 %collective-permute-done.17 = bf16[256,512]{1,0:T(8,128)(2,1)S(1)} collective-permute-done((bf16[256,512]{1,0:T(8,128)(2,1)}, bf16[256,512]{1,0:T(8,128)(2,1)S(1)}, u32[]{:S(2)}, u32[]{:S(2)}) %collective-permute-start.17) | collective-permute-done | bytes 262176 | tf_op jit(solution)/shard_map/ppermute | solution.py:335
  175.4 0.8 fusion.8
  176.2 0.8 collective-permute-start.21
  177.0 1.3 collective-permute-start.18
  178.3 6.1 %collective-permute-done.21 = bf16[256,512]{1,0:T(8,128)(2,1)} collective-permute-done((bf16[256,512]{1,0:T(8,128)(2,1)}, bf16[256,512]{1,0:T(8,128)(2,1)}, u32[]{:S(2)}, u32[]{:S(2)}) %collective-permute-start.21) | collective-permute-done | bytes 262176 | tf_op jit(solution)/shard_map/ppermute | solution.py:336
  184.4 1.0 fusion.6
  185.4 2.5 %collective-permute-start.22 = (bf16[256,512]{1,0:T(8,128)(2,1)S(1)}, bf16[256,512]{1,0:T(8,128)(2,1)}, u32[]{:S(2)}, u32[]{:S(2)}) collective-permute-start(bf16[256,512]{1,0:T(8,128)(2,1)S(1)} %fusion.6), channel_id=1, source_target_pairs={{0,38},{2,0},{4,2},{6,4},{32,6},{34,32},{36,34},{38,36},{1,39},{3,... | collective-permute-start | bytes 786440 | tf_op jit(solution)/shard_map/ppermute | solution.py:337
  187.9 4.3 %collective-permute-done.22 = bf16[256,512]{1,0:T(8,128)(2,1)} collective-permute-done((bf16[256,512]{1,0:T(8,128)(2,1)S(1)}, bf16[256,512]{1,0:T(8,128)(2,1)}, u32[]{:S(2)}, u32[]{:S(2)}) %collective-permute-start.22) | collective-permute-done | bytes 262176 | tf_op jit(solution)/shard_map/ppermute | solution.py:337
  192.2 1.0 fusion.9
  193.3 1.0 bitcast_convert_fusion
  194.3 1.0 fusion.3
  (76 shorter events, 5.0 us)
Async XLA Ops:
  6.5 65.7 %copy-start = (f32[3,3,512]{2,1,0:T(4,128)S(1)}, f32[3,3,512]{2,1,0:T(4,128)}, u32[]{:S(2)}) copy-start(f32[3,3,512]{2,1,0:T(4,128)} %param.14) | copy-start | bytes 55300
  6.5 4.1 %copy-start.7 = (bf16[512,128]{1,0:T(8,128)(2,1)S(1)}, bf16[512,128]{1,0:T(8,128)(2,1)}, u32[]{:S(2)}) copy-start(bf16[512,128]{1,0:T(8,128)(2,1)} %param.17) | copy-start | bytes 393220
  6.5 12.0 %copy-start.6 = (bf16[3,128,512]{2,1,0:T(8,128)(2,1)S(1)}, bf16[3,128,512]{2,1,0:T(8,128)(2,1)}, u32[]{:S(2)}) copy-start(bf16[3,128,512]{2,1,0:T(8,128)(2,1)} %param.13) | copy-start | bytes 1179652
  6.5 87.9 %all-gather.3.cloned.1.call-start = ((), (), s32[]{:S(2)}) async-start(), calls=%async_computation.2 | async-start | bytes 10305536 | tf_op jit(solution)/shard_map/all_gather | solution.py:382
  10.6 9.3 %collective-permute-start.2 = (bf16[256,128]{1,0:T(8,128)(2,1)S(1)}, bf16[256,128]{1,0:T(8,128)(2,1)S(1)}, u32[]{:S(2)}, u32[]{:S(2)}) collective-permute-start(bf16[256,128]{1,0:T(8,128)(2,1)S(1)} %get-tuple-element.65), channel_id=1, source_target_pairs={{0,32},{1,0},{32,33},{33,1},{2,34},{3,2},{34,35},{35,3},{4,36},{5,... | collective-permute-start | bytes 196616 | tf_op jit(solution)/shard_map/ppermute | solution.py:379
  17.9 2.1 %collective-permute-start.1 = (bf16[256,128]{1,0:T(8,128)(2,1)S(1)}, bf16[256,128]{1,0:T(8,128)(2,1)S(1)}, u32[]{:S(2)}, u32[]{:S(2)}) collective-permute-start(bf16[256,128]{1,0:T(8,128)(2,1)S(1)} %get-tuple-element.66), channel_id=1, source_target_pairs={{0,0},{1,32},{32,1},{33,33},{2,2},{3,34},{34,3},{35,35},{4,4},{5,3... | collective-permute-start | bytes 196616 | tf_op jit(solution)/shard_map/ppermute | solution.py:379
  18.6 13.0 %collective-permute-start = (bf16[3,128,256]{2,1,0:T(8,128)(2,1)S(1)}, bf16[3,128,256]{2,1,0:T(8,128)(2,1)S(1)}, u32[]{:S(2)}, u32[]{:S(2)}) collective-permute-start(bf16[3,128,256]{2,1,0:T(8,128)(2,1)S(1)} %get-tuple-element.58), channel_id=1, source_target_pairs={{0,32},{32,0},{1,33},{33,1},{2,34},{34,2},{3,35},{35,3},{4,36},{36... | collective-permute-start | bytes 589832 | tf_op jit(solution)/shard_map/ppermute | solution.py:373
  31.6 161.7 %reduce-scatter.2.cloned.1.call-start = ((), (), s32[]{:S(2)}) async-start(), calls=%async_computation.1 | async-start | bytes 2359296 | tf_op jit(solution)/shard_map/reduce_scatter | solution.py:413
  31.7 6.5 %collective-permute-start.7 = (bf16[4,128,256]{2,1,0:T(8,128)(2,1)S(1)}, bf16[4,128,256]{2,1,0:T(8,128)(2,1)S(1)}, u32[]{:S(2)}, u32[]{:S(2)}) collective-permute-start(bf16[4,128,256]{2,1,0:T(8,128)(2,1)S(1)} %constant_dynamic-update-slice_fusion), channel_id=1, source_target_pairs={{0,64},{1,193},{64,0},{65,129},{128,192},{129,65},{192,128},{193,1... | collective-permute-start | bytes 786440 | tf_op jit(solution)/shard_map/ppermute | solution.py:308
  33.4 7.9 %collective-permute-start.3 = (bf16[4,128,256]{2,1,0:T(8,128)(2,1)S(1)}, bf16[4,128,256]{2,1,0:T(8,128)(2,1)S(1)}, u32[]{:S(2)}, u32[]{:S(2)}) collective-permute-start(bf16[4,128,256]{2,1,0:T(8,128)(2,1)S(1)} %get-tuple-element.60), channel_id=1, source_target_pairs={{0,8},{1,25},{8,0},{9,17},{16,24},{17,9},{24,16},{25,1},{2,10},{3,... | collective-permute-start | bytes 786440 | tf_op jit(solution)/shard_map/ppermute | solution.py:308
  38.2 10.5 %collective-permute-start.8 = (bf16[2,4,128,256]{3,2,1,0:T(8,128)(2,1)S(1)}, bf16[2,4,128,256]{3,2,1,0:T(8,128)(2,1)S(1)}, u32[]{:S(2)}, u32[]{:S(2)}) collective-permute-start(bf16[2,4,128,256]{3,2,1,0:T(8,128)(2,1)S(1)} %pad_maximum_fusion.5), channel_id=1, source_target_pairs={{0,192},{1,65},{64,128},{65,1},{128,64},{129,193},{192,0},{193,129... | collective-permute-start | bytes 1572872 | tf_op jit(solution)/shard_map/ppermute | solution.py:308
  41.4 10.0 %collective-permute-start.4 = (bf16[2,4,128,256]{3,2,1,0:T(8,128)(2,1)S(1)}, bf16[2,4,128,256]{3,2,1,0:T(8,128)(2,1)S(1)}, u32[]{:S(2)}, u32[]{:S(2)}) collective-permute-start(bf16[2,4,128,256]{3,2,1,0:T(8,128)(2,1)S(1)} %pad_maximum_fusion.4), channel_id=1, source_target_pairs={{0,24},{1,9},{8,16},{9,1},{16,8},{17,25},{24,0},{25,17},{2,26},{3,... | collective-permute-start | bytes 1572872 | tf_op jit(solution)/shard_map/ppermute | solution.py:308
  48.9 14.9 %collective-permute-start.9 = (bf16[4,4,128,256]{3,2,1,0:T(8,128)(2,1)S(1)}, bf16[4,4,128,256]{3,2,1,0:T(8,128)(2,1)S(1)}, u32[]{:S(2)}, u32[]{:S(2)}) collective-permute-start(bf16[4,4,128,256]{3,2,1,0:T(8,128)(2,1)S(1)} %get-tuple-element.52), channel_id=1, source_target_pairs={{0,8},{1,25},{8,0},{9,17},{16,24},{17,9},{24,16},{25,1},{2,10},{3,... | collective-permute-start | bytes 3145736 | tf_op jit(solution)/shard_map/ppermute | solution.py:308
  51.6 15.2 %collective-permute-start.5 = (bf16[4,4,128,256]{3,2,1,0:T(8,128)(2,1)S(1)}, bf16[4,4,128,256]{3,2,1,0:T(8,128)(2,1)S(1)}, u32[]{:S(2)}, u32[]{:S(2)}) collective-permute-start(bf16[4,4,128,256]{3,2,1,0:T(8,128)(2,1)S(1)} %get-tuple-element.54), channel_id=1, source_target_pairs={{0,64},{1,193},{64,0},{65,129},{128,192},{129,65},{192,128},{193,1... | collective-permute-start | bytes 3145736 | tf_op jit(solution)/shard_map/ppermute | solution.py:308
  65.3 26.4 %collective-permute-start.10 = (bf16[2,4,4,128,256]{4,3,2,1,0:T(8,128)(2,1)}, bf16[2,4,4,128,256]{4,3,2,1,0:T(8,128)(2,1)}, u32[]{:S(2)}, u32[]{:S(2)}) collective-permute-start(bf16[2,4,4,128,256]{4,3,2,1,0:T(8,128)(2,1)} %pad_maximum_fusion.1.refs_2_), channel_id=1, source_target_pairs={{0,24},{1,9},{8,16},{9,1},{16,8},{17,25},{24,0},{25,17},{2,26},{3,... | collective-permute-start | bytes 6291464 | tf_op jit(solution)/shard_map/ppermute | solution.py:308
  66.8 4.7 %copy-start.8 = (bf16[32,128]{1,0:T(8,128)(2,1)S(1)}, bf16[32,128]{1,0:T(8,128)(2,1)}, u32[]{:S(2)}) copy-start(bf16[32,128]{1,0:T(8,128)(2,1)} %param.15) | copy-start | bytes 24580
  66.8 5.3 %copy-start.11 = (f32[512]{0:T(512)S(1)}, f32[512]{0:T(512)}, u32[]{:S(2)}) copy-start(f32[512]{0:T(512)} %param.16) | copy-start | bytes 6148
  66.8 5.4 %copy-start.9 = (s32[4]{0:T(128)S(1)}, s32[4]{0:T(128)}, u32[]{:S(2)}) copy-start(s32[4]{0:T(128)} %constant.114.clone) | copy-start | bytes 52
  66.8 5.4 %copy-start.10 = (s32[4]{0:T(128)S(1)}, s32[4]{0:T(128)}, u32[]{:S(2)}) copy-start(s32[4]{0:T(128)} %constant.115.clone) | copy-start | bytes 52
  67.0 27.4 %collective-permute-start.6 = (bf16[2,4,4,128,256]{4,3,2,1,0:T(8,128)(2,1)S(1)}, bf16[2,4,4,128,256]{4,3,2,1,0:T(8,128)(2,1)}, u32[]{:S(2)}, u32[]{:S(2)}) collective-permute-start(bf16[2,4,4,128,256]{4,3,2,1,0:T(8,128)(2,1)S(1)} %pad_maximum_fusion.refs_0_), channel_id=1, source_target_pairs={{0,192},{1,65},{64,128},{65,1},{128,64},{129,193},{192,0},{193,129... | collective-permute-start | bytes 6291464 | tf_op jit(solution)/shard_map/ppermute | solution.py:308
  70.1 1.3 copy-start.2
  94.4 1.6 copy-start.3
  111.3 1.4 copy-start.1
  114.2 5.9 %collective-permute-start.13 = (bf16[2,256,256]{2,1,0:T(8,128)(2,1)S(1)}, bf16[2,256,256]{2,1,0:T(8,128)(2,1)S(1)}, u32[]{:S(2)}, u32[]{:S(2)}) collective-permute-start(bf16[2,256,256]{2,1,0:T(8,128)(2,1)S(1)} %mix.2.mine_ref), channel_id=1, source_target_pairs={{0,1},{1,0},{2,3},{3,2},{4,5},{5,4},{6,7},{7,6},{8,9},{9,8},{10,11... | collective-permute-start | bytes 786440 | tf_op jit(solution)/shard_map/ppermute | solution.py:405
  114.5 10.7 %collective-permute-start.11 = (bf16[144,256]{1,0:T(8,128)(2,1)S(1)}, bf16[144,256]{1,0:T(8,128)(2,1)S(1)}, u32[]{:S(2)}, u32[]{:S(2)}) collective-permute-start(bf16[144,256]{1,0:T(8,128)(2,1)S(1)} %get-tuple-element.62), channel_id=1, source_target_pairs={{0,8},{8,16},{16,24},{24,64},{64,72},{72,80},{80,88},{88,128},{128... | collective-permute-start | bytes 221192 | tf_op jit(solution)/shard_map/ppermute | solution.py:400
  117.8 7.4 %collective-permute-start.12 = (bf16[144,256]{1,0:T(8,128)(2,1)S(1)}, bf16[144,256]{1,0:T(8,128)(2,1)S(1)}, u32[]{:S(2)}, u32[]{:S(2)}) collective-permute-start(bf16[144,256]{1,0:T(8,128)(2,1)S(1)} %get-tuple-element.61), channel_id=1, source_target_pairs={{0,8},{8,16},{16,24},{24,0},{64,72},{72,80},{80,88},{88,64},{128,1... | collective-permute-start | bytes 221192 | tf_op jit(solution)/shard_map/ppermute | solution.py:401
  126.7 1.6 collective-permute-start.14
  133.6 1.6 copy-start.4
  135.2 9.4 %collective-permute-start.15 = (bf16[128,512]{1,0:T(8,128)(2,1)S(1)}, bf16[128,512]{1,0:T(8,128)(2,1)S(1)}, u32[]{:S(2)}, u32[]{:S(2)}) collective-permute-start(bf16[128,512]{1,0:T(8,128)(2,1)S(1)} %get-tuple-element.47), channel_id=1, source_target_pairs={{0,2},{2,4},{4,6},{6,32},{32,34},{34,36},{36,38},{38,0},{1,3},{3,5... | collective-permute-start | bytes 393224 | tf_op jit(solution)/shard_map/ppermute | solution.py:329
  138.9 5.7 %collective-permute-start.19 = (bf16[128,512]{1,0:T(8,128)(2,1)S(1)}, bf16[128,512]{1,0:T(8,128)(2,1)S(1)}, u32[]{:S(2)}, u32[]{:S(2)}) collective-permute-start(bf16[128,512]{1,0:T(8,128)(2,1)S(1)} %get-tuple-element.49), channel_id=1, source_target_pairs={{0,38},{2,0},{4,2},{6,4},{32,6},{34,32},{36,34},{38,36},{1,39},{3,... | collective-permute-start | bytes 393224 | tf_op jit(solution)/shard_map/ppermute | solution.py:330
  144.7 14.8 %collective-permute-start.16 = (bf16[256,512]{1,0:T(8,128)(2,1)S(1)}, bf16[256,512]{1,0:T(8,128)(2,1)S(1)}, u32[]{:S(2)}, u32[]{:S(2)}) collective-permute-start(bf16[256,512]{1,0:T(8,128)(2,1)S(1)} %pad_maximum_fusion.7), channel_id=1, source_target_pairs={{0,2},{2,4},{4,6},{6,32},{32,34},{34,36},{36,38},{38,0},{1,3},{3,5... | collective-permute-start | bytes 786440 | tf_op jit(solution)/shard_map/ppermute | solution.py:335
  145.4 14.9 %collective-permute-start.20 = (bf16[256,512]{1,0:T(8,128)(2,1)S(1)}, bf16[256,512]{1,0:T(8,128)(2,1)S(1)}, u32[]{:S(2)}, u32[]{:S(2)}) collective-permute-start(bf16[256,512]{1,0:T(8,128)(2,1)S(1)} %pad_maximum_fusion.8), channel_id=1, source_target_pairs={{0,38},{2,0},{4,2},{6,4},{32,6},{34,32},{36,34},{38,36},{1,39},{3,... | collective-permute-start | bytes 786440 | tf_op jit(solution)/shard_map/ppermute | solution.py:336
  160.3 15.1 %collective-permute-start.17 = (bf16[256,512]{1,0:T(8,128)(2,1)}, bf16[256,512]{1,0:T(8,128)(2,1)S(1)}, u32[]{:S(2)}, u32[]{:S(2)}) collective-permute-start(bf16[256,512]{1,0:T(8,128)(2,1)} %fusion.7), channel_id=1, source_target_pairs={{0,2},{2,4},{4,6},{6,32},{32,34},{34,36},{36,38},{38,0},{1,3},{3,5... | collective-permute-start | bytes 786440 | tf_op jit(solution)/shard_map/ppermute | solution.py:335
  160.3 34.1 %copy-start.5 = (bf16[512,512]{1,0:T(8,128)(2,1)S(1)}, bf16[512,512]{1,0:T(8,128)(2,1)}, u32[]{:S(2)}) copy-start(bf16[512,512]{1,0:T(8,128)(2,1)} %param.10) | copy-start | bytes 1572868
  176.2 8.2 %collective-permute-start.21 = (bf16[256,512]{1,0:T(8,128)(2,1)}, bf16[256,512]{1,0:T(8,128)(2,1)}, u32[]{:S(2)}, u32[]{:S(2)}) collective-permute-start(bf16[256,512]{1,0:T(8,128)(2,1)} %get-tuple-element.44), channel_id=1, source_target_pairs={{0,38},{2,0},{4,2},{6,4},{32,6},{34,32},{36,34},{38,36},{1,39},{3,... | collective-permute-start | bytes 786440 | tf_op jit(solution)/shard_map/ppermute | solution.py:336
  177.0 10.9 %collective-permute-start.18 = (bf16[256,512]{1,0:T(8,128)(2,1)S(1)}, bf16[256,512]{1,0:T(8,128)(2,1)S(1)}, u32[]{:S(2)}, u32[]{:S(2)}) collective-permute-start(bf16[256,512]{1,0:T(8,128)(2,1)S(1)} %get-tuple-element.43), channel_id=1, source_target_pairs={{0,2},{2,4},{4,6},{6,32},{32,34},{34,36},{36,38},{38,0},{1,3},{3,5... | collective-permute-start | bytes 786440 | tf_op jit(solution)/shard_map/ppermute | solution.py:337
  185.4 6.8 %collective-permute-start.22 = (bf16[256,512]{1,0:T(8,128)(2,1)S(1)}, bf16[256,512]{1,0:T(8,128)(2,1)}, u32[]{:S(2)}, u32[]{:S(2)}) collective-permute-start(bf16[256,512]{1,0:T(8,128)(2,1)S(1)} %fusion.6), channel_id=1, source_target_pairs={{0,38},{2,0},{4,2},{6,4},{32,6},{34,32},{36,34},{38,36},{1,39},{3,... | collective-permute-start | bytes 786440 | tf_op jit(solution)/shard_map/ppermute | solution.py:337
Sparse Core Ops, SparseCore 0:
  31.8 62.3 all-gather.2
  133.7 48.9 reduce-scatter.1

commit v11 on v9

--- a/solution.py
+++ b/solution.py
@@ -59,13 +59,11 @@
                 y, x = (i, j) if k == 0 else (j, i)
                 start = at_ref[y] * WIDE + at_ref[4 + x] * 128
                 rows = pl.ds(pl.multiple_of(start, 128), 128)
-                for s in range(3):
-                    source = refs[2 * k + i // 2].at[i % 2, j, s]
-                    place = wide.at[k, rows, pl.ds(s * CH, CH)]
-                    copies.append(pltpu.make_async_copy(source, place, sems.at[k, i, j, s]))
+                source = refs[2 * k + i // 2].at[i % 2, j, :, pl.ds(0, 3 * CH)]
+                copies.append(pltpu.make_async_copy(source, wide.at[k, rows], sems.at[k, i, j]))
                 lanes = pl.ds(pl.multiple_of(at_ref[4 + x] * 128, 128), 128)
                 for part in range(2):
-                    source = refs[2 * k + i // 2].at[i % 2, j, 3, :, pl.ds(part * 128, 128)]
+                    source = refs[2 * k + i // 2].at[i % 2, j, :, pl.ds(3 * CH + part * 128, 128)]
                     place = out_w_ref.at[at_ref[y], pl.ds(k * CH + part * 128, 128), lanes]
                     sem = out_sems.at[k, i, j, part]
                     out_copies.append(pltpu.make_async_copy(source, place, sem))
@@ -76,8 +74,6 @@
         for copies in turns:
             for copy in copies:
                 copy.start()
-        for copy in out_copies:
-            copy.start()
 
     for k in range(2):
 
@@ -85,6 +81,11 @@
         def _(k=k):
             for copy in turns[k]:
                 copy.wait()
+
+    @pl.when(first_row & (kind == 1))
+    def _():
+        for copy in out_copies:
+            copy.start()
 
     features = jnp.concatenate([x_ref[0, y, 0] for y in range(4)], axis=1)
     products = jnp.dot(features, wide[kind], preferred_element_type=F32)
@@ -151,14 +152,14 @@
                 pl.BlockSpec((1, HALO, CH), lambda h, k, at: (h, 0, 0)),
                 pl.BlockSpec((1, HALO, CH), lambda h, k, at: (h, 0, 0)),
                 pl.BlockSpec((HALO, CH), lambda h, k, at: (0, 0)),
-                pl.BlockSpec(memory_space=pl.ANY),
+                pl.BlockSpec(memory_space=pltpu.HBM),
             ],
             scratch_shapes=[
                 pltpu.VMEM((2, 4 * WIDE, 3 * CH), BF16),
                 pltpu.VMEM((ROWS + TILE, 3 * CH), F32),
                 pltpu.VMEM((8, WIDE), F32),
                 pltpu.VMEM((3, SHARE + TILE, CH), F32),
-                pltpu.SemaphoreType.DMA((2, 4, 4, 3)),
+                pltpu.SemaphoreType.DMA((2, 4, 4)),
                 pltpu.SemaphoreType.DMA((2, 4, 4, 2)),
             ],
         ),
@@ -169,7 +170,7 @@
             jax.ShapeDtypeStruct((HALO, CH), BF16),
             jax.ShapeDtypeStruct((4, 2 * CH, WIDE), BF16),
         ],
-        compiler_params=pltpu.CompilerParams(vmem_limit_bytes=46 * MIB),
+        compiler_params=pltpu.CompilerParams(vmem_limit_bytes=42 * MIB),
         cost_estimate=pl.CostEstimate(
             flops=2 * 2 * ROWS * 4096 * 3 * CH, bytes_accessed=18_000_000, transcendentals=0
         ),
@@ -296,7 +297,7 @@
         ),
         out_shape=jax.ShapeDtypeStruct((2, 4, ROWS, WIDE), BF16),
         input_output_aliases={} if base is None else {4: 0},
-        compiler_params=pltpu.CompilerParams(vmem_limit_bytes=52 * MIB),
+        compiler_params=pltpu.CompilerParams(vmem_limit_bytes=50 * MIB),
         cost_estimate=pl.CostEstimate(
             flops=2 * 512 * 2 * CH * 2048, bytes_accessed=5_000_000, transcendentals=0
         ),
@@ -348,7 +349,10 @@
         axis=0,
     )
 
-    left, right = in_weight[..., :CH], in_weight[..., CH:]
+    left, right = (
+        jnp.concatenate([in_weight[s, :, part * CH : (part + 1) * CH] for s in range(3)], axis=1)
+        for part in range(2)
+    )
     kept = jnp.where(zh == 0, left, right)
     got = lax.ppermute(jnp.where(zh == 0, right, left), "zh", [(0, 1), (1, 0)])
     pieces = []
@@ -356,11 +360,11 @@
         chosen = lax.dynamic_slice_in_dim(out_weight, (core ^ k) * CH, CH, 0)
         pairs = [(a * 2 + b, (b ^ k) * 2 + a) for a in range(2) for b in range(2)]
         chosen = lax.ppermute(chosen, ("zh", "c"), pairs)
-        pieces.append(jnp.concatenate([chosen[:128], chosen[128:]], axis=1)[None])
+        pieces.append(jnp.concatenate([chosen[:128], chosen[128:]], axis=1))
     own, got, pieces = lax.optimization_barrier((own, got, pieces))
     gathered = lax.all_gather(own, ring).reshape(2, 4, 2, ROWS + TILE, WIDE)
-    kept = jnp.concatenate([kept, pieces[0]], axis=0)
-    got = jnp.concatenate([got, pieces[1]], axis=0)
+    kept = jnp.concatenate([kept, pieces[0]], axis=1)
+    got = jnp.concatenate([got, pieces[1]], axis=1)
     weights = (
         *ring_pairs(jnp.concatenate(ring_pairs(kept, "x"), axis=0), "y"),
         *ring_pairs(jnp.concatenate(ring_pairs(got, "y"), axis=0), "x"),

time: 197 us -> 195 us (0.990)
  waiting for transfers between devices: 112 us -> 115 us
  Pallas kernels: 29.1 us -> 26.7 us
    ppermute x8, waiting for transfers between devices: 46.3 us -> 49.7 us  [pair_step(): return lax.ppermute(value, (axis, 'c'), pairs)]
    pallas_call x2, Pallas kernels: 10.4 us -> 8.11 us  [project_out(): pl.pallas_call(out_kernel, grid_spec=pltpu.PrefetchScalarGridSpec(num_sca...]
    unnamed x21 -> x27, local copies, waits for them, and re-layouts: 4.35 us -> 2.81 us
  transfers between devices with their start and end apart: 17 -> 17, of which waited for: 9 -> 10; matrix products, arithmetic and copies ran while one was open for 3% -> 3% of each run, Pallas kernels for 3% -> 3%
where the time goes in v11:
time: 195 us; the launch traced here: 194 us
  waiting for transfers between devices  115 us (59%)
  Pallas kernels  26.7 us (14%)
  starting transfers between devices  26.4 us (14%)
  between operations  13.7 us (7%)
  other arithmetic  7.15 us (4%)
  local copies, waits for them, and re-layouts  5.06 us (3%)
    reduce_scatter x1, waiting for transfers between devices, on_device(): lax.psum_scatter(partial.reshape(8, ROWS, WIDE), ('zh', 'zl'), scatter_di...  54.3 us
    ppermute x8, waiting for transfers between devices, pair_step(): return lax.ppermute(value, (axis, 'c'), pairs)  49.7 us
    pallas_call x1, Pallas kernels, project(): pl.pallas_call(project_kernel, grid_spec=pltpu.PrefetchScalarGridSpec(num...  15.2 us
    ppermute x8, starting transfers between devices, pair_step(): return lax.ppermute(value, (axis, 'c'), pairs)  11.1 us
    ppermute x1, waiting for transfers between devices, on_device(): got = lax.ppermute(jnp.where(zh == 0, right, left), 'zh', [(0, 1), (1, 0)])  9.51 us
    pallas_call x2, Pallas kernels, project_out(): pl.pallas_call(out_kernel, grid_spec=pltpu.PrefetchScalarGridSpec(num_sca...  8.11 us
    ppermute x2, starting transfers between devices, on_device(): chosen = lax.ppermute(chosen, ('zh', 'c'), pairs)  7.93 us
  transfers between devices with their start and end apart: 17, of which 10 were waited for; matrix products, arithmetic and copies ran while one was open for 3% of the time, Pallas kernels for 3%

profile of v11, /device:TPU:2, one launch (start us, length us, event | category | flops | bytes accessed | tf_op | source)
XLA Modules:
  0.0 194.1 jit_solution(5402118842917185824)
XLA Ops:
  6.6 0.9 constant_dynamic-slice_fusion.1
  7.5 7.3 %collective-permute-start.2 = (bf16[256,128]{1,0:T(8,128)(2,1)S(1)}, bf16[256,128]{1,0:T(8,128)(2,1)S(1)}, u32[]{:S(2)}, u32[]{:S(2)}) collective-permute-start(bf16[256,128]{1,0:T(8,128)(2,1)S(1)} %get-tuple-element.59), channel_id=1, source_target_pairs={{0,32},{1,0},{32,33},{33,1},{2,34},{3,2},{34,35},{35,3},{4,36},{5,... | collective-permute-start | bytes 196616 | tf_op jit(solution)/shard_map/ppermute | solution.py:362
  14.8 0.7 collective-permute-start.1
  15.5 1.0 slice_bitcast_fusion.5
  16.6 1.4 collective-permute-start
  17.9 0.7 convert_element_type.41
  18.6 0.2 fusion.1
  18.8 0.1 fusion.5
  19.0 0.9 fusion.4
  20.0 9.5 %collective-permute-done = bf16[128,768]{1,0:T(8,128)(2,1)S(1)} collective-permute-done((bf16[128,768]{1,0:T(8,128)(2,1)S(1)}, bf16[128,768]{1,0:T(8,128)(2,1)S(1)}, u32[]{:S(2)}, u32[]{:S(2)}) %collective-permute-start) | collective-permute-done | bytes 196640 | tf_op jit(solution)/shard_map/ppermute | solution.py:357
  29.6 1.7 collective-permute-start.7
  31.3 0.6 collective-permute-start.3
  31.9 4.1 %collective-permute-done.7 = bf16[128,1024]{1,0:T(8,128)(2,1)S(1)} collective-permute-done((bf16[128,1024]{1,0:T(8,128)(2,1)S(1)}, bf16[128,1024]{1,0:T(8,128)(2,1)S(1)}, u32[]{:S(2)}, u32[]{:S(2)}) %collective-permute-start.7) | collective-permute-done | bytes 262176 | tf_op jit(solution)/shard_map/ppermute | solution.py:313
  36.1 3.1 %collective-permute-start.8 = (bf16[2,128,1024]{2,1,0:T(8,128)(2,1)S(1)}, bf16[2,128,1024]{2,1,0:T(8,128)(2,1)S(1)}, u32[]{:S(2)}, u32[]{:S(2)}) collective-permute-start(bf16[2,128,1024]{2,1,0:T(8,128)(2,1)S(1)} %pad_maximum_fusion.5), channel_id=1, source_target_pairs={{0,192},{1,65},{64,128},{65,1},{128,64},{129,193},{192,0},{193,129... | collective-permute-start | bytes 1572872 | tf_op jit(solution)/shard_map/ppermute | solution.py:313
  39.3 1.6 collective-permute-start.4
  40.8 5.7 %collective-permute-done.8 = bf16[2,128,1024]{2,1,0:T(8,128)(2,1)S(1)} collective-permute-done((bf16[2,128,1024]{2,1,0:T(8,128)(2,1)S(1)}, bf16[2,128,1024]{2,1,0:T(8,128)(2,1)S(1)}, u32[]{:S(2)}, u32[]{:S(2)}) %collective-permute-start.8) | collective-permute-done | bytes 524320 | tf_op jit(solution)/shard_map/ppermute | solution.py:313
  46.6 0.1 fusion.11
  46.7 0.4 collective-permute-start.9
  47.1 2.2 %collective-permute-done.4 = bf16[2,128,1024]{2,1,0:T(8,128)(2,1)S(1)} collective-permute-done((bf16[2,128,1024]{2,1,0:T(8,128)(2,1)S(1)}, bf16[2,128,1024]{2,1,0:T(8,128)(2,1)S(1)}, u32[]{:S(2)}, u32[]{:S(2)}) %collective-permute-start.4) | collective-permute-done | bytes 524320 | tf_op jit(solution)/shard_map/ppermute | solution.py:313
  49.3 0.1 fusion.12
  49.5 0.1 collective-permute-start.5
  49.6 12.1 %collective-permute-done.9 = bf16[4,128,1024]{2,1,0:T(8,128)(2,1)S(1)} collective-permute-done((bf16[4,128,1024]{2,1,0:T(8,128)(2,1)S(1)}, bf16[4,128,1024]{2,1,0:T(8,128)(2,1)S(1)}, u32[]{:S(2)}, u32[]{:S(2)}) %collective-permute-start.9) | collective-permute-done | bytes 1048608 | tf_op jit(solution)/shard_map/ppermute | solution.py:313
  61.6 0.2 pad_maximum_fusion.1.refs_2_
  61.8 1.6 collective-permute-start.10
  63.4 0.9 collective-permute-done.5
  64.4 1.5 pad_maximum_fusion.refs_0_
  65.8 2.1 %collective-permute-start.6 = (bf16[2,4,128,1024]{3,2,1,0:T(8,128)(2,1)}, bf16[2,4,128,1024]{3,2,1,0:T(8,128)(2,1)}, u32[]{:S(2)}, u32[]{:S(2)}) collective-permute-start(bf16[2,4,128,1024]{3,2,1,0:T(8,128)(2,1)} %pad_maximum_fusion.refs_0_), channel_id=1, source_target_pairs={{0,192},{1,65},{64,128},{65,1},{128,64},{129,193},{192,0},{193,129... | collective-permute-start | bytes 6291464 | tf_op jit(solution)/shard_map/ppermute | solution.py:313
  67.9 0.1 rev.4
  68.0 0.1 pad.19.u_ref
  68.1 0.5 toeplitz.1.band_ref
  68.6 0.1 dynamic_slice.23
  68.7 0.1 pad_add_fusion.at_ref
  68.8 19.3 %collective-permute-done.10.refs_3_ = bf16[2,4,128,1024]{3,2,1,0:T(8,128)(2,1)} collective-permute-done((bf16[2,4,128,1024]{3,2,1,0:T(8,128)(2,1)S(1)}, bf16[2,4,128,1024]{3,2,1,0:T(8,128)(2,1)}, u32[]{:S(2)}, u32[]{:S(2)}) %collective-permute-start.10) | collective-permute-done | bytes 2097184 | tf_op jit(solution)/shard_map/ppermute | solution.py:313
  88.0 5.3 %collective-permute-done.6.refs_1_ = bf16[2,4,128,1024]{3,2,1,0:T(8,128)(2,1)} collective-permute-done((bf16[2,4,128,1024]{3,2,1,0:T(8,128)(2,1)}, bf16[2,4,128,1024]{3,2,1,0:T(8,128)(2,1)}, u32[]{:S(2)}, u32[]{:S(2)}) %collective-permute-start.6) | collective-permute-done | bytes 2097184 | tf_op jit(solution)/shard_map/ppermute | solution.py:313
  93.4 1.6 copy-done.4
  95.0 15.2 %project.1 = (bf16[3,2,512,256]{3,2,1,0:T(8,128)(2,1)S(1)}, bf16[2,144,256]{2,1,0:T(8,128)(2,1)S(1)}, bf16[2,144,256]{2,1,0:T(8,128)(2,1)S(1)}, bf16[144,256]{1,0:T(8,128)(2,1)S(1)}, bf16[4,512,512]{2,1,0:T(8,128)(2,1)S(1)}) custom-call(s32[10]{0:T(128)S(1)} %pad_add_fusion.at_ref, bf16[2,4,2,592,512]{4,3,2,1,0:T(8,128)(2,1)} %bitcast.54, ...), custom_call_target="tpu_custom_call" | custom-call | flops 6442450944 | bytes 18000000 | tf_op jit(solution)/shard_map/project/pallas_call | solution.py:137
  110.2 1.5 mix.2.mine_ref
  111.7 1.2 copy-done.1
  112.9 0.9 select_bitcast_fusion.1
  113.8 3.4 %collective-permute-start.11 = (bf16[144,256]{1,0:T(8,128)(2,1)S(1)}, bf16[144,256]{1,0:T(8,128)(2,1)S(1)}, u32[]{:S(2)}, u32[]{:S(2)}) collective-permute-start(bf16[144,256]{1,0:T(8,128)(2,1)S(1)} %get-tuple-element.56), channel_id=1, source_target_pairs={{0,8},{8,16},{16,24},{24,64},{64,72},{72,80},{80,88},{88,128},{128... | collective-permute-start | bytes 221192 | tf_op jit(solution)/shard_map/ppermute | solution.py:383
  117.2 2.5 %collective-permute-start.12 = (bf16[144,256]{1,0:T(8,128)(2,1)S(1)}, bf16[144,256]{1,0:T(8,128)(2,1)S(1)}, u32[]{:S(2)}, u32[]{:S(2)}) collective-permute-start(bf16[144,256]{1,0:T(8,128)(2,1)S(1)} %get-tuple-element.55), channel_id=1, source_target_pairs={{0,8},{8,16},{16,24},{24,0},{64,72},{72,80},{80,88},{88,64},{128,1... | collective-permute-start | bytes 221192 | tf_op jit(solution)/shard_map/ppermute | solution.py:384
  119.7 4.5 %project_out.2.refs_0_ = bf16[2,4,512,512]{3,2,1,0:T(8,128)(2,1)} custom-call(s32[10]{0:T(128)S(1)} %pad_add_fusion.at_ref, bf16[2,256,256]{2,1,0:T(8,128)(2,1)S(1)} %mix.2.mine_ref, bf16[2,256,256]{2,1,0:T(8,128)(2,1)} %collective-permute-done.13.other_ref, bf16[4,512,512]{2,1,0:T(8,128)(2,1)S(1)} %get-tuple-element.35.w_ref), custom_call_target="tpu_custom_call" | custom-call | flops 1073741824 | bytes 5000000 | tf_op jit(solution)/shard_map/project_out/pallas_call | solution.py:285
  124.3 1.4 mix.3.mine_ref
  125.8 0.1 collective-permute-start.14
  125.9 1.5 collective-permute-done.14.other_ref
  127.4 3.6 %project_out.3 = bf16[2,4,512,512]{3,2,1,0:T(8,128)(2,1)} custom-call(s32[10]{0:T(128)S(1)} %pad_add_fusion.at_ref, bf16[2,256,256]{2,1,0:T(8,128)(2,1)S(1)} %mix.3.mine_ref, bf16[2,256,256]{2,1,0:T(8,128)(2,1)S(1)} %collective-permute-done.14.other_ref, bf16[4,512,512]{2,1,0:T(8,128)(2,1)S(1)} %get-tuple-element.35.w_ref, ...), custom_call_target="tpu_custom_call", output_to_operand_aliasing={{}: (4, {})} | custom-call | flops 1073741824 | bytes 5000000 | tf_op jit(solution)/shard_map/project_out/pallas_call | solution.py:285
  131.0 54.3 %reduce-scatter.2.cloned.1.call-done = bf16[1,512,512]{2,1,0:T(8,128)(2,1)} async-done(((bf16[8,512,512]{2,1,0:T(8,128)(2,1)}), bf16[1,512,512]{2,1,0:T(8,128)(2,1)}) %reduce-scatter.2.cloned.1.call-update) | async-done | bytes 524304 | tf_op jit(solution)/shard_map/reduce_scatter | solution.py:396
  185.3 2.0 %fusion.3 = bf16[512,512]{1,0:T(8,128)(2,1)} fusion(bf16[512,512]{1,0:T(8,128)(2,1)S(1)} %copy-done.7, bf16[1,512,512]{2,1,0:T(8,128)(2,1)} %reduce-scatter.2.cloned.1.call-done), kind=kLoop, calls=%fused_computation.9 | loop fusion | flops 1048576 | bytes 1572864 | tf_op jit(solution)/shard_map/convert_element_type | solution.py:399
  (54 shorter events, 0.5 us)
Async XLA Ops:
  6.5 62.2 %copy-start = (f32[3,3,512]{2,1,0:T(4,128)S(1)}, f32[3,3,512]{2,1,0:T(4,128)}, u32[]{:S(2)}) copy-start(f32[3,3,512]{2,1,0:T(4,128)} %param.14) | copy-start | bytes 55300
  6.5 12.1 %copy-start.6 = (bf16[512,512]{1,0:T(8,128)(2,1)S(1)}, bf16[512,512]{1,0:T(8,128)(2,1)}, u32[]{:S(2)}) copy-start(bf16[512,512]{1,0:T(8,128)(2,1)} %param.10) | copy-start | bytes 1572868
  6.5 12.3 %copy-start.8 = (bf16[129,512]{1,0:T(8,128)(2,1)S(1)}, bf16[129,512]{1,0:T(8,128)(2,1)}, u32[]{:S(2)}) copy-start(bf16[129,512]{1,0:T(8,128)(2,1)} %param.11) | copy-start | bytes 396292
  6.5 86.9 %all-gather.3.cloned.1.call-start = ((), (), s32[]{:S(2)}) async-start(), calls=%async_computation.2 | async-start | bytes 10305536 | tf_op jit(solution)/shard_map/all_gather | solution.py:365
  7.5 12.4 %collective-permute-start.2 = (bf16[256,128]{1,0:T(8,128)(2,1)S(1)}, bf16[256,128]{1,0:T(8,128)(2,1)S(1)}, u32[]{:S(2)}, u32[]{:S(2)}) collective-permute-start(bf16[256,128]{1,0:T(8,128)(2,1)S(1)} %get-tuple-element.59), channel_id=1, source_target_pairs={{0,32},{1,0},{32,33},{33,1},{2,34},{3,2},{34,35},{35,3},{4,36},{5,... | collective-permute-start | bytes 196616 | tf_op jit(solution)/shard_map/ppermute | solution.py:362
  14.8 5.1 %collective-permute-start.1 = (bf16[256,128]{1,0:T(8,128)(2,1)S(1)}, bf16[256,128]{1,0:T(8,128)(2,1)S(1)}, u32[]{:S(2)}, u32[]{:S(2)}) collective-permute-start(bf16[256,128]{1,0:T(8,128)(2,1)S(1)} %get-tuple-element.60), channel_id=1, source_target_pairs={{0,0},{1,32},{32,1},{33,33},{2,2},{3,34},{34,3},{35,35},{4,4},{5,3... | collective-permute-start | bytes 196616 | tf_op jit(solution)/shard_map/ppermute | solution.py:362
  16.6 12.9 %collective-permute-start = (bf16[128,768]{1,0:T(8,128)(2,1)S(1)}, bf16[128,768]{1,0:T(8,128)(2,1)S(1)}, u32[]{:S(2)}, u32[]{:S(2)}) collective-permute-start(bf16[128,768]{1,0:T(8,128)(2,1)S(1)} %get-tuple-element.46), channel_id=1, source_target_pairs={{0,32},{32,0},{1,33},{33,1},{2,34},{34,2},{3,35},{35,3},{4,36},{36... | collective-permute-start | bytes 589832 | tf_op jit(solution)/shard_map/ppermute | solution.py:357
  29.5 155.8 %reduce-scatter.2.cloned.1.call-start = ((), (), s32[]{:S(2)}) async-start(), calls=%async_computation.1 | async-start | bytes 4718592 | tf_op jit(solution)/shard_map/reduce_scatter | solution.py:396
  29.6 6.5 %collective-permute-start.7 = (bf16[128,1024]{1,0:T(8,128)(2,1)S(1)}, bf16[128,1024]{1,0:T(8,128)(2,1)S(1)}, u32[]{:S(2)}, u32[]{:S(2)}) collective-permute-start(bf16[128,1024]{1,0:T(8,128)(2,1)S(1)} %constant_dynamic-update-slice_fusion), channel_id=1, source_target_pairs={{0,64},{1,193},{64,0},{65,129},{128,192},{129,65},{192,128},{193,1... | collective-permute-start | bytes 786440 | tf_op jit(solution)/shard_map/ppermute | solution.py:313
  31.3 7.9 %collective-permute-start.3 = (bf16[128,1024]{1,0:T(8,128)(2,1)S(1)}, bf16[128,1024]{1,0:T(8,128)(2,1)S(1)}, u32[]{:S(2)}, u32[]{:S(2)}) collective-permute-start(bf16[128,1024]{1,0:T(8,128)(2,1)S(1)} %get-tuple-element.54), channel_id=1, source_target_pairs={{0,8},{1,25},{8,0},{9,17},{16,24},{17,9},{24,16},{25,1},{2,10},{3,... | collective-permute-start | bytes 786440 | tf_op jit(solution)/shard_map/ppermute | solution.py:313
  36.1 10.5 %collective-permute-start.8 = (bf16[2,128,1024]{2,1,0:T(8,128)(2,1)S(1)}, bf16[2,128,1024]{2,1,0:T(8,128)(2,1)S(1)}, u32[]{:S(2)}, u32[]{:S(2)}) collective-permute-start(bf16[2,128,1024]{2,1,0:T(8,128)(2,1)S(1)} %pad_maximum_fusion.5), channel_id=1, source_target_pairs={{0,192},{1,65},{64,128},{65,1},{128,64},{129,193},{192,0},{193,129... | collective-permute-start | bytes 1572872 | tf_op jit(solution)/shard_map/ppermute | solution.py:313
  39.3 10.0 %collective-permute-start.4 = (bf16[2,128,1024]{2,1,0:T(8,128)(2,1)S(1)}, bf16[2,128,1024]{2,1,0:T(8,128)(2,1)S(1)}, u32[]{:S(2)}, u32[]{:S(2)}) collective-permute-start(bf16[2,128,1024]{2,1,0:T(8,128)(2,1)S(1)} %pad_maximum_fusion.4), channel_id=1, source_target_pairs={{0,24},{1,9},{8,16},{9,1},{16,8},{17,25},{24,0},{25,17},{2,26},{3,... | collective-permute-start | bytes 1572872 | tf_op jit(solution)/shard_map/ppermute | solution.py:313
  46.7 14.9 %collective-permute-start.9 = (bf16[4,128,1024]{2,1,0:T(8,128)(2,1)S(1)}, bf16[4,128,1024]{2,1,0:T(8,128)(2,1)S(1)}, u32[]{:S(2)}, u32[]{:S(2)}) collective-permute-start(bf16[4,128,1024]{2,1,0:T(8,128)(2,1)S(1)} %get-tuple-element.40), channel_id=1, source_target_pairs={{0,8},{1,25},{8,0},{9,17},{16,24},{17,9},{24,16},{25,1},{2,10},{3,... | collective-permute-start | bytes 3145736 | tf_op jit(solution)/shard_map/ppermute | solution.py:313
  49.5 14.9 %collective-permute-start.5 = (bf16[4,128,1024]{2,1,0:T(8,128)(2,1)S(1)}, bf16[4,128,1024]{2,1,0:T(8,128)(2,1)S(1)}, u32[]{:S(2)}, u32[]{:S(2)}) collective-permute-start(bf16[4,128,1024]{2,1,0:T(8,128)(2,1)S(1)} %get-tuple-element.42), channel_id=1, source_target_pairs={{0,64},{1,193},{64,0},{65,129},{128,192},{129,65},{192,128},{193,1... | collective-permute-start | bytes 3145736 | tf_op jit(solution)/shard_map/ppermute | solution.py:313
  61.8 4.0 %copy-start.3 = (bf16[2,4,128,1024]{3,2,1,0:T(8,128)(2,1)}, bf16[2,4,128,1024]{3,2,1,0:T(8,128)(2,1)S(1)}, u32[]{:S(2)}) copy-start(bf16[2,4,128,1024]{3,2,1,0:T(8,128)(2,1)S(1)} %pad_maximum_fusion.1.refs_2_) | copy-start | bytes 6291460
  61.8 26.2 %collective-permute-start.10 = (bf16[2,4,128,1024]{3,2,1,0:T(8,128)(2,1)S(1)}, bf16[2,4,128,1024]{3,2,1,0:T(8,128)(2,1)}, u32[]{:S(2)}, u32[]{:S(2)}) collective-permute-start(bf16[2,4,128,1024]{3,2,1,0:T(8,128)(2,1)S(1)} %pad_maximum_fusion.1.refs_2_), channel_id=1, source_target_pairs={{0,24},{1,9},{8,16},{9,1},{16,8},{17,25},{24,0},{25,17},{2,26},{3,... | collective-permute-start | bytes 6291464 | tf_op jit(solution)/shard_map/ppermute | solution.py:313
  64.3 3.6 %copy-start.9 = (bf16[32,128]{1,0:T(8,128)(2,1)S(1)}, bf16[32,128]{1,0:T(8,128)(2,1)}, u32[]{:S(2)}) copy-start(bf16[32,128]{1,0:T(8,128)(2,1)} %param.15) | copy-start | bytes 24580
  64.3 4.2 %copy-start.12 = (f32[512]{0:T(512)S(1)}, f32[512]{0:T(512)}, u32[]{:S(2)}) copy-start(f32[512]{0:T(512)} %param.16) | copy-start | bytes 6148
  64.3 4.3 %copy-start.10 = (s32[4]{0:T(128)S(1)}, s32[4]{0:T(128)}, u32[]{:S(2)}) copy-start(s32[4]{0:T(128)} %constant.44.clone) | copy-start | bytes 52
  64.3 4.3 %copy-start.11 = (s32[4]{0:T(128)S(1)}, s32[4]{0:T(128)}, u32[]{:S(2)}) copy-start(s32[4]{0:T(128)} %constant.45.clone) | copy-start | bytes 52
  65.8 27.6 %collective-permute-start.6 = (bf16[2,4,128,1024]{3,2,1,0:T(8,128)(2,1)}, bf16[2,4,128,1024]{3,2,1,0:T(8,128)(2,1)}, u32[]{:S(2)}, u32[]{:S(2)}) collective-permute-start(bf16[2,4,128,1024]{3,2,1,0:T(8,128)(2,1)} %pad_maximum_fusion.refs_0_), channel_id=1, source_target_pairs={{0,192},{1,65},{64,128},{65,1},{128,64},{129,193},{192,0},{193,129... | collective-permute-start | bytes 6291464 | tf_op jit(solution)/shard_map/ppermute | solution.py:313
  93.4 1.6 copy-start.4
  110.2 1.5 copy-start.5
  111.7 1.2 copy-start.1
  112.9 6.8 %collective-permute-start.13 = (bf16[2,256,256]{2,1,0:T(8,128)(2,1)S(1)}, bf16[2,256,256]{2,1,0:T(8,128)(2,1)}, u32[]{:S(2)}, u32[]{:S(2)}) collective-permute-start(bf16[2,256,256]{2,1,0:T(8,128)(2,1)S(1)} %mix.2.mine_ref), channel_id=1, source_target_pairs={{0,1},{1,0},{2,3},{3,2},{4,5},{5,4},{6,7},{7,6},{8,9},{9,8},{10,11... | collective-permute-start | bytes 786440 | tf_op jit(solution)/shard_map/ppermute | solution.py:388
  113.8 10.4 %collective-permute-start.11 = (bf16[144,256]{1,0:T(8,128)(2,1)S(1)}, bf16[144,256]{1,0:T(8,128)(2,1)S(1)}, u32[]{:S(2)}, u32[]{:S(2)}) collective-permute-start(bf16[144,256]{1,0:T(8,128)(2,1)S(1)} %get-tuple-element.56), channel_id=1, source_target_pairs={{0,8},{8,16},{16,24},{24,64},{64,72},{72,80},{80,88},{88,128},{128... | collective-permute-start | bytes 221192 | tf_op jit(solution)/shard_map/ppermute | solution.py:383
  117.2 7.0 %collective-permute-start.12 = (bf16[144,256]{1,0:T(8,128)(2,1)S(1)}, bf16[144,256]{1,0:T(8,128)(2,1)S(1)}, u32[]{:S(2)}, u32[]{:S(2)}) collective-permute-start(bf16[144,256]{1,0:T(8,128)(2,1)S(1)} %get-tuple-element.55), channel_id=1, source_target_pairs={{0,8},{8,16},{16,24},{24,0},{64,72},{72,80},{80,88},{88,64},{128,1... | collective-permute-start | bytes 221192 | tf_op jit(solution)/shard_map/ppermute | solution.py:384
  119.7 4.6 %copy-start.2 = (bf16[3,2,512,256]{3,2,1,0:T(8,128)(2,1)S(1)}, bf16[3,2,512,256]{3,2,1,0:T(8,128)(2,1)}, u32[]{:S(2)}) copy-start(bf16[3,2,512,256]{3,2,1,0:T(8,128)(2,1)} %copy-done.1) | copy-start | bytes 4718596
  125.8 1.6 collective-permute-start.14
  130.9 54.3 %copy-start.7 = (bf16[512,512]{1,0:T(8,128)(2,1)S(1)}, bf16[512,512]{1,0:T(8,128)(2,1)}, u32[]{:S(2)}) copy-start(bf16[512,512]{1,0:T(8,128)(2,1)} %param.10) | copy-start | bytes 1572868
Sparse Core Ops, SparseCore 0:
  29.6 62.0 all-gather.2
  131.1 54.1 reduce-scatter.1

commit v12 on v11

--- a/solution.py
+++ b/solution.py
@@ -170,7 +170,7 @@
             jax.ShapeDtypeStruct((HALO, CH), BF16),
             jax.ShapeDtypeStruct((4, 2 * CH, WIDE), BF16),
         ],
-        compiler_params=pltpu.CompilerParams(vmem_limit_bytes=42 * MIB),
+        compiler_params=pltpu.CompilerParams(vmem_limit_bytes=50 * MIB),
         cost_estimate=pl.CostEstimate(
             flops=2 * 2 * ROWS * 4096 * 3 * CH, bytes_accessed=18_000_000, transcendentals=0
         ),
@@ -297,7 +297,7 @@
         ),
         out_shape=jax.ShapeDtypeStruct((2, 4, ROWS, WIDE), BF16),
         input_output_aliases={} if base is None else {4: 0},
-        compiler_params=pltpu.CompilerParams(vmem_limit_bytes=50 * MIB),
+        compiler_params=pltpu.CompilerParams(vmem_limit_bytes=44 * MIB),
         cost_estimate=pl.CostEstimate(
             flops=2 * 512 * 2 * CH * 2048, bytes_accessed=5_000_000, transcendentals=0
         ),

time: 195 us -> 194 us (level)
  Pallas kernels: 26.7 us -> 24.4 us
    pallas_call x2, Pallas kernels: 8.11 us -> 5.93 us  [project_out(): pl.pallas_call(out_kernel, grid_spec=pltpu.PrefetchScalarGridSpec(num_sca...]
  transfers between devices with their start and end apart: 17 -> 17, of which waited for: 10 -> 10; matrix products, arithmetic and copies ran while one was open for 3% -> 3% of each run, Pallas kernels for 3% -> 2%
where the time goes in v12:
time: 194 us; the launch traced here: 193 us
  waiting for transfers between devices  115 us (59%)
  starting transfers between devices  26.4 us (14%)
  Pallas kernels  24.4 us (13%)
  between operations  13.7 us (7%)
  other arithmetic  7.15 us (4%)
  local copies, waits for them, and re-layouts  6.11 us (3%)
    reduce_scatter x1, waiting for transfers between devices, on_device(): lax.psum_scatter(partial.reshape(8, ROWS, WIDE), ('zh', 'zl'), scatter_di...  54.3 us
    ppermute x8, waiting for transfers between devices, pair_step(): return lax.ppermute(value, (axis, 'c'), pairs)  49.7 us
    pallas_call x1, Pallas kernels, project(): pl.pallas_call(project_kernel, grid_spec=pltpu.PrefetchScalarGridSpec(num...  15.1 us
    ppermute x8, starting transfers between devices, pair_step(): return lax.ppermute(value, (axis, 'c'), pairs)  11.1 us
    ppermute x1, waiting for transfers between devices, on_device(): got = lax.ppermute(jnp.where(zh == 0, right, left), 'zh', [(0, 1), (1, 0)])  9.51 us
    ppermute x2, starting transfers between devices, on_device(): chosen = lax.ppermute(chosen, ('zh', 'c'), pairs)  7.93 us
    pallas_call x2, Pallas kernels, project_out(): pl.pallas_call(out_kernel, grid_spec=pltpu.PrefetchScalarGridSpec(num_sca...  5.93 us
  transfers between devices with their start and end apart: 17, of which 10 were waited for; matrix products, arithmetic and copies ran while one was open for 3% of the time, Pallas kernels for 2%

profile of v12, /device:TPU:2, one launch (start us, length us, event | category | flops | bytes accessed | tf_op | source)
XLA Modules:
  0.0 192.8 jit_solution(11396388506386983362)
XLA Ops:
  6.6 0.9 constant_dynamic-slice_fusion.1
  7.5 7.3 %collective-permute-start.2 = (bf16[256,128]{1,0:T(8,128)(2,1)S(1)}, bf16[256,128]{1,0:T(8,128)(2,1)S(1)}, u32[]{:S(2)}, u32[]{:S(2)}) collective-permute-start(bf16[256,128]{1,0:T(8,128)(2,1)S(1)} %get-tuple-element.59), channel_id=1, source_target_pairs={{0,32},{1,0},{32,33},{33,1},{2,34},{3,2},{34,35},{35,3},{4,36},{5,... | collective-permute-start | bytes 196616 | tf_op jit(solution)/shard_map/ppermute | solution.py:362
  14.8 0.7 collective-permute-start.1
  15.5 1.0 slice_bitcast_fusion.5
  16.6 1.4 collective-permute-start
  17.9 0.7 convert_element_type.41
  18.6 0.2 fusion.1
  18.8 0.1 fusion.5
  19.0 0.9 fusion.4
  20.0 9.5 %collective-permute-done = bf16[128,768]{1,0:T(8,128)(2,1)S(1)} collective-permute-done((bf16[128,768]{1,0:T(8,128)(2,1)S(1)}, bf16[128,768]{1,0:T(8,128)(2,1)S(1)}, u32[]{:S(2)}, u32[]{:S(2)}) %collective-permute-start) | collective-permute-done | bytes 196640 | tf_op jit(solution)/shard_map/ppermute | solution.py:357
  29.6 1.7 collective-permute-start.7
  31.3 0.6 collective-permute-start.3
  31.9 4.1 %collective-permute-done.7 = bf16[128,1024]{1,0:T(8,128)(2,1)S(1)} collective-permute-done((bf16[128,1024]{1,0:T(8,128)(2,1)S(1)}, bf16[128,1024]{1,0:T(8,128)(2,1)S(1)}, u32[]{:S(2)}, u32[]{:S(2)}) %collective-permute-start.7) | collective-permute-done | bytes 262176 | tf_op jit(solution)/shard_map/ppermute | solution.py:313
  36.1 3.1 %collective-permute-start.8 = (bf16[2,128,1024]{2,1,0:T(8,128)(2,1)S(1)}, bf16[2,128,1024]{2,1,0:T(8,128)(2,1)S(1)}, u32[]{:S(2)}, u32[]{:S(2)}) collective-permute-start(bf16[2,128,1024]{2,1,0:T(8,128)(2,1)S(1)} %pad_maximum_fusion.5), channel_id=1, source_target_pairs={{0,192},{1,65},{64,128},{65,1},{128,64},{129,193},{192,0},{193,129... | collective-permute-start | bytes 1572872 | tf_op jit(solution)/shard_map/ppermute | solution.py:313
  39.3 1.6 collective-permute-start.4
  40.8 5.7 %collective-permute-done.8 = bf16[2,128,1024]{2,1,0:T(8,128)(2,1)S(1)} collective-permute-done((bf16[2,128,1024]{2,1,0:T(8,128)(2,1)S(1)}, bf16[2,128,1024]{2,1,0:T(8,128)(2,1)S(1)}, u32[]{:S(2)}, u32[]{:S(2)}) %collective-permute-start.8) | collective-permute-done | bytes 524320 | tf_op jit(solution)/shard_map/ppermute | solution.py:313
  46.6 0.1 fusion.11
  46.7 0.4 collective-permute-start.9
  47.1 2.2 %collective-permute-done.4 = bf16[2,128,1024]{2,1,0:T(8,128)(2,1)S(1)} collective-permute-done((bf16[2,128,1024]{2,1,0:T(8,128)(2,1)S(1)}, bf16[2,128,1024]{2,1,0:T(8,128)(2,1)S(1)}, u32[]{:S(2)}, u32[]{:S(2)}) %collective-permute-start.4) | collective-permute-done | bytes 524320 | tf_op jit(solution)/shard_map/ppermute | solution.py:313
  49.3 0.1 fusion.12
  49.5 0.1 collective-permute-start.5
  49.6 12.1 %collective-permute-done.9 = bf16[4,128,1024]{2,1,0:T(8,128)(2,1)S(1)} collective-permute-done((bf16[4,128,1024]{2,1,0:T(8,128)(2,1)S(1)}, bf16[4,128,1024]{2,1,0:T(8,128)(2,1)S(1)}, u32[]{:S(2)}, u32[]{:S(2)}) %collective-permute-start.9) | collective-permute-done | bytes 1048608 | tf_op jit(solution)/shard_map/ppermute | solution.py:313
  61.6 0.2 pad_maximum_fusion.1.refs_2_
  61.8 1.6 collective-permute-start.10
  63.4 0.9 collective-permute-done.5
  64.4 1.5 pad_maximum_fusion.refs_0_
  65.8 2.1 %collective-permute-start.6 = (bf16[2,4,128,1024]{3,2,1,0:T(8,128)(2,1)}, bf16[2,4,128,1024]{3,2,1,0:T(8,128)(2,1)}, u32[]{:S(2)}, u32[]{:S(2)}) collective-permute-start(bf16[2,4,128,1024]{3,2,1,0:T(8,128)(2,1)} %pad_maximum_fusion.refs_0_), channel_id=1, source_target_pairs={{0,192},{1,65},{64,128},{65,1},{128,64},{129,193},{192,0},{193,129... | collective-permute-start | bytes 6291464 | tf_op jit(solution)/shard_map/ppermute | solution.py:313
  68.0 0.1 pad.19.u_ref
  68.1 0.5 toeplitz.1.band_ref
  68.6 0.1 dynamic_slice.23
  68.7 0.1 pad_add_fusion.at_ref
  68.8 19.3 %collective-permute-done.10.refs_3_ = bf16[2,4,128,1024]{3,2,1,0:T(8,128)(2,1)} collective-permute-done((bf16[2,4,128,1024]{3,2,1,0:T(8,128)(2,1)S(1)}, bf16[2,4,128,1024]{3,2,1,0:T(8,128)(2,1)}, u32[]{:S(2)}, u32[]{:S(2)}) %collective-permute-start.10) | collective-permute-done | bytes 2097184 | tf_op jit(solution)/shard_map/ppermute | solution.py:313
  88.0 5.3 %collective-permute-done.6.refs_1_ = bf16[2,4,128,1024]{3,2,1,0:T(8,128)(2,1)} collective-permute-done((bf16[2,4,128,1024]{3,2,1,0:T(8,128)(2,1)}, bf16[2,4,128,1024]{3,2,1,0:T(8,128)(2,1)}, u32[]{:S(2)}, u32[]{:S(2)}) %collective-permute-start.6) | collective-permute-done | bytes 2097184 | tf_op jit(solution)/shard_map/ppermute | solution.py:313
  93.4 15.1 %project.1 = (bf16[3,2,512,256]{3,2,1,0:T(8,128)(2,1)S(1)}, bf16[2,144,256]{2,1,0:T(8,128)(2,1)S(1)}, bf16[2,144,256]{2,1,0:T(8,128)(2,1)S(1)}, bf16[144,256]{1,0:T(8,128)(2,1)S(1)}, bf16[4,512,512]{2,1,0:T(8,128)(2,1)S(1)}) custom-call(s32[10]{0:T(128)S(1)} %pad_add_fusion.at_ref, bf16[2,4,2,592,512]{4,3,2,1,0:T(8,128)(2,1)} %bitcast.54, ...), custom_call_target="tpu_custom_call" | custom-call | flops 6442450944 | bytes 18000000 | tf_op jit(solution)/shard_map/project/pallas_call | solution.py:137
  108.5 0.7 copy-done.4
  109.1 1.5 mix.2.mine_ref
  110.6 1.2 copy-done.2
  111.8 0.9 select_bitcast_fusion.1
  112.7 3.4 %collective-permute-start.11 = (bf16[144,256]{1,0:T(8,128)(2,1)S(1)}, bf16[144,256]{1,0:T(8,128)(2,1)S(1)}, u32[]{:S(2)}, u32[]{:S(2)}) collective-permute-start(bf16[144,256]{1,0:T(8,128)(2,1)S(1)} %get-tuple-element.56), channel_id=1, source_target_pairs={{0,8},{8,16},{16,24},{24,64},{64,72},{72,80},{80,88},{88,128},{128... | collective-permute-start | bytes 221192 | tf_op jit(solution)/shard_map/ppermute | solution.py:383
  116.1 2.5 %collective-permute-start.12 = (bf16[144,256]{1,0:T(8,128)(2,1)S(1)}, bf16[144,256]{1,0:T(8,128)(2,1)S(1)}, u32[]{:S(2)}, u32[]{:S(2)}) collective-permute-start(bf16[144,256]{1,0:T(8,128)(2,1)S(1)} %get-tuple-element.55), channel_id=1, source_target_pairs={{0,8},{8,16},{16,24},{24,0},{64,72},{72,80},{80,88},{88,64},{128,1... | collective-permute-start | bytes 221192 | tf_op jit(solution)/shard_map/ppermute | solution.py:384
  118.6 3.4 %project_out.2.refs_0_ = bf16[2,4,512,512]{3,2,1,0:T(8,128)(2,1)S(1)} custom-call(s32[10]{0:T(128)S(1)} %pad_add_fusion.at_ref, bf16[2,256,256]{2,1,0:T(8,128)(2,1)S(1)} %mix.2.mine_ref, bf16[2,256,256]{2,1,0:T(8,128)(2,1)} %collective-permute-done.13.other_ref, bf16[4,512,512]{2,1,0:T(8,128)(2,1)S(1)} %get-tuple-element.35.w_ref), custom_call_target="tpu_custom_call" | custom-call | flops 1073741824 | bytes 5000000 | tf_op jit(solution)/shard_map/project_out/pallas_call | solution.py:285
  122.1 1.5 mix.3.mine_ref
  123.6 0.1 collective-permute-start.14
  123.7 1.5 collective-permute-done.14.other_ref
  125.2 2.5 %project_out.3 = bf16[2,4,512,512]{3,2,1,0:T(8,128)(2,1)S(1)} custom-call(s32[10]{0:T(128)S(1)} %pad_add_fusion.at_ref, bf16[2,256,256]{2,1,0:T(8,128)(2,1)S(1)} %mix.3.mine_ref, bf16[2,256,256]{2,1,0:T(8,128)(2,1)S(1)} %collective-permute-done.14.other_ref, bf16[4,512,512]{2,1,0:T(8,128)(2,1)S(1)} %get-tuple-element.35.w_ref, ...), custom_call_target="tpu_custom_call", output_to_operand_aliasing={{}: (4, {})} | custom-call | flops 1073741824 | bytes 5000000 | tf_op jit(solution)/shard_map/project_out/pallas_call | solution.py:285
  127.7 2.0 %copy-done.1 = bf16[2,4,512,512]{3,2,1,0:T(8,128)(2,1)} copy-done((bf16[2,4,512,512]{3,2,1,0:T(8,128)(2,1)}, bf16[2,4,512,512]{3,2,1,0:T(8,128)(2,1)S(1)}, u32[]{:S(2)}) %copy-start.1) | copy-done | bytes 4194328
  129.7 54.3 %reduce-scatter.2.cloned.1.call-done = bf16[1,512,512]{2,1,0:T(8,128)(2,1)} async-done(((bf16[8,512,512]{2,1,0:T(8,128)(2,1)}), bf16[1,512,512]{2,1,0:T(8,128)(2,1)}) %reduce-scatter.2.cloned.1.call-update) | async-done | bytes 524304 | tf_op jit(solution)/shard_map/reduce_scatter | solution.py:396
  184.0 2.0 %fusion.3 = bf16[512,512]{1,0:T(8,128)(2,1)} fusion(bf16[512,512]{1,0:T(8,128)(2,1)S(1)} %copy-done.6, bf16[1,512,512]{2,1,0:T(8,128)(2,1)} %reduce-scatter.2.cloned.1.call-done), kind=kLoop, calls=%fused_computation.9 | loop fusion | flops 1048576 | bytes 1572864 | tf_op jit(solution)/shard_map/convert_element_type | solution.py:399
  (54 shorter events, 0.6 us)
Async XLA Ops:
  6.5 62.2 %copy-start = (f32[3,3,512]{2,1,0:T(4,128)S(1)}, f32[3,3,512]{2,1,0:T(4,128)}, u32[]{:S(2)}) copy-start(f32[3,3,512]{2,1,0:T(4,128)} %param.14) | copy-start | bytes 55300
  6.5 12.1 %copy-start.5 = (bf16[512,512]{1,0:T(8,128)(2,1)S(1)}, bf16[512,512]{1,0:T(8,128)(2,1)}, u32[]{:S(2)}) copy-start(bf16[512,512]{1,0:T(8,128)(2,1)} %param.10) | copy-start | bytes 1572868
  6.5 12.3 %copy-start.8 = (bf16[129,512]{1,0:T(8,128)(2,1)S(1)}, bf16[129,512]{1,0:T(8,128)(2,1)}, u32[]{:S(2)}) copy-start(bf16[129,512]{1,0:T(8,128)(2,1)} %param.11) | copy-start | bytes 396292
  6.5 86.9 %all-gather.3.cloned.1.call-start = ((), (), s32[]{:S(2)}) async-start(), calls=%async_computation.2 | async-start | bytes 10305536 | tf_op jit(solution)/shard_map/all_gather | solution.py:365
  7.5 12.4 %collective-permute-start.2 = (bf16[256,128]{1,0:T(8,128)(2,1)S(1)}, bf16[256,128]{1,0:T(8,128)(2,1)S(1)}, u32[]{:S(2)}, u32[]{:S(2)}) collective-permute-start(bf16[256,128]{1,0:T(8,128)(2,1)S(1)} %get-tuple-element.59), channel_id=1, source_target_pairs={{0,32},{1,0},{32,33},{33,1},{2,34},{3,2},{34,35},{35,3},{4,36},{5,... | collective-permute-start | bytes 196616 | tf_op jit(solution)/shard_map/ppermute | solution.py:362
  14.8 5.1 %collective-permute-start.1 = (bf16[256,128]{1,0:T(8,128)(2,1)S(1)}, bf16[256,128]{1,0:T(8,128)(2,1)S(1)}, u32[]{:S(2)}, u32[]{:S(2)}) collective-permute-start(bf16[256,128]{1,0:T(8,128)(2,1)S(1)} %get-tuple-element.60), channel_id=1, source_target_pairs={{0,0},{1,32},{32,1},{33,33},{2,2},{3,34},{34,3},{35,35},{4,4},{5,3... | collective-permute-start | bytes 196616 | tf_op jit(solution)/shard_map/ppermute | solution.py:362
  16.6 12.9 %collective-permute-start = (bf16[128,768]{1,0:T(8,128)(2,1)S(1)}, bf16[128,768]{1,0:T(8,128)(2,1)S(1)}, u32[]{:S(2)}, u32[]{:S(2)}) collective-permute-start(bf16[128,768]{1,0:T(8,128)(2,1)S(1)} %get-tuple-element.46), channel_id=1, source_target_pairs={{0,32},{32,0},{1,33},{33,1},{2,34},{34,2},{3,35},{35,3},{4,36},{36... | collective-permute-start | bytes 589832 | tf_op jit(solution)/shard_map/ppermute | solution.py:357
  29.5 154.5 %reduce-scatter.2.cloned.1.call-start = ((), (), s32[]{:S(2)}) async-start(), calls=%async_computation.1 | async-start | bytes 4718592 | tf_op jit(solution)/shard_map/reduce_scatter | solution.py:396
  29.6 6.5 %collective-permute-start.7 = (bf16[128,1024]{1,0:T(8,128)(2,1)S(1)}, bf16[128,1024]{1,0:T(8,128)(2,1)S(1)}, u32[]{:S(2)}, u32[]{:S(2)}) collective-permute-start(bf16[128,1024]{1,0:T(8,128)(2,1)S(1)} %constant_dynamic-update-slice_fusion), channel_id=1, source_target_pairs={{0,64},{1,193},{64,0},{65,129},{128,192},{129,65},{192,128},{193,1... | collective-permute-start | bytes 786440 | tf_op jit(solution)/shard_map/ppermute | solution.py:313
  31.3 7.9 %collective-permute-start.3 = (bf16[128,1024]{1,0:T(8,128)(2,1)S(1)}, bf16[128,1024]{1,0:T(8,128)(2,1)S(1)}, u32[]{:S(2)}, u32[]{:S(2)}) collective-permute-start(bf16[128,1024]{1,0:T(8,128)(2,1)S(1)} %get-tuple-element.54), channel_id=1, source_target_pairs={{0,8},{1,25},{8,0},{9,17},{16,24},{17,9},{24,16},{25,1},{2,10},{3,... | collective-permute-start | bytes 786440 | tf_op jit(solution)/shard_map/ppermute | solution.py:313
  36.1 10.5 %collective-permute-start.8 = (bf16[2,128,1024]{2,1,0:T(8,128)(2,1)S(1)}, bf16[2,128,1024]{2,1,0:T(8,128)(2,1)S(1)}, u32[]{:S(2)}, u32[]{:S(2)}) collective-permute-start(bf16[2,128,1024]{2,1,0:T(8,128)(2,1)S(1)} %pad_maximum_fusion.5), channel_id=1, source_target_pairs={{0,192},{1,65},{64,128},{65,1},{128,64},{129,193},{192,0},{193,129... | collective-permute-start | bytes 1572872 | tf_op jit(solution)/shard_map/ppermute | solution.py:313
  39.3 10.0 %collective-permute-start.4 = (bf16[2,128,1024]{2,1,0:T(8,128)(2,1)S(1)}, bf16[2,128,1024]{2,1,0:T(8,128)(2,1)S(1)}, u32[]{:S(2)}, u32[]{:S(2)}) collective-permute-start(bf16[2,128,1024]{2,1,0:T(8,128)(2,1)S(1)} %pad_maximum_fusion.4), channel_id=1, source_target_pairs={{0,24},{1,9},{8,16},{9,1},{16,8},{17,25},{24,0},{25,17},{2,26},{3,... | collective-permute-start | bytes 1572872 | tf_op jit(solution)/shard_map/ppermute | solution.py:313
  46.7 14.9 %collective-permute-start.9 = (bf16[4,128,1024]{2,1,0:T(8,128)(2,1)S(1)}, bf16[4,128,1024]{2,1,0:T(8,128)(2,1)S(1)}, u32[]{:S(2)}, u32[]{:S(2)}) collective-permute-start(bf16[4,128,1024]{2,1,0:T(8,128)(2,1)S(1)} %get-tuple-element.40), channel_id=1, source_target_pairs={{0,8},{1,25},{8,0},{9,17},{16,24},{17,9},{24,16},{25,1},{2,10},{3,... | collective-permute-start | bytes 3145736 | tf_op jit(solution)/shard_map/ppermute | solution.py:313
  49.5 14.9 %collective-permute-start.5 = (bf16[4,128,1024]{2,1,0:T(8,128)(2,1)S(1)}, bf16[4,128,1024]{2,1,0:T(8,128)(2,1)S(1)}, u32[]{:S(2)}, u32[]{:S(2)}) collective-permute-start(bf16[4,128,1024]{2,1,0:T(8,128)(2,1)S(1)} %get-tuple-element.42), channel_id=1, source_target_pairs={{0,64},{1,193},{64,0},{65,129},{128,192},{129,65},{192,128},{193,1... | collective-permute-start | bytes 3145736 | tf_op jit(solution)/shard_map/ppermute | solution.py:313
  61.8 4.0 %copy-start.7 = (bf16[2,4,128,1024]{3,2,1,0:T(8,128)(2,1)}, bf16[2,4,128,1024]{3,2,1,0:T(8,128)(2,1)S(1)}, u32[]{:S(2)}) copy-start(bf16[2,4,128,1024]{3,2,1,0:T(8,128)(2,1)S(1)} %pad_maximum_fusion.1.refs_2_) | copy-start | bytes 6291460
  61.8 26.2 %collective-permute-start.10 = (bf16[2,4,128,1024]{3,2,1,0:T(8,128)(2,1)S(1)}, bf16[2,4,128,1024]{3,2,1,0:T(8,128)(2,1)}, u32[]{:S(2)}, u32[]{:S(2)}) collective-permute-start(bf16[2,4,128,1024]{3,2,1,0:T(8,128)(2,1)S(1)} %pad_maximum_fusion.1.refs_2_), channel_id=1, source_target_pairs={{0,24},{1,9},{8,16},{9,1},{16,8},{17,25},{24,0},{25,17},{2,26},{3,... | collective-permute-start | bytes 6291464 | tf_op jit(solution)/shard_map/ppermute | solution.py:313
  64.3 3.6 %copy-start.9 = (bf16[32,128]{1,0:T(8,128)(2,1)S(1)}, bf16[32,128]{1,0:T(8,128)(2,1)}, u32[]{:S(2)}) copy-start(bf16[32,128]{1,0:T(8,128)(2,1)} %param.15) | copy-start | bytes 24580
  64.3 4.2 %copy-start.12 = (f32[512]{0:T(512)S(1)}, f32[512]{0:T(512)}, u32[]{:S(2)}) copy-start(f32[512]{0:T(512)} %param.16) | copy-start | bytes 6148
  64.3 4.3 %copy-start.10 = (s32[4]{0:T(128)S(1)}, s32[4]{0:T(128)}, u32[]{:S(2)}) copy-start(s32[4]{0:T(128)} %constant.44.clone) | copy-start | bytes 52
  64.3 4.3 %copy-start.11 = (s32[4]{0:T(128)S(1)}, s32[4]{0:T(128)}, u32[]{:S(2)}) copy-start(s32[4]{0:T(128)} %constant.45.clone) | copy-start | bytes 52
  65.8 27.6 %collective-permute-start.6 = (bf16[2,4,128,1024]{3,2,1,0:T(8,128)(2,1)}, bf16[2,4,128,1024]{3,2,1,0:T(8,128)(2,1)}, u32[]{:S(2)}, u32[]{:S(2)}) collective-permute-start(bf16[2,4,128,1024]{3,2,1,0:T(8,128)(2,1)} %pad_maximum_fusion.refs_0_), channel_id=1, source_target_pairs={{0,192},{1,65},{64,128},{65,1},{128,64},{129,193},{192,0},{193,129... | collective-permute-start | bytes 6291464 | tf_op jit(solution)/shard_map/ppermute | solution.py:313
  108.5 0.7 copy-start.4
  110.6 1.2 copy-start.2
  111.8 6.8 %collective-permute-start.13 = (bf16[2,256,256]{2,1,0:T(8,128)(2,1)S(1)}, bf16[2,256,256]{2,1,0:T(8,128)(2,1)}, u32[]{:S(2)}, u32[]{:S(2)}) collective-permute-start(bf16[2,256,256]{2,1,0:T(8,128)(2,1)S(1)} %mix.2.mine_ref), channel_id=1, source_target_pairs={{0,1},{1,0},{2,3},{3,2},{4,5},{5,4},{6,7},{7,6},{8,9},{9,8},{10,11... | collective-permute-start | bytes 786440 | tf_op jit(solution)/shard_map/ppermute | solution.py:388
  112.7 9.3 %collective-permute-start.11 = (bf16[144,256]{1,0:T(8,128)(2,1)S(1)}, bf16[144,256]{1,0:T(8,128)(2,1)S(1)}, u32[]{:S(2)}, u32[]{:S(2)}) collective-permute-start(bf16[144,256]{1,0:T(8,128)(2,1)S(1)} %get-tuple-element.56), channel_id=1, source_target_pairs={{0,8},{8,16},{16,24},{24,64},{64,72},{72,80},{80,88},{88,128},{128... | collective-permute-start | bytes 221192 | tf_op jit(solution)/shard_map/ppermute | solution.py:383
  116.1 5.9 %collective-permute-start.12 = (bf16[144,256]{1,0:T(8,128)(2,1)S(1)}, bf16[144,256]{1,0:T(8,128)(2,1)S(1)}, u32[]{:S(2)}, u32[]{:S(2)}) collective-permute-start(bf16[144,256]{1,0:T(8,128)(2,1)S(1)} %get-tuple-element.55), channel_id=1, source_target_pairs={{0,8},{8,16},{16,24},{24,0},{64,72},{72,80},{80,88},{88,64},{128,1... | collective-permute-start | bytes 221192 | tf_op jit(solution)/shard_map/ppermute | solution.py:384
  118.6 3.5 %copy-start.3 = (bf16[3,2,512,256]{3,2,1,0:T(8,128)(2,1)S(1)}, bf16[3,2,512,256]{3,2,1,0:T(8,128)(2,1)}, u32[]{:S(2)}) copy-start(bf16[3,2,512,256]{3,2,1,0:T(8,128)(2,1)} %copy-done.2) | copy-start | bytes 4718596
  123.6 1.6 collective-permute-start.14
  127.7 2.0 %copy-start.1 = (bf16[2,4,512,512]{3,2,1,0:T(8,128)(2,1)}, bf16[2,4,512,512]{3,2,1,0:T(8,128)(2,1)S(1)}, u32[]{:S(2)}) copy-start(bf16[2,4,512,512]{3,2,1,0:T(8,128)(2,1)S(1)} %project_out.3) | copy-start | bytes 12582916
  129.7 54.3 %copy-start.6 = (bf16[512,512]{1,0:T(8,128)(2,1)S(1)}, bf16[512,512]{1,0:T(8,128)(2,1)}, u32[]{:S(2)}) copy-start(bf16[512,512]{1,0:T(8,128)(2,1)} %param.10) | copy-start | bytes 1572868
Sparse Core Ops, SparseCore 0:
  29.6 62.0 all-gather.2
  129.9 54.1 reduce-scatter.1

commit v13 on v12

--- a/solution.py
+++ b/solution.py
@@ -48,83 +48,63 @@
 
 def project_kernel(at_ref, x_ref, *refs):
     taps_ref, proj_ref, tail_ref, mid_ref, front_ref, out_w_ref = refs[4:10]
-    wide, acc, stat, ahead, sems, out_sems = refs[10:]
-    first_row, kind = pl.program_id(0) == 0, pl.program_id(1)
-    turns = []
+    wide, ahead, sems, out_sems = refs[10:]
+    first_row = pl.program_id(0) == 0
+    copies = []
     out_copies = []
     for k in range(2):
-        copies = []
+        half = at_ref[8] if k == 0 else 1 - at_ref[8]
         for i in range(4):
             for j in range(4):
                 y, x = (i, j) if k == 0 else (j, i)
-                start = at_ref[y] * WIDE + at_ref[4 + x] * 128
+                start = (2 * at_ref[y] + half) * WIDE + at_ref[4 + x] * 128
                 rows = pl.ds(pl.multiple_of(start, 128), 128)
                 source = refs[2 * k + i // 2].at[i % 2, j, :, pl.ds(0, 3 * CH)]
-                copies.append(pltpu.make_async_copy(source, wide.at[k, rows], sems.at[k, i, j]))
+                copies.append(pltpu.make_async_copy(source, wide.at[rows], sems.at[k, i, j]))
                 lanes = pl.ds(pl.multiple_of(at_ref[4 + x] * 128, 128), 128)
                 for part in range(2):
                     source = refs[2 * k + i // 2].at[i % 2, j, :, pl.ds(3 * CH + part * 128, 128)]
                     place = out_w_ref.at[at_ref[y], pl.ds(k * CH + part * 128, 128), lanes]
                     sem = out_sems.at[k, i, j, part]
                     out_copies.append(pltpu.make_async_copy(source, place, sem))
-        turns.append(copies)
-
-    @pl.when(first_row & (kind == 0))
+
+    @pl.when(first_row)
     def _():
-        for copies in turns:
-            for copy in copies:
-                copy.start()
-
-    for k in range(2):
-
-        @pl.when(first_row & (kind == k))
-        def _(k=k):
-            for copy in turns[k]:
-                copy.wait()
-
-    @pl.when(first_row & (kind == 1))
-    def _():
+        for copy in copies:
+            copy.start()
         for copy in out_copies:
             copy.start()
-
-    features = jnp.concatenate([x_ref[0, y, 0] for y in range(4)], axis=1)
-    products = jnp.dot(features, wide[kind], preferred_element_type=F32)
+        for copy in copies:
+            copy.wait()
+
+    features = jnp.concatenate([x_ref[0, t] for t in range(8)], axis=1)
+    products = jnp.dot(features, wide[...], preferred_element_type=F32)
     sums = jnp.zeros((8, WIDE), F32)
-    for y in range(4):
-        sums += x_ref[0, y, 0, ROWS + TILE - 16 :].astype(F32)[8:]
-
-    @pl.when(kind == 0)
-    def _():
-        acc[...] = products
-        stat[...] = sums
-
-    @pl.when(kind == 1)
-    def _():
-        total = stat[...] + sums
-        own = lax.rsqrt((total[0:1] + total[1:2]) * (1.0 / 4096.0) + 1e-6)
-        extra = lax.rsqrt((total[2:3] + total[3:4]) * (1.0 / 4096.0) + 1e-6)
-        own, extra = as_column(own), as_column(extra[:, :128])[:TILE]
-        for s in range(3):
-            lanes = slice(s * CH, (s + 1) * CH)
-            whole = acc[:, lanes] + products[:, lanes]
-            proj_ref[s, 0] = (whole[:ROWS] * own).astype(BF16)
-            carried = (whole[ROWS:] * extra).astype(BF16).astype(F32)
-
-            @pl.when(first_row)
-            def _(s=s, carried=carried):
-                ahead[s, :SHARE] = carried[:SHARE]
-
-            @pl.when(jnp.logical_not(first_row))
-            def _(s=s, carried=carried):
-                ahead[s, SHARE:] = carried
-
-        for end, ref in ((ROWS, tail_ref), (HALF, mid_ref)):
-            rows = [proj_ref[s, 0, end - HALO : end].astype(F32) for s in range(3)]
-            mixing = three_taps(rows[1], taps_ref, 1) * three_taps(rows[2], taps_ref, 2)
-            ref[0, :LH] = mixing[HALO - LH :].astype(BF16)
-            ref[0, LH:] = last_rows(rows, HALO - 16, 2)
-
-    @pl.when((pl.program_id(0) == 1) & (kind == 1))
+    for t in range(8):
+        sums += x_ref[0, t, ROWS + TILE - 16 :].astype(F32)[8:]
+    own = lax.rsqrt((sums[0:1] + sums[1:2]) * (1.0 / 4096.0) + 1e-6)
+    extra = lax.rsqrt((sums[2:3] + sums[3:4]) * (1.0 / 4096.0) + 1e-6)
+    own, extra = as_column(own), as_column(extra[:, :128])[:TILE]
+    for s in range(3):
+        lanes = slice(s * CH, (s + 1) * CH)
+        proj_ref[s, 0] = (products[:ROWS, lanes] * own).astype(BF16)
+        carried = (products[ROWS:, lanes] * extra).astype(BF16).astype(F32)
+
+        @pl.when(first_row)
+        def _(s=s, carried=carried):
+            ahead[s, :SHARE] = carried[:SHARE]
+
+        @pl.when(jnp.logical_not(first_row))
+        def _(s=s, carried=carried):
+            ahead[s, SHARE:] = carried
+
+    for end, ref in ((ROWS, tail_ref), (HALF, mid_ref)):
+        rows = [proj_ref[s, 0, end - HALO : end].astype(F32) for s in range(3)]
+        mixing = three_taps(rows[1], taps_ref, 1) * three_taps(rows[2], taps_ref, 2)
+        ref[0, :LH] = mixing[HALO - LH :].astype(BF16)
+        ref[0, LH:] = last_rows(rows, HALO - 16, 2)
+
+    @pl.when(jnp.logical_not(first_row))
     def _():
         mixing = three_taps(ahead[1], taps_ref, 1) * three_taps(ahead[2], taps_ref, 2)
         front_ref[:LH] = pltpu.roll(mixing, SHARE + TILE - 1, 0)[:LH].astype(BF16)
@@ -138,26 +118,21 @@
         project_kernel,
         grid_spec=pltpu.PrefetchScalarGridSpec(
             num_scalar_prefetch=1,
-            grid=(2, 2),
+            grid=(2,),
             in_specs=[
-                pl.BlockSpec(
-                    (1, 4, 1, ROWS + TILE, WIDE),
-                    lambda h, k, at: (h, 0, at[8] + k - 2 * at[8] * k, 0, 0),
-                ),
+                pl.BlockSpec((1, 8, ROWS + TILE, WIDE), lambda h, at: (h, 0, 0, 0)),
                 *[pl.BlockSpec(memory_space=pl.ANY)] * 4,
-                pl.BlockSpec((3, 3, CH), lambda h, k, at: (0, 0, 0)),
+                pl.BlockSpec((3, 3, CH), lambda h, at: (0, 0, 0)),
             ],
             out_specs=[
-                pl.BlockSpec((3, 1, ROWS, CH), lambda h, k, at: (0, h, 0, 0)),
-                pl.BlockSpec((1, HALO, CH), lambda h, k, at: (h, 0, 0)),
-                pl.BlockSpec((1, HALO, CH), lambda h, k, at: (h, 0, 0)),
-                pl.BlockSpec((HALO, CH), lambda h, k, at: (0, 0)),
+                pl.BlockSpec((3, 1, ROWS, CH), lambda h, at: (0, h, 0, 0)),
+                pl.BlockSpec((1, HALO, CH), lambda h, at: (h, 0, 0)),
+                pl.BlockSpec((1, HALO, CH), lambda h, at: (h, 0, 0)),
+                pl.BlockSpec((HALO, CH), lambda h, at: (0, 0)),
                 pl.BlockSpec(memory_space=pltpu.HBM),
             ],
             scratch_shapes=[
-                pltpu.VMEM((2, 4 * WIDE, 3 * CH), BF16),
-                pltpu.VMEM((ROWS + TILE, 3 * CH), F32),
-                pltpu.VMEM((8, WIDE), F32),
+                pltpu.VMEM((8 * WIDE, 3 * CH), BF16),
                 pltpu.VMEM((3, SHARE + TILE, CH), F32),
                 pltpu.SemaphoreType.DMA((2, 4, 4)),
                 pltpu.SemaphoreType.DMA((2, 4, 4, 2)),
@@ -362,7 +337,7 @@
         chosen = lax.ppermute(chosen, ("zh", "c"), pairs)
         pieces.append(jnp.concatenate([chosen[:128], chosen[128:]], axis=1))
     own, got, pieces = lax.optimization_barrier((own, got, pieces))
-    gathered = lax.all_gather(own, ring).reshape(2, 4, 2, ROWS + TILE, WIDE)
+    gathered = lax.all_gather(own, ring).reshape(2, 8, ROWS + TILE, WIDE)
     kept = jnp.concatenate([kept, pieces[0]], axis=1)
     got = jnp.concatenate([got, pieces[1]], axis=1)
     weights = (

time: 194 us -> 196 us (1.010)
  no operation moved by 1% of the time
where the time goes in v13:
time: 196 us; the launch traced here: 194 us
  waiting for transfers between devices  115 us (59%)
  starting transfers between devices  26.5 us (14%)
  Pallas kernels  25.9 us (13%)
  between operations  13.7 us (7%)
  other arithmetic  7.15 us (4%)
  local copies, waits for them, and re-layouts  6.11 us (3%)
    reduce_scatter x1, waiting for transfers between devices, on_device(): lax.psum_scatter(partial.reshape(8, ROWS, WIDE), ('zh', 'zl'), scatter_di...  54.3 us
    ppermute x8, waiting for transfers between devices, pair_step(): return lax.ppermute(value, (axis, 'c'), pairs)  49.7 us
    pallas_call x1, Pallas kernels, project(): pl.pallas_call(project_kernel, grid_spec=pltpu.PrefetchScalarGridSpec(num...  16.6 us
    ppermute x8, starting transfers between devices, pair_step(): return lax.ppermute(value, (axis, 'c'), pairs)  11.1 us
    ppermute x1, waiting for transfers between devices, on_device(): got = lax.ppermute(jnp.where(zh == 0, right, left), 'zh', [(0, 1), (1, 0)])  9.51 us
    ppermute x2, starting transfers between devices, on_device(): chosen = lax.ppermute(chosen, ('zh', 'c'), pairs)  7.93 us
    pallas_call x2, Pallas kernels, project_out(): pl.pallas_call(out_kernel, grid_spec=pltpu.PrefetchScalarGridSpec(num_sca...  5.93 us
  transfers between devices with their start and end apart: 17, of which 10 were waited for; matrix products, arithmetic and copies ran while one was open for 3% of the time, Pallas kernels for 2%

profile of v13, /device:TPU:2, one launch (start us, length us, event | category | flops | bytes accessed | tf_op | source)
XLA Modules:
  0.0 194.3 jit_solution(2945535693101691981)
XLA Ops:
  6.6 0.9 constant_dynamic-slice_fusion.1
  7.5 7.3 %collective-permute-start.2 = (bf16[256,128]{1,0:T(8,128)(2,1)S(1)}, bf16[256,128]{1,0:T(8,128)(2,1)S(1)}, u32[]{:S(2)}, u32[]{:S(2)}) collective-permute-start(bf16[256,128]{1,0:T(8,128)(2,1)S(1)} %get-tuple-element.59), channel_id=1, source_target_pairs={{0,32},{1,0},{32,33},{33,1},{2,34},{3,2},{34,35},{35,3},{4,36},{5,... | collective-permute-start | bytes 196616 | tf_op jit(solution)/shard_map/ppermute | solution.py:337
  14.8 0.7 collective-permute-start.1
  15.5 1.0 slice_bitcast_fusion.5
  16.6 1.4 collective-permute-start
  17.9 0.7 convert_element_type.41
  18.6 0.2 fusion.1
  18.8 0.1 fusion.5
  19.0 0.9 fusion.4
  20.0 9.5 %collective-permute-done = bf16[128,768]{1,0:T(8,128)(2,1)S(1)} collective-permute-done((bf16[128,768]{1,0:T(8,128)(2,1)S(1)}, bf16[128,768]{1,0:T(8,128)(2,1)S(1)}, u32[]{:S(2)}, u32[]{:S(2)}) %collective-permute-start) | collective-permute-done | bytes 196640 | tf_op jit(solution)/shard_map/ppermute | solution.py:332
  29.6 1.7 collective-permute-start.7
  31.3 0.6 collective-permute-start.3
  31.9 4.1 %collective-permute-done.7 = bf16[128,1024]{1,0:T(8,128)(2,1)S(1)} collective-permute-done((bf16[128,1024]{1,0:T(8,128)(2,1)S(1)}, bf16[128,1024]{1,0:T(8,128)(2,1)S(1)}, u32[]{:S(2)}, u32[]{:S(2)}) %collective-permute-start.7) | collective-permute-done | bytes 262176 | tf_op jit(solution)/shard_map/ppermute | solution.py:288
  36.1 3.1 %collective-permute-start.8 = (bf16[2,128,1024]{2,1,0:T(8,128)(2,1)S(1)}, bf16[2,128,1024]{2,1,0:T(8,128)(2,1)S(1)}, u32[]{:S(2)}, u32[]{:S(2)}) collective-permute-start(bf16[2,128,1024]{2,1,0:T(8,128)(2,1)S(1)} %pad_maximum_fusion.5), channel_id=1, source_target_pairs={{0,192},{1,65},{64,128},{65,1},{128,64},{129,193},{192,0},{193,129... | collective-permute-start | bytes 1572872 | tf_op jit(solution)/shard_map/ppermute | solution.py:288
  39.3 1.6 collective-permute-start.4
  40.8 5.7 %collective-permute-done.8 = bf16[2,128,1024]{2,1,0:T(8,128)(2,1)S(1)} collective-permute-done((bf16[2,128,1024]{2,1,0:T(8,128)(2,1)S(1)}, bf16[2,128,1024]{2,1,0:T(8,128)(2,1)S(1)}, u32[]{:S(2)}, u32[]{:S(2)}) %collective-permute-start.8) | collective-permute-done | bytes 524320 | tf_op jit(solution)/shard_map/ppermute | solution.py:288
  46.6 0.1 fusion.11
  46.7 0.4 collective-permute-start.9
  47.1 2.2 %collective-permute-done.4 = bf16[2,128,1024]{2,1,0:T(8,128)(2,1)S(1)} collective-permute-done((bf16[2,128,1024]{2,1,0:T(8,128)(2,1)S(1)}, bf16[2,128,1024]{2,1,0:T(8,128)(2,1)S(1)}, u32[]{:S(2)}, u32[]{:S(2)}) %collective-permute-start.4) | collective-permute-done | bytes 524320 | tf_op jit(solution)/shard_map/ppermute | solution.py:288
  49.3 0.1 fusion.12
  49.5 0.1 collective-permute-start.5
  49.6 12.1 %collective-permute-done.9 = bf16[4,128,1024]{2,1,0:T(8,128)(2,1)S(1)} collective-permute-done((bf16[4,128,1024]{2,1,0:T(8,128)(2,1)S(1)}, bf16[4,128,1024]{2,1,0:T(8,128)(2,1)S(1)}, u32[]{:S(2)}, u32[]{:S(2)}) %collective-permute-start.9) | collective-permute-done | bytes 1048608 | tf_op jit(solution)/shard_map/ppermute | solution.py:288
  61.6 0.2 pad_maximum_fusion.1.refs_2_
  61.8 1.6 collective-permute-start.10
  63.4 0.9 collective-permute-done.5
  64.4 1.5 pad_maximum_fusion.refs_0_
  65.8 2.1 %collective-permute-start.6 = (bf16[2,4,128,1024]{3,2,1,0:T(8,128)(2,1)}, bf16[2,4,128,1024]{3,2,1,0:T(8,128)(2,1)}, u32[]{:S(2)}, u32[]{:S(2)}) collective-permute-start(bf16[2,4,128,1024]{3,2,1,0:T(8,128)(2,1)} %pad_maximum_fusion.refs_0_), channel_id=1, source_target_pairs={{0,192},{1,65},{64,128},{65,1},{128,64},{129,193},{192,0},{193,129... | collective-permute-start | bytes 6291464 | tf_op jit(solution)/shard_map/ppermute | solution.py:288
  68.0 0.1 pad.19.u_ref
  68.1 0.5 toeplitz.1.band_ref
  68.6 0.1 dynamic_slice.23
  68.7 0.1 pad_add_fusion.at_ref
  68.8 19.3 %collective-permute-done.10.refs_3_ = bf16[2,4,128,1024]{3,2,1,0:T(8,128)(2,1)} collective-permute-done((bf16[2,4,128,1024]{3,2,1,0:T(8,128)(2,1)S(1)}, bf16[2,4,128,1024]{3,2,1,0:T(8,128)(2,1)}, u32[]{:S(2)}, u32[]{:S(2)}) %collective-permute-start.10) | collective-permute-done | bytes 2097184 | tf_op jit(solution)/shard_map/ppermute | solution.py:288
  88.0 5.3 %collective-permute-done.6.refs_1_ = bf16[2,4,128,1024]{3,2,1,0:T(8,128)(2,1)} collective-permute-done((bf16[2,4,128,1024]{3,2,1,0:T(8,128)(2,1)}, bf16[2,4,128,1024]{3,2,1,0:T(8,128)(2,1)}, u32[]{:S(2)}, u32[]{:S(2)}) %collective-permute-start.6) | collective-permute-done | bytes 2097184 | tf_op jit(solution)/shard_map/ppermute | solution.py:288
  93.4 16.6 %project.1 = (bf16[3,2,512,256]{3,2,1,0:T(8,128)(2,1)S(1)}, bf16[2,144,256]{2,1,0:T(8,128)(2,1)S(1)}, bf16[2,144,256]{2,1,0:T(8,128)(2,1)S(1)}, bf16[144,256]{1,0:T(8,128)(2,1)S(1)}, bf16[4,512,512]{2,1,0:T(8,128)(2,1)S(1)}) custom-call(s32[10]{0:T(128)S(1)} %pad_add_fusion.at_ref, bf16[2,8,592,512]{3,2,1,0:T(8,128)(2,1)} %bitcast.54, ...), custom_call_target="tpu_custom_call" | custom-call | flops 6442450944 | bytes 18000000 | tf_op jit(solution)/shard_map/project/pallas_call | solution.py:117
  110.0 0.7 copy-done.4
  110.7 1.5 mix.2.mine_ref
  112.1 1.2 copy-done.2
  113.3 0.9 select_bitcast_fusion.1
  114.2 3.4 %collective-permute-start.11 = (bf16[144,256]{1,0:T(8,128)(2,1)S(1)}, bf16[144,256]{1,0:T(8,128)(2,1)S(1)}, u32[]{:S(2)}, u32[]{:S(2)}) collective-permute-start(bf16[144,256]{1,0:T(8,128)(2,1)S(1)} %get-tuple-element.56), channel_id=1, source_target_pairs={{0,8},{8,16},{16,24},{24,64},{64,72},{72,80},{80,88},{88,128},{128... | collective-permute-start | bytes 221192 | tf_op jit(solution)/shard_map/ppermute | solution.py:358
  117.7 2.5 %collective-permute-start.12 = (bf16[144,256]{1,0:T(8,128)(2,1)S(1)}, bf16[144,256]{1,0:T(8,128)(2,1)S(1)}, u32[]{:S(2)}, u32[]{:S(2)}) collective-permute-start(bf16[144,256]{1,0:T(8,128)(2,1)S(1)} %get-tuple-element.55), channel_id=1, source_target_pairs={{0,8},{8,16},{16,24},{24,0},{64,72},{72,80},{80,88},{88,64},{128,1... | collective-permute-start | bytes 221192 | tf_op jit(solution)/shard_map/ppermute | solution.py:359
  120.1 3.4 %project_out.2.refs_0_ = bf16[2,4,512,512]{3,2,1,0:T(8,128)(2,1)S(1)} custom-call(s32[10]{0:T(128)S(1)} %pad_add_fusion.at_ref, bf16[2,256,256]{2,1,0:T(8,128)(2,1)S(1)} %mix.2.mine_ref, bf16[2,256,256]{2,1,0:T(8,128)(2,1)} %collective-permute-done.13.other_ref, bf16[4,512,512]{2,1,0:T(8,128)(2,1)S(1)} %get-tuple-element.35.w_ref), custom_call_target="tpu_custom_call" | custom-call | flops 1073741824 | bytes 5000000 | tf_op jit(solution)/shard_map/project_out/pallas_call | solution.py:260
  123.7 1.5 mix.3.mine_ref
  125.1 0.1 collective-permute-start.14
  125.2 1.5 collective-permute-done.14.other_ref
  126.8 2.5 %project_out.3 = bf16[2,4,512,512]{3,2,1,0:T(8,128)(2,1)S(1)} custom-call(s32[10]{0:T(128)S(1)} %pad_add_fusion.at_ref, bf16[2,256,256]{2,1,0:T(8,128)(2,1)S(1)} %mix.3.mine_ref, bf16[2,256,256]{2,1,0:T(8,128)(2,1)S(1)} %collective-permute-done.14.other_ref, bf16[4,512,512]{2,1,0:T(8,128)(2,1)S(1)} %get-tuple-element.35.w_ref, ...), custom_call_target="tpu_custom_call", output_to_operand_aliasing={{}: (4, {})} | custom-call | flops 1073741824 | bytes 5000000 | tf_op jit(solution)/shard_map/project_out/pallas_call | solution.py:260
  129.3 2.0 %copy-done.1 = bf16[2,4,512,512]{3,2,1,0:T(8,128)(2,1)} copy-done((bf16[2,4,512,512]{3,2,1,0:T(8,128)(2,1)}, bf16[2,4,512,512]{3,2,1,0:T(8,128)(2,1)S(1)}, u32[]{:S(2)}) %copy-start.1) | copy-done | bytes 4194328
  131.3 54.3 %reduce-scatter.2.cloned.1.call-done = bf16[1,512,512]{2,1,0:T(8,128)(2,1)} async-done(((bf16[8,512,512]{2,1,0:T(8,128)(2,1)}), bf16[1,512,512]{2,1,0:T(8,128)(2,1)}) %reduce-scatter.2.cloned.1.call-update) | async-done | bytes 524304 | tf_op jit(solution)/shard_map/reduce_scatter | solution.py:371
  185.5 2.0 %fusion.3 = bf16[512,512]{1,0:T(8,128)(2,1)} fusion(bf16[512,512]{1,0:T(8,128)(2,1)S(1)} %copy-done.6, bf16[1,512,512]{2,1,0:T(8,128)(2,1)} %reduce-scatter.2.cloned.1.call-done), kind=kLoop, calls=%fused_computation.9 | loop fusion | flops 1048576 | bytes 1572864 | tf_op jit(solution)/shard_map/convert_element_type | solution.py:374
  (54 shorter events, 0.6 us)
Async XLA Ops:
  6.5 62.2 %copy-start = (f32[3,3,512]{2,1,0:T(4,128)S(1)}, f32[3,3,512]{2,1,0:T(4,128)}, u32[]{:S(2)}) copy-start(f32[3,3,512]{2,1,0:T(4,128)} %param.14) | copy-start | bytes 55300
  6.5 12.1 %copy-start.5 = (bf16[512,512]{1,0:T(8,128)(2,1)S(1)}, bf16[512,512]{1,0:T(8,128)(2,1)}, u32[]{:S(2)}) copy-start(bf16[512,512]{1,0:T(8,128)(2,1)} %param.10) | copy-start | bytes 1572868
  6.5 12.3 %copy-start.8 = (bf16[129,512]{1,0:T(8,128)(2,1)S(1)}, bf16[129,512]{1,0:T(8,128)(2,1)}, u32[]{:S(2)}) copy-start(bf16[129,512]{1,0:T(8,128)(2,1)} %param.11) | copy-start | bytes 396292
  6.5 86.9 %all-gather.3.cloned.1.call-start = ((), (), s32[]{:S(2)}) async-start(), calls=%async_computation.2 | async-start | bytes 10305536 | tf_op jit(solution)/shard_map/all_gather | solution.py:340
  7.5 12.4 %collective-permute-start.2 = (bf16[256,128]{1,0:T(8,128)(2,1)S(1)}, bf16[256,128]{1,0:T(8,128)(2,1)S(1)}, u32[]{:S(2)}, u32[]{:S(2)}) collective-permute-start(bf16[256,128]{1,0:T(8,128)(2,1)S(1)} %get-tuple-element.59), channel_id=1, source_target_pairs={{0,32},{1,0},{32,33},{33,1},{2,34},{3,2},{34,35},{35,3},{4,36},{5,... | collective-permute-start | bytes 196616 | tf_op jit(solution)/shard_map/ppermute | solution.py:337
  14.8 5.1 %collective-permute-start.1 = (bf16[256,128]{1,0:T(8,128)(2,1)S(1)}, bf16[256,128]{1,0:T(8,128)(2,1)S(1)}, u32[]{:S(2)}, u32[]{:S(2)}) collective-permute-start(bf16[256,128]{1,0:T(8,128)(2,1)S(1)} %get-tuple-element.60), channel_id=1, source_target_pairs={{0,0},{1,32},{32,1},{33,33},{2,2},{3,34},{34,3},{35,35},{4,4},{5,3... | collective-permute-start | bytes 196616 | tf_op jit(solution)/shard_map/ppermute | solution.py:337
  16.6 12.9 %collective-permute-start = (bf16[128,768]{1,0:T(8,128)(2,1)S(1)}, bf16[128,768]{1,0:T(8,128)(2,1)S(1)}, u32[]{:S(2)}, u32[]{:S(2)}) collective-permute-start(bf16[128,768]{1,0:T(8,128)(2,1)S(1)} %get-tuple-element.46), channel_id=1, source_target_pairs={{0,32},{32,0},{1,33},{33,1},{2,34},{34,2},{3,35},{35,3},{4,36},{36... | collective-permute-start | bytes 589832 | tf_op jit(solution)/shard_map/ppermute | solution.py:332
  29.5 156.0 %reduce-scatter.2.cloned.1.call-start = ((), (), s32[]{:S(2)}) async-start(), calls=%async_computation.1 | async-start | bytes 4718592 | tf_op jit(solution)/shard_map/reduce_scatter | solution.py:371
  29.6 6.5 %collective-permute-start.7 = (bf16[128,1024]{1,0:T(8,128)(2,1)S(1)}, bf16[128,1024]{1,0:T(8,128)(2,1)S(1)}, u32[]{:S(2)}, u32[]{:S(2)}) collective-permute-start(bf16[128,1024]{1,0:T(8,128)(2,1)S(1)} %constant_dynamic-update-slice_fusion), channel_id=1, source_target_pairs={{0,64},{1,193},{64,0},{65,129},{128,192},{129,65},{192,128},{193,1... | collective-permute-start | bytes 786440 | tf_op jit(solution)/shard_map/ppermute | solution.py:288
  31.3 7.9 %collective-permute-start.3 = (bf16[128,1024]{1,0:T(8,128)(2,1)S(1)}, bf16[128,1024]{1,0:T(8,128)(2,1)S(1)}, u32[]{:S(2)}, u32[]{:S(2)}) collective-permute-start(bf16[128,1024]{1,0:T(8,128)(2,1)S(1)} %get-tuple-element.54), channel_id=1, source_target_pairs={{0,8},{1,25},{8,0},{9,17},{16,24},{17,9},{24,16},{25,1},{2,10},{3,... | collective-permute-start | bytes 786440 | tf_op jit(solution)/shard_map/ppermute | solution.py:288
  36.1 10.5 %collective-permute-start.8 = (bf16[2,128,1024]{2,1,0:T(8,128)(2,1)S(1)}, bf16[2,128,1024]{2,1,0:T(8,128)(2,1)S(1)}, u32[]{:S(2)}, u32[]{:S(2)}) collective-permute-start(bf16[2,128,1024]{2,1,0:T(8,128)(2,1)S(1)} %pad_maximum_fusion.5), channel_id=1, source_target_pairs={{0,192},{1,65},{64,128},{65,1},{128,64},{129,193},{192,0},{193,129... | collective-permute-start | bytes 1572872 | tf_op jit(solution)/shard_map/ppermute | solution.py:288
  39.3 10.0 %collective-permute-start.4 = (bf16[2,128,1024]{2,1,0:T(8,128)(2,1)S(1)}, bf16[2,128,1024]{2,1,0:T(8,128)(2,1)S(1)}, u32[]{:S(2)}, u32[]{:S(2)}) collective-permute-start(bf16[2,128,1024]{2,1,0:T(8,128)(2,1)S(1)} %pad_maximum_fusion.4), channel_id=1, source_target_pairs={{0,24},{1,9},{8,16},{9,1},{16,8},{17,25},{24,0},{25,17},{2,26},{3,... | collective-permute-start | bytes 1572872 | tf_op jit(solution)/shard_map/ppermute | solution.py:288
  46.7 14.9 %collective-permute-start.9 = (bf16[4,128,1024]{2,1,0:T(8,128)(2,1)S(1)}, bf16[4,128,1024]{2,1,0:T(8,128)(2,1)S(1)}, u32[]{:S(2)}, u32[]{:S(2)}) collective-permute-start(bf16[4,128,1024]{2,1,0:T(8,128)(2,1)S(1)} %get-tuple-element.40), channel_id=1, source_target_pairs={{0,8},{1,25},{8,0},{9,17},{16,24},{17,9},{24,16},{25,1},{2,10},{3,... | collective-permute-start | bytes 3145736 | tf_op jit(solution)/shard_map/ppermute | solution.py:288
  49.5 14.9 %collective-permute-start.5 = (bf16[4,128,1024]{2,1,0:T(8,128)(2,1)S(1)}, bf16[4,128,1024]{2,1,0:T(8,128)(2,1)S(1)}, u32[]{:S(2)}, u32[]{:S(2)}) collective-permute-start(bf16[4,128,1024]{2,1,0:T(8,128)(2,1)S(1)} %get-tuple-element.42), channel_id=1, source_target_pairs={{0,64},{1,193},{64,0},{65,129},{128,192},{129,65},{192,128},{193,1... | collective-permute-start | bytes 3145736 | tf_op jit(solution)/shard_map/ppermute | solution.py:288
  61.8 4.0 %copy-start.7 = (bf16[2,4,128,1024]{3,2,1,0:T(8,128)(2,1)}, bf16[2,4,128,1024]{3,2,1,0:T(8,128)(2,1)S(1)}, u32[]{:S(2)}) copy-start(bf16[2,4,128,1024]{3,2,1,0:T(8,128)(2,1)S(1)} %pad_maximum_fusion.1.refs_2_) | copy-start | bytes 6291460
  61.8 26.2 %collective-permute-start.10 = (bf16[2,4,128,1024]{3,2,1,0:T(8,128)(2,1)S(1)}, bf16[2,4,128,1024]{3,2,1,0:T(8,128)(2,1)}, u32[]{:S(2)}, u32[]{:S(2)}) collective-permute-start(bf16[2,4,128,1024]{3,2,1,0:T(8,128)(2,1)S(1)} %pad_maximum_fusion.1.refs_2_), channel_id=1, source_target_pairs={{0,24},{1,9},{8,16},{9,1},{16,8},{17,25},{24,0},{25,17},{2,26},{3,... | collective-permute-start | bytes 6291464 | tf_op jit(solution)/shard_map/ppermute | solution.py:288
  64.3 3.6 %copy-start.9 = (bf16[32,128]{1,0:T(8,128)(2,1)S(1)}, bf16[32,128]{1,0:T(8,128)(2,1)}, u32[]{:S(2)}) copy-start(bf16[32,128]{1,0:T(8,128)(2,1)} %param.15) | copy-start | bytes 24580
  64.3 4.2 %copy-start.12 = (f32[512]{0:T(512)S(1)}, f32[512]{0:T(512)}, u32[]{:S(2)}) copy-start(f32[512]{0:T(512)} %param.16) | copy-start | bytes 6148
  64.3 4.3 %copy-start.10 = (s32[4]{0:T(128)S(1)}, s32[4]{0:T(128)}, u32[]{:S(2)}) copy-start(s32[4]{0:T(128)} %constant.44.clone) | copy-start | bytes 52
  64.3 4.3 %copy-start.11 = (s32[4]{0:T(128)S(1)}, s32[4]{0:T(128)}, u32[]{:S(2)}) copy-start(s32[4]{0:T(128)} %constant.45.clone) | copy-start | bytes 52
  65.8 27.6 %collective-permute-start.6 = (bf16[2,4,128,1024]{3,2,1,0:T(8,128)(2,1)}, bf16[2,4,128,1024]{3,2,1,0:T(8,128)(2,1)}, u32[]{:S(2)}, u32[]{:S(2)}) collective-permute-start(bf16[2,4,128,1024]{3,2,1,0:T(8,128)(2,1)} %pad_maximum_fusion.refs_0_), channel_id=1, source_target_pairs={{0,192},{1,65},{64,128},{65,1},{128,64},{129,193},{192,0},{193,129... | collective-permute-start | bytes 6291464 | tf_op jit(solution)/shard_map/ppermute | solution.py:288
  110.0 0.7 copy-start.4
  112.1 1.2 copy-start.2
  113.3 6.8 %collective-permute-start.13 = (bf16[2,256,256]{2,1,0:T(8,128)(2,1)S(1)}, bf16[2,256,256]{2,1,0:T(8,128)(2,1)}, u32[]{:S(2)}, u32[]{:S(2)}) collective-permute-start(bf16[2,256,256]{2,1,0:T(8,128)(2,1)S(1)} %mix.2.mine_ref), channel_id=1, source_target_pairs={{0,1},{1,0},{2,3},{3,2},{4,5},{5,4},{6,7},{7,6},{8,9},{9,8},{10,11... | collective-permute-start | bytes 786440 | tf_op jit(solution)/shard_map/ppermute | solution.py:363
  114.2 9.4 %collective-permute-start.11 = (bf16[144,256]{1,0:T(8,128)(2,1)S(1)}, bf16[144,256]{1,0:T(8,128)(2,1)S(1)}, u32[]{:S(2)}, u32[]{:S(2)}) collective-permute-start(bf16[144,256]{1,0:T(8,128)(2,1)S(1)} %get-tuple-element.56), channel_id=1, source_target_pairs={{0,8},{8,16},{16,24},{24,64},{64,72},{72,80},{80,88},{88,128},{128... | collective-permute-start | bytes 221192 | tf_op jit(solution)/shard_map/ppermute | solution.py:358
  117.7 6.0 %collective-permute-start.12 = (bf16[144,256]{1,0:T(8,128)(2,1)S(1)}, bf16[144,256]{1,0:T(8,128)(2,1)S(1)}, u32[]{:S(2)}, u32[]{:S(2)}) collective-permute-start(bf16[144,256]{1,0:T(8,128)(2,1)S(1)} %get-tuple-element.55), channel_id=1, source_target_pairs={{0,8},{8,16},{16,24},{24,0},{64,72},{72,80},{80,88},{88,64},{128,1... | collective-permute-start | bytes 221192 | tf_op jit(solution)/shard_map/ppermute | solution.py:359
  120.1 3.5 %copy-start.3 = (bf16[3,2,512,256]{3,2,1,0:T(8,128)(2,1)S(1)}, bf16[3,2,512,256]{3,2,1,0:T(8,128)(2,1)}, u32[]{:S(2)}) copy-start(bf16[3,2,512,256]{3,2,1,0:T(8,128)(2,1)} %copy-done.2) | copy-start | bytes 4718596
  125.1 1.6 collective-permute-start.14
  129.3 2.0 %copy-start.1 = (bf16[2,4,512,512]{3,2,1,0:T(8,128)(2,1)}, bf16[2,4,512,512]{3,2,1,0:T(8,128)(2,1)S(1)}, u32[]{:S(2)}) copy-start(bf16[2,4,512,512]{3,2,1,0:T(8,128)(2,1)S(1)} %project_out.3) | copy-start | bytes 12582916
  131.2 54.3 %copy-start.6 = (bf16[512,512]{1,0:T(8,128)(2,1)S(1)}, bf16[512,512]{1,0:T(8,128)(2,1)}, u32[]{:S(2)}) copy-start(bf16[512,512]{1,0:T(8,128)(2,1)} %param.10) | copy-start | bytes 1572868
Sparse Core Ops, SparseCore 0:
  29.6 62.0 all-gather.2
  131.4 54.0 reduce-scatter.1

commit v14 on v12

--- a/solution.py
+++ b/solution.py
@@ -360,6 +360,7 @@
         chosen = lax.dynamic_slice_in_dim(out_weight, (core ^ k) * CH, CH, 0)
         pairs = [(a * 2 + b, (b ^ k) * 2 + a) for a in range(2) for b in range(2)]
         chosen = lax.ppermute(chosen, ("zh", "c"), pairs)
+        out_weight, chosen = lax.optimization_barrier((out_weight, chosen))
         pieces.append(jnp.concatenate([chosen[:128], chosen[128:]], axis=1))
     own, got, pieces = lax.optimization_barrier((own, got, pieces))
     gathered = lax.all_gather(own, ring).reshape(2, 4, 2, ROWS + TILE, WIDE)

time: 194 us -> 200 us (1.031)
  starting transfers between devices: 26.4 us -> 30.9 us
    ppermute x1, waiting for transfers between devices: 9.51 us -> 0.01 us  [on_device(): got = lax.ppermute(jnp.where(zh == 0, right, left), 'zh', [(0, 1), (1, 0)])]
    reduce_scatter x1, waiting for transfers between devices: 54.3 us -> 62.2 us  [on_device(): lax.psum_scatter(partial.reshape(8, ROWS, WIDE), ('zh', 'zl'), scatter_di...]
    ppermute x1, starting transfers between devices: 1.37 us -> 8.53 us  [on_device(): got = lax.ppermute(jnp.where(zh == 0, right, left), 'zh', [(0, 1), (1, 0)])]
    ppermute x2, waiting for transfers between devices: 0.01 us -> 3.33 us  [on_device(): chosen = lax.ppermute(chosen, ('zh', 'c'), pairs)]
    ppermute x2, starting transfers between devices: 7.93 us -> 5.08 us  [on_device(): chosen = lax.ppermute(chosen, ('zh', 'c'), pairs)]
    unnamed x27 -> x39, local copies, waits for them, and re-layouts: 3.86 us -> 5.33 us
  transfers between devices with their start and end apart: 17 -> 17, of which waited for: 10 -> 11; matrix products, arithmetic and copies ran while one was open for 3% -> 3% of each run, Pallas kernels for 2% -> 2%
where the time goes in v14:
time: 200 us; the launch traced here: 199 us
  waiting for transfers between devices  116 us (58%)
  starting transfers between devices  30.9 us (15%)
  Pallas kernels  24.3 us (12%)
  between operations  13.7 us (7%)
  other arithmetic  7.16 us (4%)
  local copies, waits for them, and re-layouts  6.64 us (3%)
    reduce_scatter x1, waiting for transfers between devices, on_device(): lax.psum_scatter(partial.reshape(8, ROWS, WIDE), ('zh', 'zl'), scatter_di...  62.2 us
    ppermute x8, waiting for transfers between devices, pair_step(): return lax.ppermute(value, (axis, 'c'), pairs)  47.8 us
    pallas_call x1, Pallas kernels, project(): pl.pallas_call(project_kernel, grid_spec=pltpu.PrefetchScalarGridSpec(num...  15.1 us
    ppermute x8, starting transfers between devices, pair_step(): return lax.ppermute(value, (axis, 'c'), pairs)  12.3 us
    ppermute x1, starting transfers between devices, on_device(): got = lax.ppermute(jnp.where(zh == 0, right, left), 'zh', [(0, 1), (1, 0)])  8.53 us
    pallas_call x2, Pallas kernels, project_out(): pl.pallas_call(out_kernel, grid_spec=pltpu.PrefetchScalarGridSpec(num_sca...  5.93 us
    unnamed x39, local copies, waits for them, and re-layouts  5.33 us
    ppermute x2, starting transfers between devices, on_device(): chosen = lax.ppermute(chosen, ('zh', 'c'), pairs)  5.08 us
  transfers between devices with their start and end apart: 17, of which 11 were waited for; matrix products, arithmetic and copies ran while one was open for 3% of the time, Pallas kernels for 2%

profile of v14, /device:TPU:2, one launch (start us, length us, event | category | flops | bytes accessed | tf_op | source)
XLA Modules:
  0.0 199.1 jit_solution(5386551768803002535)
XLA Ops:
  6.6 0.9 copy-done
  7.4 0.7 collective-permute-start.1
  8.1 1.0 slice_bitcast_fusion.5
  9.2 8.5 %collective-permute-start = (bf16[128,768]{1,0:T(8,128)(2,1)S(1)}, bf16[128,768]{1,0:T(8,128)(2,1)S(1)}, u32[]{:S(2)}, u32[]{:S(2)}) collective-permute-start(bf16[128,768]{1,0:T(8,128)(2,1)S(1)} %get-tuple-element.52), channel_id=1, source_target_pairs={{0,32},{32,0},{1,33},{33,1},{2,34},{34,2},{3,35},{35,3},{4,36},{36... | collective-permute-start | bytes 589832 | tf_op jit(solution)/shard_map/ppermute | solution.py:357
  17.8 0.7 convert_element_type.41
  18.4 0.2 fusion.1
  18.7 0.1 fusion.5
  18.9 0.9 fusion.4
  19.7 4.4 %collective-permute-start.2 = (bf16[256,128]{1,0:T(8,128)(2,1)S(1)}, bf16[256,128]{1,0:T(8,128)(2,1)S(1)}, u32[]{:S(2)}, u32[]{:S(2)}) collective-permute-start(bf16[256,128]{1,0:T(8,128)(2,1)S(1)} %constant_dynamic-slice_fusion.1), channel_id=1, source_target_pairs={{0,32},{1,0},{32,33},{33,1},{2,34},{3,2},{34,35},{35,3},{4,36},{5,... | collective-permute-start | bytes 196616 | tf_op jit(solution)/shard_map/ppermute | solution.py:362
  24.2 3.3 %collective-permute-done.2 = bf16[256,128]{1,0:T(8,128)(2,1)S(1)} collective-permute-done((bf16[256,128]{1,0:T(8,128)(2,1)S(1)}, bf16[256,128]{1,0:T(8,128)(2,1)S(1)}, u32[]{:S(2)}, u32[]{:S(2)}) %collective-permute-start.2) | collective-permute-done | bytes 65568 | tf_op jit(solution)/shard_map/ppermute | solution.py:362
  27.6 1.7 collective-permute-start.7
  29.4 0.6 collective-permute-start.3
  30.0 4.1 %collective-permute-done.7 = bf16[128,1024]{1,0:T(8,128)(2,1)S(1)} collective-permute-done((bf16[128,1024]{1,0:T(8,128)(2,1)S(1)}, bf16[128,1024]{1,0:T(8,128)(2,1)S(1)}, u32[]{:S(2)}, u32[]{:S(2)}) %collective-permute-start.7) | collective-permute-done | bytes 262176 | tf_op jit(solution)/shard_map/ppermute | solution.py:313
  34.2 3.1 %collective-permute-start.8 = (bf16[2,128,1024]{2,1,0:T(8,128)(2,1)S(1)}, bf16[2,128,1024]{2,1,0:T(8,128)(2,1)S(1)}, u32[]{:S(2)}, u32[]{:S(2)}) collective-permute-start(bf16[2,128,1024]{2,1,0:T(8,128)(2,1)S(1)} %pad_maximum_fusion.5), channel_id=1, source_target_pairs={{0,192},{1,65},{64,128},{65,1},{128,64},{129,193},{192,0},{193,129... | collective-permute-start | bytes 1572872 | tf_op jit(solution)/shard_map/ppermute | solution.py:313
  37.3 1.6 collective-permute-start.4
  38.9 5.7 %collective-permute-done.8 = bf16[2,128,1024]{2,1,0:T(8,128)(2,1)S(1)} collective-permute-done((bf16[2,128,1024]{2,1,0:T(8,128)(2,1)S(1)}, bf16[2,128,1024]{2,1,0:T(8,128)(2,1)S(1)}, u32[]{:S(2)}, u32[]{:S(2)}) %collective-permute-start.8) | collective-permute-done | bytes 524320 | tf_op jit(solution)/shard_map/ppermute | solution.py:313
  44.6 0.1 fusion.11
  44.8 0.6 collective-permute-start.9
  45.4 1.2 collective-permute-done.4
  46.6 0.1 fusion.12
  46.7 0.2 collective-permute-start.5
  47.0 12.7 %collective-permute-done.9 = bf16[4,128,1024]{2,1,0:T(8,128)(2,1)S(1)} collective-permute-done((bf16[4,128,1024]{2,1,0:T(8,128)(2,1)S(1)}, bf16[4,128,1024]{2,1,0:T(8,128)(2,1)S(1)}, u32[]{:S(2)}, u32[]{:S(2)}) %collective-permute-start.9) | collective-permute-done | bytes 1048608 | tf_op jit(solution)/shard_map/ppermute | solution.py:313
  59.7 0.2 pad_maximum_fusion.1.refs_2_
  59.9 1.6 collective-permute-start.10
  61.5 0.2 collective-permute-done.5
  61.6 1.5 pad_maximum_fusion.refs_0_
  63.1 2.9 %collective-permute-start.6 = (bf16[2,4,128,1024]{3,2,1,0:T(8,128)(2,1)}, bf16[2,4,128,1024]{3,2,1,0:T(8,128)(2,1)}, u32[]{:S(2)}, u32[]{:S(2)}) collective-permute-start(bf16[2,4,128,1024]{3,2,1,0:T(8,128)(2,1)} %pad_maximum_fusion.refs_0_), channel_id=1, source_target_pairs={{0,192},{1,65},{64,128},{65,1},{128,64},{129,193},{192,0},{193,129... | collective-permute-start | bytes 6291464 | tf_op jit(solution)/shard_map/ppermute | solution.py:313
  66.2 0.5 toeplitz.1.band_ref
  66.8 19.3 %collective-permute-done.10.refs_3_ = bf16[2,4,128,1024]{3,2,1,0:T(8,128)(2,1)} collective-permute-done((bf16[2,4,128,1024]{3,2,1,0:T(8,128)(2,1)S(1)}, bf16[2,4,128,1024]{3,2,1,0:T(8,128)(2,1)}, u32[]{:S(2)}, u32[]{:S(2)}) %collective-permute-start.10) | collective-permute-done | bytes 2097184 | tf_op jit(solution)/shard_map/ppermute | solution.py:313
  86.1 4.6 %collective-permute-done.6.refs_1_ = bf16[2,4,128,1024]{3,2,1,0:T(8,128)(2,1)} collective-permute-done((bf16[2,4,128,1024]{3,2,1,0:T(8,128)(2,1)}, bf16[2,4,128,1024]{3,2,1,0:T(8,128)(2,1)}, u32[]{:S(2)}, u32[]{:S(2)}) %collective-permute-start.6) | collective-permute-done | bytes 2097184 | tf_op jit(solution)/shard_map/ppermute | solution.py:313
  90.7 1.5 all-gather.3.cloned.1.call-done
  92.2 15.1 %project.1 = (bf16[3,2,512,256]{3,2,1,0:T(8,128)(2,1)S(1)}, bf16[2,144,256]{2,1,0:T(8,128)(2,1)S(1)}, bf16[2,144,256]{2,1,0:T(8,128)(2,1)S(1)}, bf16[144,256]{1,0:T(8,128)(2,1)S(1)}, bf16[4,512,512]{2,1,0:T(8,128)(2,1)S(1)}) custom-call(s32[10]{0:T(128)S(1)} %pad_add_fusion.at_ref, bf16[2,4,2,592,512]{4,3,2,1,0:T(8,128)(2,1)} %bitcast.54, ...), custom_call_target="tpu_custom_call" | custom-call | flops 6442450944 | bytes 18000000 | tf_op jit(solution)/shard_map/project/pallas_call | solution.py:137
  107.3 0.7 copy-done.4
  108.0 1.4 mix.2.mine_ref
  109.4 1.2 copy-done.2
  110.6 0.2 collective-permute-start.13
  110.8 0.9 select_bitcast_fusion.1
  111.8 3.4 %collective-permute-start.11 = (bf16[144,256]{1,0:T(8,128)(2,1)S(1)}, bf16[144,256]{1,0:T(8,128)(2,1)S(1)}, u32[]{:S(2)}, u32[]{:S(2)}) collective-permute-start(bf16[144,256]{1,0:T(8,128)(2,1)S(1)} %get-tuple-element.62), channel_id=1, source_target_pairs={{0,8},{8,16},{16,24},{24,64},{64,72},{72,80},{80,88},{88,128},{128... | collective-permute-start | bytes 221192 | tf_op jit(solution)/shard_map/ppermute | solution.py:384
  115.1 1.3 collective-permute-start.12
  116.4 0.6 copy-done.8
  117.0 3.4 %project_out.2.refs_0_ = bf16[2,4,512,512]{3,2,1,0:T(8,128)(2,1)S(1)} custom-call(s32[10]{0:T(128)S(1)} %copy-done.8, bf16[2,256,256]{2,1,0:T(8,128)(2,1)S(1)} %mix.2.mine_ref, bf16[2,256,256]{2,1,0:T(8,128)(2,1)} %collective-permute-done.13.other_ref, bf16[4,512,512]{2,1,0:T(8,128)(2,1)S(1)} %get-tuple-element.41.w_ref), custom_call_target="tpu_custom_call" | custom-call | flops 1073741824 | bytes 5000000 | tf_op jit(solution)/shard_map/project_out/pallas_call | solution.py:285
  120.6 1.4 mix.3.mine_ref
  122.0 0.1 collective-permute-start.14
  122.1 1.5 collective-permute-done.14.other_ref
  123.6 2.5 %project_out.3 = bf16[2,4,512,512]{3,2,1,0:T(8,128)(2,1)S(1)} custom-call(s32[10]{0:T(128)S(1)} %copy-done.9, bf16[2,256,256]{2,1,0:T(8,128)(2,1)S(1)} %mix.3.mine_ref, bf16[2,256,256]{2,1,0:T(8,128)(2,1)S(1)} %collective-permute-done.14.other_ref, bf16[4,512,512]{2,1,0:T(8,128)(2,1)S(1)} %get-tuple-element.41.w_ref, ...), custom_call_target="tpu_custom_call", output_to_operand_aliasing={{}: (4, {})} | custom-call | flops 1073741824 | bytes 5000000 | tf_op jit(solution)/shard_map/project_out/pallas_call | solution.py:285
  126.1 2.0 copy-done.1
  128.1 62.2 %reduce-scatter.2.cloned.1.call-done = bf16[1,512,512]{2,1,0:T(8,128)(2,1)} async-done(((bf16[8,512,512]{2,1,0:T(8,128)(2,1)}), bf16[1,512,512]{2,1,0:T(8,128)(2,1)}) %reduce-scatter.2.cloned.1.call-update) | async-done | bytes 524304 | tf_op jit(solution)/shard_map/reduce_scatter | solution.py:397
  190.3 2.0 fusion.3
  (67 shorter events, 0.8 us)
Async XLA Ops:
  6.5 0.9 copy-start
  6.5 11.9 %copy-start.10 = (bf16[512,512]{1,0:T(8,128)(2,1)S(1)}, bf16[512,512]{1,0:T(8,128)(2,1)}, u32[]{:S(2)}) copy-start(bf16[512,512]{1,0:T(8,128)(2,1)} %param.10) | copy-start | bytes 1572868
  6.5 12.1 %copy-start.13 = (bf16[129,512]{1,0:T(8,128)(2,1)S(1)}, bf16[129,512]{1,0:T(8,128)(2,1)}, u32[]{:S(2)}) copy-start(bf16[129,512]{1,0:T(8,128)(2,1)} %param.11) | copy-start | bytes 396292
  6.5 85.7 %all-gather.3.cloned.1.call-start = ((), (), s32[]{:S(2)}) async-start(), calls=%async_computation.2 | async-start | bytes 10305536 | tf_op jit(solution)/shard_map/all_gather | solution.py:366
  7.4 12.3 %collective-permute-start.1 = (bf16[256,128]{1,0:T(8,128)(2,1)S(1)}, bf16[256,128]{1,0:T(8,128)(2,1)S(1)}, u32[]{:S(2)}, u32[]{:S(2)}) collective-permute-start(bf16[256,128]{1,0:T(8,128)(2,1)S(1)} %constant_dynamic-slice_fusion.2), channel_id=1, source_target_pairs={{0,0},{1,32},{32,1},{33,33},{2,2},{3,34},{34,3},{35,35},{4,4},{5,3... | collective-permute-start | bytes 196616 | tf_op jit(solution)/shard_map/ppermute | solution.py:362
  9.2 18.3 %collective-permute-start = (bf16[128,768]{1,0:T(8,128)(2,1)S(1)}, bf16[128,768]{1,0:T(8,128)(2,1)S(1)}, u32[]{:S(2)}, u32[]{:S(2)}) collective-permute-start(bf16[128,768]{1,0:T(8,128)(2,1)S(1)} %get-tuple-element.52), channel_id=1, source_target_pairs={{0,32},{32,0},{1,33},{33,1},{2,34},{34,2},{3,35},{35,3},{4,36},{36... | collective-permute-start | bytes 589832 | tf_op jit(solution)/shard_map/ppermute | solution.py:357
  19.7 7.8 %collective-permute-start.2 = (bf16[256,128]{1,0:T(8,128)(2,1)S(1)}, bf16[256,128]{1,0:T(8,128)(2,1)S(1)}, u32[]{:S(2)}, u32[]{:S(2)}) collective-permute-start(bf16[256,128]{1,0:T(8,128)(2,1)S(1)} %constant_dynamic-slice_fusion.1), channel_id=1, source_target_pairs={{0,32},{1,0},{32,33},{33,1},{2,34},{3,2},{34,35},{35,3},{4,36},{5,... | collective-permute-start | bytes 196616 | tf_op jit(solution)/shard_map/ppermute | solution.py:362
  27.6 162.7 %reduce-scatter.2.cloned.1.call-start = ((), (), s32[]{:S(2)}) async-start(), calls=%async_computation.1 | async-start | bytes 4718592 | tf_op jit(solution)/shard_map/reduce_scatter | solution.py:397
  27.6 6.5 %collective-permute-start.7 = (bf16[128,1024]{1,0:T(8,128)(2,1)S(1)}, bf16[128,1024]{1,0:T(8,128)(2,1)S(1)}, u32[]{:S(2)}, u32[]{:S(2)}) collective-permute-start(bf16[128,1024]{1,0:T(8,128)(2,1)S(1)} %constant_dynamic-update-slice_fusion), channel_id=1, source_target_pairs={{0,64},{1,193},{64,0},{65,129},{128,192},{129,65},{192,128},{193,1... | collective-permute-start | bytes 786440 | tf_op jit(solution)/shard_map/ppermute | solution.py:313
  29.4 7.9 %collective-permute-start.3 = (bf16[128,1024]{1,0:T(8,128)(2,1)S(1)}, bf16[128,1024]{1,0:T(8,128)(2,1)S(1)}, u32[]{:S(2)}, u32[]{:S(2)}) collective-permute-start(bf16[128,1024]{1,0:T(8,128)(2,1)S(1)} %get-tuple-element.60), channel_id=1, source_target_pairs={{0,8},{1,25},{8,0},{9,17},{16,24},{17,9},{24,16},{25,1},{2,10},{3,... | collective-permute-start | bytes 786440 | tf_op jit(solution)/shard_map/ppermute | solution.py:313
  34.2 10.5 %collective-permute-start.8 = (bf16[2,128,1024]{2,1,0:T(8,128)(2,1)S(1)}, bf16[2,128,1024]{2,1,0:T(8,128)(2,1)S(1)}, u32[]{:S(2)}, u32[]{:S(2)}) collective-permute-start(bf16[2,128,1024]{2,1,0:T(8,128)(2,1)S(1)} %pad_maximum_fusion.5), channel_id=1, source_target_pairs={{0,192},{1,65},{64,128},{65,1},{128,64},{129,193},{192,0},{193,129... | collective-permute-start | bytes 1572872 | tf_op jit(solution)/shard_map/ppermute | solution.py:313
  37.3 9.3 %collective-permute-start.4 = (bf16[2,128,1024]{2,1,0:T(8,128)(2,1)S(1)}, bf16[2,128,1024]{2,1,0:T(8,128)(2,1)S(1)}, u32[]{:S(2)}, u32[]{:S(2)}) collective-permute-start(bf16[2,128,1024]{2,1,0:T(8,128)(2,1)S(1)} %pad_maximum_fusion.4), channel_id=1, source_target_pairs={{0,24},{1,9},{8,16},{9,1},{16,8},{17,25},{24,0},{25,17},{2,26},{3,... | collective-permute-start | bytes 1572872 | tf_op jit(solution)/shard_map/ppermute | solution.py:313
  44.8 14.9 %collective-permute-start.9 = (bf16[4,128,1024]{2,1,0:T(8,128)(2,1)S(1)}, bf16[4,128,1024]{2,1,0:T(8,128)(2,1)S(1)}, u32[]{:S(2)}, u32[]{:S(2)}) collective-permute-start(bf16[4,128,1024]{2,1,0:T(8,128)(2,1)S(1)} %get-tuple-element.46), channel_id=1, source_target_pairs={{0,8},{1,25},{8,0},{9,17},{16,24},{17,9},{24,16},{25,1},{2,10},{3,... | collective-permute-start | bytes 3145736 | tf_op jit(solution)/shard_map/ppermute | solution.py:313
  46.7 14.9 %collective-permute-start.5 = (bf16[4,128,1024]{2,1,0:T(8,128)(2,1)S(1)}, bf16[4,128,1024]{2,1,0:T(8,128)(2,1)S(1)}, u32[]{:S(2)}, u32[]{:S(2)}) collective-permute-start(bf16[4,128,1024]{2,1,0:T(8,128)(2,1)S(1)} %get-tuple-element.48), channel_id=1, source_target_pairs={{0,64},{1,193},{64,0},{65,129},{128,192},{129,65},{192,128},{193,1... | collective-permute-start | bytes 3145736 | tf_op jit(solution)/shard_map/ppermute | solution.py:313
  59.9 3.3 %copy-start.12 = (bf16[2,4,128,1024]{3,2,1,0:T(8,128)(2,1)}, bf16[2,4,128,1024]{3,2,1,0:T(8,128)(2,1)S(1)}, u32[]{:S(2)}) copy-start(bf16[2,4,128,1024]{3,2,1,0:T(8,128)(2,1)S(1)} %pad_maximum_fusion.1.refs_2_) | copy-start | bytes 6291460
  59.9 26.2 %collective-permute-start.10 = (bf16[2,4,128,1024]{3,2,1,0:T(8,128)(2,1)S(1)}, bf16[2,4,128,1024]{3,2,1,0:T(8,128)(2,1)}, u32[]{:S(2)}, u32[]{:S(2)}) collective-permute-start(bf16[2,4,128,1024]{3,2,1,0:T(8,128)(2,1)S(1)} %pad_maximum_fusion.1.refs_2_), channel_id=1, source_target_pairs={{0,24},{1,9},{8,16},{9,1},{16,8},{17,25},{24,0},{25,17},{2,26},{3,... | collective-permute-start | bytes 6291464 | tf_op jit(solution)/shard_map/ppermute | solution.py:313
  61.6 4.4 %copy-start.15 = (bf16[32,128]{1,0:T(8,128)(2,1)S(1)}, bf16[32,128]{1,0:T(8,128)(2,1)}, u32[]{:S(2)}) copy-start(bf16[32,128]{1,0:T(8,128)(2,1)} %param.15) | copy-start | bytes 24580
  61.6 5.0 %copy-start.18 = (f32[512]{0:T(512)S(1)}, f32[512]{0:T(512)}, u32[]{:S(2)}) copy-start(f32[512]{0:T(512)} %param.16) | copy-start | bytes 6148
  61.6 5.1 %copy-start.16 = (s32[4]{0:T(128)S(1)}, s32[4]{0:T(128)}, u32[]{:S(2)}) copy-start(s32[4]{0:T(128)} %constant.44.clone) | copy-start | bytes 52
  61.6 5.1 %copy-start.17 = (s32[4]{0:T(128)S(1)}, s32[4]{0:T(128)}, u32[]{:S(2)}) copy-start(s32[4]{0:T(128)} %constant.45.clone) | copy-start | bytes 52
  61.6 5.2 %copy-start.14 = (f32[3,3,512]{2,1,0:T(4,128)S(1)}, f32[3,3,512]{2,1,0:T(4,128)}, u32[]{:S(2)}) copy-start(f32[3,3,512]{2,1,0:T(4,128)} %param.14) | copy-start | bytes 55300
  63.1 27.6 %collective-permute-start.6 = (bf16[2,4,128,1024]{3,2,1,0:T(8,128)(2,1)}, bf16[2,4,128,1024]{3,2,1,0:T(8,128)(2,1)}, u32[]{:S(2)}, u32[]{:S(2)}) collective-permute-start(bf16[2,4,128,1024]{3,2,1,0:T(8,128)(2,1)} %pad_maximum_fusion.refs_0_), channel_id=1, source_target_pairs={{0,192},{1,65},{64,128},{65,1},{128,64},{129,193},{192,0},{193,129... | collective-permute-start | bytes 6291464 | tf_op jit(solution)/shard_map/ppermute | solution.py:313
  66.8 40.5 %copy-start.7 = (s32[10]{0:T(128)}, s32[10]{0:T(128)S(1)}, u32[]{:S(2)}) copy-start(s32[10]{0:T(128)S(1)} %pad_add_fusion.at_ref) | copy-start | bytes 124
  107.3 0.7 copy-start.4
  108.0 1.4 copy-start.5
  109.4 1.2 copy-start.2
  110.6 5.8 %collective-permute-start.13 = (bf16[2,256,256]{2,1,0:T(8,128)(2,1)S(1)}, bf16[2,256,256]{2,1,0:T(8,128)(2,1)}, u32[]{:S(2)}, u32[]{:S(2)}) collective-permute-start(bf16[2,256,256]{2,1,0:T(8,128)(2,1)S(1)} %mix.2.mine_ref), channel_id=1, source_target_pairs={{0,1},{1,0},{2,3},{3,2},{4,5},{5,4},{6,7},{7,6},{8,9},{9,8},{10,11... | collective-permute-start | bytes 786440 | tf_op jit(solution)/shard_map/ppermute | solution.py:389
  111.8 8.7 %collective-permute-start.11 = (bf16[144,256]{1,0:T(8,128)(2,1)S(1)}, bf16[144,256]{1,0:T(8,128)(2,1)S(1)}, u32[]{:S(2)}, u32[]{:S(2)}) collective-permute-start(bf16[144,256]{1,0:T(8,128)(2,1)S(1)} %get-tuple-element.62), channel_id=1, source_target_pairs={{0,8},{8,16},{16,24},{24,64},{64,72},{72,80},{80,88},{88,128},{128... | collective-permute-start | bytes 221192 | tf_op jit(solution)/shard_map/ppermute | solution.py:384
  115.1 5.3 %collective-permute-start.12 = (bf16[144,256]{1,0:T(8,128)(2,1)S(1)}, bf16[144,256]{1,0:T(8,128)(2,1)S(1)}, u32[]{:S(2)}, u32[]{:S(2)}) collective-permute-start(bf16[144,256]{1,0:T(8,128)(2,1)S(1)} %get-tuple-element.61), channel_id=1, source_target_pairs={{0,8},{8,16},{16,24},{24,0},{64,72},{72,80},{80,88},{88,64},{128,1... | collective-permute-start | bytes 221192 | tf_op jit(solution)/shard_map/ppermute | solution.py:385
  116.4 0.6 copy-start.8
  117.0 3.5 %copy-start.6 = (bf16[144,256]{1,0:T(8,128)(2,1)S(1)}, bf16[144,256]{1,0:T(8,128)(2,1)}, u32[]{:S(2)}) copy-start(bf16[144,256]{1,0:T(8,128)(2,1)} %copy-done.5) | copy-start | bytes 221188
  117.0 3.5 %copy-start.3 = (bf16[3,2,512,256]{3,2,1,0:T(8,128)(2,1)S(1)}, bf16[3,2,512,256]{3,2,1,0:T(8,128)(2,1)}, u32[]{:S(2)}) copy-start(bf16[3,2,512,256]{3,2,1,0:T(8,128)(2,1)} %copy-done.2) | copy-start | bytes 4718596
  120.5 3.2 %copy-start.9 = (s32[10]{0:T(128)S(1)}, s32[10]{0:T(128)}, u32[]{:S(2)}) copy-start(s32[10]{0:T(128)} %copy-done.7) | copy-start | bytes 124
  122.0 1.6 collective-permute-start.14
  126.1 2.0 copy-start.1
  128.1 62.2 %copy-start.11 = (bf16[512,512]{1,0:T(8,128)(2,1)S(1)}, bf16[512,512]{1,0:T(8,128)(2,1)}, u32[]{:S(2)}) copy-start(bf16[512,512]{1,0:T(8,128)(2,1)} %param.10) | copy-start | bytes 1572868
Sparse Core Ops, SparseCore 0:
  27.7 64.4 all-gather.2
  128.2 62.0 reduce-scatter.1
